TPU v7x, 32 devices: a whole 2x2x4 slice. The times are simulated.
32 devices in a mesh: sx: 16 (over z, x, core), sy: 2 (over y).
Axes of the slice: x: 2, y: 2, z: 4, core: 2. Of those that a mesh axis runs over, the one named last changes fastest.
Arguments:
- object_field: float32 [2, 2048, 1024], P(None, 'sx', 'sy'), may hold values from -6 to 6
- probe_field: float32 [2, 256, 256], replicated, may hold values from -4.2 to 4.2
- amplitudes: float32 [16, 2, 2, 256, 256], P('sx', 'sy'), may hold values from 0 to 2
- centres: int32 [16, 2, 2, 2], P('sx', 'sy'), may hold values from 0 to 511, as said below
- counts: int32 [16, 2], P(None, 'sy'), may hold values from 1 to 2, as said below
Outputs:
- object_next: float32 [2, 2048, 1024], P(None, 'sx', 'sy')
Inputs may be any that keep to these rules, and one draw needn't show every extreme that they name: centres[s, t, k, 0] is below 128 and centres[s, t, k, 1] below 512; slots from counts[s, t] on are unused. A device's live positions are its first counts[s, t] slots; 2 is reached in every draw.
All inputs are finite; a program needn't handle non-finite values.
Results may differ from a plain program's by a relative error of at most 0.0003.
Values sent between devices are 32-bit elements; how exact they have to be, the bound alone decides.
No kernel may reach another device: no remote copies, remote signals or barrier semaphores. Data moves between devices by JAX's collectives and lax.ppermute only.
A program may use at most 128 MiB of HBM per device.

v0:
```python
import math

import jax
import jax.numpy as jnp
from jax import lax
from jax.sharding import PartitionSpec as P

ITERS = 2


SMOOTH = 1.0
DAMPING = 1.0


def with_halo(cells, sides, width):
    for axis, dim in sides:
        count = lax.axis_size(axis)
        ends = count - 1
        head = lax.slice_in_dim(cells, 0, width, axis=dim)
        tail = lax.slice_in_dim(cells, cells.shape[dim] - width, cells.shape[dim], axis=dim)
        cells = jnp.concatenate(
            [
                lax.ppermute(tail, axis, [(i, (i + 1) % count) for i in range(ends)]),
                cells,
                lax.ppermute(head, axis, [((i + 1) % count, i) for i in range(ends)]),
            ],
            axis=dim,
        )
    return cells


def dft_tables(length):
    index_values = jnp.arange(length, dtype=jnp.int32)
    product_mod = index_values[:, None] * index_values[None, :] % length
    angles = product_mod.astype(jnp.float32) * (2.0 * math.pi / length)
    scaling = 1.0 / math.sqrt(length)
    return (jnp.cos(angles) * scaling, -jnp.sin(angles) * scaling)


def matmul_exact(left_side, right_side):
    return jnp.dot(left_side, right_side, precision=lax.Precision.HIGHEST)


def complex_left(table_real, table_imag, field_real, field_imag):
    out_real = matmul_exact(table_real, field_real) - matmul_exact(table_imag, field_imag)
    out_imag = matmul_exact(table_real, field_imag) + matmul_exact(table_imag, field_real)
    return (out_real, out_imag)


def complex_right(field_real, field_imag, table_real, table_imag):
    out_real = matmul_exact(field_real, table_real) - matmul_exact(field_imag, table_imag)
    out_imag = matmul_exact(field_real, table_imag) + matmul_exact(field_imag, table_real)
    return (out_real, out_imag)


def position_gradient(object_patch, probe_field, amplitude, table_real, table_imag):
    probe_real = probe_field[0]
    probe_imag = probe_field[1]
    exit_real = probe_real * object_patch[0] - probe_imag * object_patch[1]
    exit_imag = probe_real * object_patch[1] + probe_imag * object_patch[0]
    half_real, half_imag = complex_left(table_real, table_imag, exit_real, exit_imag)
    far_real, far_imag = complex_right(half_real, half_imag, table_real, table_imag)
    factor = 1.0 - amplitude / jnp.sqrt(far_real * far_real + far_imag * far_imag + SMOOTH)
    miss_real = far_real * factor
    miss_imag = far_imag * factor
    back_real, back_imag = complex_left(table_real, -table_imag, miss_real, miss_imag)
    near_real, near_imag = complex_right(back_real, back_imag, table_real, -table_imag)
    return jnp.stack(
        [
            probe_real * near_real + probe_imag * near_imag,
            probe_real * near_imag - probe_imag * near_real,
        ]
    )


def add_patch(canvas, patch_values, corner_row, corner_col):
    zero_index = jnp.zeros((), jnp.int32)
    starts = (zero_index, corner_row, corner_col)
    present = lax.dynamic_slice(canvas, starts, patch_values.shape)
    return lax.dynamic_update_slice(canvas, present + patch_values, starts)


def fold_rows(extended, margin, length):
    middle_part = extended[:, 2 * margin : 2 * margin + length]
    upper_rim = extended[:, :margin]
    lower_rim = extended[:, extended.shape[1] - margin :]
    middle_part = middle_part.at[:, :margin].add(upper_rim)
    return middle_part.at[:, length - margin :].add(lower_rim)


def fold_cols(extended, margin, length):
    middle_part = extended[:, :, 2 * margin : 2 * margin + length]
    left_rim = extended[:, :, :margin]
    right_rim = extended[:, :, extended.shape[2] - margin :]
    middle_part = middle_part.at[:, :, :margin].add(left_rim)
    return middle_part.at[:, :, length - margin :].add(right_rim)


def settle(stacked, margin, block_rows, block_cols):
    full_ext = with_halo(stacked, (("sx", 1), ("sy", 2)), margin)
    return fold_cols(fold_rows(full_ext, margin, block_rows), margin, block_cols)


def local_pass(canvas, extended, spots, own_amps, probe_field, table_real, table_imag, upper_bound):
    size_probe = probe_field.shape[1]

    def local_step(slot_index, canvas_state):
        row_start = spots[slot_index, 0]
        col_start = spots[slot_index, 1]
        zero_index = jnp.zeros((), jnp.int32)
        object_patch = lax.dynamic_slice(
            extended, (zero_index, row_start, col_start), (2, size_probe, size_probe)
        )
        update = position_gradient(
            object_patch, probe_field, own_amps[slot_index], table_real, table_imag
        )
        return add_patch(canvas_state, update, row_start, col_start)

    return lax.fori_loop(0, upper_bound, local_step, canvas)


def on_device(object_field, probe_field, amplitudes, centres, counts):
    size_probe = probe_field.shape[1]
    margin = size_probe // 2
    block_rows = object_field.shape[1]
    block_cols = object_field.shape[2]
    table_real, table_imag = dft_tables(size_probe)
    spots = centres[0, 0]
    own_amps = amplitudes[0, 0]
    sx_size = lax.axis_size("sx")
    sx_index = lax.axis_index("sx")
    column_counts = counts[:, 0]
    sx_positions = jnp.arange(sx_size, dtype=jnp.int32)
    own_count = jnp.sum(jnp.where(sx_positions == sx_index, column_counts, 0))
    ext_shape = (block_rows + size_probe, block_cols + size_probe)
    spot_power = (probe_field[0] * probe_field[0] + probe_field[1] * probe_field[1])[None]

    def add_power(slot_index, canvas_state):
        return add_patch(canvas_state, spot_power, spots[slot_index, 0], spots[slot_index, 1])

    power_ext = lax.fori_loop(0, own_count, add_power, jnp.zeros((1,) + ext_shape, jnp.float32))
    current = object_field
    for sweep_index in range(ITERS):
        extended = with_halo(current, (("sx", 1), ("sy", 2)), margin)
        canvas = jnp.zeros((2,) + ext_shape, jnp.float32)
        canvas = local_pass(
            canvas, extended, spots, own_amps, probe_field, table_real, table_imag, own_count
        )
        if sweep_index == 0:
            settled = settle(
                jnp.concatenate([canvas, power_ext], axis=0), margin, block_rows, block_cols
            )
            illumination = settled[2]
            gradient = settled[0:2]
        else:
            gradient = settle(canvas, margin, block_rows, block_cols)
        current = current - gradient / (illumination + DAMPING)
    return current


def solution(mesh):
    return jax.shard_map(
        on_device,
        mesh=mesh,
        in_specs=(
            P(None, "sx", "sy"),
            P(),
            P("sx", "sy", None, None, None),
            P("sx", "sy", None, None),
            P(None, "sy"),
        ),
        out_specs=P(None, "sx", "sy"),
        check_vma=False,
    )
```

profile of v0, /device:TPU:10, one launch (start us, length us, event | category | flops | bytes accessed | tf_op | source)
XLA Modules:
  0.0 329.0 jit_solution(2610525772244669586)
XLA Ops:
  0.0 2.0 collective-permute-start
  2.1 3.6 %collective-permute-start.1 = (f32[2,128,512]{2,1,0:T(8,128)}, f32[2,128,512]{2,1,0:T(8,128)S(1)}, u32[]{:S(2)}, u32[]{:S(2)}) collective-permute-start(f32[2,128,512]{2,1,0:T(8,128)} %param.35), channel_id=1, source_target_pairs={{2,0},{4,2},{6,4},{8,6},{10,8},{12,10},{14,12},{16,14},{18,16},{20... | collective-permute-start | bytes 1572872 | tf_op jit(solution)/shard_map/ppermute | solution.py:25
  8.1 8.5 %collective-permute-done = f32[2,128,512]{2,1,0:T(8,128)} collective-permute-done((f32[2,128,512]{2,1,0:T(8,128)}, f32[2,128,512]{2,1,0:T(8,128)}, u32[]{:S(2)}, u32[]{:S(2)}) %collective-permute-start) | collective-permute-done | bytes 524320 | tf_op jit(solution)/shard_map/ppermute | solution.py:23
  18.7 4.2 %collective-permute-start.2 = (f32[2,384,128]{2,1,0:T(8,128)}, f32[2,384,128]{2,1,0:T(8,128)}, u32[]{:S(2)}, u32[]{:S(2)}) collective-permute-start(f32[2,384,128]{2,1,0:T(8,128)} %get-tuple-element.608), channel_id=1, source_target_pairs={{0,1},{2,3},{4,5},{6,7},{8,9},{10,11},{12,13},{14,15},{16,17},{18,... | collective-permute-start | bytes 1179656 | tf_op jit(solution)/shard_map/ppermute | solution.py:23
  24.2 9.2 %while.48 = (s32[]{:T(128)}, f32[1,384,768]{2,1,0:T(8,128)S(1)}, s32[]{:T(128)}, s32[2,2]{1,0:T(2,128)S(1)}, f32[1,256,256]{2,1,0:T(8,128)S(1)}, /*index=5*/s32[...) while((s32[]{:T(128)}, f32[1,384,768]{2,1,0:T(8,128)S(1)}, s32[]{:T(128)}, s32[2,2]{1,0:T(2,128)S(1)}, ...), condition=%wide.region_4.5_spmd, body=%wide.region_3.4_spmd.sunk | while | flops 65547 | bytes 1310955 | solution.py:141
  29.4 3.5 %dynamic_update_slice.18 = f32[1,384,768]{2,1,0:T(8,128)S(1)} dynamic-update-slice(f32[1,384,768]{2,1,0:T(8,128)S(1)} %get-tuple-element.816, f32[1,256,256]{2,1,0:T(8,128)S(1)} %dynamic-slice_add_fusion.2, s32[]{:T(128)} %constant.291.clone.1..sunk, s32[]{:T(128)S(6)} %select_n.278, s32[]{:T(128)S(6)} %select_n.279) | dynamic-update-slice | bytes 524292 | tf_op jit(solution)/shard_map/while/body/dynamic_update_slice | solution.py:80
  34.4 2.7 pad_maximum_fusion
  38.2 39.3 %while.49 = (s32[]{:T(128)}, f32[2,384,768]{2,1,0:T(8,128)S(1)}, s32[]{:T(128)}, s32[2,2]{1,0:T(2,128)S(1)}, f32[2,256,256]{2,1,0:T(8,128)S(1)}, /*index=5*/f32[...) while((s32[]{:T(128)}, f32[2,384,768]{2,1,0:T(8,128)S(1)}, ...), condition=%wide.region_2.3_spmd.clone.clone, body=%wide.region_1.2_spmd.clone.clone.sunk | while | flops 3239837696 | bytes 16515359 | solution.py:119
  55.1 2.4 fusion.362
  69.6 6.9 %dynamic_update_slice.19 = f32[2,384,768]{2,1,0:T(8,128)S(1)} dynamic-update-slice(f32[2,384,768]{2,1,0:T(8,128)S(1)} %get-tuple-element.780, f32[2,256,256]{2,1,0:T(8,128)S(1)} %maximum_add_fusion.6, s32[]{:T(128)} %constant.291.clone.1..sunk.1, s32[]{:T(128)S(6)} %select_n.297, s32[]{:T(128)S(6)} %select_n.298) | dynamic-update-slice | bytes 1048580 | tf_op jit(solution)/shard_map/while/body/dynamic_update_slice | solution.py:80
  79.1 1.9 collective-permute-start.4
  81.0 55.0 %collective-permute-start.5 = (f32[3,128,768]{2,1,0:T(8,128)S(1)}, f32[3,128,768]{2,1,0:T(8,128)S(1)}, u32[]{:S(2)}, u32[]{:S(2)}) collective-permute-start(f32[3,128,768]{2,1,0:T(8,128)S(1)} %get-tuple-element.603), channel_id=1, source_target_pairs={{2,0},{4,2},{6,4},{8,6},{10,8},{12,10},{14,12},{16,14},{18,16},{20... | collective-permute-start | bytes 3538952 | tf_op jit(solution)/shard_map/ppermute | solution.py:25
  136.0 11.9 %collective-permute-done.4 = f32[3,128,768]{2,1,0:T(8,128)S(1)} collective-permute-done((f32[3,128,768]{2,1,0:T(8,128)S(1)}, f32[3,128,768]{2,1,0:T(8,128)S(1)}, u32[]{:S(2)}, u32[]{:S(2)}) %collective-permute-start.4) | collective-permute-done | bytes 1179680 | tf_op jit(solution)/shard_map/ppermute | solution.py:23
  147.9 10.6 %collective-permute-done.5 = f32[3,128,768]{2,1,0:T(8,128)S(1)} collective-permute-done((f32[3,128,768]{2,1,0:T(8,128)S(1)}, f32[3,128,768]{2,1,0:T(8,128)S(1)}, u32[]{:S(2)}, u32[]{:S(2)}) %collective-permute-start.5) | collective-permute-done | bytes 1179680 | tf_op jit(solution)/shard_map/ppermute | solution.py:25
  158.6 3.1 collective-permute-start.6
  163.0 13.0 %collective-permute-done.6 = f32[3,640,128]{2,1,0:T(8,128)S(1)} collective-permute-done((f32[3,640,128]{2,1,0:T(8,128)S(1)}, f32[3,640,128]{2,1,0:T(8,128)S(1)}, u32[]{:S(2)}, u32[]{:S(2)}) %collective-permute-start.6) | collective-permute-done | bytes 983072 | tf_op jit(solution)/shard_map/ppermute | solution.py:23
  176.0 4.2 %collective-permute-done.7 = f32[3,640,128]{2,1,0:T(8,128)S(1)} collective-permute-done((f32[3,640,128]{2,1,0:T(8,128)S(1)}, f32[3,640,128]{2,1,0:T(8,128)S(1)}, u32[]{:S(2)}, u32[]{:S(2)}) %collective-permute-start.7) | collective-permute-done | bytes 983072 | tf_op jit(solution)/shard_map/ppermute | solution.py:25
  182.9 1.9 collective-permute-start.8
  184.9 3.6 %collective-permute-start.9 = (f32[2,128,512]{2,1,0:T(8,128)S(1)}, f32[2,128,512]{2,1,0:T(8,128)S(1)}, u32[]{:S(2)}, u32[]{:S(2)}) collective-permute-start(f32[2,128,512]{2,1,0:T(8,128)S(1)} %fusion.228), channel_id=1, source_target_pairs={{2,0},{4,2},{6,4},{8,6},{10,8},{12,10},{14,12},{16,14},{18,16},{20... | collective-permute-start | bytes 1572872 | tf_op jit(solution)/shard_map/ppermute | solution.py:25
  188.5 10.5 %collective-permute-done.8 = f32[2,128,512]{2,1,0:T(8,128)S(1)} collective-permute-done((f32[2,128,512]{2,1,0:T(8,128)S(1)}, f32[2,128,512]{2,1,0:T(8,128)S(1)}, u32[]{:S(2)}, u32[]{:S(2)}) %collective-permute-start.8) | collective-permute-done | bytes 524320 | tf_op jit(solution)/shard_map/ppermute | solution.py:23
  202.6 4.3 %collective-permute-done.10 = f32[2,384,128]{2,1,0:T(8,128)S(1)} collective-permute-done((f32[2,384,128]{2,1,0:T(8,128)}, f32[2,384,128]{2,1,0:T(8,128)S(1)}, u32[]{:S(2)}, u32[]{:S(2)}) %collective-permute-start.10) | collective-permute-done | bytes 393248 | tf_op jit(solution)/shard_map/ppermute | solution.py:23
  206.9 4.1 %collective-permute-done.11 = f32[2,384,128]{2,1,0:T(8,128)S(1)} collective-permute-done((f32[2,384,128]{2,1,0:T(8,128)S(1)}, f32[2,384,128]{2,1,0:T(8,128)S(1)}, u32[]{:S(2)}, u32[]{:S(2)}) %collective-permute-start.11) | collective-permute-done | bytes 393248 | tf_op jit(solution)/shard_map/ppermute | solution.py:25
  212.8 38.9 %while.50 = (s32[]{:T(128)}, f32[2,384,768]{2,1,0:T(8,128)S(1)}, s32[]{:T(128)}, s32[2,2]{1,0:T(2,128)S(1)}, f32[2,256,256]{2,1,0:T(8,128)S(1)}, /*index=5*/f32[...) while((s32[]{:T(128)}, f32[2,384,768]{2,1,0:T(8,128)S(1)}, ...), condition=%wide.region_6.7_spmd.clone.clone, body=%wide.region_5.6_spmd.clone.clone.sunk | while | flops 3239837696 | bytes 16515359 | solution.py:119
  229.4 2.4 fusion.393
  243.9 6.9 %dynamic_update_slice.20 = f32[2,384,768]{2,1,0:T(8,128)S(1)} dynamic-update-slice(f32[2,384,768]{2,1,0:T(8,128)S(1)} %get-tuple-element.849, f32[2,256,256]{2,1,0:T(8,128)S(1)} %maximum_add_fusion.7, s32[]{:T(128)} %constant.291.clone.1..sunk.2, s32[]{:T(128)S(6)} %select_n.316, s32[]{:T(128)S(6)} %select_n.317) | dynamic-update-slice | bytes 1048580 | tf_op jit(solution)/shard_map/while/body/dynamic_update_slice | solution.py:80
  251.7 1.9 collective-permute-start.12
  253.7 42.3 %collective-permute-start.13 = (f32[2,128,768]{2,1,0:T(8,128)S(1)}, f32[2,128,768]{2,1,0:T(8,128)S(1)}, u32[]{:S(2)}, u32[]{:S(2)}) collective-permute-start(f32[2,128,768]{2,1,0:T(8,128)S(1)} %get-tuple-element.604), channel_id=1, source_target_pairs={{2,0},{4,2},{6,4},{8,6},{10,8},{12,10},{14,12},{16,14},{18,16},{20... | collective-permute-start | bytes 2359304 | tf_op jit(solution)/shard_map/ppermute | solution.py:25
  295.9 7.7 %collective-permute-done.12 = f32[2,128,768]{2,1,0:T(8,128)S(1)} collective-permute-done((f32[2,128,768]{2,1,0:T(8,128)S(1)}, f32[2,128,768]{2,1,0:T(8,128)S(1)}, u32[]{:S(2)}, u32[]{:S(2)}) %collective-permute-start.12) | collective-permute-done | bytes 786464 | tf_op jit(solution)/shard_map/ppermute | solution.py:23
  303.9 5.0 %collective-permute-done.13 = f32[2,128,768]{2,1,0:T(8,128)S(1)} collective-permute-done((f32[2,128,768]{2,1,0:T(8,128)S(1)}, f32[2,128,768]{2,1,0:T(8,128)S(1)}, u32[]{:S(2)}, u32[]{:S(2)}) %collective-permute-start.13) | collective-permute-done | bytes 786464 | tf_op jit(solution)/shard_map/ppermute | solution.py:25
  309.0 2.5 collective-permute-start.14
  312.9 9.4 %collective-permute-done.14 = f32[2,640,128]{2,1,0:T(8,128)S(1)} collective-permute-done((f32[2,640,128]{2,1,0:T(8,128)S(1)}, f32[2,640,128]{2,1,0:T(8,128)S(1)}, u32[]{:S(2)}, u32[]{:S(2)}) %collective-permute-start.14) | collective-permute-done | bytes 655392 | tf_op jit(solution)/shard_map/ppermute | solution.py:23
  322.3 4.2 %collective-permute-done.15 = f32[2,640,128]{2,1,0:T(8,128)S(1)} collective-permute-done((f32[2,640,128]{2,1,0:T(8,128)S(1)}, f32[2,640,128]{2,1,0:T(8,128)S(1)}, u32[]{:S(2)}, u32[]{:S(2)}) %collective-permute-start.15) | collective-permute-done | bytes 655392 | tf_op jit(solution)/shard_map/ppermute | solution.py:25
  (98 shorter events, 72.1 us)
Async XLA Ops:
  0.0 17.6 %copy-start.7 = (f32[2,128,512]{2,1,0:T(8,128)S(1)}, f32[2,128,512]{2,1,0:T(8,128)}, u32[]{:S(2)}) copy-start(f32[2,128,512]{2,1,0:T(8,128)} %param.35) | copy-start | bytes 1572868
  0.0 16.6 %collective-permute-start = (f32[2,128,512]{2,1,0:T(8,128)}, f32[2,128,512]{2,1,0:T(8,128)}, u32[]{:S(2)}, u32[]{:S(2)}) collective-permute-start(f32[2,128,512]{2,1,0:T(8,128)} %param.35), channel_id=1, source_target_pairs={{0,2},{2,4},{4,6},{6,8},{8,10},{10,12},{12,14},{14,16},{16,18},{18... | collective-permute-start | bytes 1572872 | tf_op jit(solution)/shard_map/ppermute | solution.py:23
  2.1 15.6 %collective-permute-start.1 = (f32[2,128,512]{2,1,0:T(8,128)}, f32[2,128,512]{2,1,0:T(8,128)S(1)}, u32[]{:S(2)}, u32[]{:S(2)}) collective-permute-start(f32[2,128,512]{2,1,0:T(8,128)} %param.35), channel_id=1, source_target_pairs={{2,0},{4,2},{6,4},{8,6},{10,8},{12,10},{14,12},{16,14},{18,16},{20... | collective-permute-start | bytes 1572872 | tf_op jit(solution)/shard_map/ppermute | solution.py:25
  17.7 6.5 %copy-start.9 = (s32[1,1,2,2]{3,2,1,0:T(2,128)S(1)}, s32[1,1,2,2]{3,2,1,0:T(2,128)}, u32[]{:S(2)}) copy-start(s32[1,1,2,2]{3,2,1,0:T(2,128)} %param.38) | copy-start | bytes 52
  18.7 14.8 %collective-permute-start.2 = (f32[2,384,128]{2,1,0:T(8,128)}, f32[2,384,128]{2,1,0:T(8,128)}, u32[]{:S(2)}, u32[]{:S(2)}) collective-permute-start(f32[2,384,128]{2,1,0:T(8,128)} %get-tuple-element.608), channel_id=1, source_target_pairs={{0,1},{2,3},{4,5},{6,7},{8,9},{10,11},{12,13},{14,15},{16,17},{18,... | collective-permute-start | bytes 1179656 | tf_op jit(solution)/shard_map/ppermute | solution.py:23
  22.9 10.7 %collective-permute-start.3 = (f32[2,384,128]{2,1,0:T(8,128)}, f32[2,384,128]{2,1,0:T(8,128)}, u32[]{:S(2)}, u32[]{:S(2)}) collective-permute-start(f32[2,384,128]{2,1,0:T(8,128)} %get-tuple-element.609), channel_id=1, source_target_pairs={{1,0},{3,2},{5,4},{7,6},{9,8},{11,10},{13,12},{15,14},{17,16},{19,... | collective-permute-start | bytes 1179656 | tf_op jit(solution)/shard_map/ppermute | solution.py:25
  33.4 1.0 copy-start.1
  37.2 1.0 copy-start
  77.5 1.3 copy-start.2
  79.1 68.8 %collective-permute-start.4 = (f32[3,128,768]{2,1,0:T(8,128)S(1)}, f32[3,128,768]{2,1,0:T(8,128)S(1)}, u32[]{:S(2)}, u32[]{:S(2)}) collective-permute-start(f32[3,128,768]{2,1,0:T(8,128)S(1)} %get-tuple-element.602), channel_id=1, source_target_pairs={{0,2},{2,4},{4,6},{6,8},{8,10},{10,12},{12,14},{14,16},{16,18},{18... | collective-permute-start | bytes 3538952 | tf_op jit(solution)/shard_map/ppermute | solution.py:23
  81.0 77.5 %collective-permute-start.5 = (f32[3,128,768]{2,1,0:T(8,128)S(1)}, f32[3,128,768]{2,1,0:T(8,128)S(1)}, u32[]{:S(2)}, u32[]{:S(2)}) collective-permute-start(f32[3,128,768]{2,1,0:T(8,128)S(1)} %get-tuple-element.603), channel_id=1, source_target_pairs={{2,0},{4,2},{6,4},{8,6},{10,8},{12,10},{14,12},{16,14},{18,16},{20... | collective-permute-start | bytes 3538952 | tf_op jit(solution)/shard_map/ppermute | solution.py:25
  158.6 17.4 %collective-permute-start.6 = (f32[3,640,128]{2,1,0:T(8,128)S(1)}, f32[3,640,128]{2,1,0:T(8,128)S(1)}, u32[]{:S(2)}, u32[]{:S(2)}) collective-permute-start(f32[3,640,128]{2,1,0:T(8,128)S(1)} %get-tuple-element.598), channel_id=1, source_target_pairs={{0,1},{2,3},{4,5},{6,7},{8,9},{10,11},{12,13},{14,15},{16,17},{18,... | collective-permute-start | bytes 2949128 | tf_op jit(solution)/shard_map/ppermute | solution.py:23
  161.7 18.5 %collective-permute-start.7 = (f32[3,640,128]{2,1,0:T(8,128)S(1)}, f32[3,640,128]{2,1,0:T(8,128)S(1)}, u32[]{:S(2)}, u32[]{:S(2)}) collective-permute-start(f32[3,640,128]{2,1,0:T(8,128)S(1)} %get-tuple-element.599), channel_id=1, source_target_pairs={{1,0},{3,2},{5,4},{7,6},{9,8},{11,10},{13,12},{15,14},{17,16},{19,... | collective-permute-start | bytes 2949128 | tf_op jit(solution)/shard_map/ppermute | solution.py:25
  181.8 1.0 copy-start.8
  182.8 17.1 %copy-start.5 = (f32[128,512]{1,0:T(8,128)}, f32[128,512]{1,0:T(8,128)S(1)}, u32[]{:S(2)}) copy-start(f32[128,512]{1,0:T(8,128)S(1)} %fusion.229) | copy-start | bytes 786436
  182.9 28.1 %copy-start.3 = (f32[2,128,512]{2,1,0:T(8,128)}, f32[2,128,512]{2,1,0:T(8,128)S(1)}, u32[]{:S(2)}) copy-start(f32[2,128,512]{2,1,0:T(8,128)S(1)} %fusion.228) | copy-start | bytes 1572868
  182.9 16.1 %collective-permute-start.8 = (f32[2,128,512]{2,1,0:T(8,128)S(1)}, f32[2,128,512]{2,1,0:T(8,128)S(1)}, u32[]{:S(2)}, u32[]{:S(2)}) collective-permute-start(f32[2,128,512]{2,1,0:T(8,128)S(1)} %fusion.228), channel_id=1, source_target_pairs={{0,2},{2,4},{4,6},{6,8},{8,10},{10,12},{12,14},{14,16},{16,18},{18... | collective-permute-start | bytes 1572872 | tf_op jit(solution)/shard_map/ppermute | solution.py:23
  184.9 14.2 %collective-permute-start.9 = (f32[2,128,512]{2,1,0:T(8,128)S(1)}, f32[2,128,512]{2,1,0:T(8,128)S(1)}, u32[]{:S(2)}, u32[]{:S(2)}) collective-permute-start(f32[2,128,512]{2,1,0:T(8,128)S(1)} %fusion.228), channel_id=1, source_target_pairs={{2,0},{4,2},{6,4},{8,6},{10,8},{12,10},{14,12},{16,14},{18,16},{20... | collective-permute-start | bytes 1572872 | tf_op jit(solution)/shard_map/ppermute | solution.py:25
  199.9 7.0 %collective-permute-start.10 = (f32[2,384,128]{2,1,0:T(8,128)}, f32[2,384,128]{2,1,0:T(8,128)S(1)}, u32[]{:S(2)}, u32[]{:S(2)}) collective-permute-start(f32[2,384,128]{2,1,0:T(8,128)} %get-tuple-element.606), channel_id=1, source_target_pairs={{0,1},{2,3},{4,5},{6,7},{8,9},{10,11},{12,13},{14,15},{16,17},{18,... | collective-permute-start | bytes 1179656 | tf_op jit(solution)/shard_map/ppermute | solution.py:23
  201.3 9.7 %collective-permute-start.11 = (f32[2,384,128]{2,1,0:T(8,128)S(1)}, f32[2,384,128]{2,1,0:T(8,128)S(1)}, u32[]{:S(2)}, u32[]{:S(2)}) collective-permute-start(f32[2,384,128]{2,1,0:T(8,128)S(1)} %get-tuple-element.607), channel_id=1, source_target_pairs={{1,0},{3,2},{5,4},{7,6},{9,8},{11,10},{13,12},{15,14},{17,16},{19,... | collective-permute-start | bytes 1179656 | tf_op jit(solution)/shard_map/ppermute | solution.py:25
  251.7 51.9 %collective-permute-start.12 = (f32[2,128,768]{2,1,0:T(8,128)S(1)}, f32[2,128,768]{2,1,0:T(8,128)S(1)}, u32[]{:S(2)}, u32[]{:S(2)}) collective-permute-start(f32[2,128,768]{2,1,0:T(8,128)S(1)} %get-tuple-element.605), channel_id=1, source_target_pairs={{0,2},{2,4},{4,6},{6,8},{8,10},{10,12},{12,14},{14,16},{16,18},{18... | collective-permute-start | bytes 2359304 | tf_op jit(solution)/shard_map/ppermute | solution.py:23
  253.7 55.2 %collective-permute-start.13 = (f32[2,128,768]{2,1,0:T(8,128)S(1)}, f32[2,128,768]{2,1,0:T(8,128)S(1)}, u32[]{:S(2)}, u32[]{:S(2)}) collective-permute-start(f32[2,128,768]{2,1,0:T(8,128)S(1)} %get-tuple-element.604), channel_id=1, source_target_pairs={{2,0},{4,2},{6,4},{8,6},{10,8},{12,10},{14,12},{16,14},{18,16},{20... | collective-permute-start | bytes 2359304 | tf_op jit(solution)/shard_map/ppermute | solution.py:25
  309.0 13.2 %collective-permute-start.14 = (f32[2,640,128]{2,1,0:T(8,128)S(1)}, f32[2,640,128]{2,1,0:T(8,128)S(1)}, u32[]{:S(2)}, u32[]{:S(2)}) collective-permute-start(f32[2,640,128]{2,1,0:T(8,128)S(1)} %get-tuple-element.600), channel_id=1, source_target_pairs={{0,1},{2,3},{4,5},{6,7},{8,9},{10,11},{12,13},{14,15},{16,17},{18,... | collective-permute-start | bytes 1966088 | tf_op jit(solution)/shard_map/ppermute | solution.py:23
  311.6 14.8 %collective-permute-start.15 = (f32[2,640,128]{2,1,0:T(8,128)S(1)}, f32[2,640,128]{2,1,0:T(8,128)S(1)}, u32[]{:S(2)}, u32[]{:S(2)}) collective-permute-start(f32[2,640,128]{2,1,0:T(8,128)S(1)} %get-tuple-element.601), channel_id=1, source_target_pairs={{1,0},{3,2},{5,4},{7,6},{9,8},{11,10},{13,12},{15,14},{17,16},{19,... | collective-permute-start | bytes 1966088 | tf_op jit(solution)/shard_map/ppermute | solution.py:25
  326.7 1.0 copy-start.4
  326.7 1.1 copy-start.6
where the time goes:
time: 333 us; the launch traced here: 329 us
  starting transfers between devices  129 us (39%)
  waiting for transfers between devices  93.4 us (28%)
  matrix products  49.1 us (15%)
  local copies, waits for them, and re-layouts  27.5 us (8%)
  loops' own time  15.8 us (5%)
  other arithmetic  13.7 us (4%)
    ppermute x8, starting transfers between devices, with_halo(): lax.ppermute(head, axis, [((i + 1) % count, i) for i in range(ends)])  110 us
    ppermute x8, waiting for transfers between devices, with_halo(): lax.ppermute(tail, axis, [(i, (i + 1) % count) for i in range(ends)])  65.4 us
    dot_general x32, matrix products, matmul_exact(): return jnp.dot(left_side, right_side, precision=lax.Precision.HIGHEST)  49.1 us
    ppermute x8, waiting for transfers between devices, with_halo(): lax.ppermute(head, axis, [((i + 1) % count, i) for i in range(ends)])  28 us
    ppermute x8, starting transfers between devices, with_halo(): lax.ppermute(tail, axis, [(i, (i + 1) % count) for i in range(ends)])  19.1 us
    dynamic_update_slice x3, local copies, waits for them, and re-layouts, add_patch(): return lax.dynamic_update_slice(canvas, present + patch_values, starts)  17.3 us
    another operation x2, loops' own time, local_pass(): return lax.fori_loop(0, upper_bound, local_step, canvas)  10.9 us
  transfers between devices with their start and end apart: 16, of which 13 were waited for; matrix products, arithmetic and copies ran while one was open for 2% of the time, Pallas kernels for 0%

commit v1 on v0

v1 whole, which is shorter than its diff:
```python
import math

import jax
import jax.numpy as jnp
import ml_dtypes
import numpy as np
from jax import lax
from jax.experimental import pallas as pl
from jax.experimental.pallas import tpu as pltpu
from jax.sharding import PartitionSpec as P

ITERS = 2
SMOOTH = 1.0
DAMPING = 1.0
LANES = 128
INFO = 8
VMEM_BYTES = 32 * 1024 * 1024

VMEM = pl.BlockSpec(memory_space=pltpu.VMEM)
SMEM = pl.BlockSpec(memory_space=pltpu.SMEM)


def split_numpy(table):
    high = table.astype(np.float32).astype(ml_dtypes.bfloat16)
    low = (table - high.astype(np.float64)).astype(ml_dtypes.bfloat16)
    return high, low


def dft_tables(length):
    half = length // 2
    index = np.arange(half)
    tables = []
    for parity in range(2):
        angles = 2.0 * math.pi / length * (index[:, None] * (2 * index[None, :] + parity) % length)
        cosine = np.cos(angles) / math.sqrt(length)
        sine = np.sin(angles) / math.sqrt(length)
        forward = np.block([[cosine, -sine], [sine, cosine]])
        tables.append([split_numpy(forward), split_numpy(forward.T)])
    return np.array(tables, dtype=ml_dtypes.bfloat16)


def parity_order(length):
    half = length // 2
    order = np.zeros((length, length))
    for index in range(length):
        order[index, index % 2 * half + index // 2] = 1.0
    return np.stack([order, order.T]).astype(ml_dtypes.bfloat16)


def split(values):
    high = values.astype(jnp.bfloat16)
    low = (values - high.astype(jnp.float32)).astype(jnp.bfloat16)
    return high, low


def times_table(values, table):
    high, low = split(values)
    left = jnp.concatenate([high, low, high], axis=1)
    right = jnp.concatenate([table[0], table[0], table[1]], axis=0)
    return jnp.dot(left, right, preferred_element_type=jnp.float32)


def table_times(table, values):
    high, low = split(values)
    left = jnp.concatenate([table[0], table[0], table[1]], axis=1)
    right = jnp.concatenate([high, low, high], axis=0)
    return jnp.dot(left, right, preferred_element_type=jnp.float32)


class Plan:
    def __init__(self, sx_size, sy_size, block_cols):
        self.sx_size = sx_size
        self.sy_size = sy_size
        self.own = block_cols // LANES
        self.tiles = self.own + 2
        self.paired = sy_size == 2
        self.sides = 1 if self.paired else 2

    def rights(self, t):
        return [1 - t] if self.paired else [0, 1]

    def pair_starts(self, t):
        return [right * (self.tiles - 2) for right in self.rights(t)]

    def halo_tiles(self, t):
        return [right * (self.tiles - 1) for right in self.rights(t)]

    def edge_tiles(self, t):
        return [1 + right * (self.tiles - 3) for right in self.rights(t)]

    def mid_start(self, t):
        return 1 + t if self.paired else 2

    @property
    def mid_tiles(self):
        return self.tiles - 3 if self.paired else self.tiles - 4

    def across(self, values, axis_name="sy"):
        if self.paired:
            return [lax.ppermute(values[0], axis_name, [(0, 1), (1, 0)])]
        ends = self.sy_size - 1
        return [
            lax.ppermute(values[1], axis_name, [(i, i + 1) for i in range(ends)]),
            lax.ppermute(values[0], axis_name, [(i + 1, i) for i in range(ends)]),
        ]

    def from_above(self, values):
        return lax.ppermute(values, "sx", [(i, i + 1) for i in range(self.sx_size - 1)])

    def from_below(self, values):
        return lax.ppermute(values, "sx", [(i + 1, i) for i in range(self.sx_size - 1)])


def lanes(tile, count=1):
    if isinstance(tile, int):
        return pl.ds(tile * LANES, count * LANES)
    return pl.ds(pl.multiple_of(tile * LANES, LANES), count * LANES)


def assemble(canvas, pieces, starts, tiles):
    blank = jnp.zeros(canvas.shape[:-1] + (LANES,), jnp.float32)
    canvas[:, :, lanes(0)] = blank
    canvas[:, :, lanes(tiles - 1)] = blank
    for piece, start in zip(pieces, starts):
        canvas[:, :, lanes(start, piece.shape[2] // LANES)] = piece[...]


def rows_at(ref, start, count):
    offset = start % 8
    values = ref[pl.ds(pl.multiple_of(start - offset, 8), count + 8)]
    return pltpu.roll(values, (count + 8 - offset) % (count + 8), 0)[:count]


def prepare_kernel(centres, probe, amps, order, rolled, ordered, padded):
    size = probe.shape[1]
    half = size // 2
    padded[:, :half] = jnp.zeros((2, half, size), jnp.float32)
    padded[:, half + size :] = jnp.zeros((2, half + 8, size), jnp.float32)
    padded[:, half : half + size] = probe[...]
    for slot in range(amps.shape[0]):
        row = centres[2 * slot]
        col = centres[2 * slot + 1]
        for part in range(2):
            shape = padded.at[part]
            upper = rows_at(shape, half - row, half) + rows_at(shape, half + size - row, half)
            lower = rows_at(shape, size - row, half)
            rolled[slot, part] = pltpu.roll(jnp.concatenate([upper, lower], axis=0), col % size, 1)
        high, low = split(amps[slot])
        across = jnp.dot(
            jnp.concatenate([high, low], axis=1),
            jnp.concatenate([order[0], order[0]], axis=0),
            preferred_element_type=jnp.float32,
        )
        high, low = split(across)
        ordered[slot] = jnp.dot(
            jnp.concatenate([order[1], order[1]], axis=1),
            jnp.concatenate([high, low], axis=0),
            preferred_element_type=jnp.float32,
        )


def light_kernel(plan, slots, place, info, probe, inverse, *rest):
    pairs = rest[: plan.sides]
    padded, canvas = rest[plan.sides :]
    size = probe.shape[1]
    half = size // 2
    s = place[0]
    t = place[1]
    padded[:half] = jnp.zeros((half, size), jnp.float32)
    padded[half + size :] = jnp.zeros((half + 8, size), jnp.float32)
    padded[half : half + size] = probe[0] * probe[0] + probe[1] * probe[1]
    canvas[...] = jnp.zeros(canvas.shape, jnp.float32)
    reach = 2 if plan.paired else 3
    spare = jnp.zeros((half, LANES), jnp.float32)
    for down in (-1, 0, 1):

        def add(step, carry, down=down):
            turn = step // slots
            slot = step % slots
            over = turn * (1 - 2 * t) if plan.paired else turn - 1
            there_s = s + down
            there_t = t + over
            inside = (there_s >= 0) & (there_s < plan.sx_size) & (there_t >= 0) & (there_t < plan.sy_size)
            base = (jnp.clip(there_s, 0, plan.sx_size - 1) * plan.sy_size + jnp.clip(there_t, 0, plan.sy_size - 1)) * INFO

            @pl.when(inside & (slot < info[base + 2 * slots]))
            def _():
                row = info[base + 2 * slot]
                col = info[base + 2 * slot + 1]
                power = rows_at(padded, size - half * down - row, half)
                shifted = pltpu.roll(jnp.concatenate([power, spare], axis=1), col % LANES, 1)
                first = col // LANES + plan.own * (over + 1)
                canvas[:, lanes(first, 3)] += shifted

            return carry

        lax.fori_loop(0, reach * slots, add, 0)
    result = 1.0 / (canvas[:, lanes(plan.own, plan.tiles)] + DAMPING)
    inverse[...] = result
    for pair, start in zip(pairs, plan.pair_starts(t)):
        pair[...] = inverse[:, lanes(start, 2)]


def term_kernel(plan, slot, starts, place, centres, counts, *rest):
    pieces = len(starts(0))
    above, own, below = (rest[k * pieces : (k + 1) * pieces] for k in range(3))
    probe, amps, tables, outer, inner, window, canvas = rest[3 * pieces :]
    size = probe.shape[2]
    half = size // 2
    s = place[0]
    t = place[1]
    row = centres[2 * slot]
    col = centres[2 * slot + 1]
    alive = slot < counts[s, 0]

    @pl.when(jnp.logical_not(alive))
    def _():
        outer[...] = jnp.zeros(outer.shape, jnp.float32)
        inner[...] = jnp.zeros(inner.shape, jnp.float32)

    @pl.when(alive)
    def _():
        tile = col // LANES
        first = tile % 2
        rest_col = col % LANES
        from_tile = lax.broadcasted_iota(jnp.int32, (half, LANES), 1) >= rest_col
        from_upper = lax.broadcasted_iota(jnp.int32, (half, LANES), 0) >= row
        for kind, source in enumerate((above, own, below)):
            assemble(canvas.at[kind], source, starts(t), plan.tiles)

        def pick(kind, part, index):
            return canvas[kind, part, :, lanes(index)]

        for part in range(2):
            edge = [jnp.where(from_tile, pick(kind, part, tile), pick(kind, part, tile + 2)) for kind in range(3)]
            middle = [pick(kind, part, tile + 1) for kind in range(3)]
            window[part, :half, lanes(first)] = jnp.where(from_upper, edge[0], edge[2])
            window[part, half:, lanes(first)] = edge[1]
            window[part, :half, lanes(1 - first)] = jnp.where(from_upper, middle[0], middle[2])
            window[part, half:, lanes(1 - first)] = middle[1]

        probe_real = probe[0, 0]
        probe_imag = probe[0, 1]
        exit_real = probe_real * window[0] - probe_imag * window[1]
        exit_imag = probe_real * window[1] + probe_imag * window[0]

        halves = [
            jnp.concatenate([exit_real[:, :half] + sign * exit_real[:, half:], exit_imag[:, :half] + sign * exit_imag[:, half:]], axis=1)
            for sign in (1.0, -1.0)
        ]
        across = [times_table(halves[parity], tables[parity, 0]) for parity in range(2)]
        real = jnp.concatenate([across[0][:, :half], across[1][:, :half]], axis=1)
        imag = jnp.concatenate([across[0][:, half:], across[1][:, half:]], axis=1)
        halves = [
            jnp.concatenate([real[:half] + sign * real[half:], imag[:half] + sign * imag[half:]], axis=0)
            for sign in (1.0, -1.0)
        ]
        back = []
        for parity in range(2):
            far = table_times(tables[parity, 1], halves[parity])
            far_real = far[:half]
            far_imag = far[half:]
            amplitude = amps[0, parity * half : (parity + 1) * half]
            factor = 1.0 - amplitude * lax.rsqrt(far_real * far_real + far_imag * far_imag + SMOOTH)
            miss = jnp.concatenate([far_real * factor, far_imag * factor], axis=0)
            back.append(table_times(tables[parity, 0], miss))
        real = jnp.concatenate([back[0][:half] + back[1][:half], back[0][:half] - back[1][:half]], axis=0)
        imag = jnp.concatenate([back[0][half:] + back[1][half:], back[0][half:] - back[1][half:]], axis=0)
        near = []
        for parity in range(2):
            picked = slice(parity * half, (parity + 1) * half)
            near.append(times_table(jnp.concatenate([real[:, picked], imag[:, picked]], axis=1), tables[parity, 1]))
        near_real = jnp.concatenate([near[0][:, :half] + near[1][:, :half], near[0][:, :half] - near[1][:, :half]], axis=1)
        near_imag = jnp.concatenate([near[0][:, half:] + near[1][:, half:], near[0][:, half:] - near[1][:, half:]], axis=1)
        term_real = probe_real * near_real + probe_imag * near_imag
        term_imag = probe_real * near_imag - probe_imag * near_real
        outer[0] = term_real[:half]
        outer[1] = term_imag[:half]
        inner[0] = term_real[half:]
        inner[1] = term_imag[half:]


def gather_terms(plan, slots, place, info, own, above, below, canvas):
    half = canvas.shape[1]
    s = place[0]
    t = place[1]
    canvas[...] = jnp.zeros(canvas.shape, jnp.float32)
    lane = lax.broadcasted_iota(jnp.int32, (half, LANES), 1)
    line = lax.broadcasted_iota(jnp.int32, (half, LANES), 0)
    for down, patches in ((0, own), (-1, above), (1, below)):
        base = (jnp.clip(s + down, 0, plan.sx_size - 1) * plan.sy_size + t) * INFO
        for slot in range(slots):
            row = info[base + 2 * slot]
            col = info[base + 2 * slot + 1]
            tile = col // LANES
            first = tile % 2
            from_tile = lane >= col % LANES
            if down == 0:
                left_rows = right_rows = None
            elif down == 1:
                left_rows = line >= row
            else:
                left_rows = line < row
            for part in range(2):
                edge = patches[slot][part, :, lanes(first)]
                middle = patches[slot][part, :, lanes(1 - first)]
                if left_rows is not None:
                    edge = jnp.where(left_rows, edge, 0.0)
                    middle = jnp.where(left_rows, middle, 0.0)
                canvas[part, :, lanes(tile)] += jnp.where(from_tile, edge, 0.0)
                canvas[part, :, lanes(tile + 1)] += middle
                canvas[part, :, lanes(tile + 2)] += jnp.where(from_tile, 0.0, edge)


def step_kernel(plan, slots, starts, place, info, *rest):
    patches = [rest[k * slots : (k + 1) * slots] for k in range(3)]
    rest = rest[3 * slots :]
    pieces = len(starts(0))
    own = rest[:pieces]
    inverse, middle = rest[pieces : pieces + 2]
    bases = rest[pieces + 2 : pieces + 2 + plan.sides]
    sums = rest[pieces + 2 + plan.sides : pieces + 2 + 2 * plan.sides]
    current, canvas = rest[pieces + 2 + 2 * plan.sides :]
    t = place[1]
    gather_terms(plan, slots, place, info, *patches, canvas)
    assemble(current, own, starts(t), plan.tiles)
    where = lanes(plan.mid_start(t), plan.mid_tiles)
    middle[...] = current[:, :, where] - canvas[:, :, where] * inverse[:, where][None]
    for base, total, start in zip(bases, sums, plan.pair_starts(t)):
        where = lanes(start, 2)
        partial = canvas[:, :, where]
        total[...] = partial
        base[...] = current[:, :, where] - partial * inverse[:, where][None]


def last_kernel(plan, slots, starts, place, info, *rest):
    patches = [rest[k * slots : (k + 1) * slots] for k in range(3)]
    rest = rest[3 * slots :]
    pieces = len(starts(0))
    own = rest[:pieces]
    inverse, nearly = rest[pieces : pieces + 2]
    sums = rest[pieces + 2 : pieces + 2 + plan.sides]
    current, canvas = rest[pieces + 2 + plan.sides :]
    t = place[1]
    gather_terms(plan, slots, place, info, *patches, canvas)
    assemble(current, own, starts(t), plan.tiles)
    where = lanes(1, plan.own)
    nearly[...] = current[:, :, where] - canvas[:, :, where] * inverse[:, where][None]
    for total, tile in zip(sums, plan.halo_tiles(t)):
        total[...] = canvas[:, :, lanes(tile)]


def edge_kernel(place, nearly, received, inverse, result):
    result[...] = nearly[...] - received[...] * inverse[...][None]


def call(kernel, outs, scratch, ins, flops, size, **options):
    return pl.pallas_call(
        kernel,
        out_shape=outs,
        in_specs=[SMEM if value.dtype == jnp.int32 else VMEM for value in ins],
        out_specs=jax.tree.map(lambda _: VMEM, outs),
        scratch_shapes=scratch,
        compiler_params=pltpu.CompilerParams(vmem_limit_bytes=VMEM_BYTES),
        cost_estimate=pl.CostEstimate(flops=flops, bytes_accessed=size, transcendentals=0),
        **options,
    )(*ins)


def on_device(plan, object_field, probe_field, amplitudes, centres, counts):
    f32 = jnp.float32
    shape = jax.ShapeDtypeStruct
    size = probe_field.shape[1]
    half = size // 2
    slots = amplitudes.shape[2]
    block_rows = object_field.shape[1]
    block_cols = object_field.shape[2]
    assert block_rows == half and block_cols % LANES == 0 and half == LANES
    width = plan.tiles * LANES
    s = lax.axis_index("sx")
    t = lax.axis_index("sy")
    place = jnp.stack([s, t]).astype(jnp.int32)
    spots = centres.reshape(2 * slots)
    own_amps = amplitudes[0, 0]
    tables = jnp.asarray(dft_tables(size))
    order = jnp.asarray(parity_order(size))

    rows_above = plan.from_above(object_field)
    rows_below = plan.from_below(object_field)
    edges = [
        lax.dynamic_slice(object_field, (0, 0, (tile - 1) * LANES), (2, block_rows, LANES))
        for tile in plan.edge_tiles(t)
    ]
    halos = plan.across(edges)
    own_info = jnp.concatenate([spots, lax.dynamic_slice(counts, (s, 0), (1, 1)).reshape(1)])
    own_info = jnp.pad(own_info, (0, INFO - own_info.shape[0]))
    info = lax.all_gather(own_info, ("sx", "sy"), tiled=True)

    rolled, ordered = call(
        prepare_kernel,
        [shape((slots, 2, size, size), f32), shape((slots, size, size), f32)],
        [pltpu.VMEM((2, 2 * size + 8, size), f32)],
        [spots, probe_field, own_amps, order],
        10**9, 10**6,
    )
    inverse, *inverse_pairs = call(
        lambda *refs: light_kernel(plan, slots, *refs),
        [shape((half, width), f32)] + [shape((half, 2 * LANES), f32)] * plan.sides,
        [pltpu.VMEM((2 * size + 8, size), f32), pltpu.VMEM((half, width + 2 * plan.own * LANES), f32)],
        [place, info, probe_field],
        10**9, 10**6,
    )

    own = [object_field] + halos
    above = [rows_above] + [plan.from_above(halo) for halo in halos]
    below = [rows_below] + [plan.from_below(halo) for halo in halos]

    def starts(t):
        return [1] + plan.halo_tiles(t)

    def later_starts(t):
        return [plan.mid_start(t)] + plan.pair_starts(t)

    result = None
    for sweep in range(ITERS):
        inner, outer_above, outer_below = [], [], []
        for slot in range(slots):
            outer_part, inner_part = pl.pallas_call(
                lambda *refs, slot=slot, starts=starts: term_kernel(plan, slot, starts, *refs),
                out_shape=[shape((2, half, size), f32)] * 2,
                in_specs=[SMEM] * 3 + [VMEM] * (3 * len(own)) + [
                    pl.BlockSpec((1, 2, size, size), lambda i, slot=slot: (slot, 0, 0, 0)),
                    pl.BlockSpec((1, size, size), lambda i, slot=slot: (slot, 0, 0)),
                    VMEM,
                ],
                out_specs=[VMEM] * 2,
                grid=(1,),
                scratch_shapes=[pltpu.VMEM((2, size, size), f32), pltpu.VMEM((3, 2, half, width), f32)],
                compiler_params=pltpu.CompilerParams(vmem_limit_bytes=VMEM_BYTES),
                cost_estimate=pl.CostEstimate(flops=2 * 10**9, bytes_accessed=6 * 10**6, transcendentals=0),
            )(place, spots, counts, *above, *own, *below, rolled, ordered, tables)
            inner.append(inner_part)
            outer_above.append(plan.from_above(outer_part))
            outer_below.append(plan.from_below(outer_part))
        patches = inner + outer_above + outer_below
        if sweep < ITERS - 1:
            middle, *rest = call(
                lambda *refs, starts=starts: step_kernel(plan, slots, starts, *refs),
                [shape((2, half, plan.mid_tiles * LANES), f32)] + [shape((2, half, 2 * LANES), f32)] * (2 * plan.sides),
                [pltpu.VMEM((2, half, width), f32)] * 2,
                [place, info] + patches + own + [inverse],
                10**9, 10**6,
            )
            bases, sums = rest[: plan.sides], rest[plan.sides :]
            received = plan.across(sums)
            pairs = [base - other * inv[None] for base, other, inv in zip(bases, received, inverse_pairs)]
            own = [middle] + pairs
            above = [plan.from_above(piece) for piece in own]
            below = [plan.from_below(piece) for piece in own]
            starts = later_starts
        else:
            nearly, *sums = call(
                lambda *refs, starts=starts: last_kernel(plan, slots, starts, *refs),
                [shape((2, half, block_cols), f32)] + [shape((2, half, LANES), f32)] * plan.sides,
                [pltpu.VMEM((2, half, width), f32)] * 2,
                [place, info] + patches + own + [inverse],
                10**9, 10**6,
            )
            result = nearly
            for side, received in enumerate(plan.across(sums)):
                block = pl.BlockSpec((2, half, LANES), lambda i, place, side=side: (0, 0, plan.edge_tiles(place[1])[side] - 1))
                result = pl.pallas_call(
                    edge_kernel,
                    grid_spec=pltpu.PrefetchScalarGridSpec(
                        num_scalar_prefetch=1,
                        grid=(1,),
                        in_specs=[
                            block,
                            pl.BlockSpec((2, half, LANES), lambda i, place: (0, 0, 0)),
                            pl.BlockSpec((half, LANES), lambda i, place, side=side: (0, plan.edge_tiles(place[1])[side])),
                        ],
                        out_specs=block,
                    ),
                    out_shape=shape(result.shape, f32),
                    input_output_aliases={1: 0},
                )(place, result, received, inverse)
    return result


def solution(mesh):
    sizes = dict(mesh.shape)

    def per_device(object_field, *rest):
        plan = Plan(sizes["sx"], sizes["sy"], object_field.shape[2])
        return on_device(plan, object_field, *rest)

    return jax.shard_map(
        per_device,
        mesh=mesh,
        in_specs=(
            P(None, "sx", "sy"),
            P(),
            P("sx", "sy", None, None, None),
            P("sx", "sy", None, None),
            P(None, "sy"),
        ),
        out_specs=P(None, "sx", "sy"),
        check_vma=False,
    )
```

time: 333 us -> 144 us (0.43)
  starting transfers between devices: 129 us -> 49.1 us
  waiting for transfers between devices: 93.4 us -> 23.5 us
  matrix products: 49.1 us -> 0 us
  blocking collectives: 0 us -> 40.9 us
  local copies, waits for them, and re-layouts: 27.5 us -> 11.1 us
  Pallas kernels: 0 us -> 16 us
  loops' own time: 15.8 us -> 0 us
  other arithmetic: 13.7 us -> 0.81 us
    ppermute x16 -> x19, starting transfers between devices: 129 us -> 49.1 us  [the longest x8 25.2 us: from_below(): lax.ppermute(values, 'sx', [(i + 1, i) for i in range(self.sx_size - 1)])]
    ppermute x16 -> x19, waiting for transfers between devices: 93.4 us -> 23.5 us  [the longest x3 9.12 us: across(): return [lax.ppermute(values[0], axis_name, [(0, 1), (1, 0)])]]
    dot_general x32 -> x0, matrix products: 49.1 us -> none  [matmul_exact(): return jnp.dot(left_side, right_side, precision=lax.Precision.HIGHEST)]
    unnamed x0 -> x1, blocking collectives: none -> 40.9 us
    dynamic_update_slice x3 -> x0, local copies, waits for them, and re-layouts: 17.3 us -> none  [add_patch(): return lax.dynamic_update_slice(canvas, present + patch_values, starts)]
    pallas_call x0 -> x9, Pallas kernels: none -> 16 us  [the longest x4 6.9 us: call(): pl.pallas_call(kernel, out_shape=outs, in_specs=[SMEM if value.dtype == j...]
    another operation x3 -> x0, loops' own time: 15.8 us -> none  [the longest x2 10.9 us: local_pass(): return lax.fori_loop(0, upper_bound, local_step, canvas)]
    add x8 -> x0, other arithmetic: 5.92 us -> none  [the longest x2 2.68 us: position_gradient(): exit_imag = probe_real * object_patch[1] + probe_imag * object_patch[0]]
  transfers between devices with their start and end apart: 16 -> 19, of which waited for: 13 -> 9; matrix products, arithmetic and copies ran while one was open for 2% -> 2% of each run, Pallas kernels for 0% -> 7%
where the time goes in v1:
time: 144 us; the launch traced here: 142 us
  starting transfers between devices  49.1 us (34%)
  blocking collectives  40.9 us (28%)
  waiting for transfers between devices  23.5 us (16%)
  Pallas kernels  16 us (11%)
  local copies, waits for them, and re-layouts  11.1 us (8%)
    unnamed x1, blocking collectives  40.9 us
    ppermute x8, starting transfers between devices, from_below(): lax.ppermute(values, 'sx', [(i + 1, i) for i in range(self.sx_size - 1)])  25.2 us
    ppermute x8, starting transfers between devices, from_above(): lax.ppermute(values, 'sx', [(i, i + 1) for i in range(self.sx_size - 1)])  19.2 us
    unnamed x59, local copies, waits for them, and re-layouts  9.48 us
    ppermute x3, waiting for transfers between devices, across(): return [lax.ppermute(values[0], axis_name, [(0, 1), (1, 0)])]  9.12 us
    ppermute x8, waiting for transfers between devices, from_above(): lax.ppermute(values, 'sx', [(i, i + 1) for i in range(self.sx_size - 1)])  7.57 us
    pallas_call x4, Pallas kernels, call(): pl.pallas_call(kernel, out_shape=outs, in_specs=[SMEM if value.dtype == j...  6.9 us
    ppermute x8, waiting for transfers between devices, from_below(): lax.ppermute(values, 'sx', [(i + 1, i) for i in range(self.sx_size - 1)])  6.77 us
  transfers between devices with their start and end apart: 19, of which 9 were waited for; matrix products, arithmetic and copies ran while one was open for 2% of the time, Pallas kernels for 7%

profile of v1, /device:TPU:10, one launch (start us, length us, event | category | flops | bytes accessed | tf_op | source)
XLA Modules:
  0.0 141.7 jit_solution(10250222308534454853)
XLA Ops:
  0.0 2.0 %collective-permute-start.3 = (f32[2,128,512]{2,1,0:T(8,128)}, f32[2,128,512]{2,1,0:T(8,128)S(1)}, u32[]{:S(2)}, u32[]{:S(2)}) collective-permute-start(f32[2,128,512]{2,1,0:T(8,128)} %refs_8_.1), channel_id=1, source_target_pairs={{2,0},{4,2},{6,4},{8,6},{10,8},{12,10},{14,12},{16,14},{18,16},{20... | collective-permute-start | bytes 1572872 | tf_op jit(solution)/shard_map/ppermute | solution.py:111
  2.1 2.4 %collective-permute-start = (f32[2,128,512]{2,1,0:T(8,128)}, f32[2,128,512]{2,1,0:T(8,128)S(1)}, u32[]{:S(2)}, u32[]{:S(2)}) collective-permute-start(f32[2,128,512]{2,1,0:T(8,128)} %refs_8_.1), channel_id=1, source_target_pairs={{0,2},{2,4},{4,6},{6,8},{8,10},{10,12},{12,14},{14,16},{16,18},{18... | collective-permute-start | bytes 1572872 | tf_op jit(solution)/shard_map/ppermute | solution.py:108
  5.4 1.6 %collective-permute-start.1 = (f32[2,128,128]{2,1,0:T(8,128)S(1)}, f32[2,128,128]{2,1,0:T(8,128)S(1)}, u32[]{:S(2)}, u32[]{:S(2)}) collective-permute-start(f32[2,128,128]{2,1,0:T(8,128)S(1)} %constant_dynamic-slice_fusion), channel_id=1, source_target_pairs={{0,1},{1,0},{2,3},{3,2},{4,5},{5,4},{6,7},{7,6},{8,9},{9,8},{10,11... | collective-permute-start | bytes 393224 | tf_op jit(solution)/shard_map/ppermute | solution.py:100
  7.1 3.7 %collective-permute-done.1.refs_6_.refs_9_ = f32[2,128,128]{2,1,0:T(8,128)S(1)} collective-permute-done((f32[2,128,128]{2,1,0:T(8,128)S(1)}, f32[2,128,128]{2,1,0:T(8,128)S(1)}, u32[]{:S(2)}, u32[]{:S(2)}) %collective-permute-start.1) | collective-permute-done | bytes 131104 | tf_op jit(solution)/shard_map/ppermute | solution.py:100
  10.8 3.2 %collective-permute-start.4 = (f32[2,128,128]{2,1,0:T(8,128)S(1)}, f32[2,128,128]{2,1,0:T(8,128)S(1)}, u32[]{:S(2)}, u32[]{:S(2)}) collective-permute-start(f32[2,128,128]{2,1,0:T(8,128)S(1)} %collective-permute-done.1.refs_6_.refs_9_), channel_id=1, source_target_pairs={{2,0},{4,2},{6,4},{8,6},{10,8},{12,10},{14,12},{16,14},{18,16},{20... | collective-permute-start | bytes 393224 | tf_op jit(solution)/shard_map/ppermute | solution.py:111
  14.0 1.9 %collective-permute-start.2 = (f32[2,128,128]{2,1,0:T(8,128)S(1)}, f32[2,128,128]{2,1,0:T(8,128)S(1)}, u32[]{:S(2)}, u32[]{:S(2)}) collective-permute-start(f32[2,128,128]{2,1,0:T(8,128)S(1)} %collective-permute-done.1.refs_6_.refs_9_), channel_id=1, source_target_pairs={{0,2},{2,4},{4,6},{6,8},{8,10},{10,12},{12,14},{14,16},{16,18},{18... | collective-permute-start | bytes 393224 | tf_op jit(solution)/shard_map/ppermute | solution.py:108
  18.0 1.5 %shard_map.73 = (f32[2,2,256,256]{3,2,1,0:T(8,128)S(1)}, f32[2,256,256]{2,1,0:T(8,128)S(1)}) custom-call(s32[4]{0:T(128)S(1)} %reshape.7.centres.refs_1_, f32[2,256,256]{2,1,0:T(8,128)S(1)} %copy-done.4, f32[2,256,256]{2,1,0:T(8,128)S(1)} %bitcast.4, bf16[2,256,256]{2,1,0:T(8,128)(2,1)S(1)} %copy-done.10), custom_call_target="tpu_custom_call" | custom-call | flops 1000000000 | bytes 1000000 | tf_op jit(solution)/shard_map/pallas_call | solution.py:358
  23.3 1.2 copy-done.19
  25.9 5.7 %collective-permute-start.8 = (f32[2,128,256]{2,1,0:T(8,128)S(1)}, f32[2,128,256]{2,1,0:T(8,128)S(1)}, u32[]{:S(2)}, u32[]{:S(2)}) collective-permute-start(f32[2,128,256]{2,1,0:T(8,128)S(1)} %get-tuple-element.27), channel_id=1, source_target_pairs={{2,0},{4,2},{6,4},{8,6},{10,8},{12,10},{14,12},{16,14},{18,16},{20... | collective-permute-start | bytes 786440 | tf_op jit(solution)/shard_map/ppermute | solution.py:111
  31.6 2.7 %collective-permute-start.6 = (f32[2,128,256]{2,1,0:T(8,128)S(1)}, f32[2,128,256]{2,1,0:T(8,128)S(1)}, u32[]{:S(2)}, u32[]{:S(2)}) collective-permute-start(f32[2,128,256]{2,1,0:T(8,128)S(1)} %get-tuple-element.27), channel_id=1, source_target_pairs={{0,2},{2,4},{4,6},{6,8},{8,10},{10,12},{12,14},{14,16},{16,18},{18... | collective-permute-start | bytes 786440 | tf_op jit(solution)/shard_map/ppermute | solution.py:108
  35.4 2.7 %shard_map.74 = (f32[2,128,256]{2,1,0:T(8,128)S(1)}, f32[2,128,256]{2,1,0:T(8,128)S(1)}) custom-call(s32[2]{0:T(128)S(1)} %pad_add_fusion.refs_0_.place, s32[4]{0:T(128)S(1)} %copy-done.12, s32[16,1]{1,0:T(8,128)S(1)} %copy.11.refs_2_, f32[2,128,512]{2,1,0:T(8,128)S(1)} %collective-permute-done.refs_3_, f32[2,128,128]{2,1,0:T(8,128)S(1)} %collective-permute-done.2.refs_4_, ...), custom_call_target="tpu_custom_call" | custom-call | flops 2000000000 | bytes 6000000 | tf_op jit(solution)/shard_map/pallas_call | solution.py:428
  38.7 2.9 %collective-permute-start.7 = (f32[2,128,256]{2,1,0:T(8,128)S(1)}, f32[2,128,256]{2,1,0:T(8,128)S(1)}, u32[]{:S(2)}, u32[]{:S(2)}) collective-permute-start(f32[2,128,256]{2,1,0:T(8,128)S(1)} %get-tuple-element.26), channel_id=1, source_target_pairs={{2,0},{4,2},{6,4},{8,6},{10,8},{12,10},{14,12},{16,14},{18,16},{20... | collective-permute-start | bytes 786440 | tf_op jit(solution)/shard_map/ppermute | solution.py:111
  41.6 3.6 %collective-permute-start.5 = (f32[2,128,256]{2,1,0:T(8,128)S(1)}, f32[2,128,256]{2,1,0:T(8,128)S(1)}, u32[]{:S(2)}, u32[]{:S(2)}) collective-permute-start(f32[2,128,256]{2,1,0:T(8,128)S(1)} %get-tuple-element.26), channel_id=1, source_target_pairs={{0,2},{2,4},{4,6},{6,8},{8,10},{10,12},{12,14},{14,16},{16,18},{18... | collective-permute-start | bytes 786440 | tf_op jit(solution)/shard_map/ppermute | solution.py:108
  46.0 40.9 %all-reduce.1.refs_1_ = s32[256]{0:T(256)S(1)} all-reduce(s32[256]{0:T(256)S(1)} %pad_dynamic-update-slice_fusion), channel_id=1, replica_groups=mesh['sx'=16,'sy'=2] {'sx','sy'}, use_global_device_ids=true, to_apply=%add.1 | all-reduce | flops 256 | bytes 2048
  86.9 2.5 %shard_map.76 = (f32[128,768]{1,0:T(8,128)S(1)}, f32[128,256]{1,0:T(8,128)S(1)}) custom-call(s32[2]{0:T(128)S(1)} %pad_add_fusion.refs_0_.place, s32[256]{0:T(256)S(1)} %all-reduce.1.refs_1_, f32[2,256,256]{2,1,0:T(8,128)S(1)} %copy-done.5), custom_call_target="tpu_custom_call" | custom-call | flops 1000000000 | bytes 1000000 | tf_op jit(solution)/shard_map/pallas_call | solution.py:358
  90.6 2.0 %collective-permute-start.10 = (f32[2,128,256]{2,1,0:T(8,128)S(1)}, f32[2,128,256]{2,1,0:T(8,128)S(1)}, u32[]{:S(2)}, u32[]{:S(2)}) collective-permute-start(f32[2,128,256]{2,1,0:T(8,128)S(1)} %get-tuple-element.31), channel_id=1, source_target_pairs={{0,1},{1,0},{2,3},{3,2},{4,5},{5,4},{6,7},{7,6},{8,9},{9,8},{10,11... | collective-permute-start | bytes 786440 | tf_op jit(solution)/shard_map/ppermute | solution.py:100
  92.5 1.9 %collective-permute-start.12 = (f32[2,128,384]{2,1,0:T(8,128)S(1)}, f32[2,128,384]{2,1,0:T(8,128)S(1)}, u32[]{:S(2)}, u32[]{:S(2)}) collective-permute-start(f32[2,128,384]{2,1,0:T(8,128)S(1)} %get-tuple-element.29.refs_5_.refs_8_), channel_id=1, source_target_pairs={{2,0},{4,2},{6,4},{8,6},{10,8},{12,10},{14,12},{16,14},{18,16},{20... | collective-permute-start | bytes 1179656 | tf_op jit(solution)/shard_map/ppermute | solution.py:111
  94.4 2.4 %collective-permute-start.9 = (f32[2,128,384]{2,1,0:T(8,128)S(1)}, f32[2,128,384]{2,1,0:T(8,128)S(1)}, u32[]{:S(2)}, u32[]{:S(2)}) collective-permute-start(f32[2,128,384]{2,1,0:T(8,128)S(1)} %get-tuple-element.29.refs_5_.refs_8_), channel_id=1, source_target_pairs={{0,2},{2,4},{4,6},{6,8},{8,10},{10,12},{12,14},{14,16},{16,18},{18... | collective-permute-start | bytes 1179656 | tf_op jit(solution)/shard_map/ppermute | solution.py:108
  96.9 1.6 %collective-permute-done.10 = f32[2,128,256]{2,1,0:T(8,128)S(1)} collective-permute-done((f32[2,128,256]{2,1,0:T(8,128)S(1)}, f32[2,128,256]{2,1,0:T(8,128)S(1)}, u32[]{:S(2)}, u32[]{:S(2)}) %collective-permute-start.10) | collective-permute-done | bytes 262176 | tf_op jit(solution)/shard_map/ppermute | solution.py:100
  98.5 1.9 %collective-permute-start.13 = (f32[2,128,256]{2,1,0:T(8,128)S(1)}, f32[2,128,256]{2,1,0:T(8,128)S(1)}, u32[]{:S(2)}, u32[]{:S(2)}) collective-permute-start(f32[2,128,256]{2,1,0:T(8,128)S(1)} %multiply_subtract_fusion.refs_6_.refs_9_), channel_id=1, source_target_pairs={{2,0},{4,2},{6,4},{8,6},{10,8},{12,10},{14,12},{16,14},{18,16},{20... | collective-permute-start | bytes 786440 | tf_op jit(solution)/shard_map/ppermute | solution.py:111
  100.4 2.4 %collective-permute-start.11 = (f32[2,128,256]{2,1,0:T(8,128)S(1)}, f32[2,128,256]{2,1,0:T(8,128)S(1)}, u32[]{:S(2)}, u32[]{:S(2)}) collective-permute-start(f32[2,128,256]{2,1,0:T(8,128)S(1)} %multiply_subtract_fusion.refs_6_.refs_9_), channel_id=1, source_target_pairs={{0,2},{2,4},{4,6},{6,8},{8,10},{10,12},{12,14},{14,16},{16,18},{18... | collective-permute-start | bytes 786440 | tf_op jit(solution)/shard_map/ppermute | solution.py:108
  103.9 4.7 %collective-permute-done.9.refs_3_ = f32[2,128,384]{2,1,0:T(8,128)S(1)} collective-permute-done((f32[2,128,384]{2,1,0:T(8,128)S(1)}, f32[2,128,384]{2,1,0:T(8,128)S(1)}, u32[]{:S(2)}, u32[]{:S(2)}) %collective-permute-start.9) | collective-permute-done | bytes 393248 | tf_op jit(solution)/shard_map/ppermute | solution.py:108
  109.5 1.9 %collective-permute-done.11.refs_4_ = f32[2,128,256]{2,1,0:T(8,128)S(1)} collective-permute-done((f32[2,128,256]{2,1,0:T(8,128)S(1)}, f32[2,128,256]{2,1,0:T(8,128)S(1)}, u32[]{:S(2)}, u32[]{:S(2)}) %collective-permute-start.11) | collective-permute-done | bytes 262176 | tf_op jit(solution)/shard_map/ppermute | solution.py:108
  112.2 3.9 %collective-permute-start.17 = (f32[2,128,256]{2,1,0:T(8,128)S(1)}, f32[2,128,256]{2,1,0:T(8,128)S(1)}, u32[]{:S(2)}, u32[]{:S(2)}) collective-permute-start(f32[2,128,256]{2,1,0:T(8,128)S(1)} %get-tuple-element.36), channel_id=1, source_target_pairs={{2,0},{4,2},{6,4},{8,6},{10,8},{12,10},{14,12},{16,14},{18,16},{20... | collective-permute-start | bytes 786440 | tf_op jit(solution)/shard_map/ppermute | solution.py:111
  116.1 1.9 %collective-permute-start.15 = (f32[2,128,256]{2,1,0:T(8,128)S(1)}, f32[2,128,256]{2,1,0:T(8,128)S(1)}, u32[]{:S(2)}, u32[]{:S(2)}) collective-permute-start(f32[2,128,256]{2,1,0:T(8,128)S(1)} %get-tuple-element.36), channel_id=1, source_target_pairs={{0,2},{2,4},{4,6},{6,8},{8,10},{10,12},{12,14},{14,16},{16,18},{18... | collective-permute-start | bytes 786440 | tf_op jit(solution)/shard_map/ppermute | solution.py:108
  118.0 2.6 %shard_map.78 = (f32[2,128,256]{2,1,0:T(8,128)S(1)}, f32[2,128,256]{2,1,0:T(8,128)S(1)}) custom-call(s32[2]{0:T(128)S(1)} %pad_add_fusion.refs_0_.place, s32[4]{0:T(128)S(1)} %copy-done.13, s32[16,1]{1,0:T(8,128)S(1)} %copy.11.refs_2_, f32[2,128,384]{2,1,0:T(8,128)S(1)} %collective-permute-done.9.refs_3_, ...), custom_call_target="tpu_custom_call" | custom-call | flops 2000000000 | bytes 6000000 | tf_op jit(solution)/shard_map/pallas_call | solution.py:428
  120.6 3.6 %collective-permute-start.16 = (f32[2,128,256]{2,1,0:T(8,128)S(1)}, f32[2,128,256]{2,1,0:T(8,128)S(1)}, u32[]{:S(2)}, u32[]{:S(2)}) collective-permute-start(f32[2,128,256]{2,1,0:T(8,128)S(1)} %get-tuple-element.35), channel_id=1, source_target_pairs={{2,0},{4,2},{6,4},{8,6},{10,8},{12,10},{14,12},{16,14},{18,16},{20... | collective-permute-start | bytes 786440 | tf_op jit(solution)/shard_map/ppermute | solution.py:111
  124.3 1.9 %collective-permute-start.14 = (f32[2,128,256]{2,1,0:T(8,128)S(1)}, f32[2,128,256]{2,1,0:T(8,128)S(1)}, u32[]{:S(2)}, u32[]{:S(2)}) collective-permute-start(f32[2,128,256]{2,1,0:T(8,128)S(1)} %get-tuple-element.35), channel_id=1, source_target_pairs={{0,2},{2,4},{4,6},{6,8},{8,10},{10,12},{12,14},{14,16},{16,18},{18... | collective-permute-start | bytes 786440 | tf_op jit(solution)/shard_map/ppermute | solution.py:108
  126.2 4.7 %collective-permute-done.16.refs_6_ = f32[2,128,256]{2,1,0:T(8,128)S(1)} collective-permute-done((f32[2,128,256]{2,1,0:T(8,128)S(1)}, f32[2,128,256]{2,1,0:T(8,128)S(1)}, u32[]{:S(2)}, u32[]{:S(2)}) %collective-permute-start.16) | collective-permute-done | bytes 262176 | tf_op jit(solution)/shard_map/ppermute | solution.py:111
  132.0 1.8 %shard_map.80 = (f32[2,128,512]{2,1,0:T(8,128)}, f32[2,128,128]{2,1,0:T(8,128)S(1)}) custom-call(s32[2]{0:T(128)S(1)} %pad_add_fusion.refs_0_.place, s32[256]{0:T(256)S(1)} %all-reduce.1.refs_1_, f32[2,128,256]{2,1,0:T(8,128)S(1)} %get-tuple-element.33.refs_2_, f32[2,128,256]{2,1,0:T(8,128)S(1)} %get-tuple-element.34.refs_3_, ...), custom_call_target="tpu_custom_call" | custom-call | flops 1000000000 | bytes 1000000 | tf_op jit(solution)/shard_map/pallas_call | solution.py:358
  135.0 3.8 %collective-permute-done.18.received = f32[2,128,128]{2,1,0:T(8,128)S(1)} collective-permute-done((f32[2,128,128]{2,1,0:T(8,128)S(1)}, f32[2,128,128]{2,1,0:T(8,128)S(1)}, u32[]{:S(2)}, u32[]{:S(2)}) %collective-permute-start.18) | collective-permute-done | bytes 131104 | tf_op jit(solution)/shard_map/ppermute | solution.py:100
  139.4 2.3 %shard_map.81 = f32[2,128,512]{2,1,0:T(8,128)} custom-call(s32[2]{0:T(128)} %copy-done.2, f32[2,128,512]{2,1,0:T(8,128)} %get-tuple-element.37.nearly, f32[2,128,128]{2,1,0:T(8,128)} %copy-done.25, f32[128,768]{1,0:T(8,128)} %copy-done), custom_call_target="tpu_custom_call", output_to_operand_aliasing={{}: (1, {})} | custom-call | tf_op jit(solution)/shard_map/pallas_call | solution.py:472
  (81 shorter events, 17.4 us)
Async XLA Ops:
  0.0 15.9 %copy-start.10 = (bf16[2,256,256]{2,1,0:T(8,128)(2,1)S(1)}, bf16[2,256,256]{2,1,0:T(8,128)(2,1)}, u32[]{:S(2)}) copy-start(bf16[2,256,256]{2,1,0:T(8,128)(2,1)} %constant.27.clone.order) | copy-start | bytes 786436
  0.0 22.0 %collective-permute-start.3 = (f32[2,128,512]{2,1,0:T(8,128)}, f32[2,128,512]{2,1,0:T(8,128)S(1)}, u32[]{:S(2)}, u32[]{:S(2)}) collective-permute-start(f32[2,128,512]{2,1,0:T(8,128)} %refs_8_.1), channel_id=1, source_target_pairs={{2,0},{4,2},{6,4},{8,6},{10,8},{12,10},{14,12},{16,14},{18,16},{20... | collective-permute-start | bytes 1572872 | tf_op jit(solution)/shard_map/ppermute | solution.py:111
  2.1 19.9 %collective-permute-start = (f32[2,128,512]{2,1,0:T(8,128)}, f32[2,128,512]{2,1,0:T(8,128)S(1)}, u32[]{:S(2)}, u32[]{:S(2)}) collective-permute-start(f32[2,128,512]{2,1,0:T(8,128)} %refs_8_.1), channel_id=1, source_target_pairs={{0,2},{2,4},{4,6},{6,8},{8,10},{10,12},{12,14},{14,16},{16,18},{18... | collective-permute-start | bytes 1572872 | tf_op jit(solution)/shard_map/ppermute | solution.py:108
  5.4 5.4 %collective-permute-start.1 = (f32[2,128,128]{2,1,0:T(8,128)S(1)}, f32[2,128,128]{2,1,0:T(8,128)S(1)}, u32[]{:S(2)}, u32[]{:S(2)}) collective-permute-start(f32[2,128,128]{2,1,0:T(8,128)S(1)} %constant_dynamic-slice_fusion), channel_id=1, source_target_pairs={{0,1},{1,0},{2,3},{3,2},{4,5},{5,4},{6,7},{7,6},{8,9},{9,8},{10,11... | collective-permute-start | bytes 393224 | tf_op jit(solution)/shard_map/ppermute | solution.py:100
  7.1 14.9 %copy-start.11 = (s32[4]{0:T(128)}, s32[4]{0:T(128)S(1)}, u32[]{:S(2)}) copy-start(s32[4]{0:T(128)S(1)} %reshape.7.centres.refs_1_) | copy-start | bytes 52
  10.8 23.5 %copy-start.6 = (f32[2,128,128]{2,1,0:T(8,128)}, f32[2,128,128]{2,1,0:T(8,128)S(1)}, u32[]{:S(2)}) copy-start(f32[2,128,128]{2,1,0:T(8,128)S(1)} %collective-permute-done.1.refs_6_.refs_9_) | copy-start | bytes 393220
  10.8 11.2 %collective-permute-start.4 = (f32[2,128,128]{2,1,0:T(8,128)S(1)}, f32[2,128,128]{2,1,0:T(8,128)S(1)}, u32[]{:S(2)}, u32[]{:S(2)}) collective-permute-start(f32[2,128,128]{2,1,0:T(8,128)S(1)} %collective-permute-done.1.refs_6_.refs_9_), channel_id=1, source_target_pairs={{2,0},{4,2},{6,4},{8,6},{10,8},{12,10},{14,12},{16,14},{18,16},{20... | collective-permute-start | bytes 393224 | tf_op jit(solution)/shard_map/ppermute | solution.py:111
  14.0 8.0 %collective-permute-start.2 = (f32[2,128,128]{2,1,0:T(8,128)S(1)}, f32[2,128,128]{2,1,0:T(8,128)S(1)}, u32[]{:S(2)}, u32[]{:S(2)}) collective-permute-start(f32[2,128,128]{2,1,0:T(8,128)S(1)} %collective-permute-done.1.refs_6_.refs_9_), channel_id=1, source_target_pairs={{0,2},{2,4},{4,6},{6,8},{8,10},{10,12},{12,14},{14,16},{16,18},{18... | collective-permute-start | bytes 393224 | tf_op jit(solution)/shard_map/ppermute | solution.py:108
  20.6 4.6 %copy-start.22 = (f32[2,256,256]{2,1,0:T(8,128)}, f32[2,256,256]{2,1,0:T(8,128)S(1)}, u32[]{:S(2)}) copy-start(f32[2,256,256]{2,1,0:T(8,128)S(1)} %get-tuple-element.23.refs_10_) | copy-start | bytes 1572868
  22.0 110.0 %copy-start.2 = (s32[2]{0:T(128)}, s32[2]{0:T(128)S(1)}, u32[]{:S(2)}) copy-start(s32[2]{0:T(128)S(1)} %pad_add_fusion.refs_0_.place) | copy-start | bytes 28
  24.5 9.8 %copy-start.20 = (f32[2,2,256,256]{3,2,1,0:T(8,128)S(1)}, f32[2,2,256,256]{3,2,1,0:T(8,128)}, u32[]{:S(2)}) copy-start(f32[2,2,256,256]{3,2,1,0:T(8,128)} %copy-done.18) | copy-start | bytes 3145732
  25.9 8.4 %copy-start.12 = (s32[4]{0:T(128)S(1)}, s32[4]{0:T(128)}, u32[]{:S(2)}) copy-start(s32[4]{0:T(128)} %copy-done.11) | copy-start | bytes 52
  25.9 60.9 %copy-start.5 = (f32[2,256,256]{2,1,0:T(8,128)S(1)}, f32[2,256,256]{2,1,0:T(8,128)}, u32[]{:S(2)}) copy-start(f32[2,256,256]{2,1,0:T(8,128)} %refs_2_.5) | copy-start | bytes 1572868
  25.9 63.4 %collective-permute-start.8 = (f32[2,128,256]{2,1,0:T(8,128)S(1)}, f32[2,128,256]{2,1,0:T(8,128)S(1)}, u32[]{:S(2)}, u32[]{:S(2)}) collective-permute-start(f32[2,128,256]{2,1,0:T(8,128)S(1)} %get-tuple-element.27), channel_id=1, source_target_pairs={{2,0},{4,2},{6,4},{8,6},{10,8},{12,10},{14,12},{16,14},{18,16},{20... | collective-permute-start | bytes 786440 | tf_op jit(solution)/shard_map/ppermute | solution.py:111
  31.6 57.7 %collective-permute-start.6 = (f32[2,128,256]{2,1,0:T(8,128)S(1)}, f32[2,128,256]{2,1,0:T(8,128)S(1)}, u32[]{:S(2)}, u32[]{:S(2)}) collective-permute-start(f32[2,128,256]{2,1,0:T(8,128)S(1)} %get-tuple-element.27), channel_id=1, source_target_pairs={{0,2},{2,4},{4,6},{6,8},{8,10},{10,12},{12,14},{14,16},{16,18},{18... | collective-permute-start | bytes 786440 | tf_op jit(solution)/shard_map/ppermute | solution.py:108
  38.7 50.7 %collective-permute-start.7 = (f32[2,128,256]{2,1,0:T(8,128)S(1)}, f32[2,128,256]{2,1,0:T(8,128)S(1)}, u32[]{:S(2)}, u32[]{:S(2)}) collective-permute-start(f32[2,128,256]{2,1,0:T(8,128)S(1)} %get-tuple-element.26), channel_id=1, source_target_pairs={{2,0},{4,2},{6,4},{8,6},{10,8},{12,10},{14,12},{16,14},{18,16},{20... | collective-permute-start | bytes 786440 | tf_op jit(solution)/shard_map/ppermute | solution.py:111
  41.6 47.8 %collective-permute-start.5 = (f32[2,128,256]{2,1,0:T(8,128)S(1)}, f32[2,128,256]{2,1,0:T(8,128)S(1)}, u32[]{:S(2)}, u32[]{:S(2)}) collective-permute-start(f32[2,128,256]{2,1,0:T(8,128)S(1)} %get-tuple-element.26), channel_id=1, source_target_pairs={{0,2},{2,4},{4,6},{6,8},{8,10},{10,12},{12,14},{14,16},{16,18},{18... | collective-permute-start | bytes 786440 | tf_op jit(solution)/shard_map/ppermute | solution.py:108
  89.4 42.6 %copy-start = (f32[128,768]{1,0:T(8,128)}, f32[128,768]{1,0:T(8,128)S(1)}, u32[]{:S(2)}) copy-start(f32[128,768]{1,0:T(8,128)S(1)} %get-tuple-element.28.refs_10_.inverse) | copy-start | bytes 1179652
  89.4 22.0 %copy-start.9 = (bf16[2,2,2,256,256]{4,3,2,1,0:T(8,128)(2,1)S(1)}, bf16[2,2,2,256,256]{4,3,2,1,0:T(8,128)(2,1)}, u32[]{:S(2)}) copy-start(bf16[2,2,2,256,256]{4,3,2,1,0:T(8,128)(2,1)} %constant.26.clone.refs_11_) | copy-start | bytes 3145732
  89.5 22.0 %copy-start.21 = (f32[2,2,256,256]{3,2,1,0:T(8,128)S(1)}, f32[2,2,256,256]{3,2,1,0:T(8,128)}, u32[]{:S(2)}) copy-start(f32[2,2,256,256]{3,2,1,0:T(8,128)} %copy-done.18) | copy-start | bytes 3145732
  90.5 20.9 %copy-start.24 = (f32[2,256,256]{2,1,0:T(8,128)S(1)}, f32[2,256,256]{2,1,0:T(8,128)}, u32[]{:S(2)}) copy-start(f32[2,256,256]{2,1,0:T(8,128)} %copy-done.22) | copy-start | bytes 1572868
  90.6 7.9 %collective-permute-start.10 = (f32[2,128,256]{2,1,0:T(8,128)S(1)}, f32[2,128,256]{2,1,0:T(8,128)S(1)}, u32[]{:S(2)}, u32[]{:S(2)}) collective-permute-start(f32[2,128,256]{2,1,0:T(8,128)S(1)} %get-tuple-element.31), channel_id=1, source_target_pairs={{0,1},{1,0},{2,3},{3,2},{4,5},{5,4},{6,7},{7,6},{8,9},{9,8},{10,11... | collective-permute-start | bytes 786440 | tf_op jit(solution)/shard_map/ppermute | solution.py:100
  92.5 11.4 %collective-permute-start.12 = (f32[2,128,384]{2,1,0:T(8,128)S(1)}, f32[2,128,384]{2,1,0:T(8,128)S(1)}, u32[]{:S(2)}, u32[]{:S(2)}) collective-permute-start(f32[2,128,384]{2,1,0:T(8,128)S(1)} %get-tuple-element.29.refs_5_.refs_8_), channel_id=1, source_target_pairs={{2,0},{4,2},{6,4},{8,6},{10,8},{12,10},{14,12},{16,14},{18,16},{20... | collective-permute-start | bytes 1179656 | tf_op jit(solution)/shard_map/ppermute | solution.py:111
  94.4 14.2 %collective-permute-start.9 = (f32[2,128,384]{2,1,0:T(8,128)S(1)}, f32[2,128,384]{2,1,0:T(8,128)S(1)}, u32[]{:S(2)}, u32[]{:S(2)}) collective-permute-start(f32[2,128,384]{2,1,0:T(8,128)S(1)} %get-tuple-element.29.refs_5_.refs_8_), channel_id=1, source_target_pairs={{0,2},{2,4},{4,6},{6,8},{8,10},{10,12},{12,14},{14,16},{16,18},{18... | collective-permute-start | bytes 1179656 | tf_op jit(solution)/shard_map/ppermute | solution.py:108
  98.4 13.0 %copy-start.13 = (s32[4]{0:T(128)S(1)}, s32[4]{0:T(128)}, u32[]{:S(2)}) copy-start(s32[4]{0:T(128)} %copy-done.11) | copy-start | bytes 52
  98.5 11.1 %collective-permute-start.13 = (f32[2,128,256]{2,1,0:T(8,128)S(1)}, f32[2,128,256]{2,1,0:T(8,128)S(1)}, u32[]{:S(2)}, u32[]{:S(2)}) collective-permute-start(f32[2,128,256]{2,1,0:T(8,128)S(1)} %multiply_subtract_fusion.refs_6_.refs_9_), channel_id=1, source_target_pairs={{2,0},{4,2},{6,4},{8,6},{10,8},{12,10},{14,12},{16,14},{18,16},{20... | collective-permute-start | bytes 786440 | tf_op jit(solution)/shard_map/ppermute | solution.py:111
  100.4 11.0 %collective-permute-start.11 = (f32[2,128,256]{2,1,0:T(8,128)S(1)}, f32[2,128,256]{2,1,0:T(8,128)S(1)}, u32[]{:S(2)}, u32[]{:S(2)}) collective-permute-start(f32[2,128,256]{2,1,0:T(8,128)S(1)} %multiply_subtract_fusion.refs_6_.refs_9_), channel_id=1, source_target_pairs={{0,2},{2,4},{4,6},{6,8},{8,10},{10,12},{12,14},{14,16},{16,18},{18... | collective-permute-start | bytes 786440 | tf_op jit(solution)/shard_map/ppermute | solution.py:108
  112.2 14.1 %collective-permute-start.17 = (f32[2,128,256]{2,1,0:T(8,128)S(1)}, f32[2,128,256]{2,1,0:T(8,128)S(1)}, u32[]{:S(2)}, u32[]{:S(2)}) collective-permute-start(f32[2,128,256]{2,1,0:T(8,128)S(1)} %get-tuple-element.36), channel_id=1, source_target_pairs={{2,0},{4,2},{6,4},{8,6},{10,8},{12,10},{14,12},{16,14},{18,16},{20... | collective-permute-start | bytes 786440 | tf_op jit(solution)/shard_map/ppermute | solution.py:111
  116.1 10.2 %collective-permute-start.15 = (f32[2,128,256]{2,1,0:T(8,128)S(1)}, f32[2,128,256]{2,1,0:T(8,128)S(1)}, u32[]{:S(2)}, u32[]{:S(2)}) collective-permute-start(f32[2,128,256]{2,1,0:T(8,128)S(1)} %get-tuple-element.36), channel_id=1, source_target_pairs={{0,2},{2,4},{4,6},{6,8},{8,10},{10,12},{12,14},{14,16},{16,18},{18... | collective-permute-start | bytes 786440 | tf_op jit(solution)/shard_map/ppermute | solution.py:108
  120.6 10.3 %collective-permute-start.16 = (f32[2,128,256]{2,1,0:T(8,128)S(1)}, f32[2,128,256]{2,1,0:T(8,128)S(1)}, u32[]{:S(2)}, u32[]{:S(2)}) collective-permute-start(f32[2,128,256]{2,1,0:T(8,128)S(1)} %get-tuple-element.35), channel_id=1, source_target_pairs={{2,0},{4,2},{6,4},{8,6},{10,8},{12,10},{14,12},{16,14},{18,16},{20... | collective-permute-start | bytes 786440 | tf_op jit(solution)/shard_map/ppermute | solution.py:111
  124.3 7.7 %collective-permute-start.14 = (f32[2,128,256]{2,1,0:T(8,128)S(1)}, f32[2,128,256]{2,1,0:T(8,128)S(1)}, u32[]{:S(2)}, u32[]{:S(2)}) collective-permute-start(f32[2,128,256]{2,1,0:T(8,128)S(1)} %get-tuple-element.35), channel_id=1, source_target_pairs={{0,2},{2,4},{4,6},{6,8},{8,10},{10,12},{12,14},{14,16},{16,18},{18... | collective-permute-start | bytes 786440 | tf_op jit(solution)/shard_map/ppermute | solution.py:108
  133.8 5.0 %collective-permute-start.18 = (f32[2,128,128]{2,1,0:T(8,128)S(1)}, f32[2,128,128]{2,1,0:T(8,128)S(1)}, u32[]{:S(2)}, u32[]{:S(2)}) collective-permute-start(f32[2,128,128]{2,1,0:T(8,128)S(1)} %get-tuple-element.38), channel_id=1, source_target_pairs={{0,1},{1,0},{2,3},{3,2},{4,5},{5,4},{6,7},{7,6},{8,9},{9,8},{10,11... | collective-permute-start | bytes 393224 | tf_op jit(solution)/shard_map/ppermute | solution.py:100
  (15 other events, 23.5 us)

commit v2 on v1

--- a/solution.py
+++ b/solution.py
@@ -14,7 +14,7 @@
 DAMPING = 1.0
 LANES = 128
 INFO = 8
-VMEM_BYTES = 32 * 1024 * 1024
+VMEM_BYTES = 12 * 1024 * 1024
 
 VMEM = pl.BlockSpec(memory_space=pltpu.VMEM)
 SMEM = pl.BlockSpec(memory_space=pltpu.SMEM)
@@ -104,11 +104,19 @@
             lax.ppermute(values[0], axis_name, [(i + 1, i) for i in range(ends)]),
         ]
 
-    def from_above(self, values):
-        return lax.ppermute(values, "sx", [(i, i + 1) for i in range(self.sx_size - 1)])
-
-    def from_below(self, values):
-        return lax.ppermute(values, "sx", [(i + 1, i) for i in range(self.sx_size - 1)])
+    def far_rows(self, values):
+        return lax.ppermute(values, "sx", self.swaps(1))
+
+    def near_rows(self, values):
+        return lax.ppermute(values, "sx", self.swaps(0))
+
+    def swaps(self, first):
+        pairs = [(i, i + 1) for i in range(first, self.sx_size - 1, 2)]
+        return pairs + [(j, i) for i, j in pairs]
+
+
+def far_side(s):
+    return 2 * (s % 2) - 1
 
 
 def lanes(tile, count=1):
@@ -122,7 +130,7 @@
     canvas[:, :, lanes(0)] = blank
     canvas[:, :, lanes(tiles - 1)] = blank
     for piece, start in zip(pieces, starts):
-        canvas[:, :, lanes(start, piece.shape[2] // LANES)] = piece[...]
+        canvas[:, :, lanes(start, piece.shape[2] // LANES)] = piece[:, : canvas.shape[1]]
 
 
 def rows_at(ref, start, count):
@@ -164,26 +172,22 @@
     padded, canvas = rest[plan.sides :]
     size = probe.shape[1]
     half = size // 2
-    s = place[0]
     t = place[1]
     padded[:half] = jnp.zeros((half, size), jnp.float32)
     padded[half + size :] = jnp.zeros((half + 8, size), jnp.float32)
     padded[half : half + size] = probe[0] * probe[0] + probe[1] * probe[1]
     canvas[...] = jnp.zeros(canvas.shape, jnp.float32)
-    reach = 2 if plan.paired else 3
+    reach = plan.sides + 1
     spare = jnp.zeros((half, LANES), jnp.float32)
     for down in (-1, 0, 1):
 
         def add(step, carry, down=down):
             turn = step // slots
             slot = step % slots
-            over = turn * (1 - 2 * t) if plan.paired else turn - 1
-            there_s = s + down
-            there_t = t + over
-            inside = (there_s >= 0) & (there_s < plan.sx_size) & (there_t >= 0) & (there_t < plan.sy_size)
-            base = (jnp.clip(there_s, 0, plan.sx_size - 1) * plan.sy_size + jnp.clip(there_t, 0, plan.sy_size - 1)) * INFO
-
-            @pl.when(inside & (slot < info[base + 2 * slots]))
+            over = turn * (1 - 2 * t) if plan.paired else jnp.where(turn == 0, 0, 2 * turn - 3)
+            base = ((down + 1) * reach + turn) * INFO
+
+            @pl.when(slot < info[base + 2 * slots])
             def _():
                 row = info[base + 2 * slot]
                 col = info[base + 2 * slot + 1]
@@ -203,7 +207,7 @@
 
 def term_kernel(plan, slot, starts, place, centres, counts, *rest):
     pieces = len(starts(0))
-    above, own, below = (rest[k * pieces : (k + 1) * pieces] for k in range(3))
+    own, far, near = (rest[k * pieces : (k + 1) * pieces] for k in range(3))
     probe, amps, tables, outer, inner, window, canvas = rest[3 * pieces :]
     size = probe.shape[2]
     half = size // 2
@@ -225,7 +229,8 @@
         rest_col = col % LANES
         from_tile = lax.broadcasted_iota(jnp.int32, (half, LANES), 1) >= rest_col
         from_upper = lax.broadcasted_iota(jnp.int32, (half, LANES), 0) >= row
-        for kind, source in enumerate((above, own, below)):
+        side = far_side(s)
+        for kind, source in ((1, own), (1 + side, far), (1 - side, near)):
             assemble(canvas.at[kind], source, starts(t), plan.tiles)
 
         def pick(kind, part, index):
@@ -257,21 +262,21 @@
         ]
         back = []
         for parity in range(2):
-            far = table_times(tables[parity, 1], halves[parity])
-            far_real = far[:half]
-            far_imag = far[half:]
+            pattern = table_times(tables[parity, 1], halves[parity])
+            far_real = pattern[:half]
+            far_imag = pattern[half:]
             amplitude = amps[0, parity * half : (parity + 1) * half]
             factor = 1.0 - amplitude * lax.rsqrt(far_real * far_real + far_imag * far_imag + SMOOTH)
             miss = jnp.concatenate([far_real * factor, far_imag * factor], axis=0)
             back.append(table_times(tables[parity, 0], miss))
         real = jnp.concatenate([back[0][:half] + back[1][:half], back[0][:half] - back[1][:half]], axis=0)
         imag = jnp.concatenate([back[0][half:] + back[1][half:], back[0][half:] - back[1][half:]], axis=0)
-        near = []
+        both = []
         for parity in range(2):
             picked = slice(parity * half, (parity + 1) * half)
-            near.append(times_table(jnp.concatenate([real[:, picked], imag[:, picked]], axis=1), tables[parity, 1]))
-        near_real = jnp.concatenate([near[0][:, :half] + near[1][:, :half], near[0][:, :half] - near[1][:, :half]], axis=1)
-        near_imag = jnp.concatenate([near[0][:, half:] + near[1][:, half:], near[0][:, half:] - near[1][:, half:]], axis=1)
+            both.append(times_table(jnp.concatenate([real[:, picked], imag[:, picked]], axis=1), tables[parity, 1]))
+        near_real = jnp.concatenate([both[0][:, :half] + both[1][:, :half], both[0][:, :half] - both[1][:, :half]], axis=1)
+        near_imag = jnp.concatenate([both[0][:, half:] + both[1][:, half:], both[0][:, half:] - both[1][:, half:]], axis=1)
         term_real = probe_real * near_real + probe_imag * near_imag
         term_imag = probe_real * near_imag - probe_imag * near_real
         outer[0] = term_real[:half]
@@ -280,33 +285,28 @@
         inner[1] = term_imag[half:]
 
 
-def gather_terms(plan, slots, place, info, own, above, below, canvas):
+def gather_terms(plan, slots, place, info, own, far, near, canvas):
     half = canvas.shape[1]
-    s = place[0]
-    t = place[1]
+    side = far_side(place[0])
     canvas[...] = jnp.zeros(canvas.shape, jnp.float32)
     lane = lax.broadcasted_iota(jnp.int32, (half, LANES), 1)
     line = lax.broadcasted_iota(jnp.int32, (half, LANES), 0)
-    for down, patches in ((0, own), (-1, above), (1, below)):
-        base = (jnp.clip(s + down, 0, plan.sx_size - 1) * plan.sy_size + t) * INFO
+    for down, patches in ((None, own), (side, far), (-side, near)):
+        base = (0 if down is None else down) * (plan.sides + 1) * INFO + (plan.sides + 1) * INFO
         for slot in range(slots):
             row = info[base + 2 * slot]
             col = info[base + 2 * slot + 1]
             tile = col // LANES
             first = tile % 2
             from_tile = lane >= col % LANES
-            if down == 0:
-                left_rows = right_rows = None
-            elif down == 1:
-                left_rows = line >= row
-            else:
-                left_rows = line < row
+            if down is not None:
+                there = (line >= jnp.where(down > 0, row, 0)) & (line < jnp.where(down > 0, half, row))
             for part in range(2):
                 edge = patches[slot][part, :, lanes(first)]
                 middle = patches[slot][part, :, lanes(1 - first)]
-                if left_rows is not None:
-                    edge = jnp.where(left_rows, edge, 0.0)
-                    middle = jnp.where(left_rows, middle, 0.0)
+                if down is not None:
+                    edge = jnp.where(there, edge, 0.0)
+                    middle = jnp.where(there, middle, 0.0)
                 canvas[part, :, lanes(tile)] += jnp.where(from_tile, edge, 0.0)
                 canvas[part, :, lanes(tile + 1)] += middle
                 canvas[part, :, lanes(tile + 2)] += jnp.where(from_tile, 0.0, edge)
@@ -385,16 +385,16 @@
     tables = jnp.asarray(dft_tables(size))
     order = jnp.asarray(parity_order(size))
 
-    rows_above = plan.from_above(object_field)
-    rows_below = plan.from_below(object_field)
+    own_info = jnp.concatenate([spots, lax.dynamic_slice(counts, (s, 0), (1, 1)).reshape(1)])
+    own_rows = jnp.pad(own_info.astype(f32).reshape(1, 1, -1), ((0, 1), (0, 7), (0, LANES - own_info.shape[0])))
+
+    far_block = plan.far_rows(object_field)
     edges = [
         lax.dynamic_slice(object_field, (0, 0, (tile - 1) * LANES), (2, block_rows, LANES))
         for tile in plan.edge_tiles(t)
     ]
-    halos = plan.across(edges)
-    own_info = jnp.concatenate([spots, lax.dynamic_slice(counts, (s, 0), (1, 1)).reshape(1)])
-    own_info = jnp.pad(own_info, (0, INFO - own_info.shape[0]))
-    info = lax.all_gather(own_info, ("sx", "sy"), tiled=True)
+    halos = plan.across([jnp.concatenate([edge, own_rows], axis=1) for edge in edges])
+    near_block = plan.near_rows(object_field)
 
     rolled, ordered = call(
         prepare_kernel,
@@ -403,6 +403,20 @@
         [spots, probe_field, own_amps, order],
         10**9, 10**6,
     )
+    halos, rolled, ordered = lax.optimization_barrier((halos, rolled, ordered))
+    own = [object_field] + halos
+    passed = [jnp.concatenate([halo, own_rows], axis=1) for halo in halos]
+    far = [far_block] + [plan.far_rows(message) for message in passed]
+    near = [near_block] + [plan.near_rows(message) for message in passed]
+
+    def known(messages):
+        lines = [messages[0][0, half + 8 : half + 9, :INFO]]
+        return jnp.concatenate(lines + [message[0, half : half + 1, :INFO] for message in messages], axis=0)
+
+    upper = s % 2 == 0
+    far_info, own_known, near_info = known(far[1:]), known(passed), known(near[1:])
+    info = jnp.stack([jnp.where(upper, far_info, near_info), own_known, jnp.where(upper, near_info, far_info)])
+    info = info.astype(jnp.int32).reshape(-1)
     inverse, *inverse_pairs = call(
         lambda *refs: light_kernel(plan, slots, *refs),
         [shape((half, width), f32)] + [shape((half, 2 * LANES), f32)] * plan.sides,
@@ -411,10 +425,6 @@
         10**9, 10**6,
     )
 
-    own = [object_field] + halos
-    above = [rows_above] + [plan.from_above(halo) for halo in halos]
-    below = [rows_below] + [plan.from_below(halo) for halo in halos]
-
     def starts(t):
         return [1] + plan.halo_tiles(t)
 
@@ -423,7 +433,7 @@
 
     result = None
     for sweep in range(ITERS):
-        inner, outer_above, outer_below = [], [], []
+        inner, outer_far, outer_near = [], [], []
         for slot in range(slots):
             outer_part, inner_part = pl.pallas_call(
                 lambda *refs, slot=slot, starts=starts: term_kernel(plan, slot, starts, *refs),
@@ -438,11 +448,11 @@
                 scratch_shapes=[pltpu.VMEM((2, size, size), f32), pltpu.VMEM((3, 2, half, width), f32)],
                 compiler_params=pltpu.CompilerParams(vmem_limit_bytes=VMEM_BYTES),
                 cost_estimate=pl.CostEstimate(flops=2 * 10**9, bytes_accessed=6 * 10**6, transcendentals=0),
-            )(place, spots, counts, *above, *own, *below, rolled, ordered, tables)
+            )(place, spots, counts, *own, *far, *near, rolled, ordered, tables)
             inner.append(inner_part)
-            outer_above.append(plan.from_above(outer_part))
-            outer_below.append(plan.from_below(outer_part))
-        patches = inner + outer_above + outer_below
+            outer_far.append(plan.far_rows(outer_part))
+            outer_near.append(plan.near_rows(outer_part))
+        patches = inner + outer_far + outer_near
         if sweep < ITERS - 1:
             middle, *rest = call(
                 lambda *refs, starts=starts: step_kernel(plan, slots, starts, *refs),
@@ -455,8 +465,8 @@
             received = plan.across(sums)
             pairs = [base - other * inv[None] for base, other, inv in zip(bases, received, inverse_pairs)]
             own = [middle] + pairs
-            above = [plan.from_above(piece) for piece in own]
-            below = [plan.from_below(piece) for piece in own]
+            far = [plan.far_rows(piece) for piece in own]
+            near = [plan.near_rows(piece) for piece in own]
             starts = later_starts
         else:
             nearly, *sums = call(

time: 144 us -> 99.2 us (0.69); the launches traced: 142 us -> 98.6 us
  blocking collectives: 40.9 us -> 0 us
  starting transfers between devices: 49.1 us -> 29.2 us
  waiting for transfers between devices: 23.5 us -> 34.8 us
  Pallas kernels: 16 us -> 20.2 us
  local copies, waits for them, and re-layouts: 11.1 us -> 13.2 us
    unnamed x1 -> x0, blocking collectives: 40.9 us -> none
    ppermute x16, starting transfers between devices: 44.4 us -> 25.6 us  [the longest x8 21.5 us: far_rows(): return lax.ppermute(values, 'sx', self.swaps(1))]
    ppermute x16, waiting for transfers between devices: 14.3 us -> 28.2 us  [the longest x8 28.2 us: far_rows(): return lax.ppermute(values, 'sx', self.swaps(1))]
    pallas_call x4, Pallas kernels: 6.76 us -> 11.4 us  [on_device(): pl.pallas_call(lambda *refs, slot=slot, starts=starts: term_kernel(plan,...]
    ppermute x3, waiting for transfers between devices: 9.12 us -> 6.55 us  [across(): return [lax.ppermute(values[0], axis_name, [(0, 1), (1, 0)])]]
    unnamed x59 -> x45, local copies, waits for them, and re-layouts: 9.48 us -> 10.1 us
  transfers between devices with their start and end apart: 19 -> 19, of which waited for: 9 -> 8; matrix products, arithmetic and copies ran while one was open for 2% -> 4% of each run, Pallas kernels for 7% -> 10%
where the time goes in v2:
time: 99.2 us; the launch traced here: 98.6 us
  waiting for transfers between devices  34.8 us (35%)
  starting transfers between devices  29.2 us (29%)
  Pallas kernels  20.2 us (20%)
  local copies, waits for them, and re-layouts  13.2 us (13%)
    ppermute x8, waiting for transfers between devices, far_rows(): return lax.ppermute(values, 'sx', self.swaps(1))  28.2 us
    ppermute x8, starting transfers between devices, far_rows(): return lax.ppermute(values, 'sx', self.swaps(1))  21.5 us
    pallas_call x4, Pallas kernels, on_device(): pl.pallas_call(lambda *refs, slot=slot, starts=starts: term_kernel(plan,...  11.4 us
    unnamed x45, local copies, waits for them, and re-layouts  10.1 us
    ppermute x3, waiting for transfers between devices, across(): return [lax.ppermute(values[0], axis_name, [(0, 1), (1, 0)])]  6.55 us
    pallas_call x4, Pallas kernels, call(): pl.pallas_call(kernel, out_shape=outs, in_specs=[SMEM if value.dtype == j...  6.51 us
    ppermute x8, starting transfers between devices, near_rows(): return lax.ppermute(values, 'sx', self.swaps(0))  4.1 us
    ppermute x3, starting transfers between devices, across(): return [lax.ppermute(values[0], axis_name, [(0, 1), (1, 0)])]  3.62 us
  transfers between devices with their start and end apart: 19, of which 8 were waited for; matrix products, arithmetic and copies ran while one was open for 4% of the time, Pallas kernels for 10%

profile of v2, /device:TPU:10, one launch (start us, length us, event | category | flops | bytes accessed | tf_op | source)
XLA Modules:
  0.0 98.6 jit_solution(16626584926759545492)
XLA Ops:
  0.0 2.5 %collective-permute-start.3 = (f32[2,128,512]{2,1,0:T(8,128)}, f32[2,128,512]{2,1,0:T(8,128)S(1)}, u32[]{:S(2)}, u32[]{:S(2)}) collective-permute-start(f32[2,128,512]{2,1,0:T(8,128)} %refs_8_.1), channel_id=1, source_target_pairs={{2,4},{6,8},{10,12},{14,16},{18,20},{22,24},{26,28},{4,2},{8,6},{1... | collective-permute-start | bytes 1572872 | tf_op jit(solution)/shard_map/ppermute | solution.py:108
  4.2 1.2 %constant_dynamic-slice_fusion = s32[1,1]{0,1:T(1,128)} fusion(s32[16,1]{0,1:T(1,128)} %param.11, s32[]{:T(128)S(6)} %select_n.42), kind=kLoop, calls=%fused_computation.14 | loop fusion | bytes 12 | tf_op jit(solution)/shard_map/dynamic_slice | solution.py:388
  6.2 1.6 %collective-permute-start = (f32[2,136,128]{2,1,0:T(8,128)S(1)}, f32[2,136,128]{2,1,0:T(8,128)S(1)}, u32[]{:S(2)}, u32[]{:S(2)}) collective-permute-start(f32[2,136,128]{2,1,0:T(8,128)S(1)} %pad_maximum_fusion.1), channel_id=1, source_target_pairs={{0,1},{1,0},{2,3},{3,2},{4,5},{5,4},{6,7},{7,6},{8,9},{9,8},{10,11... | collective-permute-start | bytes 417800 | tf_op jit(solution)/shard_map/ppermute | solution.py:100
  7.9 1.0 %copy-done.4 = f32[2,256,256]{2,1,0:T(8,128)S(1)} copy-done((f32[2,256,256]{2,1,0:T(8,128)S(1)}, f32[2,256,256]{2,1,0:T(8,128)}, u32[]{:S(2)}) %copy-start.4) | copy-done | bytes 524312
  9.9 1.5 %shard_map.73 = (f32[2,2,256,256]{3,2,1,0:T(8,128)S(1)}, f32[2,256,256]{2,1,0:T(8,128)S(1)}) custom-call(s32[4]{0:T(128)S(1)} %reshape.134.centres.refs_1_, f32[2,256,256]{2,1,0:T(8,128)S(1)} %copy-done.4, f32[2,256,256]{2,1,0:T(8,128)S(1)} %bitcast.10, bf16[2,256,256]{2,1,0:T(8,128)(2,1)S(1)} %copy-done.8), custom_call_target="tpu_custom_call" | custom-call | flops 1000000000 | bytes 1000000 | tf_op jit(solution)/shard_map/pallas_call | solution.py:358
  15.0 2.5 %collective-permute-start.1 = (f32[2,144,128]{2,1,0:T(8,128)S(1)}, f32[2,144,128]{2,1,0:T(8,128)S(1)}, u32[]{:S(2)}, u32[]{:S(2)}) collective-permute-start(f32[2,144,128]{2,1,0:T(8,128)S(1)} %pad_maximum_fusion), channel_id=1, source_target_pairs={{2,4},{6,8},{10,12},{14,16},{18,20},{22,24},{26,28},{4,2},{8,6},{1... | collective-permute-start | bytes 442376 | tf_op jit(solution)/shard_map/ppermute | solution.py:108
  17.5 5.5 %collective-permute-done.1.refs_6_ = f32[2,144,128]{2,1,0:T(8,128)S(1)} collective-permute-done((f32[2,144,128]{2,1,0:T(8,128)S(1)}, f32[2,144,128]{2,1,0:T(8,128)S(1)}, u32[]{:S(2)}, u32[]{:S(2)}) %collective-permute-start.1) | collective-permute-done | bytes 147488 | tf_op jit(solution)/shard_map/ppermute | solution.py:108
  23.1 1.2 %copy-done.6 = bf16[2,2,2,256,256]{4,3,2,1,0:T(8,128)(2,1)S(1)} copy-done((bf16[2,2,2,256,256]{4,3,2,1,0:T(8,128)(2,1)S(1)}, bf16[2,2,2,256,256]{4,3,2,1,0:T(8,128)(2,1)}, u32[]{:S(2)}) %copy-start.6) | copy-done | bytes 1048600
  24.3 1.2 %copy-done.14 = f32[2,2,256,256]{3,2,1,0:T(8,128)S(1)} copy-done((f32[2,2,256,256]{3,2,1,0:T(8,128)S(1)}, f32[2,2,256,256]{3,2,1,0:T(8,128)}, u32[]{:S(2)}) %copy-start.14) | copy-done | bytes 1048600
  25.5 1.0 %copy-done.17 = f32[2,256,256]{2,1,0:T(8,128)S(1)} copy-done((f32[2,256,256]{2,1,0:T(8,128)S(1)}, f32[2,256,256]{2,1,0:T(8,128)}, u32[]{:S(2)}) %copy-start.17) | copy-done | bytes 524312
  26.5 2.7 %shard_map.74 = (f32[2,128,256]{2,1,0:T(8,128)S(1)}, f32[2,128,256]{2,1,0:T(8,128)S(1)}) custom-call(s32[2]{0:T(128)S(1)} %pad_add_fusion.refs_0_.place, s32[4]{0:T(128)S(1)} %reshape.134.centres.refs_1_, s32[16,1]{1,0:T(8,128)S(1)} %copy.11.refs_2_, f32[2,128,512]{2,1,0:T(8,128)S(1)} %copy-done.1, f32[2,136,128]{2,1,0:T(8,128)S(1)} %collective-permute-done.refs_4_.refs_9_, ...), custom_call_target="tpu_custom_call" | custom-call | flops 2000000000 | bytes 6000000 | tf_op jit(solution)/shard_map/pallas_call | solution.py:438
  29.9 2.7 %collective-permute-start.5 = (f32[2,128,256]{2,1,0:T(8,128)S(1)}, f32[2,128,256]{2,1,0:T(8,128)S(1)}, u32[]{:S(2)}, u32[]{:S(2)}) collective-permute-start(f32[2,128,256]{2,1,0:T(8,128)S(1)} %get-tuple-element.32), channel_id=1, source_target_pairs={{2,4},{6,8},{10,12},{14,16},{18,20},{22,24},{26,28},{4,2},{8,6},{1... | collective-permute-start | bytes 786440 | tf_op jit(solution)/shard_map/ppermute | solution.py:108
  32.6 3.4 %shard_map.75 = (f32[2,128,256]{2,1,0:T(8,128)}, f32[2,128,256]{2,1,0:T(8,128)S(1)}) custom-call(s32[2]{0:T(128)S(1)} %pad_add_fusion.refs_0_.place, s32[4]{0:T(128)S(1)} %reshape.134.centres.refs_1_, s32[16,1]{1,0:T(8,128)S(1)} %copy.11.refs_2_, f32[2,128,512]{2,1,0:T(8,128)S(1)} %copy-done.1, f32[2,136,128]{2,1,0:T(8,128)S(1)} %collective-permute-done.refs_4_.refs_9_, ...), custom_call_target="tpu_custom_call" | custom-call | flops 2000000000 | bytes 6000000 | tf_op jit(solution)/shard_map/pallas_call | solution.py:438
  36.7 3.3 %collective-permute-start.6 = (f32[2,128,256]{2,1,0:T(8,128)}, f32[2,128,256]{2,1,0:T(8,128)S(1)}, u32[]{:S(2)}, u32[]{:S(2)}) collective-permute-start(f32[2,128,256]{2,1,0:T(8,128)} %get-tuple-element.33), channel_id=1, source_target_pairs={{2,4},{6,8},{10,12},{14,16},{18,20},{22,24},{26,28},{4,2},{8,6},{1... | collective-permute-start | bytes 786440 | tf_op jit(solution)/shard_map/ppermute | solution.py:108
  40.1 2.1 %shard_map.76 = (f32[128,768]{1,0:T(8,128)S(1)}, f32[128,256]{1,0:T(8,128)S(1)}) custom-call(s32[2]{0:T(128)S(1)} %pad_add_fusion.refs_0_.place, s32[48]{0:T(128)S(1)} %convert_element_type.21.refs_1_, f32[2,256,256]{2,1,0:T(8,128)S(1)} %copy-done.5), custom_call_target="tpu_custom_call" | custom-call | flops 1000000000 | bytes 1000000 | tf_op jit(solution)/shard_map/pallas_call | solution.py:358
  42.2 5.1 %collective-permute-done.6.refs_5_ = f32[2,128,256]{2,1,0:T(8,128)S(1)} collective-permute-done((f32[2,128,256]{2,1,0:T(8,128)}, f32[2,128,256]{2,1,0:T(8,128)S(1)}, u32[]{:S(2)}, u32[]{:S(2)}) %collective-permute-start.6) | collective-permute-done | bytes 262176 | tf_op jit(solution)/shard_map/ppermute | solution.py:108
  47.4 1.1 %shard_map.77 = (f32[2,128,384]{2,1,0:T(8,128)S(1)}, f32[2,128,256]{2,1,0:T(8,128)S(1)}, f32[2,128,256]{2,1,0:T(8,128)S(1)}) custom-call(s32[2]{0:T(128)S(1)} %pad_add_fusion.refs_0_.place, s32[48]{0:T(128)S(1)} %convert_element_type.21.refs_1_, f32[2,128,256]{2,1,0:T(8,128)S(1)} %copy-done.10, f32[2,128,256]{2,1,0:T(8,128)S(1)} %copy-done.12, ...), custom_call_target="tpu_custom_call" | custom-call | flops 1000000000 | bytes 1000000 | tf_op jit(solution)/shard_map/pallas_call | solution.py:358
  49.1 3.3 %collective-permute-start.10 = (f32[2,128,384]{2,1,0:T(8,128)S(1)}, f32[2,128,384]{2,1,0:T(8,128)S(1)}, u32[]{:S(2)}, u32[]{:S(2)}) collective-permute-start(f32[2,128,384]{2,1,0:T(8,128)S(1)} %get-tuple-element.35.refs_3_.refs_8_), channel_id=1, source_target_pairs={{2,4},{6,8},{10,12},{14,16},{18,20},{22,24},{26,28},{4,2},{8,6},{1... | collective-permute-start | bytes 1179656 | tf_op jit(solution)/shard_map/ppermute | solution.py:108
  52.4 3.0 %collective-permute-done.9 = f32[2,128,256]{2,1,0:T(8,128)S(1)} collective-permute-done((f32[2,128,256]{2,1,0:T(8,128)S(1)}, f32[2,128,256]{2,1,0:T(8,128)S(1)}, u32[]{:S(2)}, u32[]{:S(2)}) %collective-permute-start.9) | collective-permute-done | bytes 262176 | tf_op jit(solution)/shard_map/ppermute | solution.py:100
  55.6 3.4 %collective-permute-start.11 = (f32[2,128,256]{2,1,0:T(8,128)S(1)}, f32[2,128,256]{2,1,0:T(8,128)S(1)}, u32[]{:S(2)}, u32[]{:S(2)}) collective-permute-start(f32[2,128,256]{2,1,0:T(8,128)S(1)} %multiply_subtract_fusion.refs_4_.refs_9_), channel_id=1, source_target_pairs={{2,4},{6,8},{10,12},{14,16},{18,20},{22,24},{26,28},{4,2},{8,6},{1... | collective-permute-start | bytes 786440 | tf_op jit(solution)/shard_map/ppermute | solution.py:108
  59.0 6.2 %collective-permute-done.10.refs_5_ = f32[2,128,384]{2,1,0:T(8,128)S(1)} collective-permute-done((f32[2,128,384]{2,1,0:T(8,128)S(1)}, f32[2,128,384]{2,1,0:T(8,128)S(1)}, u32[]{:S(2)}, u32[]{:S(2)}) %collective-permute-start.10) | collective-permute-done | bytes 393248 | tf_op jit(solution)/shard_map/ppermute | solution.py:108
  65.2 2.8 %collective-permute-done.11.refs_6_ = f32[2,128,256]{2,1,0:T(8,128)S(1)} collective-permute-done((f32[2,128,256]{2,1,0:T(8,128)S(1)}, f32[2,128,256]{2,1,0:T(8,128)S(1)}, u32[]{:S(2)}, u32[]{:S(2)}) %collective-permute-start.11) | collective-permute-done | bytes 262176 | tf_op jit(solution)/shard_map/ppermute | solution.py:108
  68.0 2.6 %shard_map.79 = (f32[2,128,256]{2,1,0:T(8,128)S(1)}, f32[2,128,256]{2,1,0:T(8,128)S(1)}) custom-call(s32[2]{0:T(128)S(1)} %pad_add_fusion.refs_0_.place, s32[4]{0:T(128)S(1)} %reshape.134.centres.refs_1_, s32[16,1]{1,0:T(8,128)S(1)} %copy.11.refs_2_, f32[2,128,384]{2,1,0:T(8,128)S(1)} %get-tuple-element.35.refs_3_.refs_8_, ...), custom_call_target="tpu_custom_call" | custom-call | flops 2000000000 | bytes 6000000 | tf_op jit(solution)/shard_map/pallas_call | solution.py:438
  70.8 1.9 %collective-permute-start.15 = (f32[2,128,256]{2,1,0:T(8,128)S(1)}, f32[2,128,256]{2,1,0:T(8,128)S(1)}, u32[]{:S(2)}, u32[]{:S(2)}) collective-permute-start(f32[2,128,256]{2,1,0:T(8,128)S(1)} %get-tuple-element.42), channel_id=1, source_target_pairs={{2,4},{6,8},{10,12},{14,16},{18,20},{22,24},{26,28},{4,2},{8,6},{1... | collective-permute-start | bytes 786440 | tf_op jit(solution)/shard_map/ppermute | solution.py:108
  72.7 2.6 %shard_map.78 = (f32[2,128,256]{2,1,0:T(8,128)S(1)}, f32[2,128,256]{2,1,0:T(8,128)S(1)}) custom-call(s32[2]{0:T(128)S(1)} %pad_add_fusion.refs_0_.place, s32[4]{0:T(128)S(1)} %reshape.134.centres.refs_1_, s32[16,1]{1,0:T(8,128)S(1)} %copy.11.refs_2_, f32[2,128,384]{2,1,0:T(8,128)S(1)} %get-tuple-element.35.refs_3_.refs_8_, ...), custom_call_target="tpu_custom_call" | custom-call | flops 2000000000 | bytes 6000000 | tf_op jit(solution)/shard_map/pallas_call | solution.py:438
  75.3 3.0 %collective-permute-start.16 = (f32[2,128,256]{2,1,0:T(8,128)S(1)}, f32[2,128,256]{2,1,0:T(8,128)S(1)}, u32[]{:S(2)}, u32[]{:S(2)}) collective-permute-start(f32[2,128,256]{2,1,0:T(8,128)S(1)} %get-tuple-element.41), channel_id=1, source_target_pairs={{0,2},{4,6},{8,10},{12,14},{16,18},{20,22},{24,26},{28,30},{2,0},{... | collective-permute-start | bytes 786440 | tf_op jit(solution)/shard_map/ppermute | solution.py:111
  78.3 1.9 %collective-permute-start.14 = (f32[2,128,256]{2,1,0:T(8,128)S(1)}, f32[2,128,256]{2,1,0:T(8,128)S(1)}, u32[]{:S(2)}, u32[]{:S(2)}) collective-permute-start(f32[2,128,256]{2,1,0:T(8,128)S(1)} %get-tuple-element.41), channel_id=1, source_target_pairs={{2,4},{6,8},{10,12},{14,16},{18,20},{22,24},{26,28},{4,2},{8,6},{1... | collective-permute-start | bytes 786440 | tf_op jit(solution)/shard_map/ppermute | solution.py:108
  81.3 7.6 %collective-permute-done.14.refs_4_ = f32[2,128,256]{2,1,0:T(8,128)S(1)} collective-permute-done((f32[2,128,256]{2,1,0:T(8,128)S(1)}, f32[2,128,256]{2,1,0:T(8,128)S(1)}, u32[]{:S(2)}, u32[]{:S(2)}) %collective-permute-start.14) | collective-permute-done | bytes 262176 | tf_op jit(solution)/shard_map/ppermute | solution.py:108
  88.8 1.8 %shard_map.80 = (f32[2,128,512]{2,1,0:T(8,128)}, f32[2,128,128]{2,1,0:T(8,128)S(1)}) custom-call(s32[2]{0:T(128)S(1)} %pad_add_fusion.refs_0_.place, s32[48]{0:T(128)S(1)} %convert_element_type.21.refs_1_, f32[2,128,256]{2,1,0:T(8,128)S(1)} %get-tuple-element.39.refs_2_, f32[2,128,256]{2,1,0:T(8,128)S(1)} %get-tuple-element.40.refs_3_, ...), custom_call_target="tpu_custom_call" | custom-call | flops 1000000000 | bytes 1000000 | tf_op jit(solution)/shard_map/pallas_call | solution.py:358
  90.7 1.4 %collective-permute-start.18 = (f32[2,128,128]{2,1,0:T(8,128)S(1)}, f32[2,128,128]{2,1,0:T(8,128)S(1)}, u32[]{:S(2)}, u32[]{:S(2)}) collective-permute-start(f32[2,128,128]{2,1,0:T(8,128)S(1)} %get-tuple-element.44), channel_id=1, source_target_pairs={{0,1},{1,0},{2,3},{3,2},{4,5},{5,4},{6,7},{7,6},{8,9},{9,8},{10,11... | collective-permute-start | bytes 393224 | tf_op jit(solution)/shard_map/ppermute | solution.py:100
  92.1 3.5 %collective-permute-done.18.received = f32[2,128,128]{2,1,0:T(8,128)S(1)} collective-permute-done((f32[2,128,128]{2,1,0:T(8,128)S(1)}, f32[2,128,128]{2,1,0:T(8,128)S(1)}, u32[]{:S(2)}, u32[]{:S(2)}) %collective-permute-start.18) | collective-permute-done | bytes 131104 | tf_op jit(solution)/shard_map/ppermute | solution.py:100
  96.3 2.3 %shard_map.81 = f32[2,128,512]{2,1,0:T(8,128)} custom-call(s32[2]{0:T(128)} %copy-done.2, f32[2,128,512]{2,1,0:T(8,128)} %get-tuple-element.43.nearly, f32[2,128,128]{2,1,0:T(8,128)} %copy-done.19, f32[128,768]{1,0:T(8,128)} %copy-done), custom_call_target="tpu_custom_call", output_to_operand_aliasing={{}: (1, {})} | custom-call | tf_op jit(solution)/shard_map/pallas_call | solution.py:482
  (78 shorter events, 11.0 us)
Async XLA Ops:
  0.0 7.9 %copy-start.3 = (f32[1,1,2,256,256]{4,3,2,1,0:T(8,128)S(1)}, f32[1,1,2,256,256]{4,3,2,1,0:T(8,128)}, u32[]{:S(2)}) copy-start(f32[1,1,2,256,256]{4,3,2,1,0:T(8,128)} %param.9) | copy-start | bytes 1572868
  0.0 23.0 %collective-permute-start.4 = (f32[2,128,512]{2,1,0:T(8,128)}, f32[2,128,512]{2,1,0:T(8,128)S(1)}, u32[]{:S(2)}, u32[]{:S(2)}) collective-permute-start(f32[2,128,512]{2,1,0:T(8,128)} %refs_8_.1), channel_id=1, source_target_pairs={{0,2},{4,6},{8,10},{12,14},{16,18},{20,22},{24,26},{28,30},{2,0},{... | collective-permute-start | bytes 1572872 | tf_op jit(solution)/shard_map/ppermute | solution.py:111
  0.0 23.0 %collective-permute-start.3 = (f32[2,128,512]{2,1,0:T(8,128)}, f32[2,128,512]{2,1,0:T(8,128)S(1)}, u32[]{:S(2)}, u32[]{:S(2)}) collective-permute-start(f32[2,128,512]{2,1,0:T(8,128)} %refs_8_.1), channel_id=1, source_target_pairs={{2,4},{6,8},{10,12},{14,16},{18,20},{22,24},{26,28},{4,2},{8,6},{1... | collective-permute-start | bytes 1572872 | tf_op jit(solution)/shard_map/ppermute | solution.py:108
  6.2 1.6 %copy-start.21 = (s32[1,1,2,2]{3,2,1,0:T(2,128)S(1)}, s32[1,1,2,2]{3,2,1,0:T(2,128)}, u32[]{:S(2)}) copy-start(s32[1,1,2,2]{3,2,1,0:T(2,128)} %param.10) | copy-start | bytes 52
  6.2 7.8 %collective-permute-start = (f32[2,136,128]{2,1,0:T(8,128)S(1)}, f32[2,136,128]{2,1,0:T(8,128)S(1)}, u32[]{:S(2)}, u32[]{:S(2)}) collective-permute-start(f32[2,136,128]{2,1,0:T(8,128)S(1)} %pad_maximum_fusion.1), channel_id=1, source_target_pairs={{0,1},{1,0},{2,3},{3,2},{4,5},{5,4},{6,7},{7,6},{8,9},{9,8},{10,11... | collective-permute-start | bytes 417800 | tf_op jit(solution)/shard_map/ppermute | solution.py:100
  9.9 13.1 %copy-start.1 = (f32[2,128,512]{2,1,0:T(8,128)S(1)}, f32[2,128,512]{2,1,0:T(8,128)}, u32[]{:S(2)}) copy-start(f32[2,128,512]{2,1,0:T(8,128)} %refs_8_.1) | copy-start | bytes 1572868
  14.0 74.8 %copy-start.2 = (s32[2]{0:T(128)}, s32[2]{0:T(128)S(1)}, u32[]{:S(2)}) copy-start(s32[2]{0:T(128)S(1)} %pad_add_fusion.refs_0_.place) | copy-start | bytes 28
  14.0 3.5 %collective-permute-start.2 = (f32[2,144,128]{2,1,0:T(8,128)S(1)}, f32[2,144,128]{2,1,0:T(8,128)S(1)}, u32[]{:S(2)}, u32[]{:S(2)}) collective-permute-start(f32[2,144,128]{2,1,0:T(8,128)S(1)} %pad_maximum_fusion), channel_id=1, source_target_pairs={{0,2},{4,6},{8,10},{12,14},{16,18},{20,22},{24,26},{28,30},{2,0},{... | collective-permute-start | bytes 442376 | tf_op jit(solution)/shard_map/ppermute | solution.py:111
  15.0 8.0 %collective-permute-start.1 = (f32[2,144,128]{2,1,0:T(8,128)S(1)}, f32[2,144,128]{2,1,0:T(8,128)S(1)}, u32[]{:S(2)}, u32[]{:S(2)}) collective-permute-start(f32[2,144,128]{2,1,0:T(8,128)S(1)} %pad_maximum_fusion), channel_id=1, source_target_pairs={{2,4},{6,8},{10,12},{14,16},{18,20},{22,24},{26,28},{4,2},{8,6},{1... | collective-permute-start | bytes 442376 | tf_op jit(solution)/shard_map/ppermute | solution.py:108
  23.0 1.2 %copy-start.6 = (bf16[2,2,2,256,256]{4,3,2,1,0:T(8,128)(2,1)S(1)}, bf16[2,2,2,256,256]{4,3,2,1,0:T(8,128)(2,1)}, u32[]{:S(2)}) copy-start(bf16[2,2,2,256,256]{4,3,2,1,0:T(8,128)(2,1)} %constant.39.clone.refs_11_) | copy-start | bytes 3145732
  24.3 1.2 %copy-start.14 = (f32[2,2,256,256]{3,2,1,0:T(8,128)S(1)}, f32[2,2,256,256]{3,2,1,0:T(8,128)}, u32[]{:S(2)}) copy-start(f32[2,2,256,256]{3,2,1,0:T(8,128)} %copy-done.13) | copy-start | bytes 3145732
  29.9 10.2 %copy-start.5 = (f32[2,256,256]{2,1,0:T(8,128)S(1)}, f32[2,256,256]{2,1,0:T(8,128)}, u32[]{:S(2)}) copy-start(f32[2,256,256]{2,1,0:T(8,128)} %refs_2_.5) | copy-start | bytes 1572868
  29.9 12.3 %collective-permute-start.7 = (f32[2,128,256]{2,1,0:T(8,128)S(1)}, f32[2,128,256]{2,1,0:T(8,128)S(1)}, u32[]{:S(2)}, u32[]{:S(2)}) collective-permute-start(f32[2,128,256]{2,1,0:T(8,128)S(1)} %get-tuple-element.32), channel_id=1, source_target_pairs={{0,2},{4,6},{8,10},{12,14},{16,18},{20,22},{24,26},{28,30},{2,0},{... | collective-permute-start | bytes 786440 | tf_op jit(solution)/shard_map/ppermute | solution.py:111
  29.9 12.3 %collective-permute-start.5 = (f32[2,128,256]{2,1,0:T(8,128)S(1)}, f32[2,128,256]{2,1,0:T(8,128)S(1)}, u32[]{:S(2)}, u32[]{:S(2)}) collective-permute-start(f32[2,128,256]{2,1,0:T(8,128)S(1)} %get-tuple-element.32), channel_id=1, source_target_pairs={{2,4},{6,8},{10,12},{14,16},{18,20},{22,24},{26,28},{4,2},{8,6},{1... | collective-permute-start | bytes 786440 | tf_op jit(solution)/shard_map/ppermute | solution.py:108
  36.7 5.5 %collective-permute-start.8 = (f32[2,128,256]{2,1,0:T(8,128)}, f32[2,128,256]{2,1,0:T(8,128)S(1)}, u32[]{:S(2)}, u32[]{:S(2)}) collective-permute-start(f32[2,128,256]{2,1,0:T(8,128)} %get-tuple-element.33), channel_id=1, source_target_pairs={{0,2},{4,6},{8,10},{12,14},{16,18},{20,22},{24,26},{28,30},{2,0},{... | collective-permute-start | bytes 786440 | tf_op jit(solution)/shard_map/ppermute | solution.py:111
  36.7 10.7 %collective-permute-start.6 = (f32[2,128,256]{2,1,0:T(8,128)}, f32[2,128,256]{2,1,0:T(8,128)S(1)}, u32[]{:S(2)}, u32[]{:S(2)}) collective-permute-start(f32[2,128,256]{2,1,0:T(8,128)} %get-tuple-element.33), channel_id=1, source_target_pairs={{2,4},{6,8},{10,12},{14,16},{18,20},{22,24},{26,28},{4,2},{8,6},{1... | collective-permute-start | bytes 786440 | tf_op jit(solution)/shard_map/ppermute | solution.py:108
  40.1 7.3 %copy-start.10 = (f32[2,128,256]{2,1,0:T(8,128)S(1)}, f32[2,128,256]{2,1,0:T(8,128)}, u32[]{:S(2)}) copy-start(f32[2,128,256]{2,1,0:T(8,128)} %copy-done.9) | copy-start | bytes 786436
  40.1 7.3 %copy-start.12 = (f32[2,128,256]{2,1,0:T(8,128)S(1)}, f32[2,128,256]{2,1,0:T(8,128)}, u32[]{:S(2)}) copy-start(f32[2,128,256]{2,1,0:T(8,128)} %copy-done.11) | copy-start | bytes 786436
  42.2 46.6 %copy-start = (f32[128,768]{1,0:T(8,128)}, f32[128,768]{1,0:T(8,128)S(1)}, u32[]{:S(2)}) copy-start(f32[128,768]{1,0:T(8,128)S(1)} %get-tuple-element.34.refs_10_.inverse) | copy-start | bytes 1179652
  47.4 20.6 %copy-start.7 = (bf16[2,2,2,256,256]{4,3,2,1,0:T(8,128)(2,1)S(1)}, bf16[2,2,2,256,256]{4,3,2,1,0:T(8,128)(2,1)}, u32[]{:S(2)}) copy-start(bf16[2,2,2,256,256]{4,3,2,1,0:T(8,128)(2,1)} %constant.39.clone.refs_11_) | copy-start | bytes 3145732
  47.4 20.6 %copy-start.15 = (f32[2,2,256,256]{3,2,1,0:T(8,128)S(1)}, f32[2,2,256,256]{3,2,1,0:T(8,128)}, u32[]{:S(2)}) copy-start(f32[2,2,256,256]{3,2,1,0:T(8,128)} %copy-done.13) | copy-start | bytes 3145732
  48.5 19.5 %copy-start.18 = (f32[2,256,256]{2,1,0:T(8,128)S(1)}, f32[2,256,256]{2,1,0:T(8,128)}, u32[]{:S(2)}) copy-start(f32[2,256,256]{2,1,0:T(8,128)} %copy-done.16) | copy-start | bytes 1572868
  48.5 7.0 %collective-permute-start.9 = (f32[2,128,256]{2,1,0:T(8,128)S(1)}, f32[2,128,256]{2,1,0:T(8,128)S(1)}, u32[]{:S(2)}, u32[]{:S(2)}) collective-permute-start(f32[2,128,256]{2,1,0:T(8,128)S(1)} %get-tuple-element.37), channel_id=1, source_target_pairs={{0,1},{1,0},{2,3},{3,2},{4,5},{5,4},{6,7},{7,6},{8,9},{9,8},{10,11... | collective-permute-start | bytes 786440 | tf_op jit(solution)/shard_map/ppermute | solution.py:100
  49.1 9.9 %collective-permute-start.12 = (f32[2,128,384]{2,1,0:T(8,128)S(1)}, f32[2,128,384]{2,1,0:T(8,128)S(1)}, u32[]{:S(2)}, u32[]{:S(2)}) collective-permute-start(f32[2,128,384]{2,1,0:T(8,128)S(1)} %get-tuple-element.35.refs_3_.refs_8_), channel_id=1, source_target_pairs={{0,2},{4,6},{8,10},{12,14},{16,18},{20,22},{24,26},{28,30},{2,0},{... | collective-permute-start | bytes 1179656 | tf_op jit(solution)/shard_map/ppermute | solution.py:111
  49.1 16.1 %collective-permute-start.10 = (f32[2,128,384]{2,1,0:T(8,128)S(1)}, f32[2,128,384]{2,1,0:T(8,128)S(1)}, u32[]{:S(2)}, u32[]{:S(2)}) collective-permute-start(f32[2,128,384]{2,1,0:T(8,128)S(1)} %get-tuple-element.35.refs_3_.refs_8_), channel_id=1, source_target_pairs={{2,4},{6,8},{10,12},{14,16},{18,20},{22,24},{26,28},{4,2},{8,6},{1... | collective-permute-start | bytes 1179656 | tf_op jit(solution)/shard_map/ppermute | solution.py:108
  55.5 9.7 %collective-permute-start.13 = (f32[2,128,256]{2,1,0:T(8,128)S(1)}, f32[2,128,256]{2,1,0:T(8,128)S(1)}, u32[]{:S(2)}, u32[]{:S(2)}) collective-permute-start(f32[2,128,256]{2,1,0:T(8,128)S(1)} %multiply_subtract_fusion.refs_4_.refs_9_), channel_id=1, source_target_pairs={{0,2},{4,6},{8,10},{12,14},{16,18},{20,22},{24,26},{28,30},{2,0},{... | collective-permute-start | bytes 786440 | tf_op jit(solution)/shard_map/ppermute | solution.py:111
  55.6 12.4 %collective-permute-start.11 = (f32[2,128,256]{2,1,0:T(8,128)S(1)}, f32[2,128,256]{2,1,0:T(8,128)S(1)}, u32[]{:S(2)}, u32[]{:S(2)}) collective-permute-start(f32[2,128,256]{2,1,0:T(8,128)S(1)} %multiply_subtract_fusion.refs_4_.refs_9_), channel_id=1, source_target_pairs={{2,4},{6,8},{10,12},{14,16},{18,20},{22,24},{26,28},{4,2},{8,6},{1... | collective-permute-start | bytes 786440 | tf_op jit(solution)/shard_map/ppermute | solution.py:108
  70.7 9.6 %collective-permute-start.17 = (f32[2,128,256]{2,1,0:T(8,128)S(1)}, f32[2,128,256]{2,1,0:T(8,128)S(1)}, u32[]{:S(2)}, u32[]{:S(2)}) collective-permute-start(f32[2,128,256]{2,1,0:T(8,128)S(1)} %get-tuple-element.42), channel_id=1, source_target_pairs={{0,2},{4,6},{8,10},{12,14},{16,18},{20,22},{24,26},{28,30},{2,0},{... | collective-permute-start | bytes 786440 | tf_op jit(solution)/shard_map/ppermute | solution.py:111
  70.8 10.5 %collective-permute-start.15 = (f32[2,128,256]{2,1,0:T(8,128)S(1)}, f32[2,128,256]{2,1,0:T(8,128)S(1)}, u32[]{:S(2)}, u32[]{:S(2)}) collective-permute-start(f32[2,128,256]{2,1,0:T(8,128)S(1)} %get-tuple-element.42), channel_id=1, source_target_pairs={{2,4},{6,8},{10,12},{14,16},{18,20},{22,24},{26,28},{4,2},{8,6},{1... | collective-permute-start | bytes 786440 | tf_op jit(solution)/shard_map/ppermute | solution.py:108
  75.3 5.9 %collective-permute-start.16 = (f32[2,128,256]{2,1,0:T(8,128)S(1)}, f32[2,128,256]{2,1,0:T(8,128)S(1)}, u32[]{:S(2)}, u32[]{:S(2)}) collective-permute-start(f32[2,128,256]{2,1,0:T(8,128)S(1)} %get-tuple-element.41), channel_id=1, source_target_pairs={{0,2},{4,6},{8,10},{12,14},{16,18},{20,22},{24,26},{28,30},{2,0},{... | collective-permute-start | bytes 786440 | tf_op jit(solution)/shard_map/ppermute | solution.py:111
  78.3 10.5 %collective-permute-start.14 = (f32[2,128,256]{2,1,0:T(8,128)S(1)}, f32[2,128,256]{2,1,0:T(8,128)S(1)}, u32[]{:S(2)}, u32[]{:S(2)}) collective-permute-start(f32[2,128,256]{2,1,0:T(8,128)S(1)} %get-tuple-element.41), channel_id=1, source_target_pairs={{2,4},{6,8},{10,12},{14,16},{18,20},{22,24},{26,28},{4,2},{8,6},{1... | collective-permute-start | bytes 786440 | tf_op jit(solution)/shard_map/ppermute | solution.py:108
  90.7 5.0 %collective-permute-start.18 = (f32[2,128,128]{2,1,0:T(8,128)S(1)}, f32[2,128,128]{2,1,0:T(8,128)S(1)}, u32[]{:S(2)}, u32[]{:S(2)}) collective-permute-start(f32[2,128,128]{2,1,0:T(8,128)S(1)} %get-tuple-element.44), channel_id=1, source_target_pairs={{0,1},{1,0},{2,3},{3,2},{4,5},{5,4},{6,7},{7,6},{8,9},{9,8},{10,11... | collective-permute-start | bytes 393224 | tf_op jit(solution)/shard_map/ppermute | solution.py:100
  (9 other events, 7.5 us)

commit v3 on v2

--- a/solution.py
+++ b/solution.py
@@ -13,11 +13,11 @@
 SMOOTH = 1.0
 DAMPING = 1.0
 LANES = 128
-INFO = 8
 VMEM_BYTES = 12 * 1024 * 1024
 
 VMEM = pl.BlockSpec(memory_space=pltpu.VMEM)
 SMEM = pl.BlockSpec(memory_space=pltpu.SMEM)
+HBM = pl.BlockSpec(memory_space=pltpu.HBM)
 
 
 def split_numpy(table):
@@ -139,6 +139,51 @@
     return pltpu.roll(values, (count + 8 - offset) % (count + 8), 0)[:count]
 
 
+def here():
+    return lax.axis_index("sx"), lax.axis_index("sy")
+
+
+def info_rows(centres, count):
+    lane = lax.broadcasted_iota(jnp.int32, (8, LANES), 1)
+    slots = centres.shape[0]
+    values = [centres[slot, axis] for slot in range(slots) for axis in range(2)] + [count]
+    line = jnp.zeros((8, LANES), jnp.int32)
+    for index, value in enumerate(values):
+        line = jnp.where(lane == index, value, line)
+    return line.astype(jnp.float32)
+
+
+def edge_message_kernel(plan, block, centres, counts, *rest):
+    messages, sems = rest[: plan.sides], rest[plan.sides]
+    s, t = here()
+    half = block.shape[1]
+    copies = [
+        pltpu.make_async_copy(block.at[:, :, lanes(tile - 1)], message.at[:, :half], sems.at[side])
+        for side, (message, tile) in enumerate(zip(messages, plan.edge_tiles(t)))
+    ]
+    for copy in copies:
+        copy.start()
+    rows = info_rows(centres, counts[s])
+    for message in messages:
+        message[0, half:] = rows
+        message[1, half:] = rows
+    for copy in copies:
+        copy.wait()
+
+
+def halo_message_kernel(centres, counts, received, message):
+    s, _ = here()
+    rows = received.shape[1]
+    message[:, :rows] = received[...]
+    own = info_rows(centres, counts[s])
+    message[0, rows:] = own
+    message[1, rows:] = own
+
+
+def pair_kernel(base, received, inverse, result):
+    result[...] = base[...] - received[...] * inverse[...][None]
+
+
 def prepare_kernel(centres, probe, amps, order, rolled, ordered, padded):
     size = probe.shape[1]
     half = size // 2
@@ -146,8 +191,8 @@
     padded[:, half + size :] = jnp.zeros((2, half + 8, size), jnp.float32)
     padded[:, half : half + size] = probe[...]
     for slot in range(amps.shape[0]):
-        row = centres[2 * slot]
-        col = centres[2 * slot + 1]
+        row = centres[slot, 0]
+        col = centres[slot, 1]
         for part in range(2):
             shape = padded.at[part]
             upper = rows_at(shape, half - row, half) + rows_at(shape, half + size - row, half)
@@ -167,16 +212,31 @@
         )
 
 
-def light_kernel(plan, slots, place, info, probe, inverse, *rest):
-    pairs = rest[: plan.sides]
-    padded, canvas = rest[plan.sides :]
+def light_kernel(plan, slots, *rest):
+    groups = [rest[k * plan.sides : (k + 1) * plan.sides] for k in range(3)]
+    probe, inverse, info = rest[3 * plan.sides : 3 * plan.sides + 3]
+    pairs = rest[3 * plan.sides + 3 : 4 * plan.sides + 3]
+    padded, canvas, known, sem = rest[4 * plan.sides + 3 :]
     size = probe.shape[1]
     half = size // 2
-    t = place[1]
+    s, t = here()
+    upper = s % 2 == 0
+    height = half
+
+    def lines(messages):
+        return [messages[0][0, height + 8 : height + 16]] + [message[0, height : height + 8] for message in messages]
+
+    own, far, near = (lines(messages) for messages in groups)
+    for turn in range(plan.sides + 1):
+        for kind, line in ((0, jnp.where(upper, far[turn], near[turn])), (1, own[turn]), (2, jnp.where(upper, near[turn], far[turn]))):
+            known[kind * (plan.sides + 1) + turn] = line.astype(jnp.int32)
+    copy = pltpu.make_async_copy(known.at[:, 0], info, sem)
+    copy.start()
     padded[:half] = jnp.zeros((half, size), jnp.float32)
     padded[half + size :] = jnp.zeros((half + 8, size), jnp.float32)
     padded[half : half + size] = probe[0] * probe[0] + probe[1] * probe[1]
     canvas[...] = jnp.zeros(canvas.shape, jnp.float32)
+    copy.wait()
     reach = plan.sides + 1
     spare = jnp.zeros((half, LANES), jnp.float32)
     for down in (-1, 0, 1):
@@ -185,12 +245,12 @@
             turn = step // slots
             slot = step % slots
             over = turn * (1 - 2 * t) if plan.paired else jnp.where(turn == 0, 0, 2 * turn - 3)
-            base = ((down + 1) * reach + turn) * INFO
-
-            @pl.when(slot < info[base + 2 * slots])
+            index = (down + 1) * reach + turn
+
+            @pl.when(slot < info[index, 2 * slots])
             def _():
-                row = info[base + 2 * slot]
-                col = info[base + 2 * slot + 1]
+                row = info[index, 2 * slot]
+                col = info[index, 2 * slot + 1]
                 power = rows_at(padded, size - half * down - row, half)
                 shifted = pltpu.roll(jnp.concatenate([power, spare], axis=1), col % LANES, 1)
                 first = col // LANES + plan.own * (over + 1)
@@ -205,17 +265,16 @@
         pair[...] = inverse[:, lanes(start, 2)]
 
 
-def term_kernel(plan, slot, starts, place, centres, counts, *rest):
+def term_kernel(plan, slot, starts, centres, counts, *rest):
     pieces = len(starts(0))
     own, far, near = (rest[k * pieces : (k + 1) * pieces] for k in range(3))
     probe, amps, tables, outer, inner, window, canvas = rest[3 * pieces :]
     size = probe.shape[2]
     half = size // 2
-    s = place[0]
-    t = place[1]
-    row = centres[2 * slot]
-    col = centres[2 * slot + 1]
-    alive = slot < counts[s, 0]
+    s, t = here()
+    row = centres[slot, 0]
+    col = centres[slot, 1]
+    alive = slot < counts[s]
 
     @pl.when(jnp.logical_not(alive))
     def _():
@@ -285,17 +344,17 @@
         inner[1] = term_imag[half:]
 
 
-def gather_terms(plan, slots, place, info, own, far, near, canvas):
+def gather_terms(plan, slots, s, info, own, far, near, canvas):
     half = canvas.shape[1]
-    side = far_side(place[0])
+    side = far_side(s)
     canvas[...] = jnp.zeros(canvas.shape, jnp.float32)
     lane = lax.broadcasted_iota(jnp.int32, (half, LANES), 1)
     line = lax.broadcasted_iota(jnp.int32, (half, LANES), 0)
     for down, patches in ((None, own), (side, far), (-side, near)):
-        base = (0 if down is None else down) * (plan.sides + 1) * INFO + (plan.sides + 1) * INFO
+        index = (1 if down is None else 1 + down) * (plan.sides + 1)
         for slot in range(slots):
-            row = info[base + 2 * slot]
-            col = info[base + 2 * slot + 1]
+            row = info[index, 2 * slot]
+            col = info[index, 2 * slot + 1]
             tile = col // LANES
             first = tile % 2
             from_tile = lane >= col % LANES
@@ -312,7 +371,7 @@
                 canvas[part, :, lanes(tile + 2)] += jnp.where(from_tile, 0.0, edge)
 
 
-def step_kernel(plan, slots, starts, place, info, *rest):
+def step_kernel(plan, slots, starts, info, *rest):
     patches = [rest[k * slots : (k + 1) * slots] for k in range(3)]
     rest = rest[3 * slots :]
     pieces = len(starts(0))
@@ -321,8 +380,8 @@
     bases = rest[pieces + 2 : pieces + 2 + plan.sides]
     sums = rest[pieces + 2 + plan.sides : pieces + 2 + 2 * plan.sides]
     current, canvas = rest[pieces + 2 + 2 * plan.sides :]
-    t = place[1]
-    gather_terms(plan, slots, place, info, *patches, canvas)
+    s, t = here()
+    gather_terms(plan, slots, s, info, *patches, canvas)
     assemble(current, own, starts(t), plan.tiles)
     where = lanes(plan.mid_start(t), plan.mid_tiles)
     middle[...] = current[:, :, where] - canvas[:, :, where] * inverse[:, where][None]
@@ -333,33 +392,55 @@
         base[...] = current[:, :, where] - partial * inverse[:, where][None]
 
 
-def last_kernel(plan, slots, starts, place, info, *rest):
+def halo_sum_kernel(plan, slots, info, *rest):
+    patches = [rest[k * slots : (k + 1) * slots] for k in range(3)]
+    sums = rest[3 * slots : 3 * slots + plan.sides]
+    canvas = rest[3 * slots + plan.sides]
+    s, t = here()
+    gather_terms(plan, slots, s, info, *patches, canvas)
+    for total, tile in zip(sums, plan.halo_tiles(t)):
+        total[...] = canvas[:, :, lanes(tile)]
+
+
+def last_kernel(plan, slots, starts, info, *rest):
     patches = [rest[k * slots : (k + 1) * slots] for k in range(3)]
     rest = rest[3 * slots :]
     pieces = len(starts(0))
     own = rest[:pieces]
     inverse, nearly = rest[pieces : pieces + 2]
-    sums = rest[pieces + 2 : pieces + 2 + plan.sides]
-    current, canvas = rest[pieces + 2 + plan.sides :]
-    t = place[1]
-    gather_terms(plan, slots, place, info, *patches, canvas)
+    bases = rest[pieces + 2 : pieces + 2 + plan.sides]
+    current, canvas, sem = rest[pieces + 2 + plan.sides :]
+    s, t = here()
+    gather_terms(plan, slots, s, info, *patches, canvas)
     assemble(current, own, starts(t), plan.tiles)
     where = lanes(1, plan.own)
-    nearly[...] = current[:, :, where] - canvas[:, :, where] * inverse[:, where][None]
-    for total, tile in zip(sums, plan.halo_tiles(t)):
-        total[...] = canvas[:, :, lanes(tile)]
-
-
-def edge_kernel(place, nearly, received, inverse, result):
-    result[...] = nearly[...] - received[...] * inverse[...][None]
-
-
-def call(kernel, outs, scratch, ins, flops, size, **options):
+    current[:, :, where] = current[:, :, where] - canvas[:, :, where] * inverse[:, where][None]
+    copy = pltpu.make_async_copy(current.at[:, :, where], nearly, sem)
+    copy.start()
+    for base, tile in zip(bases, plan.edge_tiles(t)):
+        base[...] = current[:, :, lanes(tile)]
+    copy.wait()
+
+
+def edge_kernel(plan, inverse, *rest):
+    bases, received = rest[: plan.sides], rest[plan.sides : 2 * plan.sides]
+    _, result, sums, sems = rest[2 * plan.sides :]
+    _, t = here()
+    copies = []
+    for side, tile in enumerate(plan.edge_tiles(t)):
+        sums[side] = bases[side][...] - received[side][...] * inverse[:, lanes(tile)][None]
+        copies.append(pltpu.make_async_copy(sums.at[side], result.at[:, :, lanes(tile - 1)], sems.at[side]))
+        copies[-1].start()
+    for copy in copies:
+        copy.wait()
+
+
+def call(kernel, outs, scratch, ins, flops=10**9, size=10**6, in_specs=None, out_specs=None, **options):
     return pl.pallas_call(
         kernel,
         out_shape=outs,
-        in_specs=[SMEM if value.dtype == jnp.int32 else VMEM for value in ins],
-        out_specs=jax.tree.map(lambda _: VMEM, outs),
+        in_specs=in_specs or [SMEM if value.dtype == jnp.int32 else VMEM for value in ins],
+        out_specs=out_specs or jax.tree.map(lambda _: VMEM, outs),
         scratch_shapes=scratch,
         compiler_params=pltpu.CompilerParams(vmem_limit_bytes=VMEM_BYTES),
         cost_estimate=pl.CostEstimate(flops=flops, bytes_accessed=size, transcendentals=0),
@@ -377,52 +458,49 @@
     block_cols = object_field.shape[2]
     assert block_rows == half and block_cols % LANES == 0 and half == LANES
     width = plan.tiles * LANES
-    s = lax.axis_index("sx")
-    t = lax.axis_index("sy")
-    place = jnp.stack([s, t]).astype(jnp.int32)
-    spots = centres.reshape(2 * slots)
+    sides = plan.sides
+    spots = centres[0, 0]
+    counts = counts.reshape(-1)
     own_amps = amplitudes[0, 0]
     tables = jnp.asarray(dft_tables(size))
     order = jnp.asarray(parity_order(size))
-
-    own_info = jnp.concatenate([spots, lax.dynamic_slice(counts, (s, 0), (1, 1)).reshape(1)])
-    own_rows = jnp.pad(own_info.astype(f32).reshape(1, 1, -1), ((0, 1), (0, 7), (0, LANES - own_info.shape[0])))
-
+    dma = pltpu.SemaphoreType.DMA
+
+    messages = call(
+        lambda *refs: edge_message_kernel(plan, *refs),
+        [shape((2, half + 8, LANES), f32)] * sides,
+        [dma((sides,))],
+        [object_field, spots, counts],
+        in_specs=[HBM, SMEM, SMEM],
+    )
+    halos = plan.across(messages)
+    near_block = plan.near_rows(object_field)
     far_block = plan.far_rows(object_field)
-    edges = [
-        lax.dynamic_slice(object_field, (0, 0, (tile - 1) * LANES), (2, block_rows, LANES))
-        for tile in plan.edge_tiles(t)
-    ]
-    halos = plan.across([jnp.concatenate([edge, own_rows], axis=1) for edge in edges])
-    near_block = plan.near_rows(object_field)
-
     rolled, ordered = call(
         prepare_kernel,
         [shape((slots, 2, size, size), f32), shape((slots, size, size), f32)],
         [pltpu.VMEM((2, 2 * size + 8, size), f32)],
         [spots, probe_field, own_amps, order],
-        10**9, 10**6,
     )
     halos, rolled, ordered = lax.optimization_barrier((halos, rolled, ordered))
-    own = [object_field] + halos
-    passed = [jnp.concatenate([halo, own_rows], axis=1) for halo in halos]
+    passed = [
+        call(halo_message_kernel, shape((2, half + 16, LANES), f32), [], [spots, counts, halo], flops=10**7)
+        for halo in halos
+    ]
+    near = [near_block] + [plan.near_rows(message) for message in passed]
     far = [far_block] + [plan.far_rows(message) for message in passed]
-    near = [near_block] + [plan.near_rows(message) for message in passed]
-
-    def known(messages):
-        lines = [messages[0][0, half + 8 : half + 9, :INFO]]
-        return jnp.concatenate(lines + [message[0, half : half + 1, :INFO] for message in messages], axis=0)
-
-    upper = s % 2 == 0
-    far_info, own_known, near_info = known(far[1:]), known(passed), known(near[1:])
-    info = jnp.stack([jnp.where(upper, far_info, near_info), own_known, jnp.where(upper, near_info, far_info)])
-    info = info.astype(jnp.int32).reshape(-1)
-    inverse, *inverse_pairs = call(
+    own = [object_field] + passed
+    inverse, info, *inverse_pairs = call(
         lambda *refs: light_kernel(plan, slots, *refs),
-        [shape((half, width), f32)] + [shape((half, 2 * LANES), f32)] * plan.sides,
-        [pltpu.VMEM((2 * size + 8, size), f32), pltpu.VMEM((half, width + 2 * plan.own * LANES), f32)],
-        [place, info, probe_field],
-        10**9, 10**6,
+        [shape((half, width), f32), shape((3 * (sides + 1), LANES), jnp.int32)] + [shape((half, 2 * LANES), f32)] * sides,
+        [
+            pltpu.VMEM((2 * size + 8, size), f32),
+            pltpu.VMEM((half, width + 2 * plan.own * LANES), f32),
+            pltpu.VMEM((3 * (sides + 1), 8, LANES), jnp.int32),
+            dma,
+        ],
+        passed + far[1:] + near[1:] + [probe_field],
+        out_specs=[VMEM, SMEM] + [VMEM] * sides,
     )
 
     def starts(t):
@@ -431,14 +509,13 @@
     def later_starts(t):
         return [plan.mid_start(t)] + plan.pair_starts(t)
 
-    result = None
     for sweep in range(ITERS):
         inner, outer_far, outer_near = [], [], []
         for slot in range(slots):
             outer_part, inner_part = pl.pallas_call(
                 lambda *refs, slot=slot, starts=starts: term_kernel(plan, slot, starts, *refs),
                 out_shape=[shape((2, half, size), f32)] * 2,
-                in_specs=[SMEM] * 3 + [VMEM] * (3 * len(own)) + [
+                in_specs=[SMEM] * 2 + [VMEM] * (3 * len(own)) + [
                     pl.BlockSpec((1, 2, size, size), lambda i, slot=slot: (slot, 0, 0, 0)),
                     pl.BlockSpec((1, size, size), lambda i, slot=slot: (slot, 0, 0)),
                     VMEM,
@@ -448,53 +525,53 @@
                 scratch_shapes=[pltpu.VMEM((2, size, size), f32), pltpu.VMEM((3, 2, half, width), f32)],
                 compiler_params=pltpu.CompilerParams(vmem_limit_bytes=VMEM_BYTES),
                 cost_estimate=pl.CostEstimate(flops=2 * 10**9, bytes_accessed=6 * 10**6, transcendentals=0),
-            )(place, spots, counts, *own, *far, *near, rolled, ordered, tables)
+            )(spots, counts, *own, *far, *near, rolled, ordered, tables)
             inner.append(inner_part)
+            outer_near.append(plan.near_rows(outer_part))
             outer_far.append(plan.far_rows(outer_part))
-            outer_near.append(plan.near_rows(outer_part))
         patches = inner + outer_far + outer_near
         if sweep < ITERS - 1:
             middle, *rest = call(
                 lambda *refs, starts=starts: step_kernel(plan, slots, starts, *refs),
-                [shape((2, half, plan.mid_tiles * LANES), f32)] + [shape((2, half, 2 * LANES), f32)] * (2 * plan.sides),
+                [shape((2, half, plan.mid_tiles * LANES), f32)] + [shape((2, half, 2 * LANES), f32)] * (2 * sides),
                 [pltpu.VMEM((2, half, width), f32)] * 2,
-                [place, info] + patches + own + [inverse],
-                10**9, 10**6,
+                [info] + patches + own + [inverse],
             )
-            bases, sums = rest[: plan.sides], rest[plan.sides :]
+            bases, sums = rest[:sides], rest[sides:]
+            near_middle = plan.near_rows(middle)
             received = plan.across(sums)
-            pairs = [base - other * inv[None] for base, other, inv in zip(bases, received, inverse_pairs)]
+            far_middle = plan.far_rows(middle)
+            pairs = [
+                call(pair_kernel, shape(base.shape, f32), [], [base, other, inv], flops=10**7)
+                for base, other, inv in zip(bases, received, inverse_pairs)
+            ]
             own = [middle] + pairs
-            far = [plan.far_rows(piece) for piece in own]
-            near = [plan.near_rows(piece) for piece in own]
+            near = [near_middle] + [plan.near_rows(piece) for piece in pairs]
+            far = [far_middle] + [plan.far_rows(piece) for piece in pairs]
             starts = later_starts
-        else:
-            nearly, *sums = call(
-                lambda *refs, starts=starts: last_kernel(plan, slots, starts, *refs),
-                [shape((2, half, block_cols), f32)] + [shape((2, half, LANES), f32)] * plan.sides,
-                [pltpu.VMEM((2, half, width), f32)] * 2,
-                [place, info] + patches + own + [inverse],
-                10**9, 10**6,
-            )
-            result = nearly
-            for side, received in enumerate(plan.across(sums)):
-                block = pl.BlockSpec((2, half, LANES), lambda i, place, side=side: (0, 0, plan.edge_tiles(place[1])[side] - 1))
-                result = pl.pallas_call(
-                    edge_kernel,
-                    grid_spec=pltpu.PrefetchScalarGridSpec(
-                        num_scalar_prefetch=1,
-                        grid=(1,),
-                        in_specs=[
-                            block,
-                            pl.BlockSpec((2, half, LANES), lambda i, place: (0, 0, 0)),
-                            pl.BlockSpec((half, LANES), lambda i, place, side=side: (0, plan.edge_tiles(place[1])[side])),
-                        ],
-                        out_specs=block,
-                    ),
-                    out_shape=shape(result.shape, f32),
-                    input_output_aliases={1: 0},
-                )(place, result, received, inverse)
-    return result
+    sums = call(
+        lambda *refs: halo_sum_kernel(plan, slots, *refs),
+        [shape((2, half, LANES), f32)] * sides,
+        [pltpu.VMEM((2, half, width), f32)],
+        [info] + patches,
+    )
+    nearly, *bases = call(
+        lambda *refs: last_kernel(plan, slots, starts, *refs),
+        [shape((2, half, block_cols), f32)] + [shape((2, half, LANES), f32)] * sides,
+        [pltpu.VMEM((2, half, width), f32)] * 2 + [dma],
+        [info] + patches + own + [inverse],
+        out_specs=[HBM] + [VMEM] * sides,
+    )
+    received = plan.across(sums)
+    return call(
+        lambda *refs: edge_kernel(plan, *refs),
+        shape(nearly.shape, f32),
+        [pltpu.VMEM((sides, 2, half, LANES), f32), dma((sides,))],
+        [inverse, *bases, *received, nearly],
+        in_specs=[VMEM] * (1 + 2 * sides) + [HBM],
+        out_specs=HBM,
+        input_output_aliases={1 + 2 * sides: 0},
+    )
 
 
 def solution(mesh):

time: 99.2 us -> 87.7 us (0.88)
  local copies, waits for them, and re-layouts: 13.2 us -> 1.73 us
  waiting for transfers between devices: 34.8 us -> 40.3 us
  Pallas kernels: 20.2 us -> 16.5 us
    unnamed x45 -> x16, local copies, waits for them, and re-layouts: 10.1 us -> 1.73 us
    pallas_call x4, Pallas kernels: 11.4 us -> 6.26 us  [on_device(): pl.pallas_call(lambda *refs, slot=slot, starts=starts: term_kernel(plan,...]
    ppermute x8, starting transfers between devices: 4.1 us -> 7.4 us  [near_rows(): return lax.ppermute(values, 'sx', self.swaps(0))]
    ppermute x8, starting transfers between devices: 21.5 us -> 18.4 us  [far_rows(): return lax.ppermute(values, 'sx', self.swaps(1))]
    ppermute x3, waiting for transfers between devices: 6.55 us -> 9.49 us  [across(): return [lax.ppermute(values[0], axis_name, [(0, 1), (1, 0)])]]
    ppermute x8, waiting for transfers between devices: 28.2 us -> 30.8 us  [far_rows(): return lax.ppermute(values, 'sx', self.swaps(1))]
    dynamic_slice x2 -> x0, local copies, waits for them, and re-layouts: 2.16 us -> none  [the longest x1 1.24 us: on_device(): lax.dynamic_slice(counts, (s, 0), (1, 1)).reshape(1)]
    pallas_call x5 -> x9, Pallas kernels: 8.82 us -> 10.2 us  [call(): pl.pallas_call(kernel, out_shape=outs, in_specs=in_specs or [SMEM if valu...]
  transfers between devices with their start and end apart: 19 -> 19, of which waited for: 8 -> 8; matrix products, arithmetic and copies ran while one was open for 4% -> 0% of each run, Pallas kernels for 10% -> 14%
where the time goes in v3:
time: 87.7 us; the launch traced here: 87.2 us
  waiting for transfers between devices  40.3 us (46%)
  starting transfers between devices  28.4 us (32%)
  Pallas kernels  16.5 us (19%)
  local copies, waits for them, and re-layouts  1.73 us (2%)
    ppermute x8, waiting for transfers between devices, far_rows(): return lax.ppermute(values, 'sx', self.swaps(1))  30.8 us
    ppermute x8, starting transfers between devices, far_rows(): return lax.ppermute(values, 'sx', self.swaps(1))  18.4 us
    pallas_call x9, Pallas kernels, call(): pl.pallas_call(kernel, out_shape=outs, in_specs=in_specs or [SMEM if valu...  10.2 us
    ppermute x3, waiting for transfers between devices, across(): return [lax.ppermute(values[0], axis_name, [(0, 1), (1, 0)])]  9.49 us
    ppermute x8, starting transfers between devices, near_rows(): return lax.ppermute(values, 'sx', self.swaps(0))  7.4 us
    pallas_call x4, Pallas kernels, on_device(): pl.pallas_call(lambda *refs, slot=slot, starts=starts: term_kernel(plan,...  6.26 us
    ppermute x3, starting transfers between devices, across(): return [lax.ppermute(values[0], axis_name, [(0, 1), (1, 0)])]  2.62 us
  transfers between devices with their start and end apart: 19, of which 8 were waited for; matrix products, arithmetic and copies ran while one was open for 0% of the time, Pallas kernels for 14%

profile of v3, /device:TPU:10, one launch (start us, length us, event | category | flops | bytes accessed | tf_op | source)
XLA Modules:
  0.0 87.2 jit_solution(16836701246467702274)
XLA Ops:
  0.0 2.5 %collective-permute-start.3 = (f32[2,128,512]{2,1,0:T(8,128)}, f32[2,128,512]{2,1,0:T(8,128)S(1)}, u32[]{:S(2)}, u32[]{:S(2)}) collective-permute-start(f32[2,128,512]{2,1,0:T(8,128)} %refs_7_.1), channel_id=1, source_target_pairs={{2,4},{6,8},{10,12},{14,16},{18,20},{22,24},{26,28},{4,2},{8,6},{1... | collective-permute-start | bytes 1572872 | tf_op jit(solution)/shard_map/ppermute | solution.py:108
  2.6 0.7 copy-done
  3.2 1.0 %copy-done.4 = f32[2,128,512]{2,1,0:T(8,128)S(1)} copy-done((f32[2,128,512]{2,1,0:T(8,128)S(1)}, f32[2,128,512]{2,1,0:T(8,128)}, u32[]{:S(2)}) %copy-start.4) | copy-done | bytes 524312
  4.9 1.6 %collective-permute-start = (f32[2,136,128]{2,1,0:T(8,128)S(1)}, f32[2,136,128]{2,1,0:T(8,128)S(1)}, u32[]{:S(2)}, u32[]{:S(2)}) collective-permute-start(f32[2,136,128]{2,1,0:T(8,128)S(1)} %shard_map.73), channel_id=1, source_target_pairs={{0,1},{1,0},{2,3},{3,2},{4,5},{5,4},{6,7},{7,6},{8,9},{9,8},{10,11... | collective-permute-start | bytes 417800 | tf_op jit(solution)/shard_map/ppermute | solution.py:100
  6.5 1.5 %shard_map.74 = (f32[2,2,256,256]{3,2,1,0:T(8,128)S(1)}, f32[2,256,256]{2,1,0:T(8,128)S(1)}) custom-call(s32[2,2]{1,0:T(2,128)S(1)} %bitcast.4, f32[2,256,256]{2,1,0:T(8,128)S(1)} %copy-done.3, f32[2,256,256]{2,1,0:T(8,128)S(1)} %bitcast.16, bf16[2,256,256]{2,1,0:T(8,128)(2,1)S(1)} %copy-done.7), custom_call_target="tpu_custom_call" | custom-call | flops 1000000000 | bytes 1000000 | tf_op jit(solution)/shard_map/pallas_call | solution.py:439
  8.0 3.4 %collective-permute-done.received = f32[2,136,128]{2,1,0:T(8,128)S(1)} collective-permute-done((f32[2,136,128]{2,1,0:T(8,128)S(1)}, f32[2,136,128]{2,1,0:T(8,128)S(1)}, u32[]{:S(2)}, u32[]{:S(2)}) %collective-permute-start) | collective-permute-done | bytes 139296 | tf_op jit(solution)/shard_map/ppermute | solution.py:100
  12.3 2.4 %collective-permute-start.1 = (f32[2,144,128]{2,1,0:T(8,128)S(1)}, f32[2,144,128]{2,1,0:T(8,128)S(1)}, u32[]{:S(2)}, u32[]{:S(2)}) collective-permute-start(f32[2,144,128]{2,1,0:T(8,128)S(1)} %shard_map.75.refs_0_.refs_3_.refs_8_), channel_id=1, source_target_pairs={{2,4},{6,8},{10,12},{14,16},{18,20},{22,24},{26,28},{4,2},{8,6},{1... | collective-permute-start | bytes 442376 | tf_op jit(solution)/shard_map/ppermute | solution.py:108
  14.7 5.6 %collective-permute-done.1.refs_1_.refs_5_ = f32[2,144,128]{2,1,0:T(8,128)S(1)} collective-permute-done((f32[2,144,128]{2,1,0:T(8,128)S(1)}, f32[2,144,128]{2,1,0:T(8,128)S(1)}, u32[]{:S(2)}, u32[]{:S(2)}) %collective-permute-start.1) | collective-permute-done | bytes 147488 | tf_op jit(solution)/shard_map/ppermute | solution.py:108
  20.3 0.6 shard_map.78
  21.0 2.4 %collective-permute-start.6 = (f32[2,128,256]{2,1,0:T(8,128)S(1)}, f32[2,128,256]{2,1,0:T(8,128)S(1)}, u32[]{:S(2)}, u32[]{:S(2)}) collective-permute-start(f32[2,128,256]{2,1,0:T(8,128)S(1)} %get-tuple-element.36), channel_id=1, source_target_pairs={{2,4},{6,8},{10,12},{14,16},{18,20},{22,24},{26,28},{4,2},{8,6},{1... | collective-permute-start | bytes 786440 | tf_op jit(solution)/shard_map/ppermute | solution.py:108
  23.4 2.5 %shard_map.77 = (f32[2,128,256]{2,1,0:T(8,128)S(1)}, f32[2,128,256]{2,1,0:T(8,128)S(1)}) custom-call(s32[2,2]{1,0:T(2,128)S(1)} %bitcast.7, s32[16]{0:T(128)S(1)} %bitcast.13, f32[2,128,512]{2,1,0:T(8,128)S(1)} %copy-done.4, f32[2,144,128]{2,1,0:T(8,128)S(1)} %shard_map.75.refs_0_.refs_3_.refs_8_, f32[2,128,512]{2,1,0:T(8,128)S(1)} %collective-permute-done.3.refs_4_, ...), custom_call_target="tpu_custom_call" | custom-call | flops 2000000000 | bytes 6000000 | tf_op jit(solution)/shard_map/pallas_call | solution.py:515
  26.0 3.5 %collective-permute-start.7 = (f32[2,128,256]{2,1,0:T(8,128)S(1)}, f32[2,128,256]{2,1,0:T(8,128)S(1)}, u32[]{:S(2)}, u32[]{:S(2)}) collective-permute-start(f32[2,128,256]{2,1,0:T(8,128)S(1)} %get-tuple-element.35), channel_id=1, source_target_pairs={{0,2},{4,6},{8,10},{12,14},{16,18},{20,22},{24,26},{28,30},{2,0},{... | collective-permute-start | bytes 786440 | tf_op jit(solution)/shard_map/ppermute | solution.py:111
  29.5 1.9 %collective-permute-start.5 = (f32[2,128,256]{2,1,0:T(8,128)S(1)}, f32[2,128,256]{2,1,0:T(8,128)S(1)}, u32[]{:S(2)}, u32[]{:S(2)}) collective-permute-start(f32[2,128,256]{2,1,0:T(8,128)S(1)} %get-tuple-element.35), channel_id=1, source_target_pairs={{2,4},{6,8},{10,12},{14,16},{18,20},{22,24},{26,28},{4,2},{8,6},{1... | collective-permute-start | bytes 786440 | tf_op jit(solution)/shard_map/ppermute | solution.py:108
  31.4 2.7 %shard_map.76 = (f32[128,768]{1,0:T(8,128)S(1)}, s32[6,128]{1,0:T(8,128)S(1)}, f32[128,256]{1,0:T(8,128)S(1)}) custom-call(f32[2,144,128]{2,1,0:T(8,128)S(1)} %shard_map.75.refs_0_.refs_3_.refs_8_, f32[2,144,128]{2,1,0:T(8,128)S(1)} %collective-permute-done.1.refs_1_.refs_5_, f32[2,144,128]{2,1,0:T(8,128)S(1)} %collective-permute-done.2.refs_2_.refs_7_, ...), custom_call_target="tpu_custom_call" | custom-call | flops 1000000000 | bytes 1000000 | tf_op jit(solution)/shard_map/pallas_call | solution.py:439
  34.1 5.8 %collective-permute-done.5.refs_3_ = f32[2,128,256]{2,1,0:T(8,128)S(1)} collective-permute-done((f32[2,128,256]{2,1,0:T(8,128)S(1)}, f32[2,128,256]{2,1,0:T(8,128)S(1)}, u32[]{:S(2)}, u32[]{:S(2)}) %collective-permute-start.5) | collective-permute-done | bytes 262176 | tf_op jit(solution)/shard_map/ppermute | solution.py:108
  39.9 1.1 %shard_map.79 = (f32[2,128,384]{2,1,0:T(8,128)S(1)}, f32[2,128,256]{2,1,0:T(8,128)S(1)}, f32[2,128,256]{2,1,0:T(8,128)S(1)}) custom-call(s32[6,128]{1,0:T(8,128)S(1)} %get-tuple-element.30.refs_0_, f32[2,128,256]{2,1,0:T(8,128)S(1)} %get-tuple-element.33.refs_1_, f32[2,128,256]{2,1,0:T(8,128)S(1)} %get-tuple-element.34.refs_2_, ...), custom_call_target="tpu_custom_call" | custom-call | flops 1000000000 | bytes 1000000 | tf_op jit(solution)/shard_map/pallas_call | solution.py:439
  41.1 0.7 collective-permute-start.9
  41.8 2.6 %collective-permute-start.10 = (f32[2,128,384]{2,1,0:T(8,128)S(1)}, f32[2,128,384]{2,1,0:T(8,128)S(1)}, u32[]{:S(2)}, u32[]{:S(2)}) collective-permute-start(f32[2,128,384]{2,1,0:T(8,128)S(1)} %get-tuple-element.37.refs_2_.refs_7_), channel_id=1, source_target_pairs={{2,4},{6,8},{10,12},{14,16},{18,20},{22,24},{26,28},{4,2},{8,6},{1... | collective-permute-start | bytes 1179656 | tf_op jit(solution)/shard_map/ppermute | solution.py:108
  44.4 3.3 %collective-permute-done.9.received = f32[2,128,256]{2,1,0:T(8,128)S(1)} collective-permute-done((f32[2,128,256]{2,1,0:T(8,128)S(1)}, f32[2,128,256]{2,1,0:T(8,128)S(1)}, u32[]{:S(2)}, u32[]{:S(2)}) %collective-permute-start.9) | collective-permute-done | bytes 262176 | tf_op jit(solution)/shard_map/ppermute | solution.py:100
  47.9 1.9 %collective-permute-start.11 = (f32[2,128,256]{2,1,0:T(8,128)S(1)}, f32[2,128,256]{2,1,0:T(8,128)S(1)}, u32[]{:S(2)}, u32[]{:S(2)}) collective-permute-start(f32[2,128,256]{2,1,0:T(8,128)S(1)} %shard_map.80.refs_3_.refs_8_), channel_id=1, source_target_pairs={{2,4},{6,8},{10,12},{14,16},{18,20},{22,24},{26,28},{4,2},{8,6},{1... | collective-permute-start | bytes 786440 | tf_op jit(solution)/shard_map/ppermute | solution.py:108
  49.8 8.1 %collective-permute-done.10.refs_4_ = f32[2,128,384]{2,1,0:T(8,128)S(1)} collective-permute-done((f32[2,128,384]{2,1,0:T(8,128)S(1)}, f32[2,128,384]{2,1,0:T(8,128)S(1)}, u32[]{:S(2)}, u32[]{:S(2)}) %collective-permute-start.10) | collective-permute-done | bytes 393248 | tf_op jit(solution)/shard_map/ppermute | solution.py:108
  57.9 2.8 %collective-permute-done.11.refs_5_ = f32[2,128,256]{2,1,0:T(8,128)S(1)} collective-permute-done((f32[2,128,256]{2,1,0:T(8,128)S(1)}, f32[2,128,256]{2,1,0:T(8,128)S(1)}, u32[]{:S(2)}, u32[]{:S(2)}) %collective-permute-start.11) | collective-permute-done | bytes 262176 | tf_op jit(solution)/shard_map/ppermute | solution.py:108
  60.7 0.6 shard_map.82
  61.4 2.6 %collective-permute-start.15 = (f32[2,128,256]{2,1,0:T(8,128)S(1)}, f32[2,128,256]{2,1,0:T(8,128)S(1)}, u32[]{:S(2)}, u32[]{:S(2)}) collective-permute-start(f32[2,128,256]{2,1,0:T(8,128)S(1)} %get-tuple-element.44), channel_id=1, source_target_pairs={{2,4},{6,8},{10,12},{14,16},{18,20},{22,24},{26,28},{4,2},{8,6},{1... | collective-permute-start | bytes 786440 | tf_op jit(solution)/shard_map/ppermute | solution.py:108
  64.0 2.5 %shard_map.81 = (f32[2,128,256]{2,1,0:T(8,128)S(1)}, f32[2,128,256]{2,1,0:T(8,128)S(1)}) custom-call(s32[2,2]{1,0:T(2,128)S(1)} %bitcast.9, s32[16]{0:T(128)S(1)} %bitcast.15, f32[2,128,384]{2,1,0:T(8,128)S(1)} %get-tuple-element.37.refs_2_.refs_7_, f32[2,128,256]{2,1,0:T(8,128)S(1)} %shard_map.80.refs_3_.refs_8_, ...), custom_call_target="tpu_custom_call" | custom-call | flops 2000000000 | bytes 6000000 | tf_op jit(solution)/shard_map/pallas_call | solution.py:515
  66.6 3.5 %collective-permute-start.16 = (f32[2,128,256]{2,1,0:T(8,128)S(1)}, f32[2,128,256]{2,1,0:T(8,128)S(1)}, u32[]{:S(2)}, u32[]{:S(2)}) collective-permute-start(f32[2,128,256]{2,1,0:T(8,128)S(1)} %get-tuple-element.43), channel_id=1, source_target_pairs={{0,2},{4,6},{8,10},{12,14},{16,18},{20,22},{24,26},{28,30},{2,0},{... | collective-permute-start | bytes 786440 | tf_op jit(solution)/shard_map/ppermute | solution.py:111
  70.0 1.9 %collective-permute-start.14 = (f32[2,128,256]{2,1,0:T(8,128)S(1)}, f32[2,128,256]{2,1,0:T(8,128)S(1)}, u32[]{:S(2)}, u32[]{:S(2)}) collective-permute-start(f32[2,128,256]{2,1,0:T(8,128)S(1)} %get-tuple-element.43), channel_id=1, source_target_pairs={{2,4},{6,8},{10,12},{14,16},{18,20},{22,24},{26,28},{4,2},{8,6},{1... | collective-permute-start | bytes 786440 | tf_op jit(solution)/shard_map/ppermute | solution.py:108
  72.0 8.5 %collective-permute-done.14.refs_3_ = f32[2,128,256]{2,1,0:T(8,128)S(1)} collective-permute-done((f32[2,128,256]{2,1,0:T(8,128)S(1)}, f32[2,128,256]{2,1,0:T(8,128)S(1)}, u32[]{:S(2)}, u32[]{:S(2)}) %collective-permute-start.14) | collective-permute-done | bytes 262176 | tf_op jit(solution)/shard_map/ppermute | solution.py:108
  80.5 1.0 %shard_map.84 = f32[2,128,128]{2,1,0:T(8,128)S(1)} custom-call(s32[6,128]{1,0:T(8,128)S(1)} %get-tuple-element.30.refs_0_, f32[2,128,256]{2,1,0:T(8,128)S(1)} %get-tuple-element.41.refs_1_, f32[2,128,256]{2,1,0:T(8,128)S(1)} %get-tuple-element.42.refs_2_, f32[2,128,256]{2,1,0:T(8,128)S(1)} %collective-permute-done.14.refs_3_, ...), custom_call_target="tpu_custom_call" | custom-call | flops 1000000000 | bytes 1000000 | tf_op jit(solution)/shard_map/pallas_call | solution.py:439
  81.9 1.9 %shard_map.83 = (f32[2,128,512]{2,1,0:T(8,128)}, f32[2,128,128]{2,1,0:T(8,128)S(1)}) custom-call(s32[6,128]{1,0:T(8,128)S(1)} %get-tuple-element.30.refs_0_, f32[2,128,256]{2,1,0:T(8,128)S(1)} %get-tuple-element.41.refs_1_, f32[2,128,256]{2,1,0:T(8,128)S(1)} %get-tuple-element.42.refs_2_, f32[2,128,256]{2,1,0:T(8,128)S(1)} %collective-permute-done.14.refs_3_, ...), custom_call_target="tpu_custom_call" | custom-call | flops 1000000000 | bytes 1000000 | tf_op jit(solution)/shard_map/pallas_call | solution.py:439
  83.8 2.7 %collective-permute-done.18.refs_2_ = f32[2,128,128]{2,1,0:T(8,128)S(1)} collective-permute-done((f32[2,128,128]{2,1,0:T(8,128)S(1)}, f32[2,128,128]{2,1,0:T(8,128)S(1)}, u32[]{:S(2)}, u32[]{:S(2)}) %collective-permute-start.18) | collective-permute-done | bytes 131104 | tf_op jit(solution)/shard_map/ppermute | solution.py:100
  86.5 0.7 shard_map.85
  (35 shorter events, 2.1 us)
Async XLA Ops:
  0.0 20.3 %collective-permute-start.4 = (f32[2,128,512]{2,1,0:T(8,128)}, f32[2,128,512]{2,1,0:T(8,128)S(1)}, u32[]{:S(2)}, u32[]{:S(2)}) collective-permute-start(f32[2,128,512]{2,1,0:T(8,128)} %refs_7_.1), channel_id=1, source_target_pairs={{0,2},{4,6},{8,10},{12,14},{16,18},{20,22},{24,26},{28,30},{2,0},{... | collective-permute-start | bytes 1572872 | tf_op jit(solution)/shard_map/ppermute | solution.py:111
  0.0 20.3 %collective-permute-start.3 = (f32[2,128,512]{2,1,0:T(8,128)}, f32[2,128,512]{2,1,0:T(8,128)S(1)}, u32[]{:S(2)}, u32[]{:S(2)}) collective-permute-start(f32[2,128,512]{2,1,0:T(8,128)} %refs_7_.1), channel_id=1, source_target_pairs={{2,4},{6,8},{10,12},{14,16},{18,20},{22,24},{26,28},{4,2},{8,6},{1... | collective-permute-start | bytes 1572872 | tf_op jit(solution)/shard_map/ppermute | solution.py:108
  2.6 0.7 copy-start
  2.6 0.7 copy-start.1
  3.2 1.0 %copy-start.4 = (f32[2,128,512]{2,1,0:T(8,128)S(1)}, f32[2,128,512]{2,1,0:T(8,128)}, u32[]{:S(2)}) copy-start(f32[2,128,512]{2,1,0:T(8,128)} %refs_7_.1) | copy-start | bytes 1572868
  4.3 2.2 %copy-start.2 = (f32[1,1,2,256,256]{4,3,2,1,0:T(8,128)S(1)}, f32[1,1,2,256,256]{4,3,2,1,0:T(8,128)}, u32[]{:S(2)}) copy-start(f32[1,1,2,256,256]{4,3,2,1,0:T(8,128)} %param.9) | copy-start | bytes 1572868
  4.3 2.2 %copy-start.3 = (f32[2,256,256]{2,1,0:T(8,128)S(1)}, f32[2,256,256]{2,1,0:T(8,128)}, u32[]{:S(2)}) copy-start(f32[2,256,256]{2,1,0:T(8,128)} %refs_3_.1) | copy-start | bytes 1572868
  4.3 2.2 %copy-start.7 = (bf16[2,256,256]{2,1,0:T(8,128)(2,1)S(1)}, bf16[2,256,256]{2,1,0:T(8,128)(2,1)}, u32[]{:S(2)}) copy-start(bf16[2,256,256]{2,1,0:T(8,128)(2,1)} %constant.5.clone.order) | copy-start | bytes 786436
  4.9 6.6 %collective-permute-start = (f32[2,136,128]{2,1,0:T(8,128)S(1)}, f32[2,136,128]{2,1,0:T(8,128)S(1)}, u32[]{:S(2)}, u32[]{:S(2)}) collective-permute-start(f32[2,136,128]{2,1,0:T(8,128)S(1)} %shard_map.73), channel_id=1, source_target_pairs={{0,1},{1,0},{2,3},{3,2},{4,5},{5,4},{6,7},{7,6},{8,9},{9,8},{10,11... | collective-permute-start | bytes 417800 | tf_op jit(solution)/shard_map/ppermute | solution.py:100
  6.5 13.8 %copy-start.6 = (bf16[2,2,2,256,256]{4,3,2,1,0:T(8,128)(2,1)S(1)}, bf16[2,2,2,256,256]{4,3,2,1,0:T(8,128)(2,1)}, u32[]{:S(2)}) copy-start(bf16[2,2,2,256,256]{4,3,2,1,0:T(8,128)(2,1)} %constant.4.clone.refs_10_) | copy-start | bytes 3145732
  12.0 2.7 %collective-permute-start.2 = (f32[2,144,128]{2,1,0:T(8,128)S(1)}, f32[2,144,128]{2,1,0:T(8,128)S(1)}, u32[]{:S(2)}, u32[]{:S(2)}) collective-permute-start(f32[2,144,128]{2,1,0:T(8,128)S(1)} %shard_map.75.refs_0_.refs_3_.refs_8_), channel_id=1, source_target_pairs={{0,2},{4,6},{8,10},{12,14},{16,18},{20,22},{24,26},{28,30},{2,0},{... | collective-permute-start | bytes 442376 | tf_op jit(solution)/shard_map/ppermute | solution.py:111
  12.3 8.0 %collective-permute-start.1 = (f32[2,144,128]{2,1,0:T(8,128)S(1)}, f32[2,144,128]{2,1,0:T(8,128)S(1)}, u32[]{:S(2)}, u32[]{:S(2)}) collective-permute-start(f32[2,144,128]{2,1,0:T(8,128)S(1)} %shard_map.75.refs_0_.refs_3_.refs_8_), channel_id=1, source_target_pairs={{2,4},{6,8},{10,12},{14,16},{18,20},{22,24},{26,28},{4,2},{8,6},{1... | collective-permute-start | bytes 442376 | tf_op jit(solution)/shard_map/ppermute | solution.py:108
  20.9 13.2 %collective-permute-start.8 = (f32[2,128,256]{2,1,0:T(8,128)S(1)}, f32[2,128,256]{2,1,0:T(8,128)S(1)}, u32[]{:S(2)}, u32[]{:S(2)}) collective-permute-start(f32[2,128,256]{2,1,0:T(8,128)S(1)} %get-tuple-element.36), channel_id=1, source_target_pairs={{0,2},{4,6},{8,10},{12,14},{16,18},{20,22},{24,26},{28,30},{2,0},{... | collective-permute-start | bytes 786440 | tf_op jit(solution)/shard_map/ppermute | solution.py:111
  21.0 13.1 %collective-permute-start.6 = (f32[2,128,256]{2,1,0:T(8,128)S(1)}, f32[2,128,256]{2,1,0:T(8,128)S(1)}, u32[]{:S(2)}, u32[]{:S(2)}) collective-permute-start(f32[2,128,256]{2,1,0:T(8,128)S(1)} %get-tuple-element.36), channel_id=1, source_target_pairs={{2,4},{6,8},{10,12},{14,16},{18,20},{22,24},{26,28},{4,2},{8,6},{1... | collective-permute-start | bytes 786440 | tf_op jit(solution)/shard_map/ppermute | solution.py:108
  26.0 14.0 %copy-start.5 = (f32[2,128,512]{2,1,0:T(8,128)S(1)}, f32[2,128,512]{2,1,0:T(8,128)}, u32[]{:S(2)}) copy-start(f32[2,128,512]{2,1,0:T(8,128)} %refs_7_.1) | copy-start | bytes 1572868
  26.0 8.2 %collective-permute-start.7 = (f32[2,128,256]{2,1,0:T(8,128)S(1)}, f32[2,128,256]{2,1,0:T(8,128)S(1)}, u32[]{:S(2)}, u32[]{:S(2)}) collective-permute-start(f32[2,128,256]{2,1,0:T(8,128)S(1)} %get-tuple-element.35), channel_id=1, source_target_pairs={{0,2},{4,6},{8,10},{12,14},{16,18},{20,22},{24,26},{28,30},{2,0},{... | collective-permute-start | bytes 786440 | tf_op jit(solution)/shard_map/ppermute | solution.py:111
  29.5 10.5 %collective-permute-start.5 = (f32[2,128,256]{2,1,0:T(8,128)S(1)}, f32[2,128,256]{2,1,0:T(8,128)S(1)}, u32[]{:S(2)}, u32[]{:S(2)}) collective-permute-start(f32[2,128,256]{2,1,0:T(8,128)S(1)} %get-tuple-element.35), channel_id=1, source_target_pairs={{2,4},{6,8},{10,12},{14,16},{18,20},{22,24},{26,28},{4,2},{8,6},{1... | collective-permute-start | bytes 786440 | tf_op jit(solution)/shard_map/ppermute | solution.py:108
  41.1 6.6 %collective-permute-start.9 = (f32[2,128,256]{2,1,0:T(8,128)S(1)}, f32[2,128,256]{2,1,0:T(8,128)S(1)}, u32[]{:S(2)}, u32[]{:S(2)}) collective-permute-start(f32[2,128,256]{2,1,0:T(8,128)S(1)} %get-tuple-element.39), channel_id=1, source_target_pairs={{0,1},{1,0},{2,3},{3,2},{4,5},{5,4},{6,7},{7,6},{8,9},{9,8},{10,11... | collective-permute-start | bytes 786440 | tf_op jit(solution)/shard_map/ppermute | solution.py:100
  41.8 8.0 %collective-permute-start.12 = (f32[2,128,384]{2,1,0:T(8,128)S(1)}, f32[2,128,384]{2,1,0:T(8,128)S(1)}, u32[]{:S(2)}, u32[]{:S(2)}) collective-permute-start(f32[2,128,384]{2,1,0:T(8,128)S(1)} %get-tuple-element.37.refs_2_.refs_7_), channel_id=1, source_target_pairs={{0,2},{4,6},{8,10},{12,14},{16,18},{20,22},{24,26},{28,30},{2,0},{... | collective-permute-start | bytes 1179656 | tf_op jit(solution)/shard_map/ppermute | solution.py:111
  41.8 16.1 %collective-permute-start.10 = (f32[2,128,384]{2,1,0:T(8,128)S(1)}, f32[2,128,384]{2,1,0:T(8,128)S(1)}, u32[]{:S(2)}, u32[]{:S(2)}) collective-permute-start(f32[2,128,384]{2,1,0:T(8,128)S(1)} %get-tuple-element.37.refs_2_.refs_7_), channel_id=1, source_target_pairs={{2,4},{6,8},{10,12},{14,16},{18,20},{22,24},{26,28},{4,2},{8,6},{1... | collective-permute-start | bytes 1179656 | tf_op jit(solution)/shard_map/ppermute | solution.py:108
  47.8 10.1 %collective-permute-start.13 = (f32[2,128,256]{2,1,0:T(8,128)S(1)}, f32[2,128,256]{2,1,0:T(8,128)S(1)}, u32[]{:S(2)}, u32[]{:S(2)}) collective-permute-start(f32[2,128,256]{2,1,0:T(8,128)S(1)} %shard_map.80.refs_3_.refs_8_), channel_id=1, source_target_pairs={{0,2},{4,6},{8,10},{12,14},{16,18},{20,22},{24,26},{28,30},{2,0},{... | collective-permute-start | bytes 786440 | tf_op jit(solution)/shard_map/ppermute | solution.py:111
  47.9 12.8 %collective-permute-start.11 = (f32[2,128,256]{2,1,0:T(8,128)S(1)}, f32[2,128,256]{2,1,0:T(8,128)S(1)}, u32[]{:S(2)}, u32[]{:S(2)}) collective-permute-start(f32[2,128,256]{2,1,0:T(8,128)S(1)} %shard_map.80.refs_3_.refs_8_), channel_id=1, source_target_pairs={{2,4},{6,8},{10,12},{14,16},{18,20},{22,24},{26,28},{4,2},{8,6},{1... | collective-permute-start | bytes 786440 | tf_op jit(solution)/shard_map/ppermute | solution.py:108
  61.3 10.7 %collective-permute-start.17 = (f32[2,128,256]{2,1,0:T(8,128)S(1)}, f32[2,128,256]{2,1,0:T(8,128)S(1)}, u32[]{:S(2)}, u32[]{:S(2)}) collective-permute-start(f32[2,128,256]{2,1,0:T(8,128)S(1)} %get-tuple-element.44), channel_id=1, source_target_pairs={{0,2},{4,6},{8,10},{12,14},{16,18},{20,22},{24,26},{28,30},{2,0},{... | collective-permute-start | bytes 786440 | tf_op jit(solution)/shard_map/ppermute | solution.py:111
  61.4 10.6 %collective-permute-start.15 = (f32[2,128,256]{2,1,0:T(8,128)S(1)}, f32[2,128,256]{2,1,0:T(8,128)S(1)}, u32[]{:S(2)}, u32[]{:S(2)}) collective-permute-start(f32[2,128,256]{2,1,0:T(8,128)S(1)} %get-tuple-element.44), channel_id=1, source_target_pairs={{2,4},{6,8},{10,12},{14,16},{18,20},{22,24},{26,28},{4,2},{8,6},{1... | collective-permute-start | bytes 786440 | tf_op jit(solution)/shard_map/ppermute | solution.py:108
  66.6 5.4 %collective-permute-start.16 = (f32[2,128,256]{2,1,0:T(8,128)S(1)}, f32[2,128,256]{2,1,0:T(8,128)S(1)}, u32[]{:S(2)}, u32[]{:S(2)}) collective-permute-start(f32[2,128,256]{2,1,0:T(8,128)S(1)} %get-tuple-element.43), channel_id=1, source_target_pairs={{0,2},{4,6},{8,10},{12,14},{16,18},{20,22},{24,26},{28,30},{2,0},{... | collective-permute-start | bytes 786440 | tf_op jit(solution)/shard_map/ppermute | solution.py:111
  70.0 10.5 %collective-permute-start.14 = (f32[2,128,256]{2,1,0:T(8,128)S(1)}, f32[2,128,256]{2,1,0:T(8,128)S(1)}, u32[]{:S(2)}, u32[]{:S(2)}) collective-permute-start(f32[2,128,256]{2,1,0:T(8,128)S(1)} %get-tuple-element.43), channel_id=1, source_target_pairs={{2,4},{6,8},{10,12},{14,16},{18,20},{22,24},{26,28},{4,2},{8,6},{1... | collective-permute-start | bytes 786440 | tf_op jit(solution)/shard_map/ppermute | solution.py:108
  81.5 5.0 %collective-permute-start.18 = (f32[2,128,128]{2,1,0:T(8,128)S(1)}, f32[2,128,128]{2,1,0:T(8,128)S(1)}, u32[]{:S(2)}, u32[]{:S(2)}) collective-permute-start(f32[2,128,128]{2,1,0:T(8,128)S(1)} %shard_map.84), channel_id=1, source_target_pairs={{0,1},{1,0},{2,3},{3,2},{4,5},{5,4},{6,7},{7,6},{8,9},{9,8},{10,11... | collective-permute-start | bytes 393224 | tf_op jit(solution)/shard_map/ppermute | solution.py:100

commit v4 on v3

--- a/solution.py
+++ b/solution.py
@@ -18,6 +18,7 @@
 VMEM = pl.BlockSpec(memory_space=pltpu.VMEM)
 SMEM = pl.BlockSpec(memory_space=pltpu.SMEM)
 HBM = pl.BlockSpec(memory_space=pltpu.HBM)
+ANY = pl.BlockSpec(memory_space=pl.ANY)
 
 
 def split_numpy(table):
@@ -125,12 +126,39 @@
     return pl.ds(pl.multiple_of(tile * LANES, LANES), count * LANES)
 
 
-def assemble(canvas, pieces, starts, tiles):
-    blank = jnp.zeros(canvas.shape[:-1] + (LANES,), jnp.float32)
-    canvas[:, :, lanes(0)] = blank
-    canvas[:, :, lanes(tiles - 1)] = blank
-    for piece, start in zip(pieces, starts):
-        canvas[:, :, lanes(start, piece.shape[2] // LANES)] = piece[:, : canvas.shape[1]]
+def pick_tile(plan, target, pieces, tile, t):
+    rows = target.shape[1]
+    if plan.paired:
+
+        @pl.when(tile == (plan.tiles - 1) * t)
+        def _():
+            target[...] = jnp.zeros(target.shape, jnp.float32)
+
+    for ref, offset, count, start in pieces:
+
+        @pl.when((tile >= start) & (tile < start + count))
+        def _(ref=ref, offset=offset, start=start):
+            target[...] = ref[:, :rows, lanes(tile - start + offset)]
+
+
+def lay_out(refs, starts):
+    return [(ref, 0, ref.shape[2] // LANES, start) for ref, start in zip(refs, starts)]
+
+
+def chunks(count):
+    return [min(2, count - first) for first in range(0, count, 2)]
+
+
+def chunk_starts(start, count):
+    return [start + 2 * index for index in range(len(chunks(count)))]
+
+
+def spread(source, targets):
+    offset = 0
+    for target in targets:
+        columns = target.shape[2]
+        target[...] = source[:, :, offset : offset + columns]
+        offset += columns
 
 
 def rows_at(ref, start, count):
@@ -171,17 +199,26 @@
         copy.wait()
 
 
-def halo_message_kernel(centres, counts, received, message):
+def halo_message_kernel(plan, block, centres, counts, *rest):
     s, _ = here()
-    rows = received.shape[1]
-    message[:, :rows] = received[...]
+    received, messages, near = rest[: plan.sides], rest[plan.sides : 2 * plan.sides], rest[2 * plan.sides :]
     own = info_rows(centres, counts[s])
-    message[0, rows:] = own
-    message[1, rows:] = own
-
-
-def pair_kernel(base, received, inverse, result):
-    result[...] = base[...] - received[...] * inverse[...][None]
+    for source, message in zip(received, messages):
+        rows = source.shape[1]
+        message[:, :rows] = source[...]
+        message[0, rows:] = own
+        message[1, rows:] = own
+    spread(block, near)
+
+
+def pair_kernel(sides, middle, *rest):
+    bases, received, inverses, results = (rest[k * sides : (k + 1) * sides] for k in range(4))
+    near = rest[4 * sides :]
+    for base, other, inverse, result, copy in zip(bases, received, inverses, results, near):
+        values = base[...] - other[...] * inverse[...][None]
+        result[...] = values
+        copy[...] = values
+    spread(middle, near[sides:])
 
 
 def prepare_kernel(centres, probe, amps, order, rolled, ordered, padded):
@@ -265,10 +302,10 @@
         pair[...] = inverse[:, lanes(start, 2)]
 
 
-def term_kernel(plan, slot, starts, centres, counts, *rest):
-    pieces = len(starts(0))
-    own, far, near = (rest[k * pieces : (k + 1) * pieces] for k in range(3))
-    probe, amps, tables, outer, inner, window, canvas = rest[3 * pieces :]
+def term_kernel(plan, slot, layout, pieces, copied, centres, counts, *rest):
+    refs, rest = rest[:pieces], rest[pieces:]
+    earlier, (probe, amps, tables, outer, inner), rest = rest[:copied], rest[copied : copied + 5], rest[copied + 5 :]
+    near_outers, (window, picked) = rest[:-2], rest[-2:]
     size = probe.shape[2]
     half = size // 2
     s, t = here()
@@ -289,22 +326,20 @@
         from_tile = lax.broadcasted_iota(jnp.int32, (half, LANES), 1) >= rest_col
         from_upper = lax.broadcasted_iota(jnp.int32, (half, LANES), 0) >= row
         side = far_side(s)
+        own, far, near = layout(refs, t)
         for kind, source in ((1, own), (1 + side, far), (1 - side, near)):
-            assemble(canvas.at[kind], source, starts(t), plan.tiles)
-
-        def pick(kind, part, index):
-            return canvas[kind, part, :, lanes(index)]
+            for step in range(3):
+                pick_tile(plan, picked.at[kind, step], source, tile + step, t)
 
         for part in range(2):
-            edge = [jnp.where(from_tile, pick(kind, part, tile), pick(kind, part, tile + 2)) for kind in range(3)]
-            middle = [pick(kind, part, tile + 1) for kind in range(3)]
+            edge = [jnp.where(from_tile, picked[kind, 0, part], picked[kind, 2, part]) for kind in range(3)]
             window[part, :half, lanes(first)] = jnp.where(from_upper, edge[0], edge[2])
             window[part, half:, lanes(first)] = edge[1]
-            window[part, :half, lanes(1 - first)] = jnp.where(from_upper, middle[0], middle[2])
-            window[part, half:, lanes(1 - first)] = middle[1]
-
-        probe_real = probe[0, 0]
-        probe_imag = probe[0, 1]
+            window[part, :half, lanes(1 - first)] = jnp.where(from_upper, picked[0, 1, part], picked[2, 1, part])
+            window[part, half:, lanes(1 - first)] = picked[1, 1, part]
+
+        probe_real = probe[slot, 0]
+        probe_imag = probe[slot, 1]
         exit_real = probe_real * window[0] - probe_imag * window[1]
         exit_imag = probe_real * window[1] + probe_imag * window[0]
 
@@ -324,7 +359,7 @@
             pattern = table_times(tables[parity, 1], halves[parity])
             far_real = pattern[:half]
             far_imag = pattern[half:]
-            amplitude = amps[0, parity * half : (parity + 1) * half]
+            amplitude = amps[slot, parity * half : (parity + 1) * half]
             factor = 1.0 - amplitude * lax.rsqrt(far_real * far_real + far_imag * far_imag + SMOOTH)
             miss = jnp.concatenate([far_real * factor, far_imag * factor], axis=0)
             back.append(table_times(tables[parity, 0], miss))
@@ -332,8 +367,8 @@
         imag = jnp.concatenate([back[0][half:] + back[1][half:], back[0][half:] - back[1][half:]], axis=0)
         both = []
         for parity in range(2):
-            picked = slice(parity * half, (parity + 1) * half)
-            both.append(times_table(jnp.concatenate([real[:, picked], imag[:, picked]], axis=1), tables[parity, 1]))
+            columns = slice(parity * half, (parity + 1) * half)
+            both.append(times_table(jnp.concatenate([real[:, columns], imag[:, columns]], axis=1), tables[parity, 1]))
         near_real = jnp.concatenate([both[0][:, :half] + both[1][:, :half], both[0][:, :half] - both[1][:, :half]], axis=1)
         near_imag = jnp.concatenate([both[0][:, half:] + both[1][:, half:], both[0][:, half:] - both[1][:, half:]], axis=1)
         term_real = probe_real * near_real + probe_imag * near_imag
@@ -343,82 +378,119 @@
         inner[0] = term_real[half:]
         inner[1] = term_imag[half:]
 
-
-def gather_terms(plan, slots, s, info, own, far, near, canvas):
-    half = canvas.shape[1]
-    side = far_side(s)
+    for source, target in zip((*earlier, outer), near_outers):
+        target[...] = source[...]
+
+
+class Patch:
+    def __init__(self, plan, info, s, patch, slot, down):
+        half = patch.shape[1]
+        index = (1 if down is None else 1 + down) * (plan.sides + 1)
+        row = info[index, 2 * slot]
+        col = info[index, 2 * slot + 1]
+        self.patch = patch
+        self.tile = col // LANES
+        self.first = self.tile % 2
+        self.from_tile = lax.broadcasted_iota(jnp.int32, (half, LANES), 1) >= col % LANES
+        self.rows = None
+        if down is not None:
+            line = lax.broadcasted_iota(jnp.int32, (half, LANES), 0)
+            self.rows = (line >= jnp.where(down > 0, row, 0)) & (line < jnp.where(down > 0, half, row))
+
+    def lines(self, part, place):
+        values = self.patch[part, :, lanes(place)]
+        return values if self.rows is None else jnp.where(self.rows, values, 0.0)
+
+    def tiles(self, part):
+        edge = self.lines(part, self.first)
+        middle = self.lines(part, 1 - self.first)
+        return jnp.where(self.from_tile, edge, 0.0), middle, jnp.where(self.from_tile, 0.0, edge)
+
+    def add_to(self, canvas):
+        for part in range(2):
+            for step, values in enumerate(self.tiles(part)):
+                canvas[part, :, lanes(self.tile + step)] += values
+
+    def add_tile_to(self, total, tile):
+        for step in range(3):
+
+            @pl.when(self.tile + step == tile)
+            def _(step=step):
+                for part in range(2):
+                    total[part] += self.tiles(part)[step]
+
+
+def early_sum_kernel(plan, slots, info, *rest):
+    inner, far, canvas = rest[:slots], rest[slots : 2 * slots - 1], rest[2 * slots - 1]
+    s, _ = here()
     canvas[...] = jnp.zeros(canvas.shape, jnp.float32)
-    lane = lax.broadcasted_iota(jnp.int32, (half, LANES), 1)
-    line = lax.broadcasted_iota(jnp.int32, (half, LANES), 0)
-    for down, patches in ((None, own), (side, far), (-side, near)):
-        index = (1 if down is None else 1 + down) * (plan.sides + 1)
-        for slot in range(slots):
-            row = info[index, 2 * slot]
-            col = info[index, 2 * slot + 1]
-            tile = col // LANES
-            first = tile % 2
-            from_tile = lane >= col % LANES
-            if down is not None:
-                there = (line >= jnp.where(down > 0, row, 0)) & (line < jnp.where(down > 0, half, row))
-            for part in range(2):
-                edge = patches[slot][part, :, lanes(first)]
-                middle = patches[slot][part, :, lanes(1 - first)]
-                if down is not None:
-                    edge = jnp.where(there, edge, 0.0)
-                    middle = jnp.where(there, middle, 0.0)
-                canvas[part, :, lanes(tile)] += jnp.where(from_tile, edge, 0.0)
-                canvas[part, :, lanes(tile + 1)] += middle
-                canvas[part, :, lanes(tile + 2)] += jnp.where(from_tile, 0.0, edge)
-
-
-def step_kernel(plan, slots, starts, info, *rest):
-    patches = [rest[k * slots : (k + 1) * slots] for k in range(3)]
-    rest = rest[3 * slots :]
-    pieces = len(starts(0))
-    own = rest[:pieces]
-    inverse, middle = rest[pieces : pieces + 2]
-    bases = rest[pieces + 2 : pieces + 2 + plan.sides]
-    sums = rest[pieces + 2 + plan.sides : pieces + 2 + 2 * plan.sides]
-    current, canvas = rest[pieces + 2 + 2 * plan.sides :]
-    s, t = here()
-    gather_terms(plan, slots, s, info, *patches, canvas)
-    assemble(current, own, starts(t), plan.tiles)
-    where = lanes(plan.mid_start(t), plan.mid_tiles)
-    middle[...] = current[:, :, where] - canvas[:, :, where] * inverse[:, where][None]
+    for slot in range(slots):
+        Patch(plan, info, s, inner[slot], slot, None).add_to(canvas)
+    for slot in range(slots - 1):
+        Patch(plan, info, s, far[slot], slot, far_side(s)).add_to(canvas)
+
+
+def near_sum_kernel(plan, slots, info, early, *rest):
+    near, canvas = rest[:slots], rest[slots]
+    s, _ = here()
+    canvas[...] = early[...]
+    for slot in range(slots):
+        Patch(plan, info, s, near[slot], slot, -far_side(s)).add_to(canvas)
+
+
+def last_patch(plan, slots, info, patch):
+    s, _ = here()
+    return Patch(plan, info, s, patch, slots - 1, far_side(s))
+
+
+def middle_kernel(plan, slots, layout, pieces, info, early, patch, inverse, *rest):
+    refs, (middle, canvas) = rest[:pieces], rest[pieces:]
+    _, t = here()
+    canvas[...] = early[...]
+    last_patch(plan, slots, info, patch).add_to(canvas)
+    for step in range(plan.mid_tiles):
+        tile = plan.mid_start(t) + step
+        where = lanes(step)
+        pick_tile(plan, middle.at[:, :, where], layout(refs, t)[0], tile, t)
+        middle[:, :, where] -= canvas[:, :, lanes(tile)] * inverse[:, lanes(tile)][None]
+
+
+def boundary_kernel(plan, layout, pieces, canvas, inverse, _, *rest):
+    refs, outs = rest[:pieces], rest[pieces:]
+    bases, sums = outs[: plan.sides], outs[plan.sides :]
+    _, t = here()
     for base, total, start in zip(bases, sums, plan.pair_starts(t)):
-        where = lanes(start, 2)
-        partial = canvas[:, :, where]
-        total[...] = partial
-        base[...] = current[:, :, where] - partial * inverse[:, where][None]
-
-
-def halo_sum_kernel(plan, slots, info, *rest):
-    patches = [rest[k * slots : (k + 1) * slots] for k in range(3)]
-    sums = rest[3 * slots : 3 * slots + plan.sides]
-    canvas = rest[3 * slots + plan.sides]
-    s, t = here()
-    gather_terms(plan, slots, s, info, *patches, canvas)
+        total[...] = canvas[:, :, lanes(start, 2)]
+        for step in range(2):
+            where = lanes(step)
+            pick_tile(plan, base.at[:, :, where], layout(refs, t)[0], start + step, t)
+            base[:, :, where] -= total[:, :, where] * inverse[:, lanes(start + step)][None]
+
+
+def halo_sum_kernel(plan, slots, info, early, patch, *sums):
+    _, t = here()
+    last = last_patch(plan, slots, info, patch)
     for total, tile in zip(sums, plan.halo_tiles(t)):
-        total[...] = canvas[:, :, lanes(tile)]
-
-
-def last_kernel(plan, slots, starts, info, *rest):
-    patches = [rest[k * slots : (k + 1) * slots] for k in range(3)]
-    rest = rest[3 * slots :]
-    pieces = len(starts(0))
-    own = rest[:pieces]
-    inverse, nearly = rest[pieces : pieces + 2]
-    bases = rest[pieces + 2 : pieces + 2 + plan.sides]
-    current, canvas, sem = rest[pieces + 2 + plan.sides :]
-    s, t = here()
-    gather_terms(plan, slots, s, info, *patches, canvas)
-    assemble(current, own, starts(t), plan.tiles)
-    where = lanes(1, plan.own)
-    current[:, :, where] = current[:, :, where] - canvas[:, :, where] * inverse[:, where][None]
-    copy = pltpu.make_async_copy(current.at[:, :, where], nearly, sem)
+        total[...] = early[:, :, lanes(tile)]
+        last.add_tile_to(total, tile)
+
+
+def last_kernel(plan, slots, layout, pieces, info, early, patch, inverse, _, *rest):
+    refs, rest = rest[:pieces], rest[pieces:]
+    nearly, bases = rest[0], rest[1 : 1 + plan.sides]
+    current, canvas, sem = rest[1 + plan.sides :]
+    _, t = here()
+    canvas[...] = early[...]
+    last_patch(plan, slots, info, patch).add_to(canvas)
+    for step in range(plan.own):
+        tile = 1 + step
+        where = lanes(step)
+        pick_tile(plan, current.at[:, :, where], layout(refs, t)[0], tile, t)
+        current[:, :, where] -= canvas[:, :, lanes(tile)] * inverse[:, lanes(tile)][None]
+    copy = pltpu.make_async_copy(current, nearly, sem)
     copy.start()
     for base, tile in zip(bases, plan.edge_tiles(t)):
-        base[...] = current[:, :, lanes(tile)]
+        base[...] = current[:, :, lanes(tile - 1)]
     copy.wait()
 
 
@@ -435,8 +507,8 @@
         copy.wait()
 
 
-def call(kernel, outs, scratch, ins, flops=10**9, size=10**6, in_specs=None, out_specs=None, **options):
-    return pl.pallas_call(
+def call(kernel, outs, scratch, ins, flops=10**5, size=10**4, in_specs=None, out_specs=None, **options):
+    result = pl.pallas_call(
         kernel,
         out_shape=outs,
         in_specs=in_specs or [SMEM if value.dtype == jnp.int32 else VMEM for value in ins],
@@ -446,6 +518,7 @@
         cost_estimate=pl.CostEstimate(flops=flops, bytes_accessed=size, transcendentals=0),
         **options,
     )(*ins)
+    return list(result) if isinstance(outs, list) else result
 
 
 def on_device(plan, object_field, probe_field, amplitudes, centres, counts):
@@ -474,7 +547,6 @@
         in_specs=[HBM, SMEM, SMEM],
     )
     halos = plan.across(messages)
-    near_block = plan.near_rows(object_field)
     far_block = plan.far_rows(object_field)
     rolled, ordered = call(
         prepare_kernel,
@@ -483,12 +555,16 @@
         [spots, probe_field, own_amps, order],
     )
     halos, rolled, ordered = lax.optimization_barrier((halos, rolled, ordered))
-    passed = [
-        call(halo_message_kernel, shape((2, half + 16, LANES), f32), [], [spots, counts, halo], flops=10**7)
-        for halo in halos
-    ]
-    near = [near_block] + [plan.near_rows(message) for message in passed]
+    near_runs = [shape((2, half, count * LANES), f32) for count in chunks(plan.own)]
+    messages = call(
+        lambda *refs: halo_message_kernel(plan, *refs),
+        [shape((2, half + 16, LANES), f32)] * sides + near_runs,
+        [],
+        [object_field, spots, counts, *halos],
+    )
+    passed = messages[:sides]
     far = [far_block] + [plan.far_rows(message) for message in passed]
+    near = [plan.near_rows(piece) for piece in messages]
     own = [object_field] + passed
     inverse, info, *inverse_pairs = call(
         lambda *refs: light_kernel(plan, slots, *refs),
@@ -499,67 +575,95 @@
             pltpu.VMEM((3 * (sides + 1), 8, LANES), jnp.int32),
             dma,
         ],
-        passed + far[1:] + near[1:] + [probe_field],
+        passed + far[1:] + near[:sides] + [probe_field],
         out_specs=[VMEM, SMEM] + [VMEM] * sides,
     )
 
-    def starts(t):
-        return [1] + plan.halo_tiles(t)
-
-    def later_starts(t):
-        return [plan.mid_start(t)] + plan.pair_starts(t)
+    def runs_layout(refs, main, count, side_starts):
+        starts = [main] + side_starts
+        own, far, near = refs[: 1 + sides], refs[1 + sides : 2 + 2 * sides], refs[2 + 2 * sides :]
+        return lay_out(own, starts), lay_out(far, starts), lay_out(near, side_starts + chunk_starts(main, count))
+
+    def first_layout(refs, t):
+        return runs_layout(refs, 1, plan.own, plan.halo_tiles(t))
+
+    def later_layout(refs, t):
+        return runs_layout(refs, plan.mid_start(t), plan.mid_tiles, plan.pair_starts(t))
+
+    layout = first_layout
 
     for sweep in range(ITERS):
-        inner, outer_far, outer_near = [], [], []
+        pieces = own + far + near
+        inner, outer, outer_far = [], [], []
         for slot in range(slots):
-            outer_part, inner_part = pl.pallas_call(
-                lambda *refs, slot=slot, starts=starts: term_kernel(plan, slot, starts, *refs),
-                out_shape=[shape((2, half, size), f32)] * 2,
-                in_specs=[SMEM] * 2 + [VMEM] * (3 * len(own)) + [
-                    pl.BlockSpec((1, 2, size, size), lambda i, slot=slot: (slot, 0, 0, 0)),
-                    pl.BlockSpec((1, size, size), lambda i, slot=slot: (slot, 0, 0)),
-                    VMEM,
-                ],
-                out_specs=[VMEM] * 2,
-                grid=(1,),
-                scratch_shapes=[pltpu.VMEM((2, size, size), f32), pltpu.VMEM((3, 2, half, width), f32)],
-                compiler_params=pltpu.CompilerParams(vmem_limit_bytes=VMEM_BYTES),
-                cost_estimate=pl.CostEstimate(flops=2 * 10**9, bytes_accessed=6 * 10**6, transcendentals=0),
-            )(spots, counts, *own, *far, *near, rolled, ordered, tables)
+            last = slot == slots - 1
+            earlier = outer if last else []
+            patch = shape((2, half, size), f32)
+            outer_part, inner_part, *copies = call(
+                lambda *refs, slot=slot, layout=layout, copied=len(earlier): term_kernel(
+                    plan, slot, layout, len(pieces), copied, *refs
+                ),
+                [patch] * (2 + slots * last),
+                [pltpu.VMEM((2, size, size), f32), pltpu.VMEM((3, 3, 2, half, LANES), f32)],
+                [spots, counts, *pieces, *earlier, rolled, ordered, tables],
+            )
             inner.append(inner_part)
-            outer_near.append(plan.near_rows(outer_part))
+            outer.append(outer_part)
             outer_far.append(plan.far_rows(outer_part))
-        patches = inner + outer_far + outer_near
+        outer_near = [plan.near_rows(copy) for copy in copies]
+        early = call(
+            lambda *refs: early_sum_kernel(plan, slots, *refs),
+            shape((2, half, width), f32),
+            [],
+            [info, *inner, *outer_far[:-1]],
+        )
+        early = call(
+            lambda *refs: near_sum_kernel(plan, slots, *refs),
+            shape((2, half, width), f32),
+            [],
+            [info, early, *outer_near],
+        )
         if sweep < ITERS - 1:
-            middle, *rest = call(
-                lambda *refs, starts=starts: step_kernel(plan, slots, starts, *refs),
-                [shape((2, half, plan.mid_tiles * LANES), f32)] + [shape((2, half, 2 * LANES), f32)] * (2 * sides),
-                [pltpu.VMEM((2, half, width), f32)] * 2,
-                [info] + patches + own + [inverse],
+            middle, total = call(
+                lambda *refs, layout=layout: middle_kernel(plan, slots, layout, len(own), *refs),
+                [shape((2, half, plan.mid_tiles * LANES), f32), shape((2, half, width), f32)],
+                [],
+                [info, early, outer_far[-1], inverse, *own],
             )
-            bases, sums = rest[:sides], rest[sides:]
-            near_middle = plan.near_rows(middle)
+            far_middle = plan.far_rows(middle)
+            boundary = call(
+                lambda *refs, layout=layout: boundary_kernel(plan, layout, len(own), *refs),
+                [shape((2, half, 2 * LANES), f32)] * (2 * sides),
+                [],
+                [total, inverse, middle, *own],
+                in_specs=[VMEM, VMEM, ANY] + [VMEM] * len(own),
+            )
+            bases, sums = boundary[:sides], boundary[sides:]
             received = plan.across(sums)
-            far_middle = plan.far_rows(middle)
-            pairs = [
-                call(pair_kernel, shape(base.shape, f32), [], [base, other, inv], flops=10**7)
-                for base, other, inv in zip(bases, received, inverse_pairs)
-            ]
+            near_runs = [shape((2, half, count * LANES), f32) for count in chunks(plan.mid_tiles)]
+            updated = call(
+                lambda *refs: pair_kernel(sides, *refs),
+                [shape((2, half, 2 * LANES), f32)] * (2 * sides) + near_runs,
+                [],
+                [middle, *bases, *received, *inverse_pairs],
+            )
+            pairs = updated[:sides]
             own = [middle] + pairs
-            near = [near_middle] + [plan.near_rows(piece) for piece in pairs]
             far = [far_middle] + [plan.far_rows(piece) for piece in pairs]
-            starts = later_starts
+            near = [plan.near_rows(piece) for piece in updated[sides:]]
+            layout = later_layout
     sums = call(
         lambda *refs: halo_sum_kernel(plan, slots, *refs),
         [shape((2, half, LANES), f32)] * sides,
-        [pltpu.VMEM((2, half, width), f32)],
-        [info] + patches,
+        [],
+        [info, early, outer_far[-1]],
     )
     nearly, *bases = call(
-        lambda *refs: last_kernel(plan, slots, starts, *refs),
+        lambda *refs: last_kernel(plan, slots, layout, len(own), *refs),
         [shape((2, half, block_cols), f32)] + [shape((2, half, LANES), f32)] * sides,
-        [pltpu.VMEM((2, half, width), f32)] * 2 + [dma],
-        [info] + patches + own + [inverse],
+        [pltpu.VMEM((2, half, block_cols), f32), pltpu.VMEM((2, half, width), f32), dma],
+        [info, early, outer_far[-1], inverse, sums[0], *own],
+        in_specs=[SMEM, VMEM, VMEM, VMEM, ANY] + [VMEM] * len(own),
         out_specs=[HBM] + [VMEM] * sides,
     )
     received = plan.across(sums)

time: 87.7 us -> 86.1 us (0.982)
  waiting for transfers between devices: 40.3 us -> 26.8 us
  Pallas kernels: 16.5 us -> 23.9 us
  local copies, waits for them, and re-layouts: 1.73 us -> 4.75 us
  starting transfers between devices: 28.4 us -> 29.5 us
    pallas_call x9 -> x18, Pallas kernels: 10.2 us -> 23.9 us  [call(): pl.pallas_call(kernel, out_shape=outs, in_specs=in_specs or [SMEM if valu...]
    ppermute x8, waiting for transfers between devices: 30.8 us -> 20.6 us  [far_rows(): return lax.ppermute(values, 'sx', self.swaps(1))]
    pallas_call x4 -> x0, Pallas kernels: 6.26 us -> none  [on_device(): pl.pallas_call(lambda *refs, slot=slot, starts=starts: term_kernel(plan,...]
    ppermute x3, waiting for transfers between devices: 9.49 us -> 6.18 us  [across(): return [lax.ppermute(values[0], axis_name, [(0, 1), (1, 0)])]]
    unnamed x16 -> x18, local copies, waits for them, and re-layouts: 1.73 us -> 4.75 us
    ppermute x8 -> x10, starting transfers between devices: 7.4 us -> 6.15 us  [near_rows(): return lax.ppermute(values, 'sx', self.swaps(0))]
    ppermute x8, starting transfers between devices: 18.4 us -> 19.6 us  [far_rows(): return lax.ppermute(values, 'sx', self.swaps(1))]
    ppermute x3, starting transfers between devices: 2.62 us -> 3.74 us  [across(): return [lax.ppermute(values[0], axis_name, [(0, 1), (1, 0)])]]
  transfers between devices with their start and end apart: 19 -> 21, of which waited for: 8 -> 7; matrix products, arithmetic and copies ran while one was open for 0% -> 0% of each run, Pallas kernels for 14% -> 19%
where the time goes in v4:
time: 86.1 us; the launch traced here: 85.2 us
  starting transfers between devices  29.5 us (34%)
  waiting for transfers between devices  26.8 us (31%)
  Pallas kernels  23.9 us (28%)
  local copies, waits for them, and re-layouts  4.75 us (6%)
    pallas_call x18, Pallas kernels, call(): pl.pallas_call(kernel, out_shape=outs, in_specs=in_specs or [SMEM if valu...  23.9 us
    ppermute x8, waiting for transfers between devices, far_rows(): return lax.ppermute(values, 'sx', self.swaps(1))  20.6 us
    ppermute x8, starting transfers between devices, far_rows(): return lax.ppermute(values, 'sx', self.swaps(1))  19.6 us
    ppermute x3, waiting for transfers between devices, across(): return [lax.ppermute(values[0], axis_name, [(0, 1), (1, 0)])]  6.18 us
    ppermute x10, starting transfers between devices, near_rows(): return lax.ppermute(values, 'sx', self.swaps(0))  6.15 us
    unnamed x18, local copies, waits for them, and re-layouts  4.75 us
    ppermute x3, starting transfers between devices, across(): return [lax.ppermute(values[0], axis_name, [(0, 1), (1, 0)])]  3.74 us
  transfers between devices with their start and end apart: 21, of which 7 were waited for; matrix products, arithmetic and copies ran while one was open for 0% of the time, Pallas kernels for 19%

profile of v4, /device:TPU:10, one launch (start us, length us, event | category | flops | bytes accessed | tf_op | source)
XLA Modules:
  0.0 85.2 jit_solution(6063848087145668598)
XLA Ops:
  0.0 1.9 %collective-permute-start.3 = (f32[2,128,512]{2,1,0:T(8,128)}, f32[2,128,512]{2,1,0:T(8,128)S(1)}, u32[]{:S(2)}, u32[]{:S(2)}) collective-permute-start(f32[2,128,512]{2,1,0:T(8,128)} %refs_3_.3), channel_id=1, source_target_pairs={{2,4},{6,8},{10,12},{14,16},{18,20},{22,24},{26,28},{4,2},{8,6},{1... | collective-permute-start | bytes 1572872 | tf_op jit(solution)/shard_map/ppermute | solution.py:109
  2.6 1.0 %copy-done = f32[2,128,512]{2,1,0:T(8,128)S(1)} copy-done((f32[2,128,512]{2,1,0:T(8,128)S(1)}, f32[2,128,512]{2,1,0:T(8,128)}, u32[]{:S(2)}) %copy-start) | copy-done | bytes 524312
  4.3 1.6 %collective-permute-start = (f32[2,136,128]{2,1,0:T(8,128)S(1)}, f32[2,136,128]{2,1,0:T(8,128)S(1)}, u32[]{:S(2)}, u32[]{:S(2)}) collective-permute-start(f32[2,136,128]{2,1,0:T(8,128)S(1)} %shard_map.73), channel_id=1, source_target_pairs={{0,1},{1,0},{2,3},{3,2},{4,5},{5,4},{6,7},{7,6},{8,9},{9,8},{10,11... | collective-permute-start | bytes 417800 | tf_op jit(solution)/shard_map/ppermute | solution.py:101
  5.8 1.0 %copy-done.3 = f32[2,256,256]{2,1,0:T(8,128)S(1)} copy-done((f32[2,256,256]{2,1,0:T(8,128)S(1)}, f32[2,256,256]{2,1,0:T(8,128)}, u32[]{:S(2)}) %copy-start.3) | copy-done | bytes 524312
  6.9 1.0 %copy-done.5 = f32[1,1,2,256,256]{4,3,2,1,0:T(8,128)S(1)} copy-done((f32[1,1,2,256,256]{4,3,2,1,0:T(8,128)S(1)}, f32[1,1,2,256,256]{4,3,2,1,0:T(8,128)}, u32[]{:S(2)}) %copy-start.5) | copy-done | bytes 524312
  7.9 0.9 %copy-done.6 = bf16[2,256,256]{2,1,0:T(8,128)(2,1)S(1)} copy-done((bf16[2,256,256]{2,1,0:T(8,128)(2,1)S(1)}, bf16[2,256,256]{2,1,0:T(8,128)(2,1)}, u32[]{:S(2)}) %copy-start.6) | copy-done | bytes 262168
  8.9 1.5 %shard_map.74 = (f32[2,2,256,256]{3,2,1,0:T(8,128)S(1)}, f32[2,256,256]{2,1,0:T(8,128)S(1)}) custom-call(s32[2,2]{1,0:T(2,128)S(1)} %bitcast.5, f32[2,256,256]{2,1,0:T(8,128)S(1)} %copy-done.3, f32[2,256,256]{2,1,0:T(8,128)S(1)} %bitcast.3, bf16[2,256,256]{2,1,0:T(8,128)(2,1)S(1)} %copy-done.6), custom_call_target="tpu_custom_call" | custom-call | flops 100000 | bytes 10000 | tf_op jit(solution)/shard_map/pallas_call | solution.py:511
  11.0 1.4 %collective-permute-start.4 = (f32[2,128,256]{2,1,0:T(8,128)S(1)}, f32[2,128,256]{2,1,0:T(8,128)S(1)}, u32[]{:S(2)}, u32[]{:S(2)}) collective-permute-start(f32[2,128,256]{2,1,0:T(8,128)S(1)} %get-tuple-element.44), channel_id=1, source_target_pairs={{0,2},{4,6},{8,10},{12,14},{16,18},{20,22},{24,26},{28,30},{2,0},{... | collective-permute-start | bytes 786440 | tf_op jit(solution)/shard_map/ppermute | solution.py:112
  12.5 2.4 %collective-permute-start.1 = (f32[2,144,128]{2,1,0:T(8,128)S(1)}, f32[2,144,128]{2,1,0:T(8,128)S(1)}, u32[]{:S(2)}, u32[]{:S(2)}) collective-permute-start(f32[2,144,128]{2,1,0:T(8,128)S(1)} %get-tuple-element.41.refs_0_.refs_3_.refs_5_.refs_4_), channel_id=1, source_target_pairs={{2,4},{6,8},{10,12},{14,16},{18,20},{22,24},{26,28},{4,2},{8,6},{1... | collective-permute-start | bytes 442376 | tf_op jit(solution)/shard_map/ppermute | solution.py:109
  15.0 1.3 %collective-permute-start.2 = (f32[2,144,128]{2,1,0:T(8,128)S(1)}, f32[2,144,128]{2,1,0:T(8,128)S(1)}, u32[]{:S(2)}, u32[]{:S(2)}) collective-permute-start(f32[2,144,128]{2,1,0:T(8,128)S(1)} %get-tuple-element.41.refs_0_.refs_3_.refs_5_.refs_4_), channel_id=1, source_target_pairs={{0,2},{4,6},{8,10},{12,14},{16,18},{20,22},{24,26},{28,30},{2,0},{... | collective-permute-start | bytes 442376 | tf_op jit(solution)/shard_map/ppermute | solution.py:112
  16.3 2.9 %collective-permute-done.1.refs_1_.refs_5_ = f32[2,144,128]{2,1,0:T(8,128)S(1)} collective-permute-done((f32[2,144,128]{2,1,0:T(8,128)S(1)}, f32[2,144,128]{2,1,0:T(8,128)S(1)}, u32[]{:S(2)}, u32[]{:S(2)}) %collective-permute-start.1) | collective-permute-done | bytes 147488 | tf_op jit(solution)/shard_map/ppermute | solution.py:109
  19.2 2.6 %shard_map.77 = (f32[2,128,256]{2,1,0:T(8,128)S(1)}, f32[2,128,256]{2,1,0:T(8,128)S(1)}) custom-call(s32[2,2]{1,0:T(2,128)S(1)} %bitcast.7, s32[16]{0:T(128)S(1)} %bitcast.13, f32[2,128,512]{2,1,0:T(8,128)S(1)} %copy-done.1, f32[2,144,128]{2,1,0:T(8,128)S(1)} %get-tuple-element.41.refs_0_.refs_3_.refs_5_.refs_4_, ...), custom_call_target="tpu_custom_call" | custom-call | flops 100000 | bytes 10000 | tf_op jit(solution)/shard_map/pallas_call | solution.py:511
  21.9 4.0 %collective-permute-start.6 = (f32[2,128,256]{2,1,0:T(8,128)S(1)}, f32[2,128,256]{2,1,0:T(8,128)S(1)}, u32[]{:S(2)}, u32[]{:S(2)}) collective-permute-start(f32[2,128,256]{2,1,0:T(8,128)S(1)} %get-tuple-element.49.refs_9_), channel_id=1, source_target_pairs={{2,4},{6,8},{10,12},{14,16},{18,20},{22,24},{26,28},{4,2},{8,6},{1... | collective-permute-start | bytes 786440 | tf_op jit(solution)/shard_map/ppermute | solution.py:109
  25.8 2.6 %shard_map.78 = (f32[2,128,256]{2,1,0:T(8,128)S(1)}, f32[2,128,256]{2,1,0:T(8,128)S(1)}, f32[2,128,256]{2,1,0:T(8,128)S(1)}, f32[2,128,256]{2,1,0:T(8,128)S(1)}) custom-call(s32[2,2]{1,0:T(2,128)S(1)} %bitcast.8, s32[16]{0:T(128)S(1)} %bitcast.14, f32[2,128,512]{2,1,0:T(8,128)S(1)} %copy-done.1, ...), custom_call_target="tpu_custom_call" | custom-call | flops 100000 | bytes 10000 | tf_op jit(solution)/shard_map/pallas_call | solution.py:511
  29.3 1.9 %collective-permute-start.9 = (f32[2,128,256]{2,1,0:T(8,128)S(1)}, f32[2,128,256]{2,1,0:T(8,128)S(1)}, u32[]{:S(2)}, u32[]{:S(2)}) collective-permute-start(f32[2,128,256]{2,1,0:T(8,128)S(1)} %get-tuple-element.53), channel_id=1, source_target_pairs={{2,4},{6,8},{10,12},{14,16},{18,20},{22,24},{26,28},{4,2},{8,6},{1... | collective-permute-start | bytes 786440 | tf_op jit(solution)/shard_map/ppermute | solution.py:109
  31.2 3.5 %shard_map.76 = (f32[128,768]{1,0:T(8,128)S(1)}, s32[6,128]{1,0:T(8,128)S(1)}, f32[128,256]{1,0:T(8,128)S(1)}) custom-call(f32[2,144,128]{2,1,0:T(8,128)S(1)} %get-tuple-element.41.refs_0_.refs_3_.refs_5_.refs_4_, f32[2,144,128]{2,1,0:T(8,128)S(1)} %collective-permute-done.1.refs_1_.refs_5_, f32[2,144,128]{2,1,0:T(8,128)S(1)} %collective-permute-done.2.refs_2_.refs_6_, ...), custom_call_target="tpu_custom_call" | custom-call | flops 100000 | bytes 10000 | tf_op jit(solution)/shard_map/pallas_call | solution.py:511
  36.4 3.4 %collective-permute-done.9.refs_2_ = f32[2,128,256]{2,1,0:T(8,128)S(1)} collective-permute-done((f32[2,128,256]{2,1,0:T(8,128)S(1)}, f32[2,128,256]{2,1,0:T(8,128)S(1)}, u32[]{:S(2)}, u32[]{:S(2)}) %collective-permute-start.9) | collective-permute-done | bytes 262176 | tf_op jit(solution)/shard_map/ppermute | solution.py:109
  39.8 0.8 shard_map.81
  40.7 1.6 %collective-permute-start.10 = (f32[2,128,256]{2,1,0:T(8,128)S(1)}, f32[2,128,256]{2,1,0:T(8,128)S(1)}, u32[]{:S(2)}, u32[]{:S(2)}) collective-permute-start(f32[2,128,256]{2,1,0:T(8,128)S(1)} %get-tuple-element.57), channel_id=1, source_target_pairs={{0,1},{1,0},{2,3},{3,2},{4,5},{5,4},{6,7},{7,6},{8,9},{9,8},{10,11... | collective-permute-start | bytes 786440 | tf_op jit(solution)/shard_map/ppermute | solution.py:101
  42.3 1.9 %collective-permute-start.11 = (f32[2,128,384]{2,1,0:T(8,128)S(1)}, f32[2,128,384]{2,1,0:T(8,128)S(1)}, u32[]{:S(2)}, u32[]{:S(2)}) collective-permute-start(f32[2,128,384]{2,1,0:T(8,128)S(1)} %get-tuple-element.54.refs_2_.refs_0_.refs_5_), channel_id=1, source_target_pairs={{2,4},{6,8},{10,12},{14,16},{18,20},{22,24},{26,28},{4,2},{8,6},{1... | collective-permute-start | bytes 1179656 | tf_op jit(solution)/shard_map/ppermute | solution.py:109
  44.3 3.4 %collective-permute-done.10.refs_2_ = f32[2,128,256]{2,1,0:T(8,128)S(1)} collective-permute-done((f32[2,128,256]{2,1,0:T(8,128)S(1)}, f32[2,128,256]{2,1,0:T(8,128)S(1)}, u32[]{:S(2)}, u32[]{:S(2)}) %collective-permute-start.10) | collective-permute-done | bytes 262176 | tf_op jit(solution)/shard_map/ppermute | solution.py:101
  47.7 1.9 %collective-permute-start.12 = (f32[2,128,256]{2,1,0:T(8,128)S(1)}, f32[2,128,256]{2,1,0:T(8,128)S(1)}, u32[]{:S(2)}, u32[]{:S(2)}) collective-permute-start(f32[2,128,256]{2,1,0:T(8,128)S(1)} %get-tuple-element.59.refs_3_.refs_6_), channel_id=1, source_target_pairs={{2,4},{6,8},{10,12},{14,16},{18,20},{22,24},{26,28},{4,2},{8,6},{1... | collective-permute-start | bytes 786440 | tf_op jit(solution)/shard_map/ppermute | solution.py:109
  49.6 1.4 %collective-permute-start.13 = (f32[2,128,256]{2,1,0:T(8,128)S(1)}, f32[2,128,256]{2,1,0:T(8,128)S(1)}, u32[]{:S(2)}, u32[]{:S(2)}) collective-permute-start(f32[2,128,256]{2,1,0:T(8,128)S(1)} %get-tuple-element.60), channel_id=1, source_target_pairs={{0,2},{4,6},{8,10},{12,14},{16,18},{20,22},{24,26},{28,30},{2,0},{... | collective-permute-start | bytes 786440 | tf_op jit(solution)/shard_map/ppermute | solution.py:112
  51.6 6.3 %collective-permute-done.11.refs_4_ = f32[2,128,384]{2,1,0:T(8,128)S(1)} collective-permute-done((f32[2,128,384]{2,1,0:T(8,128)S(1)}, f32[2,128,384]{2,1,0:T(8,128)S(1)}, u32[]{:S(2)}, u32[]{:S(2)}) %collective-permute-start.11) | collective-permute-done | bytes 393248 | tf_op jit(solution)/shard_map/ppermute | solution.py:109
  57.9 2.8 %collective-permute-done.12.refs_5_ = f32[2,128,256]{2,1,0:T(8,128)S(1)} collective-permute-done((f32[2,128,256]{2,1,0:T(8,128)S(1)}, f32[2,128,256]{2,1,0:T(8,128)S(1)}, u32[]{:S(2)}, u32[]{:S(2)}) %collective-permute-start.12) | collective-permute-done | bytes 262176 | tf_op jit(solution)/shard_map/ppermute | solution.py:109
  60.7 2.6 %shard_map.84 = (f32[2,128,256]{2,1,0:T(8,128)S(1)}, f32[2,128,256]{2,1,0:T(8,128)S(1)}) custom-call(s32[2,2]{1,0:T(2,128)S(1)} %bitcast.9, s32[16]{0:T(128)S(1)} %bitcast.15, f32[2,128,384]{2,1,0:T(8,128)S(1)} %get-tuple-element.54.refs_2_.refs_0_.refs_5_, f32[2,128,256]{2,1,0:T(8,128)S(1)} %get-tuple-element.59.refs_3_.refs_6_, ...), custom_call_target="tpu_custom_call" | custom-call | flops 100000 | bytes 10000 | tf_op jit(solution)/shard_map/pallas_call | solution.py:511
  63.3 1.9 %collective-permute-start.16 = (f32[2,128,256]{2,1,0:T(8,128)S(1)}, f32[2,128,256]{2,1,0:T(8,128)S(1)}, u32[]{:S(2)}, u32[]{:S(2)}) collective-permute-start(f32[2,128,256]{2,1,0:T(8,128)S(1)} %get-tuple-element.64.refs_9_), channel_id=1, source_target_pairs={{2,4},{6,8},{10,12},{14,16},{18,20},{22,24},{26,28},{4,2},{8,6},{1... | collective-permute-start | bytes 786440 | tf_op jit(solution)/shard_map/ppermute | solution.py:109
  65.2 2.6 %shard_map.85 = (f32[2,128,256]{2,1,0:T(8,128)S(1)}, f32[2,128,256]{2,1,0:T(8,128)S(1)}, f32[2,128,256]{2,1,0:T(8,128)S(1)}, f32[2,128,256]{2,1,0:T(8,128)S(1)}) custom-call(s32[2,2]{1,0:T(2,128)S(1)} %bitcast.10, s32[16]{0:T(128)S(1)} %bitcast.16, f32[2,128,384]{2,1,0:T(8,128)S(1)} %get-tuple-element.54.refs_2_.refs_0_.refs_5_, ...), custom_call_target="tpu_custom_call" | custom-call | flops 100000 | bytes 10000 | tf_op jit(solution)/shard_map/pallas_call | solution.py:511
  68.4 3.6 %collective-permute-start.19 = (f32[2,128,256]{2,1,0:T(8,128)S(1)}, f32[2,128,256]{2,1,0:T(8,128)S(1)}, u32[]{:S(2)}, u32[]{:S(2)}) collective-permute-start(f32[2,128,256]{2,1,0:T(8,128)S(1)} %get-tuple-element.68), channel_id=1, source_target_pairs={{2,4},{6,8},{10,12},{14,16},{18,20},{22,24},{26,28},{4,2},{8,6},{1... | collective-permute-start | bytes 786440 | tf_op jit(solution)/shard_map/ppermute | solution.py:109
  73.6 5.2 %collective-permute-done.19.refs_2_ = f32[2,128,256]{2,1,0:T(8,128)S(1)} collective-permute-done((f32[2,128,256]{2,1,0:T(8,128)S(1)}, f32[2,128,256]{2,1,0:T(8,128)S(1)}, u32[]{:S(2)}, u32[]{:S(2)}) %collective-permute-start.19) | collective-permute-done | bytes 262176 | tf_op jit(solution)/shard_map/ppermute | solution.py:109
  80.1 1.7 %shard_map.89 = (f32[2,128,512]{2,1,0:T(8,128)}, f32[2,128,128]{2,1,0:T(8,128)S(1)}) custom-call(s32[6,128]{1,0:T(8,128)S(1)} %get-tuple-element.43.refs_0_, f32[2,128,768]{2,1,0:T(8,128)S(1)} %shard_map.87.refs_1_, f32[2,128,256]{2,1,0:T(8,128)S(1)} %collective-permute-done.19.refs_2_, f32[128,768]{1,0:T(8,128)S(1)} %get-tuple-element.42.refs_3_.refs_1_.refs_0_, ...), custom_call_target="tpu_custom_call" | custom-call | flops 100000 | bytes 10000 | tf_op jit(solution)/shard_map/pallas_call | solution.py:511
  81.8 2.8 %collective-permute-done.20.refs_2_ = f32[2,128,128]{2,1,0:T(8,128)S(1)} collective-permute-done((f32[2,128,128]{2,1,0:T(8,128)S(1)}, f32[2,128,128]{2,1,0:T(8,128)S(1)}, u32[]{:S(2)}, u32[]{:S(2)}) %collective-permute-start.20) | collective-permute-done | bytes 131104 | tf_op jit(solution)/shard_map/ppermute | solution.py:101
  (46 shorter events, 9.1 us)
Async XLA Ops:
  0.0 19.2 %collective-permute-start.3 = (f32[2,128,512]{2,1,0:T(8,128)}, f32[2,128,512]{2,1,0:T(8,128)S(1)}, u32[]{:S(2)}, u32[]{:S(2)}) collective-permute-start(f32[2,128,512]{2,1,0:T(8,128)} %refs_3_.3), channel_id=1, source_target_pairs={{2,4},{6,8},{10,12},{14,16},{18,20},{22,24},{26,28},{4,2},{8,6},{1... | collective-permute-start | bytes 1572872 | tf_op jit(solution)/shard_map/ppermute | solution.py:109
  1.9 0.7 copy-start.7
  1.9 0.7 copy-start.8
  2.6 1.0 %copy-start = (f32[2,128,512]{2,1,0:T(8,128)S(1)}, f32[2,128,512]{2,1,0:T(8,128)}, u32[]{:S(2)}) copy-start(f32[2,128,512]{2,1,0:T(8,128)} %refs_3_.3) | copy-start | bytes 1572868
  3.6 15.6 %copy-start.2 = (bf16[2,2,2,256,256]{4,3,2,1,0:T(8,128)(2,1)S(1)}, bf16[2,2,2,256,256]{4,3,2,1,0:T(8,128)(2,1)}, u32[]{:S(2)}) copy-start(bf16[2,2,2,256,256]{4,3,2,1,0:T(8,128)(2,1)} %constant.4.clone.refs_11_.refs_12_) | copy-start | bytes 3145732
  4.3 6.2 %collective-permute-start = (f32[2,136,128]{2,1,0:T(8,128)S(1)}, f32[2,136,128]{2,1,0:T(8,128)S(1)}, u32[]{:S(2)}, u32[]{:S(2)}) collective-permute-start(f32[2,136,128]{2,1,0:T(8,128)S(1)} %shard_map.73), channel_id=1, source_target_pairs={{0,1},{1,0},{2,3},{3,2},{4,5},{5,4},{6,7},{7,6},{8,9},{9,8},{10,11... | collective-permute-start | bytes 417800 | tf_op jit(solution)/shard_map/ppermute | solution.py:101
  5.8 1.0 %copy-start.3 = (f32[2,256,256]{2,1,0:T(8,128)S(1)}, f32[2,256,256]{2,1,0:T(8,128)}, u32[]{:S(2)}) copy-start(f32[2,256,256]{2,1,0:T(8,128)} %refs_3_.2) | copy-start | bytes 1572868
  6.9 1.0 %copy-start.5 = (f32[1,1,2,256,256]{4,3,2,1,0:T(8,128)S(1)}, f32[1,1,2,256,256]{4,3,2,1,0:T(8,128)}, u32[]{:S(2)}) copy-start(f32[1,1,2,256,256]{4,3,2,1,0:T(8,128)} %param.9) | copy-start | bytes 1572868
  7.9 0.9 %copy-start.6 = (bf16[2,256,256]{2,1,0:T(8,128)(2,1)S(1)}, bf16[2,256,256]{2,1,0:T(8,128)(2,1)}, u32[]{:S(2)}) copy-start(bf16[2,256,256]{2,1,0:T(8,128)(2,1)} %constant.5.clone.order) | copy-start | bytes 786436
  8.9 1.5 %copy-start.1 = (f32[2,128,512]{2,1,0:T(8,128)S(1)}, f32[2,128,512]{2,1,0:T(8,128)}, u32[]{:S(2)}) copy-start(f32[2,128,512]{2,1,0:T(8,128)} %refs_3_.3) | copy-start | bytes 1572868
  11.0 8.2 %collective-permute-start.4 = (f32[2,128,256]{2,1,0:T(8,128)S(1)}, f32[2,128,256]{2,1,0:T(8,128)S(1)}, u32[]{:S(2)}, u32[]{:S(2)}) collective-permute-start(f32[2,128,256]{2,1,0:T(8,128)S(1)} %get-tuple-element.44), channel_id=1, source_target_pairs={{0,2},{4,6},{8,10},{12,14},{16,18},{20,22},{24,26},{28,30},{2,0},{... | collective-permute-start | bytes 786440 | tf_op jit(solution)/shard_map/ppermute | solution.py:112
  12.5 6.7 %collective-permute-start.5 = (f32[2,128,256]{2,1,0:T(8,128)S(1)}, f32[2,128,256]{2,1,0:T(8,128)S(1)}, u32[]{:S(2)}, u32[]{:S(2)}) collective-permute-start(f32[2,128,256]{2,1,0:T(8,128)S(1)} %get-tuple-element.45), channel_id=1, source_target_pairs={{0,2},{4,6},{8,10},{12,14},{16,18},{20,22},{24,26},{28,30},{2,0},{... | collective-permute-start | bytes 786440 | tf_op jit(solution)/shard_map/ppermute | solution.py:112
  12.5 6.6 %collective-permute-start.1 = (f32[2,144,128]{2,1,0:T(8,128)S(1)}, f32[2,144,128]{2,1,0:T(8,128)S(1)}, u32[]{:S(2)}, u32[]{:S(2)}) collective-permute-start(f32[2,144,128]{2,1,0:T(8,128)S(1)} %get-tuple-element.41.refs_0_.refs_3_.refs_5_.refs_4_), channel_id=1, source_target_pairs={{2,4},{6,8},{10,12},{14,16},{18,20},{22,24},{26,28},{4,2},{8,6},{1... | collective-permute-start | bytes 442376 | tf_op jit(solution)/shard_map/ppermute | solution.py:109
  15.0 4.2 %collective-permute-start.2 = (f32[2,144,128]{2,1,0:T(8,128)S(1)}, f32[2,144,128]{2,1,0:T(8,128)S(1)}, u32[]{:S(2)}, u32[]{:S(2)}) collective-permute-start(f32[2,144,128]{2,1,0:T(8,128)S(1)} %get-tuple-element.41.refs_0_.refs_3_.refs_5_.refs_4_), channel_id=1, source_target_pairs={{0,2},{4,6},{8,10},{12,14},{16,18},{20,22},{24,26},{28,30},{2,0},{... | collective-permute-start | bytes 442376 | tf_op jit(solution)/shard_map/ppermute | solution.py:112
  21.8 9.3 %copy-start.4 = (f32[2,256,256]{2,1,0:T(8,128)S(1)}, f32[2,256,256]{2,1,0:T(8,128)}, u32[]{:S(2)}) copy-start(f32[2,256,256]{2,1,0:T(8,128)} %refs_3_.2) | copy-start | bytes 1572868
  21.9 12.9 %collective-permute-start.6 = (f32[2,128,256]{2,1,0:T(8,128)S(1)}, f32[2,128,256]{2,1,0:T(8,128)S(1)}, u32[]{:S(2)}, u32[]{:S(2)}) collective-permute-start(f32[2,128,256]{2,1,0:T(8,128)S(1)} %get-tuple-element.49.refs_9_), channel_id=1, source_target_pairs={{2,4},{6,8},{10,12},{14,16},{18,20},{22,24},{26,28},{4,2},{8,6},{1... | collective-permute-start | bytes 786440 | tf_op jit(solution)/shard_map/ppermute | solution.py:109
  28.5 7.1 %collective-permute-start.7 = (f32[2,128,256]{2,1,0:T(8,128)S(1)}, f32[2,128,256]{2,1,0:T(8,128)S(1)}, u32[]{:S(2)}, u32[]{:S(2)}) collective-permute-start(f32[2,128,256]{2,1,0:T(8,128)S(1)} %get-tuple-element.51), channel_id=1, source_target_pairs={{0,2},{4,6},{8,10},{12,14},{16,18},{20,22},{24,26},{28,30},{2,0},{... | collective-permute-start | bytes 786440 | tf_op jit(solution)/shard_map/ppermute | solution.py:112
  29.2 6.4 %collective-permute-start.8 = (f32[2,128,256]{2,1,0:T(8,128)S(1)}, f32[2,128,256]{2,1,0:T(8,128)S(1)}, u32[]{:S(2)}, u32[]{:S(2)}) collective-permute-start(f32[2,128,256]{2,1,0:T(8,128)S(1)} %get-tuple-element.52), channel_id=1, source_target_pairs={{0,2},{4,6},{8,10},{12,14},{16,18},{20,22},{24,26},{28,30},{2,0},{... | collective-permute-start | bytes 786440 | tf_op jit(solution)/shard_map/ppermute | solution.py:112
  29.3 10.5 %collective-permute-start.9 = (f32[2,128,256]{2,1,0:T(8,128)S(1)}, f32[2,128,256]{2,1,0:T(8,128)S(1)}, u32[]{:S(2)}, u32[]{:S(2)}) collective-permute-start(f32[2,128,256]{2,1,0:T(8,128)S(1)} %get-tuple-element.53), channel_id=1, source_target_pairs={{2,4},{6,8},{10,12},{14,16},{18,20},{22,24},{26,28},{4,2},{8,6},{1... | collective-permute-start | bytes 786440 | tf_op jit(solution)/shard_map/ppermute | solution.py:109
  40.7 6.9 %collective-permute-start.10 = (f32[2,128,256]{2,1,0:T(8,128)S(1)}, f32[2,128,256]{2,1,0:T(8,128)S(1)}, u32[]{:S(2)}, u32[]{:S(2)}) collective-permute-start(f32[2,128,256]{2,1,0:T(8,128)S(1)} %get-tuple-element.57), channel_id=1, source_target_pairs={{0,1},{1,0},{2,3},{3,2},{4,5},{5,4},{6,7},{7,6},{8,9},{9,8},{10,11... | collective-permute-start | bytes 786440 | tf_op jit(solution)/shard_map/ppermute | solution.py:101
  42.3 15.5 %collective-permute-start.11 = (f32[2,128,384]{2,1,0:T(8,128)S(1)}, f32[2,128,384]{2,1,0:T(8,128)S(1)}, u32[]{:S(2)}, u32[]{:S(2)}) collective-permute-start(f32[2,128,384]{2,1,0:T(8,128)S(1)} %get-tuple-element.54.refs_2_.refs_0_.refs_5_), channel_id=1, source_target_pairs={{2,4},{6,8},{10,12},{14,16},{18,20},{22,24},{26,28},{4,2},{8,6},{1... | collective-permute-start | bytes 1179656 | tf_op jit(solution)/shard_map/ppermute | solution.py:109
  47.7 13.0 %collective-permute-start.12 = (f32[2,128,256]{2,1,0:T(8,128)S(1)}, f32[2,128,256]{2,1,0:T(8,128)S(1)}, u32[]{:S(2)}, u32[]{:S(2)}) collective-permute-start(f32[2,128,256]{2,1,0:T(8,128)S(1)} %get-tuple-element.59.refs_3_.refs_6_), channel_id=1, source_target_pairs={{2,4},{6,8},{10,12},{14,16},{18,20},{22,24},{26,28},{4,2},{8,6},{1... | collective-permute-start | bytes 786440 | tf_op jit(solution)/shard_map/ppermute | solution.py:109
  49.6 11.1 %collective-permute-start.13 = (f32[2,128,256]{2,1,0:T(8,128)S(1)}, f32[2,128,256]{2,1,0:T(8,128)S(1)}, u32[]{:S(2)}, u32[]{:S(2)}) collective-permute-start(f32[2,128,256]{2,1,0:T(8,128)S(1)} %get-tuple-element.60), channel_id=1, source_target_pairs={{0,2},{4,6},{8,10},{12,14},{16,18},{20,22},{24,26},{28,30},{2,0},{... | collective-permute-start | bytes 786440 | tf_op jit(solution)/shard_map/ppermute | solution.py:112
  51.0 9.6 %collective-permute-start.14 = (f32[2,128,256]{2,1,0:T(8,128)S(1)}, f32[2,128,256]{2,1,0:T(8,128)S(1)}, u32[]{:S(2)}, u32[]{:S(2)}) collective-permute-start(f32[2,128,256]{2,1,0:T(8,128)S(1)} %get-tuple-element.61), channel_id=1, source_target_pairs={{0,2},{4,6},{8,10},{12,14},{16,18},{20,22},{24,26},{28,30},{2,0},{... | collective-permute-start | bytes 786440 | tf_op jit(solution)/shard_map/ppermute | solution.py:112
  51.1 6.8 %collective-permute-start.15 = (f32[2,128,128]{2,1,0:T(8,128)S(1)}, f32[2,128,128]{2,1,0:T(8,128)S(1)}, u32[]{:S(2)}, u32[]{:S(2)}) collective-permute-start(f32[2,128,128]{2,1,0:T(8,128)S(1)} %get-tuple-element.62), channel_id=1, source_target_pairs={{0,2},{4,6},{8,10},{12,14},{16,18},{20,22},{24,26},{28,30},{2,0},{... | collective-permute-start | bytes 393224 | tf_op jit(solution)/shard_map/ppermute | solution.py:112
  63.3 8.8 %collective-permute-start.16 = (f32[2,128,256]{2,1,0:T(8,128)S(1)}, f32[2,128,256]{2,1,0:T(8,128)S(1)}, u32[]{:S(2)}, u32[]{:S(2)}) collective-permute-start(f32[2,128,256]{2,1,0:T(8,128)S(1)} %get-tuple-element.64.refs_9_), channel_id=1, source_target_pairs={{2,4},{6,8},{10,12},{14,16},{18,20},{22,24},{26,28},{4,2},{8,6},{1... | collective-permute-start | bytes 786440 | tf_op jit(solution)/shard_map/ppermute | solution.py:109
  67.8 5.0 %collective-permute-start.17 = (f32[2,128,256]{2,1,0:T(8,128)S(1)}, f32[2,128,256]{2,1,0:T(8,128)S(1)}, u32[]{:S(2)}, u32[]{:S(2)}) collective-permute-start(f32[2,128,256]{2,1,0:T(8,128)S(1)} %get-tuple-element.66), channel_id=1, source_target_pairs={{0,2},{4,6},{8,10},{12,14},{16,18},{20,22},{24,26},{28,30},{2,0},{... | collective-permute-start | bytes 786440 | tf_op jit(solution)/shard_map/ppermute | solution.py:112
  67.9 5.0 %collective-permute-start.18 = (f32[2,128,256]{2,1,0:T(8,128)S(1)}, f32[2,128,256]{2,1,0:T(8,128)S(1)}, u32[]{:S(2)}, u32[]{:S(2)}) collective-permute-start(f32[2,128,256]{2,1,0:T(8,128)S(1)} %get-tuple-element.67), channel_id=1, source_target_pairs={{0,2},{4,6},{8,10},{12,14},{16,18},{20,22},{24,26},{28,30},{2,0},{... | collective-permute-start | bytes 786440 | tf_op jit(solution)/shard_map/ppermute | solution.py:112
  68.4 10.5 %collective-permute-start.19 = (f32[2,128,256]{2,1,0:T(8,128)S(1)}, f32[2,128,256]{2,1,0:T(8,128)S(1)}, u32[]{:S(2)}, u32[]{:S(2)}) collective-permute-start(f32[2,128,256]{2,1,0:T(8,128)S(1)} %get-tuple-element.68), channel_id=1, source_target_pairs={{2,4},{6,8},{10,12},{14,16},{18,20},{22,24},{26,28},{4,2},{8,6},{1... | collective-permute-start | bytes 786440 | tf_op jit(solution)/shard_map/ppermute | solution.py:109
  79.5 5.0 %collective-permute-start.20 = (f32[2,128,128]{2,1,0:T(8,128)S(1)}, f32[2,128,128]{2,1,0:T(8,128)S(1)}, u32[]{:S(2)}, u32[]{:S(2)}) collective-permute-start(f32[2,128,128]{2,1,0:T(8,128)S(1)} %shard_map.88.refs_4_), channel_id=1, source_target_pairs={{0,1},{1,0},{2,3},{3,2},{4,5},{5,4},{6,7},{7,6},{8,9},{9,8},{10,11... | collective-permute-start | bytes 393224 | tf_op jit(solution)/shard_map/ppermute | solution.py:101

commit v5 on v4

--- a/solution.py
+++ b/solution.py
@@ -113,7 +113,11 @@
 
     def swaps(self, first):
         pairs = [(i, i + 1) for i in range(first, self.sx_size - 1, 2)]
-        return pairs + [(j, i) for i, j in pairs]
+        alone = [(i, i) for i in (0, self.sx_size - 1) if first]
+        return pairs + [(j, i) for i, j in pairs] + alone
+
+    def outermost(self, s):
+        return (s == 0) | (s == self.sx_size - 1)
 
 
 def far_side(s):
@@ -264,6 +268,7 @@
         return [messages[0][0, height + 8 : height + 16]] + [message[0, height : height + 8] for message in messages]
 
     own, far, near = (lines(messages) for messages in groups)
+    far = [jnp.where(plan.outermost(s), 0.0, line) for line in far]
     for turn in range(plan.sides + 1):
         for kind, line in ((0, jnp.where(upper, far[turn], near[turn])), (1, own[turn]), (2, jnp.where(upper, near[turn], far[turn]))):
             known[kind * (plan.sides + 1) + turn] = line.astype(jnp.int32)
@@ -330,6 +335,10 @@
         for kind, source in ((1, own), (1 + side, far), (1 - side, near)):
             for step in range(3):
                 pick_tile(plan, picked.at[kind, step], source, tile + step, t)
+
+        @pl.when(plan.outermost(s))
+        def _():
+            picked[1 + side] = jnp.zeros(picked.shape[1:], jnp.float32)
 
         for part in range(2):
             edge = [jnp.where(from_tile, picked[kind, 0, part], picked[kind, 2, part]) for kind in range(3)]
@@ -383,7 +392,7 @@
 
 
 class Patch:
-    def __init__(self, plan, info, s, patch, slot, down):
+    def __init__(self, plan, info, s, patch, slot, down, far=False):
         half = patch.shape[1]
         index = (1 if down is None else 1 + down) * (plan.sides + 1)
         row = info[index, 2 * slot]
@@ -395,7 +404,10 @@
         self.rows = None
         if down is not None:
             line = lax.broadcasted_iota(jnp.int32, (half, LANES), 0)
-            self.rows = (line >= jnp.where(down > 0, row, 0)) & (line < jnp.where(down > 0, half, row))
+            after = jnp.where(down > 0, half, row)
+            if far:
+                after = jnp.where(plan.outermost(s), 0, after)
+            self.rows = (line >= jnp.where(down > 0, row, 0)) & (line < after)
 
     def lines(self, part, place):
         values = self.patch[part, :, lanes(place)]
@@ -427,7 +439,7 @@
     for slot in range(slots):
         Patch(plan, info, s, inner[slot], slot, None).add_to(canvas)
     for slot in range(slots - 1):
-        Patch(plan, info, s, far[slot], slot, far_side(s)).add_to(canvas)
+        Patch(plan, info, s, far[slot], slot, far_side(s), True).add_to(canvas)
 
 
 def near_sum_kernel(plan, slots, info, early, *rest):
@@ -440,7 +452,7 @@
 
 def last_patch(plan, slots, info, patch):
     s, _ = here()
-    return Patch(plan, info, s, patch, slots - 1, far_side(s))
+    return Patch(plan, info, s, patch, slots - 1, far_side(s), True)
 
 
 def middle_kernel(plan, slots, layout, pieces, info, early, patch, inverse, *rest):

time: 86.1 us -> 86.5 us (level)
  Pallas kernels: 23.9 us -> 19.6 us
  starting transfers between devices: 29.5 us -> 32.8 us
  waiting for transfers between devices: 26.8 us -> 27.8 us
    pallas_call x18, Pallas kernels: 23.9 us -> 19.6 us  [call(): pl.pallas_call(kernel, out_shape=outs, in_specs=in_specs or [SMEM if valu...]
    ppermute x8, starting transfers between devices: 19.6 us -> 21.5 us  [far_rows(): return lax.ppermute(values, 'sx', self.swaps(1))]
    ppermute x10, starting transfers between devices: 6.15 us -> 7.58 us  [near_rows(): return lax.ppermute(values, 'sx', self.swaps(0))]
    ppermute x8, waiting for transfers between devices: 20.6 us -> 21.5 us  [far_rows(): return lax.ppermute(values, 'sx', self.swaps(1))]
  transfers between devices with their start and end apart: 21 -> 21, of which waited for: 7 -> 7; matrix products, arithmetic and copies ran while one was open for 0% -> 0% of each run, Pallas kernels for 19% -> 14%
where the time goes in v5:
time: 86.5 us; the launch traced here: 85.3 us
  starting transfers between devices  32.8 us (38%)
  waiting for transfers between devices  27.8 us (32%)
  Pallas kernels  19.6 us (23%)
  local copies, waits for them, and re-layouts  4.75 us (5%)
    ppermute x8, waiting for transfers between devices, far_rows(): return lax.ppermute(values, 'sx', self.swaps(1))  21.5 us
    ppermute x8, starting transfers between devices, far_rows(): return lax.ppermute(values, 'sx', self.swaps(1))  21.5 us
    pallas_call x18, Pallas kernels, call(): pl.pallas_call(kernel, out_shape=outs, in_specs=in_specs or [SMEM if valu...  19.6 us
    ppermute x10, starting transfers between devices, near_rows(): return lax.ppermute(values, 'sx', self.swaps(0))  7.58 us
    ppermute x3, waiting for transfers between devices, across(): return [lax.ppermute(values[0], axis_name, [(0, 1), (1, 0)])]  6.18 us
    unnamed x18, local copies, waits for them, and re-layouts  4.75 us
    ppermute x3, starting transfers between devices, across(): return [lax.ppermute(values[0], axis_name, [(0, 1), (1, 0)])]  3.74 us
  transfers between devices with their start and end apart: 21, of which 7 were waited for; matrix products, arithmetic and copies ran while one was open for 0% of the time, Pallas kernels for 14%

profile of v5, /device:TPU:10, one launch (start us, length us, event | category | flops | bytes accessed | tf_op | source)
XLA Modules:
  0.0 85.3 jit_solution(12624237213649090725)
XLA Ops:
  0.0 1.9 %collective-permute-start.3 = (f32[2,128,512]{2,1,0:T(8,128)}, f32[2,128,512]{2,1,0:T(8,128)S(1)}, u32[]{:S(2)}, u32[]{:S(2)}) collective-permute-start(f32[2,128,512]{2,1,0:T(8,128)} %refs_3_.3), channel_id=1, source_target_pairs={{2,4},{6,8},{10,12},{14,16},{18,20},{22,24},{26,28},{4,2},{8,6},{1... | collective-permute-start | bytes 1572872 | tf_op jit(solution)/shard_map/ppermute | solution.py:109
  2.6 1.0 %copy-done = f32[2,128,512]{2,1,0:T(8,128)S(1)} copy-done((f32[2,128,512]{2,1,0:T(8,128)S(1)}, f32[2,128,512]{2,1,0:T(8,128)}, u32[]{:S(2)}) %copy-start) | copy-done | bytes 524312
  4.3 1.6 %collective-permute-start = (f32[2,136,128]{2,1,0:T(8,128)S(1)}, f32[2,136,128]{2,1,0:T(8,128)S(1)}, u32[]{:S(2)}, u32[]{:S(2)}) collective-permute-start(f32[2,136,128]{2,1,0:T(8,128)S(1)} %shard_map.73), channel_id=1, source_target_pairs={{0,1},{1,0},{2,3},{3,2},{4,5},{5,4},{6,7},{7,6},{8,9},{9,8},{10,11... | collective-permute-start | bytes 417800 | tf_op jit(solution)/shard_map/ppermute | solution.py:101
  5.8 1.0 %copy-done.3 = f32[2,256,256]{2,1,0:T(8,128)S(1)} copy-done((f32[2,256,256]{2,1,0:T(8,128)S(1)}, f32[2,256,256]{2,1,0:T(8,128)}, u32[]{:S(2)}) %copy-start.3) | copy-done | bytes 524312
  6.9 1.0 %copy-done.5 = f32[1,1,2,256,256]{4,3,2,1,0:T(8,128)S(1)} copy-done((f32[1,1,2,256,256]{4,3,2,1,0:T(8,128)S(1)}, f32[1,1,2,256,256]{4,3,2,1,0:T(8,128)}, u32[]{:S(2)}) %copy-start.5) | copy-done | bytes 524312
  7.9 0.9 %copy-done.6 = bf16[2,256,256]{2,1,0:T(8,128)(2,1)S(1)} copy-done((bf16[2,256,256]{2,1,0:T(8,128)(2,1)S(1)}, bf16[2,256,256]{2,1,0:T(8,128)(2,1)}, u32[]{:S(2)}) %copy-start.6) | copy-done | bytes 262168
  8.9 1.5 %shard_map.74 = (f32[2,2,256,256]{3,2,1,0:T(8,128)S(1)}, f32[2,256,256]{2,1,0:T(8,128)S(1)}) custom-call(s32[2,2]{1,0:T(2,128)S(1)} %bitcast.5, f32[2,256,256]{2,1,0:T(8,128)S(1)} %copy-done.3, f32[2,256,256]{2,1,0:T(8,128)S(1)} %bitcast.3, bf16[2,256,256]{2,1,0:T(8,128)(2,1)S(1)} %copy-done.6), custom_call_target="tpu_custom_call" | custom-call | flops 100000 | bytes 10000 | tf_op jit(solution)/shard_map/pallas_call | solution.py:523
  11.0 1.4 %collective-permute-start.4 = (f32[2,128,256]{2,1,0:T(8,128)S(1)}, f32[2,128,256]{2,1,0:T(8,128)S(1)}, u32[]{:S(2)}, u32[]{:S(2)}) collective-permute-start(f32[2,128,256]{2,1,0:T(8,128)S(1)} %get-tuple-element.44), channel_id=1, source_target_pairs={{0,2},{4,6},{8,10},{12,14},{16,18},{20,22},{24,26},{28,30},{2,0},{... | collective-permute-start | bytes 786440 | tf_op jit(solution)/shard_map/ppermute | solution.py:112
  12.5 2.4 %collective-permute-start.1 = (f32[2,144,128]{2,1,0:T(8,128)S(1)}, f32[2,144,128]{2,1,0:T(8,128)S(1)}, u32[]{:S(2)}, u32[]{:S(2)}) collective-permute-start(f32[2,144,128]{2,1,0:T(8,128)S(1)} %get-tuple-element.41.refs_0_.refs_3_.refs_5_.refs_4_), channel_id=1, source_target_pairs={{2,4},{6,8},{10,12},{14,16},{18,20},{22,24},{26,28},{4,2},{8,6},{1... | collective-permute-start | bytes 442376 | tf_op jit(solution)/shard_map/ppermute | solution.py:109
  15.0 1.3 %collective-permute-start.2 = (f32[2,144,128]{2,1,0:T(8,128)S(1)}, f32[2,144,128]{2,1,0:T(8,128)S(1)}, u32[]{:S(2)}, u32[]{:S(2)}) collective-permute-start(f32[2,144,128]{2,1,0:T(8,128)S(1)} %get-tuple-element.41.refs_0_.refs_3_.refs_5_.refs_4_), channel_id=1, source_target_pairs={{0,2},{4,6},{8,10},{12,14},{16,18},{20,22},{24,26},{28,30},{2,0},{... | collective-permute-start | bytes 442376 | tf_op jit(solution)/shard_map/ppermute | solution.py:112
  16.3 2.9 %collective-permute-done.1.refs_1_.refs_5_ = f32[2,144,128]{2,1,0:T(8,128)S(1)} collective-permute-done((f32[2,144,128]{2,1,0:T(8,128)S(1)}, f32[2,144,128]{2,1,0:T(8,128)S(1)}, u32[]{:S(2)}, u32[]{:S(2)}) %collective-permute-start.1) | collective-permute-done | bytes 147488 | tf_op jit(solution)/shard_map/ppermute | solution.py:109
  19.2 2.6 %shard_map.77 = (f32[2,128,256]{2,1,0:T(8,128)S(1)}, f32[2,128,256]{2,1,0:T(8,128)S(1)}) custom-call(s32[2,2]{1,0:T(2,128)S(1)} %bitcast.7, s32[16]{0:T(128)S(1)} %bitcast.13, f32[2,128,512]{2,1,0:T(8,128)S(1)} %copy-done.1, f32[2,144,128]{2,1,0:T(8,128)S(1)} %get-tuple-element.41.refs_0_.refs_3_.refs_5_.refs_4_, ...), custom_call_target="tpu_custom_call" | custom-call | flops 100000 | bytes 10000 | tf_op jit(solution)/shard_map/pallas_call | solution.py:523
  21.9 3.9 %collective-permute-start.6 = (f32[2,128,256]{2,1,0:T(8,128)S(1)}, f32[2,128,256]{2,1,0:T(8,128)S(1)}, u32[]{:S(2)}, u32[]{:S(2)}) collective-permute-start(f32[2,128,256]{2,1,0:T(8,128)S(1)} %get-tuple-element.49.refs_9_), channel_id=1, source_target_pairs={{2,4},{6,8},{10,12},{14,16},{18,20},{22,24},{26,28},{4,2},{8,6},{1... | collective-permute-start | bytes 786440 | tf_op jit(solution)/shard_map/ppermute | solution.py:109
  26.5 2.8 %collective-permute-start.7 = (f32[2,128,256]{2,1,0:T(8,128)S(1)}, f32[2,128,256]{2,1,0:T(8,128)S(1)}, u32[]{:S(2)}, u32[]{:S(2)}) collective-permute-start(f32[2,128,256]{2,1,0:T(8,128)S(1)} %get-tuple-element.51), channel_id=1, source_target_pairs={{0,2},{4,6},{8,10},{12,14},{16,18},{20,22},{24,26},{28,30},{2,0},{... | collective-permute-start | bytes 786440 | tf_op jit(solution)/shard_map/ppermute | solution.py:112
  29.3 1.9 %collective-permute-start.9 = (f32[2,128,256]{2,1,0:T(8,128)S(1)}, f32[2,128,256]{2,1,0:T(8,128)S(1)}, u32[]{:S(2)}, u32[]{:S(2)}) collective-permute-start(f32[2,128,256]{2,1,0:T(8,128)S(1)} %get-tuple-element.53), channel_id=1, source_target_pairs={{2,4},{6,8},{10,12},{14,16},{18,20},{22,24},{26,28},{4,2},{8,6},{1... | collective-permute-start | bytes 786440 | tf_op jit(solution)/shard_map/ppermute | solution.py:109
  31.2 3.2 %shard_map.76 = (f32[128,768]{1,0:T(8,128)S(1)}, s32[6,128]{1,0:T(8,128)S(1)}, f32[128,256]{1,0:T(8,128)S(1)}) custom-call(f32[2,144,128]{2,1,0:T(8,128)S(1)} %get-tuple-element.41.refs_0_.refs_3_.refs_5_.refs_4_, f32[2,144,128]{2,1,0:T(8,128)S(1)} %collective-permute-done.1.refs_1_.refs_5_, f32[2,144,128]{2,1,0:T(8,128)S(1)} %collective-permute-done.2.refs_2_.refs_6_, ...), custom_call_target="tpu_custom_call" | custom-call | flops 100000 | bytes 10000 | tf_op jit(solution)/shard_map/pallas_call | solution.py:523
  34.5 0.8 shard_map.79.refs_1_
  36.1 3.7 %collective-permute-done.9.refs_2_ = f32[2,128,256]{2,1,0:T(8,128)S(1)} collective-permute-done((f32[2,128,256]{2,1,0:T(8,128)S(1)}, f32[2,128,256]{2,1,0:T(8,128)S(1)}, u32[]{:S(2)}, u32[]{:S(2)}) %collective-permute-start.9) | collective-permute-done | bytes 262176 | tf_op jit(solution)/shard_map/ppermute | solution.py:109
  39.8 0.8 shard_map.81
  40.8 1.6 %collective-permute-start.10 = (f32[2,128,256]{2,1,0:T(8,128)S(1)}, f32[2,128,256]{2,1,0:T(8,128)S(1)}, u32[]{:S(2)}, u32[]{:S(2)}) collective-permute-start(f32[2,128,256]{2,1,0:T(8,128)S(1)} %get-tuple-element.57), channel_id=1, source_target_pairs={{0,1},{1,0},{2,3},{3,2},{4,5},{5,4},{6,7},{7,6},{8,9},{9,8},{10,11... | collective-permute-start | bytes 786440 | tf_op jit(solution)/shard_map/ppermute | solution.py:101
  42.4 1.9 %collective-permute-start.11 = (f32[2,128,384]{2,1,0:T(8,128)S(1)}, f32[2,128,384]{2,1,0:T(8,128)S(1)}, u32[]{:S(2)}, u32[]{:S(2)}) collective-permute-start(f32[2,128,384]{2,1,0:T(8,128)S(1)} %get-tuple-element.54.refs_2_.refs_0_.refs_5_), channel_id=1, source_target_pairs={{2,4},{6,8},{10,12},{14,16},{18,20},{22,24},{26,28},{4,2},{8,6},{1... | collective-permute-start | bytes 1179656 | tf_op jit(solution)/shard_map/ppermute | solution.py:109
  44.3 3.4 %collective-permute-done.10.refs_2_ = f32[2,128,256]{2,1,0:T(8,128)S(1)} collective-permute-done((f32[2,128,256]{2,1,0:T(8,128)S(1)}, f32[2,128,256]{2,1,0:T(8,128)S(1)}, u32[]{:S(2)}, u32[]{:S(2)}) %collective-permute-start.10) | collective-permute-done | bytes 262176 | tf_op jit(solution)/shard_map/ppermute | solution.py:101
  47.8 1.9 %collective-permute-start.12 = (f32[2,128,256]{2,1,0:T(8,128)S(1)}, f32[2,128,256]{2,1,0:T(8,128)S(1)}, u32[]{:S(2)}, u32[]{:S(2)}) collective-permute-start(f32[2,128,256]{2,1,0:T(8,128)S(1)} %get-tuple-element.59.refs_3_.refs_6_), channel_id=1, source_target_pairs={{2,4},{6,8},{10,12},{14,16},{18,20},{22,24},{26,28},{4,2},{8,6},{1... | collective-permute-start | bytes 786440 | tf_op jit(solution)/shard_map/ppermute | solution.py:109
  51.0 6.9 %collective-permute-done.11.refs_4_ = f32[2,128,384]{2,1,0:T(8,128)S(1)} collective-permute-done((f32[2,128,384]{2,1,0:T(8,128)S(1)}, f32[2,128,384]{2,1,0:T(8,128)S(1)}, u32[]{:S(2)}, u32[]{:S(2)}) %collective-permute-start.11) | collective-permute-done | bytes 393248 | tf_op jit(solution)/shard_map/ppermute | solution.py:109
  57.9 2.8 %collective-permute-done.12.refs_5_ = f32[2,128,256]{2,1,0:T(8,128)S(1)} collective-permute-done((f32[2,128,256]{2,1,0:T(8,128)S(1)}, f32[2,128,256]{2,1,0:T(8,128)S(1)}, u32[]{:S(2)}, u32[]{:S(2)}) %collective-permute-start.12) | collective-permute-done | bytes 262176 | tf_op jit(solution)/shard_map/ppermute | solution.py:109
  60.7 2.6 %shard_map.84 = (f32[2,128,256]{2,1,0:T(8,128)S(1)}, f32[2,128,256]{2,1,0:T(8,128)S(1)}) custom-call(s32[2,2]{1,0:T(2,128)S(1)} %bitcast.9, s32[16]{0:T(128)S(1)} %bitcast.15, f32[2,128,384]{2,1,0:T(8,128)S(1)} %get-tuple-element.54.refs_2_.refs_0_.refs_5_, f32[2,128,256]{2,1,0:T(8,128)S(1)} %get-tuple-element.59.refs_3_.refs_6_, ...), custom_call_target="tpu_custom_call" | custom-call | flops 100000 | bytes 10000 | tf_op jit(solution)/shard_map/pallas_call | solution.py:523
  63.3 1.9 %collective-permute-start.16 = (f32[2,128,256]{2,1,0:T(8,128)S(1)}, f32[2,128,256]{2,1,0:T(8,128)S(1)}, u32[]{:S(2)}, u32[]{:S(2)}) collective-permute-start(f32[2,128,256]{2,1,0:T(8,128)S(1)} %get-tuple-element.64.refs_9_), channel_id=1, source_target_pairs={{2,4},{6,8},{10,12},{14,16},{18,20},{22,24},{26,28},{4,2},{8,6},{1... | collective-permute-start | bytes 786440 | tf_op jit(solution)/shard_map/ppermute | solution.py:109
  66.4 5.6 %collective-permute-start.19 = (f32[2,128,256]{2,1,0:T(8,128)S(1)}, f32[2,128,256]{2,1,0:T(8,128)S(1)}, u32[]{:S(2)}, u32[]{:S(2)}) collective-permute-start(f32[2,128,256]{2,1,0:T(8,128)S(1)} %get-tuple-element.68), channel_id=1, source_target_pairs={{2,4},{6,8},{10,12},{14,16},{18,20},{22,24},{26,28},{4,2},{8,6},{1... | collective-permute-start | bytes 786440 | tf_op jit(solution)/shard_map/ppermute | solution.py:109
  72.1 0.8 shard_map.86.refs_1_
  73.7 5.2 %collective-permute-done.19.refs_2_ = f32[2,128,256]{2,1,0:T(8,128)S(1)} collective-permute-done((f32[2,128,256]{2,1,0:T(8,128)S(1)}, f32[2,128,256]{2,1,0:T(8,128)S(1)}, u32[]{:S(2)}, u32[]{:S(2)}) %collective-permute-start.19) | collective-permute-done | bytes 262176 | tf_op jit(solution)/shard_map/ppermute | solution.py:109
  80.1 1.7 %shard_map.89 = (f32[2,128,512]{2,1,0:T(8,128)}, f32[2,128,128]{2,1,0:T(8,128)S(1)}) custom-call(s32[6,128]{1,0:T(8,128)S(1)} %get-tuple-element.43.refs_0_, f32[2,128,768]{2,1,0:T(8,128)S(1)} %shard_map.87.refs_1_, f32[2,128,256]{2,1,0:T(8,128)S(1)} %collective-permute-done.19.refs_2_, f32[128,768]{1,0:T(8,128)S(1)} %get-tuple-element.42.refs_3_.refs_1_.refs_0_, ...), custom_call_target="tpu_custom_call" | custom-call | flops 100000 | bytes 10000 | tf_op jit(solution)/shard_map/pallas_call | solution.py:523
  81.8 2.8 %collective-permute-done.20.refs_2_ = f32[2,128,128]{2,1,0:T(8,128)S(1)} collective-permute-done((f32[2,128,128]{2,1,0:T(8,128)S(1)}, f32[2,128,128]{2,1,0:T(8,128)S(1)}, u32[]{:S(2)}, u32[]{:S(2)}) %collective-permute-start.20) | collective-permute-done | bytes 131104 | tf_op jit(solution)/shard_map/ppermute | solution.py:101
  (46 shorter events, 8.9 us)
Async XLA Ops:
  0.0 19.2 %collective-permute-start.3 = (f32[2,128,512]{2,1,0:T(8,128)}, f32[2,128,512]{2,1,0:T(8,128)S(1)}, u32[]{:S(2)}, u32[]{:S(2)}) collective-permute-start(f32[2,128,512]{2,1,0:T(8,128)} %refs_3_.3), channel_id=1, source_target_pairs={{2,4},{6,8},{10,12},{14,16},{18,20},{22,24},{26,28},{4,2},{8,6},{1... | collective-permute-start | bytes 1572872 | tf_op jit(solution)/shard_map/ppermute | solution.py:109
  1.9 0.7 copy-start.7
  1.9 0.7 copy-start.8
  2.6 1.0 %copy-start = (f32[2,128,512]{2,1,0:T(8,128)S(1)}, f32[2,128,512]{2,1,0:T(8,128)}, u32[]{:S(2)}) copy-start(f32[2,128,512]{2,1,0:T(8,128)} %refs_3_.3) | copy-start | bytes 1572868
  3.6 15.6 %copy-start.2 = (bf16[2,2,2,256,256]{4,3,2,1,0:T(8,128)(2,1)S(1)}, bf16[2,2,2,256,256]{4,3,2,1,0:T(8,128)(2,1)}, u32[]{:S(2)}) copy-start(bf16[2,2,2,256,256]{4,3,2,1,0:T(8,128)(2,1)} %constant.4.clone.refs_11_.refs_12_) | copy-start | bytes 3145732
  4.3 6.2 %collective-permute-start = (f32[2,136,128]{2,1,0:T(8,128)S(1)}, f32[2,136,128]{2,1,0:T(8,128)S(1)}, u32[]{:S(2)}, u32[]{:S(2)}) collective-permute-start(f32[2,136,128]{2,1,0:T(8,128)S(1)} %shard_map.73), channel_id=1, source_target_pairs={{0,1},{1,0},{2,3},{3,2},{4,5},{5,4},{6,7},{7,6},{8,9},{9,8},{10,11... | collective-permute-start | bytes 417800 | tf_op jit(solution)/shard_map/ppermute | solution.py:101
  5.8 1.0 %copy-start.3 = (f32[2,256,256]{2,1,0:T(8,128)S(1)}, f32[2,256,256]{2,1,0:T(8,128)}, u32[]{:S(2)}) copy-start(f32[2,256,256]{2,1,0:T(8,128)} %refs_3_.2) | copy-start | bytes 1572868
  6.9 1.0 %copy-start.5 = (f32[1,1,2,256,256]{4,3,2,1,0:T(8,128)S(1)}, f32[1,1,2,256,256]{4,3,2,1,0:T(8,128)}, u32[]{:S(2)}) copy-start(f32[1,1,2,256,256]{4,3,2,1,0:T(8,128)} %param.9) | copy-start | bytes 1572868
  7.9 0.9 %copy-start.6 = (bf16[2,256,256]{2,1,0:T(8,128)(2,1)S(1)}, bf16[2,256,256]{2,1,0:T(8,128)(2,1)}, u32[]{:S(2)}) copy-start(bf16[2,256,256]{2,1,0:T(8,128)(2,1)} %constant.5.clone.order) | copy-start | bytes 786436
  8.9 1.5 %copy-start.1 = (f32[2,128,512]{2,1,0:T(8,128)S(1)}, f32[2,128,512]{2,1,0:T(8,128)}, u32[]{:S(2)}) copy-start(f32[2,128,512]{2,1,0:T(8,128)} %refs_3_.3) | copy-start | bytes 1572868
  11.0 8.2 %collective-permute-start.4 = (f32[2,128,256]{2,1,0:T(8,128)S(1)}, f32[2,128,256]{2,1,0:T(8,128)S(1)}, u32[]{:S(2)}, u32[]{:S(2)}) collective-permute-start(f32[2,128,256]{2,1,0:T(8,128)S(1)} %get-tuple-element.44), channel_id=1, source_target_pairs={{0,2},{4,6},{8,10},{12,14},{16,18},{20,22},{24,26},{28,30},{2,0},{... | collective-permute-start | bytes 786440 | tf_op jit(solution)/shard_map/ppermute | solution.py:112
  12.5 6.7 %collective-permute-start.5 = (f32[2,128,256]{2,1,0:T(8,128)S(1)}, f32[2,128,256]{2,1,0:T(8,128)S(1)}, u32[]{:S(2)}, u32[]{:S(2)}) collective-permute-start(f32[2,128,256]{2,1,0:T(8,128)S(1)} %get-tuple-element.45), channel_id=1, source_target_pairs={{0,2},{4,6},{8,10},{12,14},{16,18},{20,22},{24,26},{28,30},{2,0},{... | collective-permute-start | bytes 786440 | tf_op jit(solution)/shard_map/ppermute | solution.py:112
  12.5 6.6 %collective-permute-start.1 = (f32[2,144,128]{2,1,0:T(8,128)S(1)}, f32[2,144,128]{2,1,0:T(8,128)S(1)}, u32[]{:S(2)}, u32[]{:S(2)}) collective-permute-start(f32[2,144,128]{2,1,0:T(8,128)S(1)} %get-tuple-element.41.refs_0_.refs_3_.refs_5_.refs_4_), channel_id=1, source_target_pairs={{2,4},{6,8},{10,12},{14,16},{18,20},{22,24},{26,28},{4,2},{8,6},{1... | collective-permute-start | bytes 442376 | tf_op jit(solution)/shard_map/ppermute | solution.py:109
  15.0 4.2 %collective-permute-start.2 = (f32[2,144,128]{2,1,0:T(8,128)S(1)}, f32[2,144,128]{2,1,0:T(8,128)S(1)}, u32[]{:S(2)}, u32[]{:S(2)}) collective-permute-start(f32[2,144,128]{2,1,0:T(8,128)S(1)} %get-tuple-element.41.refs_0_.refs_3_.refs_5_.refs_4_), channel_id=1, source_target_pairs={{0,2},{4,6},{8,10},{12,14},{16,18},{20,22},{24,26},{28,30},{2,0},{... | collective-permute-start | bytes 442376 | tf_op jit(solution)/shard_map/ppermute | solution.py:112
  21.8 9.4 %copy-start.4 = (f32[2,256,256]{2,1,0:T(8,128)S(1)}, f32[2,256,256]{2,1,0:T(8,128)}, u32[]{:S(2)}) copy-start(f32[2,256,256]{2,1,0:T(8,128)} %refs_3_.2) | copy-start | bytes 1572868
  21.9 12.6 %collective-permute-start.6 = (f32[2,128,256]{2,1,0:T(8,128)S(1)}, f32[2,128,256]{2,1,0:T(8,128)S(1)}, u32[]{:S(2)}, u32[]{:S(2)}) collective-permute-start(f32[2,128,256]{2,1,0:T(8,128)S(1)} %get-tuple-element.49.refs_9_), channel_id=1, source_target_pairs={{2,4},{6,8},{10,12},{14,16},{18,20},{22,24},{26,28},{4,2},{8,6},{1... | collective-permute-start | bytes 786440 | tf_op jit(solution)/shard_map/ppermute | solution.py:109
  26.5 8.8 %collective-permute-start.7 = (f32[2,128,256]{2,1,0:T(8,128)S(1)}, f32[2,128,256]{2,1,0:T(8,128)S(1)}, u32[]{:S(2)}, u32[]{:S(2)}) collective-permute-start(f32[2,128,256]{2,1,0:T(8,128)S(1)} %get-tuple-element.51), channel_id=1, source_target_pairs={{0,2},{4,6},{8,10},{12,14},{16,18},{20,22},{24,26},{28,30},{2,0},{... | collective-permute-start | bytes 786440 | tf_op jit(solution)/shard_map/ppermute | solution.py:112
  29.2 6.1 %collective-permute-start.8 = (f32[2,128,256]{2,1,0:T(8,128)S(1)}, f32[2,128,256]{2,1,0:T(8,128)S(1)}, u32[]{:S(2)}, u32[]{:S(2)}) collective-permute-start(f32[2,128,256]{2,1,0:T(8,128)S(1)} %get-tuple-element.52), channel_id=1, source_target_pairs={{0,2},{4,6},{8,10},{12,14},{16,18},{20,22},{24,26},{28,30},{2,0},{... | collective-permute-start | bytes 786440 | tf_op jit(solution)/shard_map/ppermute | solution.py:112
  29.3 10.5 %collective-permute-start.9 = (f32[2,128,256]{2,1,0:T(8,128)S(1)}, f32[2,128,256]{2,1,0:T(8,128)S(1)}, u32[]{:S(2)}, u32[]{:S(2)}) collective-permute-start(f32[2,128,256]{2,1,0:T(8,128)S(1)} %get-tuple-element.53), channel_id=1, source_target_pairs={{2,4},{6,8},{10,12},{14,16},{18,20},{22,24},{26,28},{4,2},{8,6},{1... | collective-permute-start | bytes 786440 | tf_op jit(solution)/shard_map/ppermute | solution.py:109
  40.8 6.9 %collective-permute-start.10 = (f32[2,128,256]{2,1,0:T(8,128)S(1)}, f32[2,128,256]{2,1,0:T(8,128)S(1)}, u32[]{:S(2)}, u32[]{:S(2)}) collective-permute-start(f32[2,128,256]{2,1,0:T(8,128)S(1)} %get-tuple-element.57), channel_id=1, source_target_pairs={{0,1},{1,0},{2,3},{3,2},{4,5},{5,4},{6,7},{7,6},{8,9},{9,8},{10,11... | collective-permute-start | bytes 786440 | tf_op jit(solution)/shard_map/ppermute | solution.py:101
  42.4 15.5 %collective-permute-start.11 = (f32[2,128,384]{2,1,0:T(8,128)S(1)}, f32[2,128,384]{2,1,0:T(8,128)S(1)}, u32[]{:S(2)}, u32[]{:S(2)}) collective-permute-start(f32[2,128,384]{2,1,0:T(8,128)S(1)} %get-tuple-element.54.refs_2_.refs_0_.refs_5_), channel_id=1, source_target_pairs={{2,4},{6,8},{10,12},{14,16},{18,20},{22,24},{26,28},{4,2},{8,6},{1... | collective-permute-start | bytes 1179656 | tf_op jit(solution)/shard_map/ppermute | solution.py:109
  47.8 12.9 %collective-permute-start.12 = (f32[2,128,256]{2,1,0:T(8,128)S(1)}, f32[2,128,256]{2,1,0:T(8,128)S(1)}, u32[]{:S(2)}, u32[]{:S(2)}) collective-permute-start(f32[2,128,256]{2,1,0:T(8,128)S(1)} %get-tuple-element.59.refs_3_.refs_6_), channel_id=1, source_target_pairs={{2,4},{6,8},{10,12},{14,16},{18,20},{22,24},{26,28},{4,2},{8,6},{1... | collective-permute-start | bytes 786440 | tf_op jit(solution)/shard_map/ppermute | solution.py:109
  49.7 11.0 %collective-permute-start.13 = (f32[2,128,256]{2,1,0:T(8,128)S(1)}, f32[2,128,256]{2,1,0:T(8,128)S(1)}, u32[]{:S(2)}, u32[]{:S(2)}) collective-permute-start(f32[2,128,256]{2,1,0:T(8,128)S(1)} %get-tuple-element.60), channel_id=1, source_target_pairs={{0,2},{4,6},{8,10},{12,14},{16,18},{20,22},{24,26},{28,30},{2,0},{... | collective-permute-start | bytes 786440 | tf_op jit(solution)/shard_map/ppermute | solution.py:112
  50.5 10.2 %collective-permute-start.14 = (f32[2,128,256]{2,1,0:T(8,128)S(1)}, f32[2,128,256]{2,1,0:T(8,128)S(1)}, u32[]{:S(2)}, u32[]{:S(2)}) collective-permute-start(f32[2,128,256]{2,1,0:T(8,128)S(1)} %get-tuple-element.61), channel_id=1, source_target_pairs={{0,2},{4,6},{8,10},{12,14},{16,18},{20,22},{24,26},{28,30},{2,0},{... | collective-permute-start | bytes 786440 | tf_op jit(solution)/shard_map/ppermute | solution.py:112
  50.5 7.4 %collective-permute-start.15 = (f32[2,128,128]{2,1,0:T(8,128)S(1)}, f32[2,128,128]{2,1,0:T(8,128)S(1)}, u32[]{:S(2)}, u32[]{:S(2)}) collective-permute-start(f32[2,128,128]{2,1,0:T(8,128)S(1)} %get-tuple-element.62), channel_id=1, source_target_pairs={{0,2},{4,6},{8,10},{12,14},{16,18},{20,22},{24,26},{28,30},{2,0},{... | collective-permute-start | bytes 393224 | tf_op jit(solution)/shard_map/ppermute | solution.py:112
  63.3 8.8 %collective-permute-start.16 = (f32[2,128,256]{2,1,0:T(8,128)S(1)}, f32[2,128,256]{2,1,0:T(8,128)S(1)}, u32[]{:S(2)}, u32[]{:S(2)}) collective-permute-start(f32[2,128,256]{2,1,0:T(8,128)S(1)} %get-tuple-element.64.refs_9_), channel_id=1, source_target_pairs={{2,4},{6,8},{10,12},{14,16},{18,20},{22,24},{26,28},{4,2},{8,6},{1... | collective-permute-start | bytes 786440 | tf_op jit(solution)/shard_map/ppermute | solution.py:109
  65.9 7.0 %collective-permute-start.17 = (f32[2,128,256]{2,1,0:T(8,128)S(1)}, f32[2,128,256]{2,1,0:T(8,128)S(1)}, u32[]{:S(2)}, u32[]{:S(2)}) collective-permute-start(f32[2,128,256]{2,1,0:T(8,128)S(1)} %get-tuple-element.66), channel_id=1, source_target_pairs={{0,2},{4,6},{8,10},{12,14},{16,18},{20,22},{24,26},{28,30},{2,0},{... | collective-permute-start | bytes 786440 | tf_op jit(solution)/shard_map/ppermute | solution.py:112
  66.0 6.9 %collective-permute-start.18 = (f32[2,128,256]{2,1,0:T(8,128)S(1)}, f32[2,128,256]{2,1,0:T(8,128)S(1)}, u32[]{:S(2)}, u32[]{:S(2)}) collective-permute-start(f32[2,128,256]{2,1,0:T(8,128)S(1)} %get-tuple-element.67), channel_id=1, source_target_pairs={{0,2},{4,6},{8,10},{12,14},{16,18},{20,22},{24,26},{28,30},{2,0},{... | collective-permute-start | bytes 786440 | tf_op jit(solution)/shard_map/ppermute | solution.py:112
  66.4 12.4 %collective-permute-start.19 = (f32[2,128,256]{2,1,0:T(8,128)S(1)}, f32[2,128,256]{2,1,0:T(8,128)S(1)}, u32[]{:S(2)}, u32[]{:S(2)}) collective-permute-start(f32[2,128,256]{2,1,0:T(8,128)S(1)} %get-tuple-element.68), channel_id=1, source_target_pairs={{2,4},{6,8},{10,12},{14,16},{18,20},{22,24},{26,28},{4,2},{8,6},{1... | collective-permute-start | bytes 786440 | tf_op jit(solution)/shard_map/ppermute | solution.py:109
  79.5 5.0 %collective-permute-start.20 = (f32[2,128,128]{2,1,0:T(8,128)S(1)}, f32[2,128,128]{2,1,0:T(8,128)S(1)}, u32[]{:S(2)}, u32[]{:S(2)}) collective-permute-start(f32[2,128,128]{2,1,0:T(8,128)S(1)} %shard_map.88.refs_4_), channel_id=1, source_target_pairs={{0,1},{1,0},{2,3},{3,2},{4,5},{5,4},{6,7},{7,6},{8,9},{9,8},{10,11... | collective-permute-start | bytes 393224 | tf_op jit(solution)/shard_map/ppermute | solution.py:101

commit v6 on v4

--- a/solution.py
+++ b/solution.py
@@ -106,14 +106,21 @@
         ]
 
     def far_rows(self, values):
-        return lax.ppermute(values, "sx", self.swaps(1))
+        pairs = [(2 * chip + (chip + 1) % 2, 2 * chip + 2 + (chip + 1) % 2) for chip in range(self.sx_size // 2 - 1)]
+        return lax.ppermute(values, "sx", pairs + [(j, i) for i, j in pairs])
+
+    def first_far_rows(self, values):
+        pairs = []
+        for chip in range(self.sx_size // 2 - 1):
+            core = (chip + 1) % 2
+            pairs += [(2 * chip + 2, 2 * chip + core), (2 * chip + 1, 2 * chip + 2 + core)]
+        return lax.ppermute(values, "sx", pairs)
 
     def near_rows(self, values):
-        return lax.ppermute(values, "sx", self.swaps(0))
-
-    def swaps(self, first):
-        pairs = [(i, i + 1) for i in range(first, self.sx_size - 1, 2)]
-        return pairs + [(j, i) for i, j in pairs]
+        return lax.ppermute(values, "sx", [(i, i ^ 1) for i in range(self.sx_size)])
+
+    def swapped_rows(self, values):
+        return lax.ppermute(values, "sx", [(i, i ^ 1) for i in range(self.sx_size) if i // 2 % 2])
 
 
 def far_side(s):
@@ -134,15 +141,18 @@
         def _():
             target[...] = jnp.zeros(target.shape, jnp.float32)
 
-    for ref, offset, count, start in pieces:
-
-        @pl.when((tile >= start) & (tile < start + count))
+    for ref, offset, count, start, guard in pieces:
+        inside = (tile >= start) & (tile < start + count)
+        if inside is False:
+            continue
+
+        @pl.when(inside if guard is None else inside & guard)
         def _(ref=ref, offset=offset, start=start):
             target[...] = ref[:, :rows, lanes(tile - start + offset)]
 
 
-def lay_out(refs, starts):
-    return [(ref, 0, ref.shape[2] // LANES, start) for ref, start in zip(refs, starts)]
+def lay_out(refs, starts, guard=None):
+    return [(ref, 0, ref.shape[2] // LANES, start, guard) for ref, start in zip(refs, starts)]
 
 
 def chunks(count):
@@ -167,8 +177,18 @@
     return pltpu.roll(values, (count + 8 - offset) % (count + 8), 0)[:count]
 
 
+def traded():
+    return lax.axis_index("sx") // 2 % 2
+
+
 def here():
-    return lax.axis_index("sx"), lax.axis_index("sy")
+    s = lax.axis_index("sx")
+    return s + traded() * (1 - 2 * (s % 2)), lax.axis_index("sy")
+
+
+def role_centre(centres, near_centres, slot):
+    swap = traded() == 1
+    return tuple(jnp.where(swap, near_centres[slot, axis], centres[slot, axis]) for axis in range(2))
 
 
 def info_rows(centres, count):
@@ -183,7 +203,7 @@
 
 def edge_message_kernel(plan, block, centres, counts, *rest):
     messages, sems = rest[: plan.sides], rest[plan.sides]
-    s, t = here()
+    s, t = lax.axis_index("sx"), lax.axis_index("sy")
     half = block.shape[1]
     copies = [
         pltpu.make_async_copy(block.at[:, :, lanes(tile - 1)], message.at[:, :half], sems.at[side])
@@ -200,7 +220,7 @@
 
 
 def halo_message_kernel(plan, block, centres, counts, *rest):
-    s, _ = here()
+    s = lax.axis_index("sx")
     received, messages, near = rest[: plan.sides], rest[plan.sides : 2 * plan.sides], rest[2 * plan.sides :]
     own = info_rows(centres, counts[s])
     for source, message in zip(received, messages):
@@ -221,21 +241,24 @@
     spread(middle, near[sides:])
 
 
-def prepare_kernel(centres, probe, amps, order, rolled, ordered, padded):
+def token_kernel(_, token):
+    token[...] = jnp.zeros(token.shape, jnp.float32)
+
+
+def prepare_kernel(centres, near_centres, probe, amps, near_amps, order, rolled, ordered, padded):
     size = probe.shape[1]
     half = size // 2
     padded[:, :half] = jnp.zeros((2, half, size), jnp.float32)
     padded[:, half + size :] = jnp.zeros((2, half + 8, size), jnp.float32)
     padded[:, half : half + size] = probe[...]
     for slot in range(amps.shape[0]):
-        row = centres[slot, 0]
-        col = centres[slot, 1]
+        row, col = role_centre(centres, near_centres, slot)
         for part in range(2):
             shape = padded.at[part]
             upper = rows_at(shape, half - row, half) + rows_at(shape, half + size - row, half)
             lower = rows_at(shape, size - row, half)
             rolled[slot, part] = pltpu.roll(jnp.concatenate([upper, lower], axis=0), col % size, 1)
-        high, low = split(amps[slot])
+        high, low = split(jnp.where(traded() == 1, near_amps[slot], amps[slot]))
         across = jnp.dot(
             jnp.concatenate([high, low], axis=1),
             jnp.concatenate([order[0], order[0]], axis=0),
@@ -263,7 +286,10 @@
     def lines(messages):
         return [messages[0][0, height + 8 : height + 16]] + [message[0, height : height + 8] for message in messages]
 
-    own, far, near = (lines(messages) for messages in groups)
+    swap = traded() == 1
+    home, far, other = (lines(messages) for messages in groups)
+    own = [jnp.where(swap, theirs, mine) for mine, theirs in zip(home, other)]
+    near = [jnp.where(swap, mine, theirs) for mine, theirs in zip(home, other)]
     for turn in range(plan.sides + 1):
         for kind, line in ((0, jnp.where(upper, far[turn], near[turn])), (1, own[turn]), (2, jnp.where(upper, near[turn], far[turn]))):
             known[kind * (plan.sides + 1) + turn] = line.astype(jnp.int32)
@@ -302,15 +328,14 @@
         pair[...] = inverse[:, lanes(start, 2)]
 
 
-def term_kernel(plan, slot, layout, pieces, copied, centres, counts, *rest):
+def term_kernel(plan, slot, layout, pieces, copied, centres, near_centres, counts, *rest):
     refs, rest = rest[:pieces], rest[pieces:]
-    earlier, (probe, amps, tables, outer, inner), rest = rest[:copied], rest[copied : copied + 5], rest[copied + 5 :]
+    earlier, (probe, amps, tables, _, outer, inner), rest = rest[:copied], rest[copied : copied + 6], rest[copied + 6 :]
     near_outers, (window, picked) = rest[:-2], rest[-2:]
     size = probe.shape[2]
     half = size // 2
     s, t = here()
-    row = centres[slot, 0]
-    col = centres[slot, 1]
+    row, col = role_centre(centres, near_centres, slot)
     alive = slot < counts[s]
 
     @pl.when(jnp.logical_not(alive))
@@ -378,17 +403,18 @@
         inner[0] = term_real[half:]
         inner[1] = term_imag[half:]
 
-    for source, target in zip((*earlier, outer), near_outers):
-        target[...] = source[...]
+    for index, source in enumerate((*earlier, outer)):
+        for part in range(2 if near_outers else 0):
+            near_outers[2 * index + part][0] = source[part]
 
 
 class Patch:
     def __init__(self, plan, info, s, patch, slot, down):
-        half = patch.shape[1]
+        half = (patch[0] if isinstance(patch, (list, tuple)) else patch).shape[1]
         index = (1 if down is None else 1 + down) * (plan.sides + 1)
         row = info[index, 2 * slot]
         col = info[index, 2 * slot + 1]
-        self.patch = patch
+        self.parts = patch if isinstance(patch, (list, tuple)) else [patch.at[0:1], patch.at[1:2]]
         self.tile = col // LANES
         self.first = self.tile % 2
         self.from_tile = lax.broadcasted_iota(jnp.int32, (half, LANES), 1) >= col % LANES
@@ -398,7 +424,7 @@
             self.rows = (line >= jnp.where(down > 0, row, 0)) & (line < jnp.where(down > 0, half, row))
 
     def lines(self, part, place):
-        values = self.patch[part, :, lanes(place)]
+        values = self.parts[part][0, :, lanes(place)]
         return values if self.rows is None else jnp.where(self.rows, values, 0.0)
 
     def tiles(self, part):
@@ -431,11 +457,11 @@
 
 
 def near_sum_kernel(plan, slots, info, early, *rest):
-    near, canvas = rest[:slots], rest[slots]
+    near, canvas = rest[: 2 * slots], rest[2 * slots]
     s, _ = here()
     canvas[...] = early[...]
     for slot in range(slots):
-        Patch(plan, info, s, near[slot], slot, -far_side(s)).add_to(canvas)
+        Patch(plan, info, s, near[2 * slot : 2 * slot + 2], slot, -far_side(s)).add_to(canvas)
 
 
 def last_patch(plan, slots, info, patch):
@@ -467,40 +493,55 @@
             base[:, :, where] -= total[:, :, where] * inverse[:, lanes(start + step)][None]
 
 
-def halo_sum_kernel(plan, slots, info, early, patch, *sums):
+def halo_sum_kernel(plan, slots, info, early, patch, inverse, *sums):
     _, t = here()
     last = last_patch(plan, slots, info, patch)
     for total, tile in zip(sums, plan.halo_tiles(t)):
         total[...] = early[:, :, lanes(tile)]
         last.add_tile_to(total, tile)
+        total[...] *= inverse[:, lanes(tile)][None]
 
 
 def last_kernel(plan, slots, layout, pieces, info, early, patch, inverse, _, *rest):
-    refs, rest = rest[:pieces], rest[pieces:]
-    nearly, bases = rest[0], rest[1 : 1 + plan.sides]
-    current, canvas, sem = rest[1 + plan.sides :]
+    refs, nearly, canvas = rest[:pieces], rest[pieces:-1], rest[-1]
     _, t = here()
     canvas[...] = early[...]
     last_patch(plan, slots, info, patch).add_to(canvas)
     for step in range(plan.own):
         tile = 1 + step
-        where = lanes(step)
-        pick_tile(plan, current.at[:, :, where], layout(refs, t)[0], tile, t)
-        current[:, :, where] -= canvas[:, :, lanes(tile)] * inverse[:, lanes(tile)][None]
-    copy = pltpu.make_async_copy(current, nearly, sem)
-    copy.start()
-    for base, tile in zip(bases, plan.edge_tiles(t)):
-        base[...] = current[:, :, lanes(tile - 1)]
-    copy.wait()
-
-
-def edge_kernel(plan, inverse, *rest):
-    bases, received = rest[: plan.sides], rest[plan.sides : 2 * plan.sides]
-    _, result, sums, sems = rest[2 * plan.sides :]
-    _, t = here()
+        target = nearly[step]
+        pick_tile(plan, target, layout(refs, t)[0], tile, t)
+        target[...] -= canvas[:, :, lanes(tile)] * inverse[:, lanes(tile)][None]
+
+
+def home_kernel(plan, runs, *rest):
+    nearly, near_nearly = rest[:runs], rest[runs : 2 * runs]
+    result, bases, sem = rest[2 * runs], rest[2 * runs + 1 : -1], rest[-1]
+    t = lax.axis_index("sy")
+    for swap, source in ((0, nearly), (1, near_nearly)):
+
+        @pl.when(traded() == swap)
+        def _(source=source):
+            copies = [
+                pltpu.make_async_copy(run, result.at[:, :, lanes(index)], sem.at[index])
+                for index, run in enumerate(source)
+            ]
+            for copy in copies:
+                copy.start()
+            for base, tile in zip(bases, plan.edge_tiles(t)):
+                pick_tile(plan, base, lay_out(source, range(1, 1 + plan.own)), tile, t)
+            for copy in copies:
+                copy.wait()
+
+
+def edge_kernel(plan, *rest):
+    bases, received, others = (rest[k * plan.sides : (k + 1) * plan.sides] for k in range(3))
+    _, result, sums, sems = rest[3 * plan.sides :]
+    t = lax.axis_index("sy")
     copies = []
     for side, tile in enumerate(plan.edge_tiles(t)):
-        sums[side] = bases[side][...] - received[side][...] * inverse[:, lanes(tile)][None]
+        terms = jnp.where(traded() == 1, others[side][...], received[side][...])
+        sums[side] = bases[side][...] - terms
         copies.append(pltpu.make_async_copy(sums.at[side], result.at[:, :, lanes(tile - 1)], sems.at[side]))
         copies[-1].start()
     for copy in copies:
@@ -547,12 +588,14 @@
         in_specs=[HBM, SMEM, SMEM],
     )
     halos = plan.across(messages)
-    far_block = plan.far_rows(object_field)
+    far_block = plan.first_far_rows(object_field)
+    near_spots = plan.near_rows(spots)
+    near_amps = plan.near_rows(own_amps)
     rolled, ordered = call(
         prepare_kernel,
         [shape((slots, 2, size, size), f32), shape((slots, size, size), f32)],
         [pltpu.VMEM((2, 2 * size + 8, size), f32)],
-        [spots, probe_field, own_amps, order],
+        [spots, near_spots, probe_field, own_amps, near_amps, order],
     )
     halos, rolled, ordered = lax.optimization_barrier((halos, rolled, ordered))
     near_runs = [shape((2, half, count * LANES), f32) for count in chunks(plan.own)]
@@ -563,7 +606,7 @@
         [object_field, spots, counts, *halos],
     )
     passed = messages[:sides]
-    far = [far_block] + [plan.far_rows(message) for message in passed]
+    far = [far_block] + [plan.first_far_rows(message) for message in passed]
     near = [plan.near_rows(piece) for piece in messages]
     own = [object_field] + passed
     inverse, info, *inverse_pairs = call(
@@ -579,18 +622,22 @@
         out_specs=[VMEM, SMEM] + [VMEM] * sides,
     )
 
-    def runs_layout(refs, main, count, side_starts):
+    def runs(refs, main, count, side_starts):
         starts = [main] + side_starts
         own, far, near = refs[: 1 + sides], refs[1 + sides : 2 + 2 * sides], refs[2 + 2 * sides :]
-        return lay_out(own, starts), lay_out(far, starts), lay_out(near, side_starts + chunk_starts(main, count))
+        return (own, starts), (far, starts), (near, side_starts + chunk_starts(main, count))
 
     def first_layout(refs, t):
-        return runs_layout(refs, 1, plan.own, plan.halo_tiles(t))
+        home, far, other = runs(refs, 1, plan.own, plan.halo_tiles(t))
+        stay, swap = traded() == 0, traded() == 1
+        own = lay_out(*home, stay) + lay_out(*other, swap)
+        return own, lay_out(*far), lay_out(*other, stay) + lay_out(*home, swap)
 
     def later_layout(refs, t):
-        return runs_layout(refs, plan.mid_start(t), plan.mid_tiles, plan.pair_starts(t))
+        return tuple(lay_out(*group) for group in runs(refs, plan.mid_start(t), plan.mid_tiles, plan.pair_starts(t)))
 
     layout = first_layout
+    token = spots
 
     for sweep in range(ITERS):
         pieces = own + far + near
@@ -603,9 +650,9 @@
                 lambda *refs, slot=slot, layout=layout, copied=len(earlier): term_kernel(
                     plan, slot, layout, len(pieces), copied, *refs
                 ),
-                [patch] * (2 + slots * last),
+                [patch] * 2 + [shape((1, half, size), f32)] * (2 * slots * last),
                 [pltpu.VMEM((2, size, size), f32), pltpu.VMEM((3, 3, 2, half, LANES), f32)],
-                [spots, counts, *pieces, *earlier, rolled, ordered, tables],
+                [spots, near_spots, counts, *pieces, *earlier, rolled, ordered, tables, token],
             )
             inner.append(inner_part)
             outer.append(outer_part)
@@ -625,18 +672,18 @@
         )
         if sweep < ITERS - 1:
             middle, total = call(
-                lambda *refs, layout=layout: middle_kernel(plan, slots, layout, len(own), *refs),
+                lambda *refs, layout=layout: middle_kernel(plan, slots, layout, len(pieces), *refs),
                 [shape((2, half, plan.mid_tiles * LANES), f32), shape((2, half, width), f32)],
                 [],
-                [info, early, outer_far[-1], inverse, *own],
+                [info, early, outer_far[-1], inverse, *pieces],
             )
             far_middle = plan.far_rows(middle)
             boundary = call(
-                lambda *refs, layout=layout: boundary_kernel(plan, layout, len(own), *refs),
+                lambda *refs, layout=layout: boundary_kernel(plan, layout, len(pieces), *refs),
                 [shape((2, half, 2 * LANES), f32)] * (2 * sides),
                 [],
-                [total, inverse, middle, *own],
-                in_specs=[VMEM, VMEM, ANY] + [VMEM] * len(own),
+                [total, inverse, middle, *pieces],
+                in_specs=[VMEM, VMEM, ANY] + [VMEM] * len(pieces),
             )
             bases, sums = boundary[:sides], boundary[sides:]
             received = plan.across(sums)
@@ -652,29 +699,44 @@
             far = [far_middle] + [plan.far_rows(piece) for piece in pairs]
             near = [plan.near_rows(piece) for piece in updated[sides:]]
             layout = later_layout
+            token = call(
+                token_kernel,
+                shape((8, LANES), f32),
+                [],
+                [far_middle],
+                in_specs=[ANY],
+                flops=10**11,
+            )
     sums = call(
         lambda *refs: halo_sum_kernel(plan, slots, *refs),
         [shape((2, half, LANES), f32)] * sides,
         [],
-        [info, early, outer_far[-1]],
-    )
-    nearly, *bases = call(
-        lambda *refs: last_kernel(plan, slots, layout, len(own), *refs),
+        [info, early, outer_far[-1], inverse],
+    )
+    received = plan.across(sums)
+    nearly = call(
+        lambda *refs: last_kernel(plan, slots, layout, len(pieces), *refs),
+        [shape((2, half, LANES), f32)] * plan.own,
+        [pltpu.VMEM((2, half, width), f32)],
+        [info, early, outer_far[-1], inverse, sums[0], *pieces],
+        in_specs=[SMEM, VMEM, VMEM, VMEM, ANY] + [VMEM] * len(pieces),
+    )
+    others = [plan.swapped_rows(terms) for terms in received]
+    home, *bases = call(
+        lambda *refs: home_kernel(plan, len(nearly), *refs),
         [shape((2, half, block_cols), f32)] + [shape((2, half, LANES), f32)] * sides,
-        [pltpu.VMEM((2, half, block_cols), f32), pltpu.VMEM((2, half, width), f32), dma],
-        [info, early, outer_far[-1], inverse, sums[0], *own],
-        in_specs=[SMEM, VMEM, VMEM, VMEM, ANY] + [VMEM] * len(own),
+        [dma((len(nearly),))],
+        [*nearly, *[plan.swapped_rows(run) for run in nearly]],
         out_specs=[HBM] + [VMEM] * sides,
     )
-    received = plan.across(sums)
     return call(
         lambda *refs: edge_kernel(plan, *refs),
-        shape(nearly.shape, f32),
+        shape(home.shape, f32),
         [pltpu.VMEM((sides, 2, half, LANES), f32), dma((sides,))],
-        [inverse, *bases, *received, nearly],
-        in_specs=[VMEM] * (1 + 2 * sides) + [HBM],
+        [*bases, *received, *others, home],
+        in_specs=[VMEM] * (3 * sides) + [HBM],
         out_specs=HBM,
-        input_output_aliases={1 + 2 * sides: 0},
+        input_output_aliases={3 * sides: 0},
     )
 
 

time: 86.1 us -> 98.1 us (1.14)
  starting transfers between devices: 29.5 us -> 51.5 us
  waiting for transfers between devices: 26.8 us -> 21.1 us
  Pallas kernels: 23.9 us -> 20.1 us
  local copies, waits for them, and re-layouts: 4.75 us -> 3.72 us
    ppermute x18 -> x29, starting transfers between devices: 25.7 us -> 47.4 us  [the longest x6 23.3 us: far_rows(): return lax.ppermute(values, 'sx', pairs + [(j, i) for i, j in pairs])]
    ppermute x18 -> x29, waiting for transfers between devices: 20.7 us -> 13.2 us  [the longest x6 6.82 us: far_rows(): return lax.ppermute(values, 'sx', pairs + [(j, i) for i, j in pairs])]
    pallas_call x18 -> x20, Pallas kernels: 23.9 us -> 20.1 us  [call(): pl.pallas_call(kernel, out_shape=outs, in_specs=in_specs or [SMEM if valu...]
    ppermute x3, waiting for transfers between devices: 6.18 us -> 7.82 us  [across(): return [lax.ppermute(values[0], axis_name, [(0, 1), (1, 0)])]]
    unnamed x18 -> x16, local copies, waits for them, and re-layouts: 4.75 us -> 3.72 us
  transfers between devices with their start and end apart: 21 -> 32, of which waited for: 7 -> 6; matrix products, arithmetic and copies ran while one was open for 0% -> 0% of each run, Pallas kernels for 19% -> 13%
where the time goes in v6:
time: 98.1 us; the launch traced here: 96.8 us
  starting transfers between devices  51.5 us (52%)
  waiting for transfers between devices  21.1 us (22%)
  Pallas kernels  20.1 us (20%)
  local copies, waits for them, and re-layouts  3.72 us (4%)
    ppermute x6, starting transfers between devices, far_rows(): return lax.ppermute(values, 'sx', pairs + [(j, i) for i, j in pairs])  23.3 us
    pallas_call x20, Pallas kernels, call(): pl.pallas_call(kernel, out_shape=outs, in_specs=in_specs or [SMEM if valu...  20.1 us
    ppermute x5, starting transfers between devices, swapped_rows(): lax.ppermute(values, 'sx', [(i, i ^ 1) for i in range(self.sx_size) if i...  11.2 us
    ppermute x16, starting transfers between devices, near_rows(): return lax.ppermute(values, 'sx', [(i, i ^ 1) for i in range(self.sx_size)])  7.83 us
    ppermute x3, waiting for transfers between devices, across(): return [lax.ppermute(values[0], axis_name, [(0, 1), (1, 0)])]  7.82 us
    ppermute x6, waiting for transfers between devices, far_rows(): return lax.ppermute(values, 'sx', pairs + [(j, i) for i, j in pairs])  6.82 us
    ppermute x2, waiting for transfers between devices, first_far_rows(): return lax.ppermute(values, 'sx', pairs)  5.35 us
    ppermute x2, starting transfers between devices, first_far_rows(): return lax.ppermute(values, 'sx', pairs)  5.1 us
  transfers between devices with their start and end apart: 32, of which 6 were waited for; matrix products, arithmetic and copies ran while one was open for 0% of the time, Pallas kernels for 13%

profile of v6, /device:TPU:10, one launch (start us, length us, event | category | flops | bytes accessed | tf_op | source)
XLA Modules:
  0.0 96.8 jit_solution(8778704164320266230)
XLA Ops:
  0.0 2.5 %collective-permute-start.5 = (f32[2,128,512]{2,1,0:T(8,128)}, f32[2,128,512]{2,1,0:T(8,128)S(1)}, u32[]{:S(2)}, u32[]{:S(2)}) collective-permute-start(f32[2,128,512]{2,1,0:T(8,128)} %refs_3_.7), channel_id=1, source_target_pairs={{4,2},{2,6},{8,4},{6,8},{12,10},{10,14},{16,12},{14,16},{20,18},{1... | collective-permute-start | bytes 1572872 | tf_op jit(solution)/shard_map/ppermute | solution.py:117
  3.2 1.0 %copy-done = f32[2,128,512]{2,1,0:T(8,128)S(1)} copy-done((f32[2,128,512]{2,1,0:T(8,128)S(1)}, f32[2,128,512]{2,1,0:T(8,128)}, u32[]{:S(2)}) %copy-start) | copy-done | bytes 524312
  4.9 1.6 %collective-permute-start = (f32[2,136,128]{2,1,0:T(8,128)S(1)}, f32[2,136,128]{2,1,0:T(8,128)S(1)}, u32[]{:S(2)}, u32[]{:S(2)}) collective-permute-start(f32[2,136,128]{2,1,0:T(8,128)S(1)} %shard_map.73), channel_id=1, source_target_pairs={{0,1},{1,0},{2,3},{3,2},{4,5},{5,4},{6,7},{7,6},{8,9},{9,8},{10,11... | collective-permute-start | bytes 417800 | tf_op jit(solution)/shard_map/ppermute | solution.py:101
  7.2 0.8 collective-permute-done.1.near_centres.refs_1_
  8.1 1.0 %copy-done.4 = f32[1,1,2,256,256]{4,3,2,1,0:T(8,128)S(1)} copy-done((f32[1,1,2,256,256]{4,3,2,1,0:T(8,128)S(1)}, f32[1,1,2,256,256]{4,3,2,1,0:T(8,128)}, u32[]{:S(2)}) %copy-start.4) | copy-done | bytes 524312
  9.1 0.9 copy-done.5
  10.1 1.6 %shard_map.74 = (f32[2,2,256,256]{3,2,1,0:T(8,128)S(1)}, f32[2,256,256]{2,1,0:T(8,128)S(1)}) custom-call(s32[2,2]{1,0:T(2,128)S(1)} %bitcast.7, s32[2,2]{1,0:T(2,128)S(1)} %collective-permute-done.1.near_centres.refs_1_, f32[2,256,256]{2,1,0:T(8,128)S(1)} %copy-done.3, f32[2,256,256]{2,1,0:T(8,128)S(1)} %bitcast.4, ...), custom_call_target="tpu_custom_call" | custom-call | flops 100000 | bytes 10000 | tf_op jit(solution)/shard_map/pallas_call | solution.py:552
  13.1 2.6 %collective-permute-start.3 = (f32[2,144,128]{2,1,0:T(8,128)S(1)}, f32[2,144,128]{2,1,0:T(8,128)S(1)}, u32[]{:S(2)}, u32[]{:S(2)}) collective-permute-start(f32[2,144,128]{2,1,0:T(8,128)S(1)} %get-tuple-element.49.refs_0_.refs_4_.refs_5_), channel_id=1, source_target_pairs={{4,2},{2,6},{8,4},{6,8},{12,10},{10,14},{16,12},{14,16},{20,18},{1... | collective-permute-start | bytes 442376 | tf_op jit(solution)/shard_map/ppermute | solution.py:117
  15.7 5.3 %collective-permute-done.3.refs_1_.refs_6_.refs_7_ = f32[2,144,128]{2,1,0:T(8,128)S(1)} collective-permute-done((f32[2,144,128]{2,1,0:T(8,128)S(1)}, f32[2,144,128]{2,1,0:T(8,128)S(1)}, u32[]{:S(2)}, u32[]{:S(2)}) %collective-permute-start.3) | collective-permute-done | bytes 147488 | tf_op jit(solution)/shard_map/ppermute | solution.py:117
  21.1 2.8 %shard_map.77 = (f32[2,128,256]{2,1,0:T(8,128)S(1)}, f32[2,128,256]{2,1,0:T(8,128)S(1)}) custom-call(s32[2,2]{1,0:T(2,128)S(1)} %bitcast.9, s32[2,2]{1,0:T(2,128)S(1)} %collective-permute-done.1.near_centres.refs_1_, s32[16]{0:T(128)S(1)} %bitcast.17, f32[2,128,512]{2,1,0:T(8,128)S(1)} %copy-done.1, ...), custom_call_target="tpu_custom_call" | custom-call | flops 100000 | bytes 10000 | tf_op jit(solution)/shard_map/pallas_call | solution.py:552
  23.9 3.2 %collective-permute-start.8 = (f32[2,128,256]{2,1,0:T(8,128)S(1)}, f32[2,128,256]{2,1,0:T(8,128)S(1)}, u32[]{:S(2)}, u32[]{:S(2)}) collective-permute-start(f32[2,128,256]{2,1,0:T(8,128)S(1)} %get-tuple-element.56.refs_10_), channel_id=1, source_target_pairs={{2,6},{4,8},{10,14},{12,16},{18,22},{20,24},{26,30},{6,2},{8,4},{1... | collective-permute-start | bytes 786440 | tf_op jit(solution)/shard_map/ppermute | solution.py:110
  27.8 5.7 %collective-permute-start.13 = (f32[2,128,256]{2,1,0:T(8,128)S(1)}, f32[2,128,256]{2,1,0:T(8,128)S(1)}, u32[]{:S(2)}, u32[]{:S(2)}) collective-permute-start(f32[2,128,256]{2,1,0:T(8,128)S(1)} %get-tuple-element.62), channel_id=1, source_target_pairs={{2,6},{4,8},{10,14},{12,16},{18,22},{20,24},{26,30},{6,2},{8,4},{1... | collective-permute-start | bytes 786440 | tf_op jit(solution)/shard_map/ppermute | solution.py:110
  34.6 3.2 %shard_map.76 = (f32[128,768]{1,0:T(8,128)S(1)}, s32[6,128]{1,0:T(8,128)S(1)}, f32[128,256]{1,0:T(8,128)S(1)}) custom-call(f32[2,144,128]{2,1,0:T(8,128)S(1)} %get-tuple-element.49.refs_0_.refs_4_.refs_5_, f32[2,144,128]{2,1,0:T(8,128)S(1)} %collective-permute-done.3.refs_1_.refs_6_.refs_7_, ...), custom_call_target="tpu_custom_call" | custom-call | flops 100000 | bytes 10000 | tf_op jit(solution)/shard_map/pallas_call | solution.py:552
  37.8 0.8 shard_map.79.refs_1_
  39.5 0.9 shard_map.81
  40.3 3.3 %collective-permute-start.15 = (f32[2,128,384]{2,1,0:T(8,128)S(1)}, f32[2,128,384]{2,1,0:T(8,128)S(1)}, u32[]{:S(2)}, u32[]{:S(2)}) collective-permute-start(f32[2,128,384]{2,1,0:T(8,128)S(1)} %get-tuple-element.64.refs_2_.refs_0_.refs_3_.refs_5_), channel_id=1, source_target_pairs={{2,6},{4,8},{10,14},{12,16},{18,22},{20,24},{26,30},{6,2},{8,4},{1... | collective-permute-start | bytes 1179656 | tf_op jit(solution)/shard_map/ppermute | solution.py:110
  43.8 1.3 %collective-permute-start.14 = (f32[2,128,256]{2,1,0:T(8,128)S(1)}, f32[2,128,256]{2,1,0:T(8,128)S(1)}, u32[]{:S(2)}, u32[]{:S(2)}) collective-permute-start(f32[2,128,256]{2,1,0:T(8,128)S(1)} %get-tuple-element.67), channel_id=1, source_target_pairs={{0,1},{1,0},{2,3},{3,2},{4,5},{5,4},{6,7},{7,6},{8,9},{9,8},{10,11... | collective-permute-start | bytes 786440 | tf_op jit(solution)/shard_map/ppermute | solution.py:101
  45.1 7.8 %collective-permute-done.14.refs_2_ = f32[2,128,256]{2,1,0:T(8,128)S(1)} collective-permute-done((f32[2,128,256]{2,1,0:T(8,128)S(1)}, f32[2,128,256]{2,1,0:T(8,128)S(1)}, u32[]{:S(2)}, u32[]{:S(2)}) %collective-permute-start.14) | collective-permute-done | bytes 262176 | tf_op jit(solution)/shard_map/ppermute | solution.py:101
  53.7 2.4 %collective-permute-start.16 = (f32[2,128,256]{2,1,0:T(8,128)S(1)}, f32[2,128,256]{2,1,0:T(8,128)S(1)}, u32[]{:S(2)}, u32[]{:S(2)}) collective-permute-start(f32[2,128,256]{2,1,0:T(8,128)S(1)} %get-tuple-element.69.refs_4_.refs_6_), channel_id=1, source_target_pairs={{2,6},{4,8},{10,14},{12,16},{18,22},{20,24},{26,30},{6,2},{8,4},{1... | collective-permute-start | bytes 786440 | tf_op jit(solution)/shard_map/ppermute | solution.py:110
  56.1 6.8 %collective-permute-done.16.refs_6_.refs_8_ = f32[2,128,256]{2,1,0:T(8,128)S(1)} collective-permute-done((f32[2,128,256]{2,1,0:T(8,128)S(1)}, f32[2,128,256]{2,1,0:T(8,128)S(1)}, u32[]{:S(2)}, u32[]{:S(2)}) %collective-permute-start.16) | collective-permute-done | bytes 262176 | tf_op jit(solution)/shard_map/ppermute | solution.py:110
  62.9 2.6 %shard_map.85 = (f32[2,128,256]{2,1,0:T(8,128)S(1)}, f32[2,128,256]{2,1,0:T(8,128)S(1)}) custom-call(s32[2,2]{1,0:T(2,128)S(1)} %bitcast.13, s32[2,2]{1,0:T(2,128)S(1)} %collective-permute-done.1.near_centres.refs_1_, s32[16]{0:T(128)S(1)} %bitcast.19, f32[2,128,384]{2,1,0:T(8,128)S(1)} %get-tuple-element.64.refs_2_.refs_0_.refs_3_.refs_5_, ...), custom_call_target="tpu_custom_call" | custom-call | flops 100000 | bytes 10000 | tf_op jit(solution)/shard_map/pallas_call | solution.py:552
  65.5 2.4 %collective-permute-start.20 = (f32[2,128,256]{2,1,0:T(8,128)S(1)}, f32[2,128,256]{2,1,0:T(8,128)S(1)}, u32[]{:S(2)}, u32[]{:S(2)}) collective-permute-start(f32[2,128,256]{2,1,0:T(8,128)S(1)} %get-tuple-element.74.refs_10_), channel_id=1, source_target_pairs={{2,6},{4,8},{10,14},{12,16},{18,22},{20,24},{26,30},{6,2},{8,4},{1... | collective-permute-start | bytes 786440 | tf_op jit(solution)/shard_map/ppermute | solution.py:110
  68.6 6.3 %collective-permute-start.25 = (f32[2,128,256]{2,1,0:T(8,128)S(1)}, f32[2,128,256]{2,1,0:T(8,128)S(1)}, u32[]{:S(2)}, u32[]{:S(2)}) collective-permute-start(f32[2,128,256]{2,1,0:T(8,128)S(1)} %get-tuple-element.80), channel_id=1, source_target_pairs={{2,6},{4,8},{10,14},{12,16},{18,22},{20,24},{26,30},{6,2},{8,4},{1... | collective-permute-start | bytes 786440 | tf_op jit(solution)/shard_map/ppermute | solution.py:110
  75.6 3.8 %collective-permute-start.24 = (f32[1,128,256]{2,1,0:T(8,128)S(1)}, f32[1,128,256]{2,1,0:T(8,128)S(1)}, u32[]{:S(2)}, u32[]{:S(2)}) collective-permute-start(f32[1,128,256]{2,1,0:T(8,128)S(1)} %get-tuple-element.79), channel_id=1, source_target_pairs={{0,2},{2,0},{4,6},{6,4},{8,10},{10,8},{12,14},{14,12},{16,18},{18,... | collective-permute-start | bytes 393224 | tf_op jit(solution)/shard_map/ppermute | solution.py:120
  81.9 1.2 %collective-permute-start.30 = (f32[2,128,128]{2,1,0:T(8,128)S(1)}, f32[2,128,128]{2,1,0:T(8,128)S(1)}, u32[]{:S(2)}, u32[]{:S(2)}) collective-permute-start(f32[2,128,128]{2,1,0:T(8,128)S(1)} %shard_map.89.refs_4_), channel_id=1, source_target_pairs={{0,1},{1,0},{2,3},{3,2},{4,5},{5,4},{6,7},{7,6},{8,9},{9,8},{10,11... | collective-permute-start | bytes 393224 | tf_op jit(solution)/shard_map/ppermute | solution.py:101
  83.1 0.9 shard_map.90
  83.9 2.5 %collective-permute-start.26 = (f32[2,128,128]{2,1,0:T(8,128)S(1)}, f32[2,128,128]{2,1,0:T(8,128)S(1)}, u32[]{:S(2)}, u32[]{:S(2)}) collective-permute-start(f32[2,128,128]{2,1,0:T(8,128)S(1)} %get-tuple-element.81.refs_0_), channel_id=1, source_target_pairs={{4,6},{6,4},{12,14},{14,12},{20,22},{22,20},{28,30},{30,28},{5,7},... | collective-permute-start | bytes 393224 | tf_op jit(solution)/shard_map/ppermute | solution.py:123
  86.5 1.9 %collective-permute-start.27 = (f32[2,128,128]{2,1,0:T(8,128)S(1)}, f32[2,128,128]{2,1,0:T(8,128)S(1)}, u32[]{:S(2)}, u32[]{:S(2)}) collective-permute-start(f32[2,128,128]{2,1,0:T(8,128)S(1)} %get-tuple-element.82.refs_1_), channel_id=1, source_target_pairs={{4,6},{6,4},{12,14},{14,12},{20,22},{22,20},{28,30},{30,28},{5,7},... | collective-permute-start | bytes 393224 | tf_op jit(solution)/shard_map/ppermute | solution.py:123
  88.4 2.4 %collective-permute-start.28 = (f32[2,128,128]{2,1,0:T(8,128)S(1)}, f32[2,128,128]{2,1,0:T(8,128)S(1)}, u32[]{:S(2)}, u32[]{:S(2)}) collective-permute-start(f32[2,128,128]{2,1,0:T(8,128)S(1)} %get-tuple-element.83.refs_2_), channel_id=1, source_target_pairs={{4,6},{6,4},{12,14},{14,12},{20,22},{22,20},{28,30},{30,28},{5,7},... | collective-permute-start | bytes 393224 | tf_op jit(solution)/shard_map/ppermute | solution.py:123
  90.8 1.9 %collective-permute-start.29 = (f32[2,128,128]{2,1,0:T(8,128)S(1)}, f32[2,128,128]{2,1,0:T(8,128)S(1)}, u32[]{:S(2)}, u32[]{:S(2)}) collective-permute-start(f32[2,128,128]{2,1,0:T(8,128)S(1)} %get-tuple-element.84.refs_3_), channel_id=1, source_target_pairs={{4,6},{6,4},{12,14},{14,12},{20,22},{22,20},{28,30},{30,28},{5,7},... | collective-permute-start | bytes 393224 | tf_op jit(solution)/shard_map/ppermute | solution.py:123
  92.8 2.4 %collective-permute-start.31 = (f32[2,128,128]{2,1,0:T(8,128)S(1)}, f32[2,128,128]{2,1,0:T(8,128)S(1)}, u32[]{:S(2)}, u32[]{:S(2)}) collective-permute-start(f32[2,128,128]{2,1,0:T(8,128)S(1)} %collective-permute-done.30.refs_1_), channel_id=1, source_target_pairs={{4,6},{6,4},{12,14},{14,12},{20,22},{22,20},{28,30},{30,28},{5,7},... | collective-permute-start | bytes 393224 | tf_op jit(solution)/shard_map/ppermute | solution.py:123
  95.2 0.8 shard_map.91
  (68 shorter events, 11.5 us)
Async XLA Ops:
  0.0 8.1 %collective-permute-start.2 = (f32[2,256,256]{2,1,0:T(8,128)}, f32[2,256,256]{2,1,0:T(8,128)S(1)}, u32[]{:S(2)}, u32[]{:S(2)}) collective-permute-start(f32[2,256,256]{2,1,0:T(8,128)} %bitcast.3), channel_id=1, source_target_pairs={{0,2},{2,0},{4,6},{6,4},{8,10},{10,8},{12,14},{14,12},{16,18},{18,... | collective-permute-start | bytes 1572872 | tf_op jit(solution)/shard_map/ppermute | solution.py:120
  0.0 15.7 %collective-permute-start.5 = (f32[2,128,512]{2,1,0:T(8,128)}, f32[2,128,512]{2,1,0:T(8,128)S(1)}, u32[]{:S(2)}, u32[]{:S(2)}) collective-permute-start(f32[2,128,512]{2,1,0:T(8,128)} %refs_3_.7), channel_id=1, source_target_pairs={{4,2},{2,6},{8,4},{6,8},{12,10},{10,14},{16,12},{14,16},{20,18},{1... | collective-permute-start | bytes 1572872 | tf_op jit(solution)/shard_map/ppermute | solution.py:117
  4.9 6.7 %collective-permute-start = (f32[2,136,128]{2,1,0:T(8,128)S(1)}, f32[2,136,128]{2,1,0:T(8,128)S(1)}, u32[]{:S(2)}, u32[]{:S(2)}) collective-permute-start(f32[2,136,128]{2,1,0:T(8,128)S(1)} %shard_map.73), channel_id=1, source_target_pairs={{0,1},{1,0},{2,3},{3,2},{4,5},{5,4},{6,7},{7,6},{8,9},{9,8},{10,11... | collective-permute-start | bytes 417800 | tf_op jit(solution)/shard_map/ppermute | solution.py:101
  6.5 1.6 %collective-permute-start.1 = (s32[2,2]{1,0:T(2,128)S(1)}, s32[2,2]{1,0:T(2,128)S(1)}, u32[]{:S(2)}, u32[]{:S(2)}) collective-permute-start(s32[2,2]{1,0:T(2,128)S(1)} %bitcast.6), channel_id=1, source_target_pairs={{0,2},{2,0},{4,6},{6,4},{8,10},{10,8},{12,14},{14,12},{16,18},{18,... | collective-permute-start | bytes 56 | tf_op jit(solution)/shard_map/ppermute | solution.py:120
  12.3 8.8 %collective-permute-start.6 = (f32[2,128,256]{2,1,0:T(8,128)S(1)}, f32[2,128,256]{2,1,0:T(8,128)S(1)}, u32[]{:S(2)}, u32[]{:S(2)}) collective-permute-start(f32[2,128,256]{2,1,0:T(8,128)S(1)} %get-tuple-element.51), channel_id=1, source_target_pairs={{0,2},{2,0},{4,6},{6,4},{8,10},{10,8},{12,14},{14,12},{16,18},{18,... | collective-permute-start | bytes 786440 | tf_op jit(solution)/shard_map/ppermute | solution.py:120
  12.6 8.4 %collective-permute-start.7 = (f32[2,128,256]{2,1,0:T(8,128)S(1)}, f32[2,128,256]{2,1,0:T(8,128)S(1)}, u32[]{:S(2)}, u32[]{:S(2)}) collective-permute-start(f32[2,128,256]{2,1,0:T(8,128)S(1)} %get-tuple-element.52), channel_id=1, source_target_pairs={{0,2},{2,0},{4,6},{6,4},{8,10},{10,8},{12,14},{14,12},{16,18},{18,... | collective-permute-start | bytes 786440 | tf_op jit(solution)/shard_map/ppermute | solution.py:120
  12.8 2.9 %collective-permute-start.4 = (f32[2,144,128]{2,1,0:T(8,128)S(1)}, f32[2,144,128]{2,1,0:T(8,128)S(1)}, u32[]{:S(2)}, u32[]{:S(2)}) collective-permute-start(f32[2,144,128]{2,1,0:T(8,128)S(1)} %get-tuple-element.49.refs_0_.refs_4_.refs_5_), channel_id=1, source_target_pairs={{0,2},{2,0},{4,6},{6,4},{8,10},{10,8},{12,14},{14,12},{16,18},{18,... | collective-permute-start | bytes 442376 | tf_op jit(solution)/shard_map/ppermute | solution.py:120
  13.1 7.9 %collective-permute-start.3 = (f32[2,144,128]{2,1,0:T(8,128)S(1)}, f32[2,144,128]{2,1,0:T(8,128)S(1)}, u32[]{:S(2)}, u32[]{:S(2)}) collective-permute-start(f32[2,144,128]{2,1,0:T(8,128)S(1)} %get-tuple-element.49.refs_0_.refs_4_.refs_5_), channel_id=1, source_target_pairs={{4,2},{2,6},{8,4},{6,8},{12,10},{10,14},{16,12},{14,16},{20,18},{1... | collective-permute-start | bytes 442376 | tf_op jit(solution)/shard_map/ppermute | solution.py:117
  23.9 10.3 %collective-permute-start.8 = (f32[2,128,256]{2,1,0:T(8,128)S(1)}, f32[2,128,256]{2,1,0:T(8,128)S(1)}, u32[]{:S(2)}, u32[]{:S(2)}) collective-permute-start(f32[2,128,256]{2,1,0:T(8,128)S(1)} %get-tuple-element.56.refs_10_), channel_id=1, source_target_pairs={{2,6},{4,8},{10,14},{12,16},{18,22},{20,24},{26,30},{6,2},{8,4},{1... | collective-permute-start | bytes 786440 | tf_op jit(solution)/shard_map/ppermute | solution.py:110
  27.8 11.7 %collective-permute-start.13 = (f32[2,128,256]{2,1,0:T(8,128)S(1)}, f32[2,128,256]{2,1,0:T(8,128)S(1)}, u32[]{:S(2)}, u32[]{:S(2)}) collective-permute-start(f32[2,128,256]{2,1,0:T(8,128)S(1)} %get-tuple-element.62), channel_id=1, source_target_pairs={{2,6},{4,8},{10,14},{12,16},{18,22},{20,24},{26,30},{6,2},{8,4},{1... | collective-permute-start | bytes 786440 | tf_op jit(solution)/shard_map/ppermute | solution.py:110
  33.5 5.1 %collective-permute-start.9 = (f32[1,128,256]{2,1,0:T(8,128)S(1)}, f32[1,128,256]{2,1,0:T(8,128)S(1)}, u32[]{:S(2)}, u32[]{:S(2)}) collective-permute-start(f32[1,128,256]{2,1,0:T(8,128)S(1)} %get-tuple-element.58), channel_id=1, source_target_pairs={{0,2},{2,0},{4,6},{6,4},{8,10},{10,8},{12,14},{14,12},{16,18},{18,... | collective-permute-start | bytes 393224 | tf_op jit(solution)/shard_map/ppermute | solution.py:120
  33.6 5.1 %collective-permute-start.10 = (f32[1,128,256]{2,1,0:T(8,128)S(1)}, f32[1,128,256]{2,1,0:T(8,128)S(1)}, u32[]{:S(2)}, u32[]{:S(2)}) collective-permute-start(f32[1,128,256]{2,1,0:T(8,128)S(1)} %get-tuple-element.59), channel_id=1, source_target_pairs={{0,2},{2,0},{4,6},{6,4},{8,10},{10,8},{12,14},{14,12},{16,18},{18,... | collective-permute-start | bytes 393224 | tf_op jit(solution)/shard_map/ppermute | solution.py:120
  34.1 4.6 %collective-permute-start.11 = (f32[1,128,256]{2,1,0:T(8,128)S(1)}, f32[1,128,256]{2,1,0:T(8,128)S(1)}, u32[]{:S(2)}, u32[]{:S(2)}) collective-permute-start(f32[1,128,256]{2,1,0:T(8,128)S(1)} %get-tuple-element.60), channel_id=1, source_target_pairs={{0,2},{2,0},{4,6},{6,4},{8,10},{10,8},{12,14},{14,12},{16,18},{18,... | collective-permute-start | bytes 393224 | tf_op jit(solution)/shard_map/ppermute | solution.py:120
  34.2 4.5 %collective-permute-start.12 = (f32[1,128,256]{2,1,0:T(8,128)S(1)}, f32[1,128,256]{2,1,0:T(8,128)S(1)}, u32[]{:S(2)}, u32[]{:S(2)}) collective-permute-start(f32[1,128,256]{2,1,0:T(8,128)S(1)} %get-tuple-element.61), channel_id=1, source_target_pairs={{0,2},{2,0},{4,6},{6,4},{8,10},{10,8},{12,14},{14,12},{16,18},{18,... | collective-permute-start | bytes 393224 | tf_op jit(solution)/shard_map/ppermute | solution.py:120
  40.3 15.7 %collective-permute-start.15 = (f32[2,128,384]{2,1,0:T(8,128)S(1)}, f32[2,128,384]{2,1,0:T(8,128)S(1)}, u32[]{:S(2)}, u32[]{:S(2)}) collective-permute-start(f32[2,128,384]{2,1,0:T(8,128)S(1)} %get-tuple-element.64.refs_2_.refs_0_.refs_3_.refs_5_), channel_id=1, source_target_pairs={{2,6},{4,8},{10,14},{12,16},{18,22},{20,24},{26,30},{6,2},{8,4},{1... | collective-permute-start | bytes 1179656 | tf_op jit(solution)/shard_map/ppermute | solution.py:110
  43.8 9.1 %collective-permute-start.14 = (f32[2,128,256]{2,1,0:T(8,128)S(1)}, f32[2,128,256]{2,1,0:T(8,128)S(1)}, u32[]{:S(2)}, u32[]{:S(2)}) collective-permute-start(f32[2,128,256]{2,1,0:T(8,128)S(1)} %get-tuple-element.67), channel_id=1, source_target_pairs={{0,1},{1,0},{2,3},{3,2},{4,5},{5,4},{6,7},{7,6},{8,9},{9,8},{10,11... | collective-permute-start | bytes 786440 | tf_op jit(solution)/shard_map/ppermute | solution.py:101
  53.0 3.1 %collective-permute-start.19 = (f32[2,128,128]{2,1,0:T(8,128)S(1)}, f32[2,128,128]{2,1,0:T(8,128)S(1)}, u32[]{:S(2)}, u32[]{:S(2)}) collective-permute-start(f32[2,128,128]{2,1,0:T(8,128)S(1)} %get-tuple-element.72), channel_id=1, source_target_pairs={{0,2},{2,0},{4,6},{6,4},{8,10},{10,8},{12,14},{14,12},{16,18},{18,... | collective-permute-start | bytes 393224 | tf_op jit(solution)/shard_map/ppermute | solution.py:120
  53.1 3.0 %collective-permute-start.17 = (f32[2,128,256]{2,1,0:T(8,128)S(1)}, f32[2,128,256]{2,1,0:T(8,128)S(1)}, u32[]{:S(2)}, u32[]{:S(2)}) collective-permute-start(f32[2,128,256]{2,1,0:T(8,128)S(1)} %get-tuple-element.70), channel_id=1, source_target_pairs={{0,2},{2,0},{4,6},{6,4},{8,10},{10,8},{12,14},{14,12},{16,18},{18,... | collective-permute-start | bytes 786440 | tf_op jit(solution)/shard_map/ppermute | solution.py:120
  53.6 2.5 %collective-permute-start.18 = (f32[2,128,256]{2,1,0:T(8,128)S(1)}, f32[2,128,256]{2,1,0:T(8,128)S(1)}, u32[]{:S(2)}, u32[]{:S(2)}) collective-permute-start(f32[2,128,256]{2,1,0:T(8,128)S(1)} %get-tuple-element.71), channel_id=1, source_target_pairs={{0,2},{2,0},{4,6},{6,4},{8,10},{10,8},{12,14},{14,12},{16,18},{18,... | collective-permute-start | bytes 786440 | tf_op jit(solution)/shard_map/ppermute | solution.py:120
  53.7 9.3 %collective-permute-start.16 = (f32[2,128,256]{2,1,0:T(8,128)S(1)}, f32[2,128,256]{2,1,0:T(8,128)S(1)}, u32[]{:S(2)}, u32[]{:S(2)}) collective-permute-start(f32[2,128,256]{2,1,0:T(8,128)S(1)} %get-tuple-element.69.refs_4_.refs_6_), channel_id=1, source_target_pairs={{2,6},{4,8},{10,14},{12,16},{18,22},{20,24},{26,30},{6,2},{8,4},{1... | collective-permute-start | bytes 786440 | tf_op jit(solution)/shard_map/ppermute | solution.py:110
  65.5 10.1 %collective-permute-start.20 = (f32[2,128,256]{2,1,0:T(8,128)S(1)}, f32[2,128,256]{2,1,0:T(8,128)S(1)}, u32[]{:S(2)}, u32[]{:S(2)}) collective-permute-start(f32[2,128,256]{2,1,0:T(8,128)S(1)} %get-tuple-element.74.refs_10_), channel_id=1, source_target_pairs={{2,6},{4,8},{10,14},{12,16},{18,22},{20,24},{26,30},{6,2},{8,4},{1... | collective-permute-start | bytes 786440 | tf_op jit(solution)/shard_map/ppermute | solution.py:110
  68.6 12.6 %collective-permute-start.25 = (f32[2,128,256]{2,1,0:T(8,128)S(1)}, f32[2,128,256]{2,1,0:T(8,128)S(1)}, u32[]{:S(2)}, u32[]{:S(2)}) collective-permute-start(f32[2,128,256]{2,1,0:T(8,128)S(1)} %get-tuple-element.80), channel_id=1, source_target_pairs={{2,6},{4,8},{10,14},{12,16},{18,22},{20,24},{26,30},{6,2},{8,4},{1... | collective-permute-start | bytes 786440 | tf_op jit(solution)/shard_map/ppermute | solution.py:110
  74.9 5.3 %collective-permute-start.21 = (f32[1,128,256]{2,1,0:T(8,128)S(1)}, f32[1,128,256]{2,1,0:T(8,128)S(1)}, u32[]{:S(2)}, u32[]{:S(2)}) collective-permute-start(f32[1,128,256]{2,1,0:T(8,128)S(1)} %get-tuple-element.76), channel_id=1, source_target_pairs={{0,2},{2,0},{4,6},{6,4},{8,10},{10,8},{12,14},{14,12},{16,18},{18,... | collective-permute-start | bytes 393224 | tf_op jit(solution)/shard_map/ppermute | solution.py:120
  75.0 5.2 %collective-permute-start.22 = (f32[1,128,256]{2,1,0:T(8,128)S(1)}, f32[1,128,256]{2,1,0:T(8,128)S(1)}, u32[]{:S(2)}, u32[]{:S(2)}) collective-permute-start(f32[1,128,256]{2,1,0:T(8,128)S(1)} %get-tuple-element.77), channel_id=1, source_target_pairs={{0,2},{2,0},{4,6},{6,4},{8,10},{10,8},{12,14},{14,12},{16,18},{18,... | collective-permute-start | bytes 393224 | tf_op jit(solution)/shard_map/ppermute | solution.py:120
  75.5 4.8 %collective-permute-start.23 = (f32[1,128,256]{2,1,0:T(8,128)S(1)}, f32[1,128,256]{2,1,0:T(8,128)S(1)}, u32[]{:S(2)}, u32[]{:S(2)}) collective-permute-start(f32[1,128,256]{2,1,0:T(8,128)S(1)} %get-tuple-element.78), channel_id=1, source_target_pairs={{0,2},{2,0},{4,6},{6,4},{8,10},{10,8},{12,14},{14,12},{16,18},{18,... | collective-permute-start | bytes 393224 | tf_op jit(solution)/shard_map/ppermute | solution.py:120
  75.6 4.8 %collective-permute-start.24 = (f32[1,128,256]{2,1,0:T(8,128)S(1)}, f32[1,128,256]{2,1,0:T(8,128)S(1)}, u32[]{:S(2)}, u32[]{:S(2)}) collective-permute-start(f32[1,128,256]{2,1,0:T(8,128)S(1)} %get-tuple-element.79), channel_id=1, source_target_pairs={{0,2},{2,0},{4,6},{6,4},{8,10},{10,8},{12,14},{14,12},{16,18},{18,... | collective-permute-start | bytes 393224 | tf_op jit(solution)/shard_map/ppermute | solution.py:120
  81.9 10.8 %collective-permute-start.30 = (f32[2,128,128]{2,1,0:T(8,128)S(1)}, f32[2,128,128]{2,1,0:T(8,128)S(1)}, u32[]{:S(2)}, u32[]{:S(2)}) collective-permute-start(f32[2,128,128]{2,1,0:T(8,128)S(1)} %shard_map.89.refs_4_), channel_id=1, source_target_pairs={{0,1},{1,0},{2,3},{3,2},{4,5},{5,4},{6,7},{7,6},{8,9},{9,8},{10,11... | collective-permute-start | bytes 393224 | tf_op jit(solution)/shard_map/ppermute | solution.py:101
  83.9 11.2 %collective-permute-start.26 = (f32[2,128,128]{2,1,0:T(8,128)S(1)}, f32[2,128,128]{2,1,0:T(8,128)S(1)}, u32[]{:S(2)}, u32[]{:S(2)}) collective-permute-start(f32[2,128,128]{2,1,0:T(8,128)S(1)} %get-tuple-element.81.refs_0_), channel_id=1, source_target_pairs={{4,6},{6,4},{12,14},{14,12},{20,22},{22,20},{28,30},{30,28},{5,7},... | collective-permute-start | bytes 393224 | tf_op jit(solution)/shard_map/ppermute | solution.py:123
  86.5 8.7 %collective-permute-start.27 = (f32[2,128,128]{2,1,0:T(8,128)S(1)}, f32[2,128,128]{2,1,0:T(8,128)S(1)}, u32[]{:S(2)}, u32[]{:S(2)}) collective-permute-start(f32[2,128,128]{2,1,0:T(8,128)S(1)} %get-tuple-element.82.refs_1_), channel_id=1, source_target_pairs={{4,6},{6,4},{12,14},{14,12},{20,22},{22,20},{28,30},{30,28},{5,7},... | collective-permute-start | bytes 393224 | tf_op jit(solution)/shard_map/ppermute | solution.py:123
  88.4 6.8 %collective-permute-start.28 = (f32[2,128,128]{2,1,0:T(8,128)S(1)}, f32[2,128,128]{2,1,0:T(8,128)S(1)}, u32[]{:S(2)}, u32[]{:S(2)}) collective-permute-start(f32[2,128,128]{2,1,0:T(8,128)S(1)} %get-tuple-element.83.refs_2_), channel_id=1, source_target_pairs={{4,6},{6,4},{12,14},{14,12},{20,22},{22,20},{28,30},{30,28},{5,7},... | collective-permute-start | bytes 393224 | tf_op jit(solution)/shard_map/ppermute | solution.py:123
  90.8 4.4 %collective-permute-start.29 = (f32[2,128,128]{2,1,0:T(8,128)S(1)}, f32[2,128,128]{2,1,0:T(8,128)S(1)}, u32[]{:S(2)}, u32[]{:S(2)}) collective-permute-start(f32[2,128,128]{2,1,0:T(8,128)S(1)} %get-tuple-element.84.refs_3_), channel_id=1, source_target_pairs={{4,6},{6,4},{12,14},{14,12},{20,22},{22,20},{28,30},{30,28},{5,7},... | collective-permute-start | bytes 393224 | tf_op jit(solution)/shard_map/ppermute | solution.py:123
  92.8 3.4 %collective-permute-start.31 = (f32[2,128,128]{2,1,0:T(8,128)S(1)}, f32[2,128,128]{2,1,0:T(8,128)S(1)}, u32[]{:S(2)}, u32[]{:S(2)}) collective-permute-start(f32[2,128,128]{2,1,0:T(8,128)S(1)} %collective-permute-done.30.refs_1_), channel_id=1, source_target_pairs={{4,6},{6,4},{12,14},{14,12},{20,22},{22,20},{28,30},{30,28},{5,7},... | collective-permute-start | bytes 393224 | tf_op jit(solution)/shard_map/ppermute | solution.py:123
  (8 other events, 31.1 us)

commit v7 on v5

--- a/solution.py
+++ b/solution.py
@@ -113,8 +113,8 @@
 
     def swaps(self, first):
         pairs = [(i, i + 1) for i in range(first, self.sx_size - 1, 2)]
-        alone = [(i, i) for i in (0, self.sx_size - 1) if first]
-        return pairs + [(j, i) for i, j in pairs] + alone
+        pairs += [(0, self.sx_size - 1)] * first
+        return pairs + [(j, i) for i, j in pairs]
 
     def outermost(self, s):
         return (s == 0) | (s == self.sx_size - 1)
@@ -223,6 +223,10 @@
         result[...] = values
         copy[...] = values
     spread(middle, near[sides:])
+
+
+def token_kernel(_, token):
+    token[...] = jnp.zeros(token.shape, jnp.float32)
 
 
 def prepare_kernel(centres, probe, amps, order, rolled, ordered, padded):
@@ -309,7 +313,7 @@
 
 def term_kernel(plan, slot, layout, pieces, copied, centres, counts, *rest):
     refs, rest = rest[:pieces], rest[pieces:]
-    earlier, (probe, amps, tables, outer, inner), rest = rest[:copied], rest[copied : copied + 5], rest[copied + 5 :]
+    earlier, (probe, amps, tables, _, outer, inner), rest = rest[:copied], rest[copied : copied + 6], rest[copied + 6 :]
     near_outers, (window, picked) = rest[:-2], rest[-2:]
     size = probe.shape[2]
     half = size // 2
@@ -387,17 +391,18 @@
         inner[0] = term_real[half:]
         inner[1] = term_imag[half:]
 
-    for source, target in zip((*earlier, outer), near_outers):
-        target[...] = source[...]
+    for index, source in enumerate((*earlier, outer)):
+        for part in range(2 if near_outers else 0):
+            near_outers[2 * index + part][0] = source[part]
 
 
 class Patch:
     def __init__(self, plan, info, s, patch, slot, down, far=False):
-        half = patch.shape[1]
+        half = (patch[0] if isinstance(patch, (list, tuple)) else patch).shape[1]
         index = (1 if down is None else 1 + down) * (plan.sides + 1)
         row = info[index, 2 * slot]
         col = info[index, 2 * slot + 1]
-        self.patch = patch
+        self.parts = patch if isinstance(patch, (list, tuple)) else [patch.at[0:1], patch.at[1:2]]
         self.tile = col // LANES
         self.first = self.tile % 2
         self.from_tile = lax.broadcasted_iota(jnp.int32, (half, LANES), 1) >= col % LANES
@@ -410,7 +415,7 @@
             self.rows = (line >= jnp.where(down > 0, row, 0)) & (line < after)
 
     def lines(self, part, place):
-        values = self.patch[part, :, lanes(place)]
+        values = self.parts[part][0, :, lanes(place)]
         return values if self.rows is None else jnp.where(self.rows, values, 0.0)
 
     def tiles(self, part):
@@ -443,11 +448,11 @@
 
 
 def near_sum_kernel(plan, slots, info, early, *rest):
-    near, canvas = rest[:slots], rest[slots]
+    near, canvas = rest[: 2 * slots], rest[2 * slots]
     s, _ = here()
     canvas[...] = early[...]
     for slot in range(slots):
-        Patch(plan, info, s, near[slot], slot, -far_side(s)).add_to(canvas)
+        Patch(plan, info, s, near[2 * slot : 2 * slot + 2], slot, -far_side(s)).add_to(canvas)
 
 
 def last_patch(plan, slots, info, patch):
@@ -603,6 +608,7 @@
         return runs_layout(refs, plan.mid_start(t), plan.mid_tiles, plan.pair_starts(t))
 
     layout = first_layout
+    token = spots
 
     for sweep in range(ITERS):
         pieces = own + far + near
@@ -615,9 +621,9 @@
                 lambda *refs, slot=slot, layout=layout, copied=len(earlier): term_kernel(
                     plan, slot, layout, len(pieces), copied, *refs
                 ),
-                [patch] * (2 + slots * last),
+                [patch] * 2 + [shape((1, half, size), f32)] * (2 * slots * last),
                 [pltpu.VMEM((2, size, size), f32), pltpu.VMEM((3, 3, 2, half, LANES), f32)],
-                [spots, counts, *pieces, *earlier, rolled, ordered, tables],
+                [spots, counts, *pieces, *earlier, rolled, ordered, tables, token],
             )
             inner.append(inner_part)
             outer.append(outer_part)
@@ -664,6 +670,14 @@
             far = [far_middle] + [plan.far_rows(piece) for piece in pairs]
             near = [plan.near_rows(piece) for piece in updated[sides:]]
             layout = later_layout
+            token = call(
+                token_kernel,
+                shape((8, LANES), f32),
+                [],
+                [far_middle],
+                in_specs=[ANY],
+                flops=10**11,
+            )
     sums = call(
         lambda *refs: halo_sum_kernel(plan, slots, *refs),
         [shape((2, half, LANES), f32)] * sides,

time: 86.5 us -> 80.4 us (0.929)
  the two profiles are of different devices: /device:TPU:10 before, /device:TPU:0 now
where the time goes in v7:
time: 80.4 us; the launch traced here: 79.1 us
  starting transfers between devices  31 us (39%)
  waiting for transfers between devices  24 us (30%)
  Pallas kernels  19 us (24%)
  local copies, waits for them, and re-layouts  4.77 us (6%)
    ppermute x8, starting transfers between devices, far_rows(): return lax.ppermute(values, 'sx', self.swaps(1))  24.4 us
    pallas_call x19, Pallas kernels, call(): pl.pallas_call(kernel, out_shape=outs, in_specs=in_specs or [SMEM if valu...  19 us
    ppermute x8, waiting for transfers between devices, far_rows(): return lax.ppermute(values, 'sx', self.swaps(1))  13.9 us
    ppermute x3, waiting for transfers between devices, across(): return [lax.ppermute(values[0], axis_name, [(0, 1), (1, 0)])]  8.37 us
    unnamed x18, local copies, waits for them, and re-layouts  4.77 us
    ppermute x3, starting transfers between devices, across(): return [lax.ppermute(values[0], axis_name, [(0, 1), (1, 0)])]  4.11 us
    ppermute x14, starting transfers between devices, near_rows(): return lax.ppermute(values, 'sx', self.swaps(0))  2.48 us
    ppermute x14, waiting for transfers between devices, near_rows(): return lax.ppermute(values, 'sx', self.swaps(0))  1.75 us
  transfers between devices with their start and end apart: 25, of which 9 were waited for; matrix products, arithmetic and copies ran while one was open for 0% of the time, Pallas kernels for 15%

profile of v7, /device:TPU:0, one launch (start us, length us, event | category | flops | bytes accessed | tf_op | source)
XLA Modules:
  0.0 79.1 jit_solution(11863926638996317036)
XLA Ops:
  0.0 5.4 %collective-permute-start.3 = (f32[2,128,512]{2,1,0:T(8,128)}, f32[2,128,512]{2,1,0:T(8,128)S(1)}, u32[]{:S(2)}, u32[]{:S(2)}) collective-permute-start(f32[2,128,512]{2,1,0:T(8,128)} %refs_3_.3), channel_id=1, source_target_pairs={{2,4},{6,8},{10,12},{14,16},{18,20},{22,24},{26,28},{0,30},{4,2},{... | collective-permute-start | bytes 1572872 | tf_op jit(solution)/shard_map/ppermute | solution.py:109
  6.1 1.0 %copy-done = f32[2,128,512]{2,1,0:T(8,128)S(1)} copy-done((f32[2,128,512]{2,1,0:T(8,128)S(1)}, f32[2,128,512]{2,1,0:T(8,128)}, u32[]{:S(2)}) %copy-start) | copy-done | bytes 524312
  7.7 1.6 %collective-permute-start = (f32[2,136,128]{2,1,0:T(8,128)S(1)}, f32[2,136,128]{2,1,0:T(8,128)S(1)}, u32[]{:S(2)}, u32[]{:S(2)}) collective-permute-start(f32[2,136,128]{2,1,0:T(8,128)S(1)} %shard_map.73), channel_id=1, source_target_pairs={{0,1},{1,0},{2,3},{3,2},{4,5},{5,4},{6,7},{7,6},{8,9},{9,8},{10,11... | collective-permute-start | bytes 417800 | tf_op jit(solution)/shard_map/ppermute | solution.py:101
  9.3 1.0 %copy-done.3 = f32[2,256,256]{2,1,0:T(8,128)S(1)} copy-done((f32[2,256,256]{2,1,0:T(8,128)S(1)}, f32[2,256,256]{2,1,0:T(8,128)}, u32[]{:S(2)}) %copy-start.3) | copy-done | bytes 524312
  10.4 1.0 %copy-done.5 = f32[1,1,2,256,256]{4,3,2,1,0:T(8,128)S(1)} copy-done((f32[1,1,2,256,256]{4,3,2,1,0:T(8,128)S(1)}, f32[1,1,2,256,256]{4,3,2,1,0:T(8,128)}, u32[]{:S(2)}) %copy-start.5) | copy-done | bytes 524312
  11.4 0.9 %copy-done.6 = bf16[2,256,256]{2,1,0:T(8,128)(2,1)S(1)} copy-done((bf16[2,256,256]{2,1,0:T(8,128)(2,1)S(1)}, bf16[2,256,256]{2,1,0:T(8,128)(2,1)}, u32[]{:S(2)}) %copy-start.6) | copy-done | bytes 262168
  12.4 1.5 %shard_map.74 = (f32[2,2,256,256]{3,2,1,0:T(8,128)S(1)}, f32[2,256,256]{2,1,0:T(8,128)S(1)}) custom-call(s32[2,2]{1,0:T(2,128)S(1)} %bitcast.5, f32[2,256,256]{2,1,0:T(8,128)S(1)} %copy-done.3, f32[2,256,256]{2,1,0:T(8,128)S(1)} %bitcast.3, bf16[2,256,256]{2,1,0:T(8,128)(2,1)S(1)} %copy-done.6), custom_call_target="tpu_custom_call" | custom-call | flops 100000 | bytes 10000 | tf_op jit(solution)/shard_map/pallas_call | solution.py:528
  15.4 7.0 %collective-permute-done.1.refs_1_.refs_5_ = f32[2,144,128]{2,1,0:T(8,128)S(1)} collective-permute-done((f32[2,144,128]{2,1,0:T(8,128)S(1)}, f32[2,144,128]{2,1,0:T(8,128)S(1)}, u32[]{:S(2)}, u32[]{:S(2)}) %collective-permute-start.1) | collective-permute-done | bytes 147488 | tf_op jit(solution)/shard_map/ppermute | solution.py:109
  22.4 2.6 %shard_map.77 = (f32[2,128,256]{2,1,0:T(8,128)S(1)}, f32[2,128,256]{2,1,0:T(8,128)S(1)}) custom-call(s32[2,2]{1,0:T(2,128)S(1)} %bitcast.7, s32[16]{0:T(128)S(1)} %bitcast.15, f32[2,128,512]{2,1,0:T(8,128)S(1)} %copy-done.1, f32[2,144,128]{2,1,0:T(8,128)S(1)} %get-tuple-element.45.refs_0_.refs_3_.refs_5_.refs_4_, ...), custom_call_target="tpu_custom_call" | custom-call | flops 100000 | bytes 10000 | tf_op jit(solution)/shard_map/pallas_call | solution.py:528
  26.2 6.1 %collective-permute-start.11 = (f32[2,128,256]{2,1,0:T(8,128)S(1)}, f32[2,128,256]{2,1,0:T(8,128)S(1)}, u32[]{:S(2)}, u32[]{:S(2)}) collective-permute-start(f32[2,128,256]{2,1,0:T(8,128)S(1)} %get-tuple-element.59), channel_id=1, source_target_pairs={{2,4},{6,8},{10,12},{14,16},{18,20},{22,24},{26,28},{0,30},{4,2},{... | collective-permute-start | bytes 786440 | tf_op jit(solution)/shard_map/ppermute | solution.py:109
  32.8 0.9 %collective-permute-done.6.refs_3_ = f32[2,128,256]{2,1,0:T(8,128)S(1)} collective-permute-done((f32[2,128,256]{2,1,0:T(8,128)S(1)}, f32[2,128,256]{2,1,0:T(8,128)S(1)}, u32[]{:S(2)}, u32[]{:S(2)}) %collective-permute-start.6) | collective-permute-done | bytes 262176 | tf_op jit(solution)/shard_map/ppermute | solution.py:109
  33.7 2.6 %shard_map.76 = (f32[128,768]{1,0:T(8,128)S(1)}, s32[6,128]{1,0:T(8,128)S(1)}, f32[128,256]{1,0:T(8,128)S(1)}) custom-call(f32[2,144,128]{2,1,0:T(8,128)S(1)} %get-tuple-element.45.refs_0_.refs_3_.refs_5_.refs_4_, f32[2,144,128]{2,1,0:T(8,128)S(1)} %collective-permute-done.1.refs_1_.refs_5_, f32[2,144,128]{2,1,0:T(8,128)S(1)} %collective-permute-done.2.refs_2_.refs_6_, ...), custom_call_target="tpu_custom_call" | custom-call | flops 100000 | bytes 10000 | tf_op jit(solution)/shard_map/pallas_call | solution.py:528
  36.3 0.8 %shard_map.79.refs_1_ = f32[2,128,768]{2,1,0:T(8,128)S(1)} custom-call(s32[6,128]{1,0:T(8,128)S(1)} %get-tuple-element.47.refs_0_, f32[2,128,256]{2,1,0:T(8,128)S(1)} %get-tuple-element.52.refs_1_, f32[2,128,256]{2,1,0:T(8,128)S(1)} %get-tuple-element.54.refs_2_, f32[2,128,256]{2,1,0:T(8,128)S(1)} %collective-permute-done.6.refs_3_), custom_call_target="tpu_custom_call" | custom-call | flops 100000 | bytes 10000 | tf_op jit(solution)/shard_map/pallas_call | solution.py:528
  37.2 0.8 shard_map.80.refs_1_
  38.0 0.8 %shard_map.81 = (f32[2,128,384]{2,1,0:T(8,128)S(1)}, f32[2,128,768]{2,1,0:T(8,128)S(1)}) custom-call(s32[6,128]{1,0:T(8,128)S(1)} %get-tuple-element.47.refs_0_, f32[2,128,768]{2,1,0:T(8,128)S(1)} %shard_map.80.refs_1_, f32[2,128,256]{2,1,0:T(8,128)S(1)} %collective-permute-done.11.refs_2_, f32[128,768]{1,0:T(8,128)S(1)} %get-tuple-element.46.refs_3_.refs_1_.refs_0_, ...), custom_call_target="tpu_custom_call" | custom-call | flops 100000 | bytes 10000 | tf_op jit(solution)/shard_map/pallas_call | solution.py:528
  38.8 2.9 %collective-permute-start.13 = (f32[2,128,384]{2,1,0:T(8,128)S(1)}, f32[2,128,384]{2,1,0:T(8,128)S(1)}, u32[]{:S(2)}, u32[]{:S(2)}) collective-permute-start(f32[2,128,384]{2,1,0:T(8,128)S(1)} %get-tuple-element.60.refs_2_.refs_0_.refs_5_), channel_id=1, source_target_pairs={{2,4},{6,8},{10,12},{14,16},{18,20},{22,24},{26,28},{0,30},{4,2},{... | collective-permute-start | bytes 1179656 | tf_op jit(solution)/shard_map/ppermute | solution.py:109
  41.8 0.9 %collective-permute-start.12 = (f32[2,128,256]{2,1,0:T(8,128)S(1)}, f32[2,128,256]{2,1,0:T(8,128)S(1)}, u32[]{:S(2)}, u32[]{:S(2)}) collective-permute-start(f32[2,128,256]{2,1,0:T(8,128)S(1)} %get-tuple-element.63), channel_id=1, source_target_pairs={{0,1},{1,0},{2,3},{3,2},{4,5},{5,4},{6,7},{7,6},{8,9},{9,8},{10,11... | collective-permute-start | bytes 786440 | tf_op jit(solution)/shard_map/ppermute | solution.py:101
  42.7 6.3 %collective-permute-done.12.refs_2_ = f32[2,128,256]{2,1,0:T(8,128)S(1)} collective-permute-done((f32[2,128,256]{2,1,0:T(8,128)S(1)}, f32[2,128,256]{2,1,0:T(8,128)S(1)}, u32[]{:S(2)}, u32[]{:S(2)}) %collective-permute-start.12) | collective-permute-done | bytes 262176 | tf_op jit(solution)/shard_map/ppermute | solution.py:101
  49.0 2.7 %collective-permute-start.14 = (f32[2,128,256]{2,1,0:T(8,128)S(1)}, f32[2,128,256]{2,1,0:T(8,128)S(1)}, u32[]{:S(2)}, u32[]{:S(2)}) collective-permute-start(f32[2,128,256]{2,1,0:T(8,128)S(1)} %get-tuple-element.65.refs_3_.refs_6_), channel_id=1, source_target_pairs={{2,4},{6,8},{10,12},{14,16},{18,20},{22,24},{26,28},{0,30},{4,2},{... | collective-permute-start | bytes 786440 | tf_op jit(solution)/shard_map/ppermute | solution.py:109
  52.2 1.6 %collective-permute-done.17.refs_8_ = f32[2,128,128]{2,1,0:T(8,128)S(1)} collective-permute-done((f32[2,128,128]{2,1,0:T(8,128)S(1)}, f32[2,128,128]{2,1,0:T(8,128)S(1)}, u32[]{:S(2)}, u32[]{:S(2)}) %collective-permute-start.17) | collective-permute-done | bytes 131104 | tf_op jit(solution)/shard_map/ppermute | solution.py:112
  53.8 3.8 %collective-permute-done.14.refs_5_ = f32[2,128,256]{2,1,0:T(8,128)S(1)} collective-permute-done((f32[2,128,256]{2,1,0:T(8,128)S(1)}, f32[2,128,256]{2,1,0:T(8,128)S(1)}, u32[]{:S(2)}, u32[]{:S(2)}) %collective-permute-start.14) | collective-permute-done | bytes 262176 | tf_op jit(solution)/shard_map/ppermute | solution.py:109
  57.6 2.6 %shard_map.85 = (f32[2,128,256]{2,1,0:T(8,128)S(1)}, f32[2,128,256]{2,1,0:T(8,128)S(1)}) custom-call(s32[2,2]{1,0:T(2,128)S(1)} %bitcast.11, s32[16]{0:T(128)S(1)} %bitcast.17, f32[2,128,384]{2,1,0:T(8,128)S(1)} %get-tuple-element.60.refs_2_.refs_0_.refs_5_, f32[2,128,256]{2,1,0:T(8,128)S(1)} %get-tuple-element.65.refs_3_.refs_6_, ...), custom_call_target="tpu_custom_call" | custom-call | flops 100000 | bytes 10000 | tf_op jit(solution)/shard_map/pallas_call | solution.py:528
  60.2 2.7 %collective-permute-start.18 = (f32[2,128,256]{2,1,0:T(8,128)S(1)}, f32[2,128,256]{2,1,0:T(8,128)S(1)}, u32[]{:S(2)}, u32[]{:S(2)}) collective-permute-start(f32[2,128,256]{2,1,0:T(8,128)S(1)} %get-tuple-element.70.refs_9_), channel_id=1, source_target_pairs={{2,4},{6,8},{10,12},{14,16},{18,20},{22,24},{26,28},{0,30},{4,2},{... | collective-permute-start | bytes 786440 | tf_op jit(solution)/shard_map/ppermute | solution.py:109
  63.6 3.8 %collective-permute-start.23 = (f32[2,128,256]{2,1,0:T(8,128)S(1)}, f32[2,128,256]{2,1,0:T(8,128)S(1)}, u32[]{:S(2)}, u32[]{:S(2)}) collective-permute-start(f32[2,128,256]{2,1,0:T(8,128)S(1)} %get-tuple-element.76), channel_id=1, source_target_pairs={{2,4},{6,8},{10,12},{14,16},{18,20},{22,24},{26,28},{0,30},{4,2},{... | collective-permute-start | bytes 786440 | tf_op jit(solution)/shard_map/ppermute | solution.py:109
  67.9 0.9 %collective-permute-done.18.refs_3_ = f32[2,128,256]{2,1,0:T(8,128)S(1)} collective-permute-done((f32[2,128,256]{2,1,0:T(8,128)S(1)}, f32[2,128,256]{2,1,0:T(8,128)S(1)}, u32[]{:S(2)}, u32[]{:S(2)}) %collective-permute-start.18) | collective-permute-done | bytes 262176 | tf_op jit(solution)/shard_map/ppermute | solution.py:109
  69.2 0.8 %shard_map.87.refs_1_ = f32[2,128,768]{2,1,0:T(8,128)S(1)} custom-call(s32[6,128]{1,0:T(8,128)S(1)} %get-tuple-element.47.refs_0_, f32[2,128,256]{2,1,0:T(8,128)S(1)} %get-tuple-element.69.refs_1_, f32[2,128,256]{2,1,0:T(8,128)S(1)} %get-tuple-element.71.refs_2_, f32[2,128,256]{2,1,0:T(8,128)S(1)} %collective-permute-done.18.refs_3_), custom_call_target="tpu_custom_call" | custom-call | flops 100000 | bytes 10000 | tf_op jit(solution)/shard_map/pallas_call | solution.py:528
  70.2 0.8 shard_map.88.refs_1_
  71.0 1.3 %collective-permute-done.23.refs_2_ = f32[2,128,256]{2,1,0:T(8,128)S(1)} collective-permute-done((f32[2,128,256]{2,1,0:T(8,128)S(1)}, f32[2,128,256]{2,1,0:T(8,128)S(1)}, u32[]{:S(2)}, u32[]{:S(2)}) %collective-permute-start.23) | collective-permute-done | bytes 262176 | tf_op jit(solution)/shard_map/ppermute | solution.py:109
  72.9 1.7 %collective-permute-start.24 = (f32[2,128,128]{2,1,0:T(8,128)S(1)}, f32[2,128,128]{2,1,0:T(8,128)S(1)}, u32[]{:S(2)}, u32[]{:S(2)}) collective-permute-start(f32[2,128,128]{2,1,0:T(8,128)S(1)} %shard_map.89.refs_4_), channel_id=1, source_target_pairs={{0,1},{1,0},{2,3},{3,2},{4,5},{5,4},{6,7},{7,6},{8,9},{9,8},{10,11... | collective-permute-start | bytes 393224 | tf_op jit(solution)/shard_map/ppermute | solution.py:101
  74.6 1.7 %shard_map.90 = (f32[2,128,512]{2,1,0:T(8,128)}, f32[2,128,128]{2,1,0:T(8,128)S(1)}) custom-call(s32[6,128]{1,0:T(8,128)S(1)} %get-tuple-element.47.refs_0_, f32[2,128,768]{2,1,0:T(8,128)S(1)} %shard_map.88.refs_1_, f32[2,128,256]{2,1,0:T(8,128)S(1)} %collective-permute-done.23.refs_2_, f32[128,768]{1,0:T(8,128)S(1)} %get-tuple-element.46.refs_3_.refs_1_.refs_0_, ...), custom_call_target="tpu_custom_call" | custom-call | flops 100000 | bytes 10000 | tf_op jit(solution)/shard_map/pallas_call | solution.py:528
  76.3 2.1 %collective-permute-done.24.refs_2_ = f32[2,128,128]{2,1,0:T(8,128)S(1)} collective-permute-done((f32[2,128,128]{2,1,0:T(8,128)S(1)}, f32[2,128,128]{2,1,0:T(8,128)S(1)}, u32[]{:S(2)}, u32[]{:S(2)}) %collective-permute-start.24) | collective-permute-done | bytes 131104 | tf_op jit(solution)/shard_map/ppermute | solution.py:101
  78.4 0.7 shard_map.91
  (55 shorter events, 7.4 us)
Async XLA Ops:
  0.0 22.4 %collective-permute-start.3 = (f32[2,128,512]{2,1,0:T(8,128)}, f32[2,128,512]{2,1,0:T(8,128)S(1)}, u32[]{:S(2)}, u32[]{:S(2)}) collective-permute-start(f32[2,128,512]{2,1,0:T(8,128)} %refs_3_.3), channel_id=1, source_target_pairs={{2,4},{6,8},{10,12},{14,16},{18,20},{22,24},{26,28},{0,30},{4,2},{... | collective-permute-start | bytes 1572872 | tf_op jit(solution)/shard_map/ppermute | solution.py:109
  6.1 1.0 %copy-start = (f32[2,128,512]{2,1,0:T(8,128)S(1)}, f32[2,128,512]{2,1,0:T(8,128)}, u32[]{:S(2)}) copy-start(f32[2,128,512]{2,1,0:T(8,128)} %refs_3_.3) | copy-start | bytes 1572868
  7.1 15.3 %copy-start.2 = (bf16[2,2,2,256,256]{4,3,2,1,0:T(8,128)(2,1)S(1)}, bf16[2,2,2,256,256]{4,3,2,1,0:T(8,128)(2,1)}, u32[]{:S(2)}) copy-start(bf16[2,2,2,256,256]{4,3,2,1,0:T(8,128)(2,1)} %constant.4.clone.refs_11_.refs_12_) | copy-start | bytes 3145732
  7.7 6.2 %collective-permute-start = (f32[2,136,128]{2,1,0:T(8,128)S(1)}, f32[2,136,128]{2,1,0:T(8,128)S(1)}, u32[]{:S(2)}, u32[]{:S(2)}) collective-permute-start(f32[2,136,128]{2,1,0:T(8,128)S(1)} %shard_map.73), channel_id=1, source_target_pairs={{0,1},{1,0},{2,3},{3,2},{4,5},{5,4},{6,7},{7,6},{8,9},{9,8},{10,11... | collective-permute-start | bytes 417800 | tf_op jit(solution)/shard_map/ppermute | solution.py:101
  9.3 1.0 %copy-start.3 = (f32[2,256,256]{2,1,0:T(8,128)S(1)}, f32[2,256,256]{2,1,0:T(8,128)}, u32[]{:S(2)}) copy-start(f32[2,256,256]{2,1,0:T(8,128)} %refs_3_.2) | copy-start | bytes 1572868
  10.4 1.0 %copy-start.5 = (f32[1,1,2,256,256]{4,3,2,1,0:T(8,128)S(1)}, f32[1,1,2,256,256]{4,3,2,1,0:T(8,128)}, u32[]{:S(2)}) copy-start(f32[1,1,2,256,256]{4,3,2,1,0:T(8,128)} %param.9) | copy-start | bytes 1572868
  11.4 0.9 %copy-start.6 = (bf16[2,256,256]{2,1,0:T(8,128)(2,1)S(1)}, bf16[2,256,256]{2,1,0:T(8,128)(2,1)}, u32[]{:S(2)}) copy-start(bf16[2,256,256]{2,1,0:T(8,128)(2,1)} %constant.5.clone.order) | copy-start | bytes 786436
  12.4 1.6 %copy-start.1 = (f32[2,128,512]{2,1,0:T(8,128)S(1)}, f32[2,128,512]{2,1,0:T(8,128)}, u32[]{:S(2)}) copy-start(f32[2,128,512]{2,1,0:T(8,128)} %refs_3_.3) | copy-start | bytes 1572868
  14.5 7.8 %collective-permute-start.4 = (f32[2,128,256]{2,1,0:T(8,128)S(1)}, f32[2,128,256]{2,1,0:T(8,128)S(1)}, u32[]{:S(2)}, u32[]{:S(2)}) collective-permute-start(f32[2,128,256]{2,1,0:T(8,128)S(1)} %get-tuple-element.48), channel_id=1, source_target_pairs={{0,2},{4,6},{8,10},{12,14},{16,18},{20,22},{24,26},{28,30},{2,0},{... | collective-permute-start | bytes 786440 | tf_op jit(solution)/shard_map/ppermute | solution.py:112
  14.6 7.8 %collective-permute-start.5 = (f32[2,128,256]{2,1,0:T(8,128)S(1)}, f32[2,128,256]{2,1,0:T(8,128)S(1)}, u32[]{:S(2)}, u32[]{:S(2)}) collective-permute-start(f32[2,128,256]{2,1,0:T(8,128)S(1)} %get-tuple-element.49), channel_id=1, source_target_pairs={{0,2},{4,6},{8,10},{12,14},{16,18},{20,22},{24,26},{28,30},{2,0},{... | collective-permute-start | bytes 786440 | tf_op jit(solution)/shard_map/ppermute | solution.py:112
  15.1 7.3 %collective-permute-start.1 = (f32[2,144,128]{2,1,0:T(8,128)S(1)}, f32[2,144,128]{2,1,0:T(8,128)S(1)}, u32[]{:S(2)}, u32[]{:S(2)}) collective-permute-start(f32[2,144,128]{2,1,0:T(8,128)S(1)} %get-tuple-element.45.refs_0_.refs_3_.refs_5_.refs_4_), channel_id=1, source_target_pairs={{2,4},{6,8},{10,12},{14,16},{18,20},{22,24},{26,28},{0,30},{4,2},{... | collective-permute-start | bytes 442376 | tf_op jit(solution)/shard_map/ppermute | solution.py:109
  15.4 7.0 %collective-permute-start.2 = (f32[2,144,128]{2,1,0:T(8,128)S(1)}, f32[2,144,128]{2,1,0:T(8,128)S(1)}, u32[]{:S(2)}, u32[]{:S(2)}) collective-permute-start(f32[2,144,128]{2,1,0:T(8,128)S(1)} %get-tuple-element.45.refs_0_.refs_3_.refs_5_.refs_4_), channel_id=1, source_target_pairs={{0,2},{4,6},{8,10},{12,14},{16,18},{20,22},{24,26},{28,30},{2,0},{... | collective-permute-start | bytes 442376 | tf_op jit(solution)/shard_map/ppermute | solution.py:112
  25.1 8.7 %copy-start.4 = (f32[2,256,256]{2,1,0:T(8,128)S(1)}, f32[2,256,256]{2,1,0:T(8,128)}, u32[]{:S(2)}) copy-start(f32[2,256,256]{2,1,0:T(8,128)} %refs_3_.2) | copy-start | bytes 1572868
  25.1 8.7 %collective-permute-start.6 = (f32[2,128,256]{2,1,0:T(8,128)S(1)}, f32[2,128,256]{2,1,0:T(8,128)S(1)}, u32[]{:S(2)}, u32[]{:S(2)}) collective-permute-start(f32[2,128,256]{2,1,0:T(8,128)S(1)} %get-tuple-element.53.refs_9_), channel_id=1, source_target_pairs={{2,4},{6,8},{10,12},{14,16},{18,20},{22,24},{26,28},{0,30},{4,2},{... | collective-permute-start | bytes 786440 | tf_op jit(solution)/shard_map/ppermute | solution.py:109
  26.2 11.8 %collective-permute-start.11 = (f32[2,128,256]{2,1,0:T(8,128)S(1)}, f32[2,128,256]{2,1,0:T(8,128)S(1)}, u32[]{:S(2)}, u32[]{:S(2)}) collective-permute-start(f32[2,128,256]{2,1,0:T(8,128)S(1)} %get-tuple-element.59), channel_id=1, source_target_pairs={{2,4},{6,8},{10,12},{14,16},{18,20},{22,24},{26,28},{0,30},{4,2},{... | collective-permute-start | bytes 786440 | tf_op jit(solution)/shard_map/ppermute | solution.py:109
  32.3 4.8 %collective-permute-start.7 = (f32[1,128,256]{2,1,0:T(8,128)S(1)}, f32[1,128,256]{2,1,0:T(8,128)S(1)}, u32[]{:S(2)}, u32[]{:S(2)}) collective-permute-start(f32[1,128,256]{2,1,0:T(8,128)S(1)} %get-tuple-element.55), channel_id=1, source_target_pairs={{0,2},{4,6},{8,10},{12,14},{16,18},{20,22},{24,26},{28,30},{2,0},{... | collective-permute-start | bytes 393224 | tf_op jit(solution)/shard_map/ppermute | solution.py:112
  32.3 4.8 %collective-permute-start.8 = (f32[1,128,256]{2,1,0:T(8,128)S(1)}, f32[1,128,256]{2,1,0:T(8,128)S(1)}, u32[]{:S(2)}, u32[]{:S(2)}) collective-permute-start(f32[1,128,256]{2,1,0:T(8,128)S(1)} %get-tuple-element.56), channel_id=1, source_target_pairs={{0,2},{4,6},{8,10},{12,14},{16,18},{20,22},{24,26},{28,30},{2,0},{... | collective-permute-start | bytes 393224 | tf_op jit(solution)/shard_map/ppermute | solution.py:112
  32.8 4.3 %collective-permute-start.9 = (f32[1,128,256]{2,1,0:T(8,128)S(1)}, f32[1,128,256]{2,1,0:T(8,128)S(1)}, u32[]{:S(2)}, u32[]{:S(2)}) collective-permute-start(f32[1,128,256]{2,1,0:T(8,128)S(1)} %get-tuple-element.57), channel_id=1, source_target_pairs={{0,2},{4,6},{8,10},{12,14},{16,18},{20,22},{24,26},{28,30},{2,0},{... | collective-permute-start | bytes 393224 | tf_op jit(solution)/shard_map/ppermute | solution.py:112
  33.7 3.4 %collective-permute-start.10 = (f32[1,128,256]{2,1,0:T(8,128)S(1)}, f32[1,128,256]{2,1,0:T(8,128)S(1)}, u32[]{:S(2)}, u32[]{:S(2)}) collective-permute-start(f32[1,128,256]{2,1,0:T(8,128)S(1)} %get-tuple-element.58), channel_id=1, source_target_pairs={{0,2},{4,6},{8,10},{12,14},{16,18},{20,22},{24,26},{28,30},{2,0},{... | collective-permute-start | bytes 393224 | tf_op jit(solution)/shard_map/ppermute | solution.py:112
  38.8 13.4 %collective-permute-start.13 = (f32[2,128,384]{2,1,0:T(8,128)S(1)}, f32[2,128,384]{2,1,0:T(8,128)S(1)}, u32[]{:S(2)}, u32[]{:S(2)}) collective-permute-start(f32[2,128,384]{2,1,0:T(8,128)S(1)} %get-tuple-element.60.refs_2_.refs_0_.refs_5_), channel_id=1, source_target_pairs={{2,4},{6,8},{10,12},{14,16},{18,20},{22,24},{26,28},{0,30},{4,2},{... | collective-permute-start | bytes 1179656 | tf_op jit(solution)/shard_map/ppermute | solution.py:109
  41.8 7.1 %collective-permute-start.12 = (f32[2,128,256]{2,1,0:T(8,128)S(1)}, f32[2,128,256]{2,1,0:T(8,128)S(1)}, u32[]{:S(2)}, u32[]{:S(2)}) collective-permute-start(f32[2,128,256]{2,1,0:T(8,128)S(1)} %get-tuple-element.63), channel_id=1, source_target_pairs={{0,1},{1,0},{2,3},{3,2},{4,5},{5,4},{6,7},{7,6},{8,9},{9,8},{10,11... | collective-permute-start | bytes 786440 | tf_op jit(solution)/shard_map/ppermute | solution.py:101
  49.0 8.6 %collective-permute-start.14 = (f32[2,128,256]{2,1,0:T(8,128)S(1)}, f32[2,128,256]{2,1,0:T(8,128)S(1)}, u32[]{:S(2)}, u32[]{:S(2)}) collective-permute-start(f32[2,128,256]{2,1,0:T(8,128)S(1)} %get-tuple-element.65.refs_3_.refs_6_), channel_id=1, source_target_pairs={{2,4},{6,8},{10,12},{14,16},{18,20},{22,24},{26,28},{0,30},{4,2},{... | collective-permute-start | bytes 786440 | tf_op jit(solution)/shard_map/ppermute | solution.py:109
  51.7 5.9 %collective-permute-start.15 = (f32[2,128,256]{2,1,0:T(8,128)S(1)}, f32[2,128,256]{2,1,0:T(8,128)S(1)}, u32[]{:S(2)}, u32[]{:S(2)}) collective-permute-start(f32[2,128,256]{2,1,0:T(8,128)S(1)} %get-tuple-element.66), channel_id=1, source_target_pairs={{0,2},{4,6},{8,10},{12,14},{16,18},{20,22},{24,26},{28,30},{2,0},{... | collective-permute-start | bytes 786440 | tf_op jit(solution)/shard_map/ppermute | solution.py:112
  51.7 5.9 %collective-permute-start.16 = (f32[2,128,256]{2,1,0:T(8,128)S(1)}, f32[2,128,256]{2,1,0:T(8,128)S(1)}, u32[]{:S(2)}, u32[]{:S(2)}) collective-permute-start(f32[2,128,256]{2,1,0:T(8,128)S(1)} %get-tuple-element.67), channel_id=1, source_target_pairs={{0,2},{4,6},{8,10},{12,14},{16,18},{20,22},{24,26},{28,30},{2,0},{... | collective-permute-start | bytes 786440 | tf_op jit(solution)/shard_map/ppermute | solution.py:112
  52.2 1.6 %collective-permute-start.17 = (f32[2,128,128]{2,1,0:T(8,128)S(1)}, f32[2,128,128]{2,1,0:T(8,128)S(1)}, u32[]{:S(2)}, u32[]{:S(2)}) collective-permute-start(f32[2,128,128]{2,1,0:T(8,128)S(1)} %get-tuple-element.68), channel_id=1, source_target_pairs={{0,2},{4,6},{8,10},{12,14},{16,18},{20,22},{24,26},{28,30},{2,0},{... | collective-permute-start | bytes 393224 | tf_op jit(solution)/shard_map/ppermute | solution.py:112
  60.2 8.7 %collective-permute-start.18 = (f32[2,128,256]{2,1,0:T(8,128)S(1)}, f32[2,128,256]{2,1,0:T(8,128)S(1)}, u32[]{:S(2)}, u32[]{:S(2)}) collective-permute-start(f32[2,128,256]{2,1,0:T(8,128)S(1)} %get-tuple-element.70.refs_9_), channel_id=1, source_target_pairs={{2,4},{6,8},{10,12},{14,16},{18,20},{22,24},{26,28},{0,30},{4,2},{... | collective-permute-start | bytes 786440 | tf_op jit(solution)/shard_map/ppermute | solution.py:109
  63.6 8.7 %collective-permute-start.23 = (f32[2,128,256]{2,1,0:T(8,128)S(1)}, f32[2,128,256]{2,1,0:T(8,128)S(1)}, u32[]{:S(2)}, u32[]{:S(2)}) collective-permute-start(f32[2,128,256]{2,1,0:T(8,128)S(1)} %get-tuple-element.76), channel_id=1, source_target_pairs={{2,4},{6,8},{10,12},{14,16},{18,20},{22,24},{26,28},{0,30},{4,2},{... | collective-permute-start | bytes 786440 | tf_op jit(solution)/shard_map/ppermute | solution.py:109
  67.4 2.6 %collective-permute-start.19 = (f32[1,128,256]{2,1,0:T(8,128)S(1)}, f32[1,128,256]{2,1,0:T(8,128)S(1)}, u32[]{:S(2)}, u32[]{:S(2)}) collective-permute-start(f32[1,128,256]{2,1,0:T(8,128)S(1)} %get-tuple-element.72), channel_id=1, source_target_pairs={{0,2},{4,6},{8,10},{12,14},{16,18},{20,22},{24,26},{28,30},{2,0},{... | collective-permute-start | bytes 393224 | tf_op jit(solution)/shard_map/ppermute | solution.py:112
  67.4 2.6 %collective-permute-start.20 = (f32[1,128,256]{2,1,0:T(8,128)S(1)}, f32[1,128,256]{2,1,0:T(8,128)S(1)}, u32[]{:S(2)}, u32[]{:S(2)}) collective-permute-start(f32[1,128,256]{2,1,0:T(8,128)S(1)} %get-tuple-element.73), channel_id=1, source_target_pairs={{0,2},{4,6},{8,10},{12,14},{16,18},{20,22},{24,26},{28,30},{2,0},{... | collective-permute-start | bytes 393224 | tf_op jit(solution)/shard_map/ppermute | solution.py:112
  67.9 2.1 %collective-permute-start.21 = (f32[1,128,256]{2,1,0:T(8,128)S(1)}, f32[1,128,256]{2,1,0:T(8,128)S(1)}, u32[]{:S(2)}, u32[]{:S(2)}) collective-permute-start(f32[1,128,256]{2,1,0:T(8,128)S(1)} %get-tuple-element.74), channel_id=1, source_target_pairs={{0,2},{4,6},{8,10},{12,14},{16,18},{20,22},{24,26},{28,30},{2,0},{... | collective-permute-start | bytes 393224 | tf_op jit(solution)/shard_map/ppermute | solution.py:112
  68.9 1.4 %collective-permute-start.22 = (f32[1,128,256]{2,1,0:T(8,128)S(1)}, f32[1,128,256]{2,1,0:T(8,128)S(1)}, u32[]{:S(2)}, u32[]{:S(2)}) collective-permute-start(f32[1,128,256]{2,1,0:T(8,128)S(1)} %get-tuple-element.75), channel_id=1, source_target_pairs={{0,2},{4,6},{8,10},{12,14},{16,18},{20,22},{24,26},{28,30},{2,0},{... | collective-permute-start | bytes 393224 | tf_op jit(solution)/shard_map/ppermute | solution.py:112
  72.9 5.5 %collective-permute-start.24 = (f32[2,128,128]{2,1,0:T(8,128)S(1)}, f32[2,128,128]{2,1,0:T(8,128)S(1)}, u32[]{:S(2)}, u32[]{:S(2)}) collective-permute-start(f32[2,128,128]{2,1,0:T(8,128)S(1)} %shard_map.89.refs_4_), channel_id=1, source_target_pairs={{0,1},{1,0},{2,3},{3,2},{4,5},{5,4},{6,7},{7,6},{8,9},{9,8},{10,11... | collective-permute-start | bytes 393224 | tf_op jit(solution)/shard_map/ppermute | solution.py:101
  (2 other events, 1.4 us)

commit v8 on v7

--- a/solution.py
+++ b/solution.py
@@ -106,15 +106,14 @@
         ]
 
     def far_rows(self, values):
-        return lax.ppermute(values, "sx", self.swaps(1))
+        rows, columns = self.sx_size, self.sy_size
+        pairs = [(i * columns + t, (i + 1) * columns + t) for i in range(1, rows - 1, 2) for t in range(columns)]
+        for i in (0, rows - 1):
+            pairs += [(i * columns + t, i * columns + t + 1) for t in range(0, columns - 1, 2)]
+        return lax.ppermute(values, ("sx", "sy"), pairs + [(j, i) for i, j in pairs])
 
     def near_rows(self, values):
-        return lax.ppermute(values, "sx", self.swaps(0))
-
-    def swaps(self, first):
-        pairs = [(i, i + 1) for i in range(first, self.sx_size - 1, 2)]
-        pairs += [(0, self.sx_size - 1)] * first
-        return pairs + [(j, i) for i, j in pairs]
+        return lax.ppermute(values, "sx", [(i, i ^ 1) for i in range(self.sx_size)])
 
     def outermost(self, s):
         return (s == 0) | (s == self.sx_size - 1)
@@ -571,7 +570,6 @@
         [pltpu.VMEM((2, 2 * size + 8, size), f32)],
         [spots, probe_field, own_amps, order],
     )
-    halos, rolled, ordered = lax.optimization_barrier((halos, rolled, ordered))
     near_runs = [shape((2, half, count * LANES), f32) for count in chunks(plan.own)]
     messages = call(
         lambda *refs: halo_message_kernel(plan, *refs),
@@ -628,6 +626,7 @@
             inner.append(inner_part)
             outer.append(outer_part)
             outer_far.append(plan.far_rows(outer_part))
+            token = info if sweep == 0 else token
         outer_near = [plan.near_rows(copy) for copy in copies]
         early = call(
             lambda *refs: early_sum_kernel(plan, slots, *refs),

time: 80.4 us -> 76.5 us (0.951); the launches traced: 79.1 us -> 76.2 us
  starting transfers between devices: 31 us -> 17.8 us
  waiting for transfers between devices: 24 us -> 36.6 us
  local copies, waits for them, and re-layouts: 4.77 us -> 2.69 us
    ppermute x3, waiting for transfers between devices: 8.37 us -> 23.4 us  [across(): return [lax.ppermute(values[0], axis_name, [(0, 1), (1, 0)])]]
    ppermute x22, starting transfers between devices: 26.9 us -> 15.5 us  [the longest x8 9.71 us: far_rows(): lax.ppermute(values, ('sx', 'sy'), pairs + [(j, i) for i, j in pairs])]
    ppermute x22, waiting for transfers between devices: 15.6 us -> 13.1 us  [the longest x8 11.3 us: far_rows(): lax.ppermute(values, ('sx', 'sy'), pairs + [(j, i) for i, j in pairs])]
    unnamed x18 -> x16, local copies, waits for them, and re-layouts: 4.77 us -> 2.69 us
    ppermute x3, starting transfers between devices: 4.11 us -> 2.26 us  [across(): return [lax.ppermute(values[0], axis_name, [(0, 1), (1, 0)])]]
  transfers between devices with their start and end apart: 25 -> 25, of which waited for: 9 -> 11; matrix products, arithmetic and copies ran while one was open for 0% -> 0% of each run, Pallas kernels for 15% -> 15%
where the time goes in v8:
time: 76.5 us; the launch traced here: 76.2 us
  waiting for transfers between devices  36.6 us (48%)
  Pallas kernels  18.9 us (25%)
  starting transfers between devices  17.8 us (23%)
  local copies, waits for them, and re-layouts  2.69 us (4%)
    ppermute x3, waiting for transfers between devices, across(): return [lax.ppermute(values[0], axis_name, [(0, 1), (1, 0)])]  23.4 us
    pallas_call x19, Pallas kernels, call(): pl.pallas_call(kernel, out_shape=outs, in_specs=in_specs or [SMEM if valu...  18.9 us
    ppermute x8, waiting for transfers between devices, far_rows(): lax.ppermute(values, ('sx', 'sy'), pairs + [(j, i) for i, j in pairs])  11.3 us
    ppermute x8, starting transfers between devices, far_rows(): lax.ppermute(values, ('sx', 'sy'), pairs + [(j, i) for i, j in pairs])  9.71 us
    ppermute x14, starting transfers between devices, near_rows(): return lax.ppermute(values, 'sx', [(i, i ^ 1) for i in range(self.sx_size)])  5.8 us
    unnamed x16, local copies, waits for them, and re-layouts  2.69 us
    ppermute x3, starting transfers between devices, across(): return [lax.ppermute(values[0], axis_name, [(0, 1), (1, 0)])]  2.26 us
    ppermute x14, waiting for transfers between devices, near_rows(): return lax.ppermute(values, 'sx', [(i, i ^ 1) for i in range(self.sx_size)])  1.83 us
  transfers between devices with their start and end apart: 25, of which 11 were waited for; matrix products, arithmetic and copies ran while one was open for 0% of the time, Pallas kernels for 15%

profile of v8, /device:TPU:0, one launch (start us, length us, event | category | flops | bytes accessed | tf_op | source)
XLA Modules:
  0.0 76.2 jit_solution(5073727224174235717)
XLA Ops:
  0.0 3.0 %collective-permute-start.3 = (f32[2,128,512]{2,1,0:T(8,128)}, f32[2,128,512]{2,1,0:T(8,128)S(1)}, u32[]{:S(2)}, u32[]{:S(2)}) collective-permute-start(f32[2,128,512]{2,1,0:T(8,128)} %refs_3_.3), channel_id=1, source_target_pairs={{2,4},{3,5},{6,8},{7,9},{10,12},{11,13},{14,16},{15,17},{18,20},{1... | collective-permute-start | bytes 1572872 | tf_op jit(solution)/shard_map/ppermute | solution.py:113
  3.0 0.7 copy-done.6
  3.7 1.0 %copy-done = f32[2,128,512]{2,1,0:T(8,128)S(1)} copy-done((f32[2,128,512]{2,1,0:T(8,128)S(1)}, f32[2,128,512]{2,1,0:T(8,128)}, u32[]{:S(2)}) %copy-start) | copy-done | bytes 524312
  4.7 0.6 shard_map.73
  5.4 7.9 %collective-permute-done.refs_3_ = f32[2,136,128]{2,1,0:T(8,128)S(1)} collective-permute-done((f32[2,136,128]{2,1,0:T(8,128)S(1)}, f32[2,136,128]{2,1,0:T(8,128)S(1)}, u32[]{:S(2)}, u32[]{:S(2)}) %collective-permute-start) | collective-permute-done | bytes 139296 | tf_op jit(solution)/shard_map/ppermute | solution.py:101
  14.5 2.0 %collective-permute-start.1 = (f32[2,144,128]{2,1,0:T(8,128)S(1)}, f32[2,144,128]{2,1,0:T(8,128)S(1)}, u32[]{:S(2)}, u32[]{:S(2)}) collective-permute-start(f32[2,144,128]{2,1,0:T(8,128)S(1)} %get-tuple-element.39.refs_0_.refs_3_.refs_5_.refs_4_), channel_id=1, source_target_pairs={{2,4},{3,5},{6,8},{7,9},{10,12},{11,13},{14,16},{15,17},{18,20},{1... | collective-permute-start | bytes 442376 | tf_op jit(solution)/shard_map/ppermute | solution.py:113
  16.5 0.9 %copy-done.5 = bf16[2,256,256]{2,1,0:T(8,128)(2,1)S(1)} copy-done((bf16[2,256,256]{2,1,0:T(8,128)(2,1)S(1)}, bf16[2,256,256]{2,1,0:T(8,128)(2,1)}, u32[]{:S(2)}) %copy-start.5) | copy-done | bytes 262168
  17.5 1.5 %shard_map.76 = (f32[2,2,256,256]{3,2,1,0:T(8,128)S(1)}, f32[2,256,256]{2,1,0:T(8,128)S(1)}) custom-call(s32[2,2]{1,0:T(2,128)S(1)} %bitcast.6, f32[2,256,256]{2,1,0:T(8,128)S(1)} %copy-done.3, f32[2,256,256]{2,1,0:T(8,128)S(1)} %bitcast.3, bf16[2,256,256]{2,1,0:T(8,128)(2,1)S(1)} %copy-done.5), custom_call_target="tpu_custom_call" | custom-call | flops 100000 | bytes 10000 | tf_op jit(solution)/shard_map/pallas_call | solution.py:527
  19.0 0.6 collective-permute-done.1.refs_1_.refs_5_
  19.7 2.6 %shard_map.77 = (f32[2,128,256]{2,1,0:T(8,128)S(1)}, f32[2,128,256]{2,1,0:T(8,128)S(1)}) custom-call(s32[2,2]{1,0:T(2,128)S(1)} %bitcast.7, s32[16]{0:T(128)S(1)} %bitcast.14, f32[2,128,512]{2,1,0:T(8,128)S(1)} %copy-done.1, f32[2,144,128]{2,1,0:T(8,128)S(1)} %get-tuple-element.39.refs_0_.refs_3_.refs_5_.refs_4_, ...), custom_call_target="tpu_custom_call" | custom-call | flops 100000 | bytes 10000 | tf_op jit(solution)/shard_map/pallas_call | solution.py:527
  22.3 2.1 %collective-permute-start.6 = (f32[2,128,256]{2,1,0:T(8,128)S(1)}, f32[2,128,256]{2,1,0:T(8,128)S(1)}, u32[]{:S(2)}, u32[]{:S(2)}) collective-permute-start(f32[2,128,256]{2,1,0:T(8,128)S(1)} %get-tuple-element.47.refs_9_), channel_id=1, source_target_pairs={{2,4},{3,5},{6,8},{7,9},{10,12},{11,13},{14,16},{15,17},{18,20},{1... | collective-permute-start | bytes 786440 | tf_op jit(solution)/shard_map/ppermute | solution.py:113
  24.4 2.4 %shard_map.75 = (f32[128,768]{1,0:T(8,128)S(1)}, s32[6,128]{1,0:T(8,128)S(1)}, f32[128,256]{1,0:T(8,128)S(1)}) custom-call(f32[2,144,128]{2,1,0:T(8,128)S(1)} %get-tuple-element.39.refs_0_.refs_3_.refs_5_.refs_4_, f32[2,144,128]{2,1,0:T(8,128)S(1)} %collective-permute-done.1.refs_1_.refs_5_, f32[2,144,128]{2,1,0:T(8,128)S(1)} %collective-permute-done.2.refs_2_.refs_6_, ...), custom_call_target="tpu_custom_call" | custom-call | flops 100000 | bytes 10000 | tf_op jit(solution)/shard_map/pallas_call | solution.py:527
  26.8 0.7 shard_map.78
  29.3 0.8 %shard_map.79.refs_1_ = f32[2,128,768]{2,1,0:T(8,128)S(1)} custom-call(s32[6,128]{1,0:T(8,128)S(1)} %get-tuple-element.41.refs_13_.refs_0_, f32[2,128,256]{2,1,0:T(8,128)S(1)} %get-tuple-element.46.refs_1_, f32[2,128,256]{2,1,0:T(8,128)S(1)} %get-tuple-element.48.refs_2_, f32[2,128,256]{2,1,0:T(8,128)S(1)} %collective-permute-done.6.refs_3_), custom_call_target="tpu_custom_call" | custom-call | flops 100000 | bytes 10000 | tf_op jit(solution)/shard_map/pallas_call | solution.py:527
  30.3 0.8 %shard_map.80.refs_1_ = f32[2,128,768]{2,1,0:T(8,128)S(1)} custom-call(s32[6,128]{1,0:T(8,128)S(1)} %get-tuple-element.41.refs_13_.refs_0_, f32[2,128,768]{2,1,0:T(8,128)S(1)} %shard_map.79.refs_1_, f32[1,128,256]{2,1,0:T(8,128)S(1)} %collective-permute-done.7.refs_2_, f32[1,128,256]{2,1,0:T(8,128)S(1)} %collective-permute-done.8.refs_3_, ...), custom_call_target="tpu_custom_call" | custom-call | flops 100000 | bytes 10000 | tf_op jit(solution)/shard_map/pallas_call | solution.py:527
  31.1 2.9 %collective-permute-done.11.refs_2_ = f32[2,128,256]{2,1,0:T(8,128)S(1)} collective-permute-done((f32[2,128,256]{2,1,0:T(8,128)S(1)}, f32[2,128,256]{2,1,0:T(8,128)S(1)}, u32[]{:S(2)}, u32[]{:S(2)}) %collective-permute-start.11) | collective-permute-done | bytes 262176 | tf_op jit(solution)/shard_map/ppermute | solution.py:113
  34.0 0.9 %shard_map.81 = (f32[2,128,384]{2,1,0:T(8,128)S(1)}, f32[2,128,768]{2,1,0:T(8,128)S(1)}) custom-call(s32[6,128]{1,0:T(8,128)S(1)} %get-tuple-element.41.refs_13_.refs_0_, f32[2,128,768]{2,1,0:T(8,128)S(1)} %shard_map.80.refs_1_, f32[2,128,256]{2,1,0:T(8,128)S(1)} %collective-permute-done.11.refs_2_, ...), custom_call_target="tpu_custom_call" | custom-call | flops 100000 | bytes 10000 | tf_op jit(solution)/shard_map/pallas_call | solution.py:527
  35.3 1.8 %collective-permute-start.12 = (f32[2,128,256]{2,1,0:T(8,128)S(1)}, f32[2,128,256]{2,1,0:T(8,128)S(1)}, u32[]{:S(2)}, u32[]{:S(2)}) collective-permute-start(f32[2,128,256]{2,1,0:T(8,128)S(1)} %get-tuple-element.57), channel_id=1, source_target_pairs={{0,1},{1,0},{2,3},{3,2},{4,5},{5,4},{6,7},{7,6},{8,9},{9,8},{10,11... | collective-permute-start | bytes 786440 | tf_op jit(solution)/shard_map/ppermute | solution.py:101
  37.1 11.2 %collective-permute-done.12.refs_2_ = f32[2,128,256]{2,1,0:T(8,128)S(1)} collective-permute-done((f32[2,128,256]{2,1,0:T(8,128)S(1)}, f32[2,128,256]{2,1,0:T(8,128)S(1)}, u32[]{:S(2)}, u32[]{:S(2)}) %collective-permute-start.12) | collective-permute-done | bytes 262176 | tf_op jit(solution)/shard_map/ppermute | solution.py:101
  49.1 1.5 %collective-permute-done.17.refs_8_ = f32[2,128,128]{2,1,0:T(8,128)S(1)} collective-permute-done((f32[2,128,128]{2,1,0:T(8,128)S(1)}, f32[2,128,128]{2,1,0:T(8,128)S(1)}, u32[]{:S(2)}, u32[]{:S(2)}) %collective-permute-start.17) | collective-permute-done | bytes 131104 | tf_op jit(solution)/shard_map/ppermute | solution.py:116
  50.6 4.2 %collective-permute-done.14.refs_5_ = f32[2,128,256]{2,1,0:T(8,128)S(1)} collective-permute-done((f32[2,128,256]{2,1,0:T(8,128)S(1)}, f32[2,128,256]{2,1,0:T(8,128)S(1)}, u32[]{:S(2)}, u32[]{:S(2)}) %collective-permute-start.14) | collective-permute-done | bytes 262176 | tf_op jit(solution)/shard_map/ppermute | solution.py:113
  54.8 2.6 %shard_map.85 = (f32[2,128,256]{2,1,0:T(8,128)S(1)}, f32[2,128,256]{2,1,0:T(8,128)S(1)}) custom-call(s32[2,2]{1,0:T(2,128)S(1)} %bitcast.10, s32[16]{0:T(128)S(1)} %bitcast.16, f32[2,128,384]{2,1,0:T(8,128)S(1)} %get-tuple-element.54.refs_2_.refs_0_.refs_5_, f32[2,128,256]{2,1,0:T(8,128)S(1)} %get-tuple-element.59.refs_3_.refs_6_, ...), custom_call_target="tpu_custom_call" | custom-call | flops 100000 | bytes 10000 | tf_op jit(solution)/shard_map/pallas_call | solution.py:527
  57.5 0.7 shard_map.86
  58.2 2.1 %collective-permute-start.23 = (f32[2,128,256]{2,1,0:T(8,128)S(1)}, f32[2,128,256]{2,1,0:T(8,128)S(1)}, u32[]{:S(2)}, u32[]{:S(2)}) collective-permute-start(f32[2,128,256]{2,1,0:T(8,128)S(1)} %get-tuple-element.70), channel_id=1, source_target_pairs={{2,4},{3,5},{6,8},{7,9},{10,12},{11,13},{14,16},{15,17},{18,20},{1... | collective-permute-start | bytes 786440 | tf_op jit(solution)/shard_map/ppermute | solution.py:113
  60.7 3.1 %collective-permute-done.18.refs_3_ = f32[2,128,256]{2,1,0:T(8,128)S(1)} collective-permute-done((f32[2,128,256]{2,1,0:T(8,128)S(1)}, f32[2,128,256]{2,1,0:T(8,128)S(1)}, u32[]{:S(2)}, u32[]{:S(2)}) %collective-permute-start.18) | collective-permute-done | bytes 262176 | tf_op jit(solution)/shard_map/ppermute | solution.py:113
  63.9 2.9 %collective-permute-start.22 = (f32[1,128,256]{2,1,0:T(8,128)S(1)}, f32[1,128,256]{2,1,0:T(8,128)S(1)}, u32[]{:S(2)}, u32[]{:S(2)}) collective-permute-start(f32[1,128,256]{2,1,0:T(8,128)S(1)} %get-tuple-element.69), channel_id=1, source_target_pairs={{0,2},{2,0},{4,6},{6,4},{8,10},{10,8},{12,14},{14,12},{16,18},{18,... | collective-permute-start | bytes 393224 | tf_op jit(solution)/shard_map/ppermute | solution.py:116
  66.7 0.8 %shard_map.87.refs_1_ = f32[2,128,768]{2,1,0:T(8,128)S(1)} custom-call(s32[6,128]{1,0:T(8,128)S(1)} %get-tuple-element.41.refs_13_.refs_0_, f32[2,128,256]{2,1,0:T(8,128)S(1)} %get-tuple-element.63.refs_1_, f32[2,128,256]{2,1,0:T(8,128)S(1)} %get-tuple-element.65.refs_2_, f32[2,128,256]{2,1,0:T(8,128)S(1)} %collective-permute-done.18.refs_3_), custom_call_target="tpu_custom_call" | custom-call | flops 100000 | bytes 10000 | tf_op jit(solution)/shard_map/pallas_call | solution.py:527
  67.7 0.8 %shard_map.88.refs_1_ = f32[2,128,768]{2,1,0:T(8,128)S(1)} custom-call(s32[6,128]{1,0:T(8,128)S(1)} %get-tuple-element.41.refs_13_.refs_0_, f32[2,128,768]{2,1,0:T(8,128)S(1)} %shard_map.87.refs_1_, f32[1,128,256]{2,1,0:T(8,128)S(1)} %collective-permute-done.19.refs_2_, f32[1,128,256]{2,1,0:T(8,128)S(1)} %collective-permute-done.20.refs_3_, ...), custom_call_target="tpu_custom_call" | custom-call | flops 100000 | bytes 10000 | tf_op jit(solution)/shard_map/pallas_call | solution.py:527
  68.5 0.6 shard_map.89.refs_4_
  69.5 1.7 %shard_map.90 = (f32[2,128,512]{2,1,0:T(8,128)}, f32[2,128,128]{2,1,0:T(8,128)S(1)}) custom-call(s32[6,128]{1,0:T(8,128)S(1)} %get-tuple-element.41.refs_13_.refs_0_, f32[2,128,768]{2,1,0:T(8,128)S(1)} %shard_map.88.refs_1_, f32[2,128,256]{2,1,0:T(8,128)S(1)} %collective-permute-done.23.refs_2_, f32[128,768]{1,0:T(8,128)S(1)} %get-tuple-element.40.refs_3_.refs_1_.refs_0_, ...), custom_call_target="tpu_custom_call" | custom-call | flops 100000 | bytes 10000 | tf_op jit(solution)/shard_map/pallas_call | solution.py:527
  71.2 4.3 %collective-permute-done.24.refs_2_ = f32[2,128,128]{2,1,0:T(8,128)S(1)} collective-permute-done((f32[2,128,128]{2,1,0:T(8,128)S(1)}, f32[2,128,128]{2,1,0:T(8,128)S(1)}, u32[]{:S(2)}, u32[]{:S(2)}) %collective-permute-start.24) | collective-permute-done | bytes 131104 | tf_op jit(solution)/shard_map/ppermute | solution.py:101
  75.5 0.7 shard_map.91
  (53 shorter events, 5.5 us)
Async XLA Ops:
  0.0 19.7 %collective-permute-start.3 = (f32[2,128,512]{2,1,0:T(8,128)}, f32[2,128,512]{2,1,0:T(8,128)S(1)}, u32[]{:S(2)}, u32[]{:S(2)}) collective-permute-start(f32[2,128,512]{2,1,0:T(8,128)} %refs_3_.3), channel_id=1, source_target_pairs={{2,4},{3,5},{6,8},{7,9},{10,12},{11,13},{14,16},{15,17},{18,20},{1... | collective-permute-start | bytes 1572872 | tf_op jit(solution)/shard_map/ppermute | solution.py:113
  3.0 0.7 copy-start.7
  3.6 1.0 %copy-start = (f32[2,128,512]{2,1,0:T(8,128)S(1)}, f32[2,128,512]{2,1,0:T(8,128)}, u32[]{:S(2)}) copy-start(f32[2,128,512]{2,1,0:T(8,128)} %refs_3_.3) | copy-start | bytes 1572868
  4.7 11.8 %copy-start.3 = (f32[2,256,256]{2,1,0:T(8,128)S(1)}, f32[2,256,256]{2,1,0:T(8,128)}, u32[]{:S(2)}) copy-start(f32[2,256,256]{2,1,0:T(8,128)} %probe.1) | copy-start | bytes 1572868
  4.7 11.8 %copy-start.4 = (f32[1,1,2,256,256]{4,3,2,1,0:T(8,128)S(1)}, f32[1,1,2,256,256]{4,3,2,1,0:T(8,128)}, u32[]{:S(2)}) copy-start(f32[1,1,2,256,256]{4,3,2,1,0:T(8,128)} %param.9) | copy-start | bytes 1572868
  5.3 14.4 %copy-start.2 = (bf16[2,2,2,256,256]{4,3,2,1,0:T(8,128)(2,1)S(1)}, bf16[2,2,2,256,256]{4,3,2,1,0:T(8,128)(2,1)}, u32[]{:S(2)}) copy-start(bf16[2,2,2,256,256]{4,3,2,1,0:T(8,128)(2,1)} %constant.4.clone.refs_11_.refs_12_) | copy-start | bytes 3145732
  5.3 8.0 %collective-permute-start = (f32[2,136,128]{2,1,0:T(8,128)S(1)}, f32[2,136,128]{2,1,0:T(8,128)S(1)}, u32[]{:S(2)}, u32[]{:S(2)}) collective-permute-start(f32[2,136,128]{2,1,0:T(8,128)S(1)} %shard_map.73), channel_id=1, source_target_pairs={{0,1},{1,0},{2,3},{3,2},{4,5},{5,4},{6,7},{7,6},{8,9},{9,8},{10,11... | collective-permute-start | bytes 417800 | tf_op jit(solution)/shard_map/ppermute | solution.py:101
  13.9 5.7 %collective-permute-start.4 = (f32[2,128,256]{2,1,0:T(8,128)S(1)}, f32[2,128,256]{2,1,0:T(8,128)S(1)}, u32[]{:S(2)}, u32[]{:S(2)}) collective-permute-start(f32[2,128,256]{2,1,0:T(8,128)S(1)} %get-tuple-element.42), channel_id=1, source_target_pairs={{0,2},{2,0},{4,6},{6,4},{8,10},{10,8},{12,14},{14,12},{16,18},{18,... | collective-permute-start | bytes 786440 | tf_op jit(solution)/shard_map/ppermute | solution.py:116
  14.0 5.7 %collective-permute-start.5 = (f32[2,128,256]{2,1,0:T(8,128)S(1)}, f32[2,128,256]{2,1,0:T(8,128)S(1)}, u32[]{:S(2)}, u32[]{:S(2)}) collective-permute-start(f32[2,128,256]{2,1,0:T(8,128)S(1)} %get-tuple-element.43), channel_id=1, source_target_pairs={{0,2},{2,0},{4,6},{6,4},{8,10},{10,8},{12,14},{14,12},{16,18},{18,... | collective-permute-start | bytes 786440 | tf_op jit(solution)/shard_map/ppermute | solution.py:116
  14.5 5.1 %collective-permute-start.1 = (f32[2,144,128]{2,1,0:T(8,128)S(1)}, f32[2,144,128]{2,1,0:T(8,128)S(1)}, u32[]{:S(2)}, u32[]{:S(2)}) collective-permute-start(f32[2,144,128]{2,1,0:T(8,128)S(1)} %get-tuple-element.39.refs_0_.refs_3_.refs_5_.refs_4_), channel_id=1, source_target_pairs={{2,4},{3,5},{6,8},{7,9},{10,12},{11,13},{14,16},{15,17},{18,20},{1... | collective-permute-start | bytes 442376 | tf_op jit(solution)/shard_map/ppermute | solution.py:113
  16.5 3.1 %collective-permute-start.2 = (f32[2,144,128]{2,1,0:T(8,128)S(1)}, f32[2,144,128]{2,1,0:T(8,128)S(1)}, u32[]{:S(2)}, u32[]{:S(2)}) collective-permute-start(f32[2,144,128]{2,1,0:T(8,128)S(1)} %get-tuple-element.39.refs_0_.refs_3_.refs_5_.refs_4_), channel_id=1, source_target_pairs={{0,2},{2,0},{4,6},{6,4},{8,10},{10,8},{12,14},{14,12},{16,18},{18,... | collective-permute-start | bytes 442376 | tf_op jit(solution)/shard_map/ppermute | solution.py:116
  16.5 1.0 %copy-start.5 = (bf16[2,256,256]{2,1,0:T(8,128)(2,1)S(1)}, bf16[2,256,256]{2,1,0:T(8,128)(2,1)}, u32[]{:S(2)}) copy-start(bf16[2,256,256]{2,1,0:T(8,128)(2,1)} %constant.5.clone.order) | copy-start | bytes 786436
  17.5 2.2 %copy-start.1 = (f32[2,128,512]{2,1,0:T(8,128)S(1)}, f32[2,128,512]{2,1,0:T(8,128)}, u32[]{:S(2)}) copy-start(f32[2,128,512]{2,1,0:T(8,128)} %refs_3_.3) | copy-start | bytes 1572868
  22.3 6.5 %collective-permute-start.6 = (f32[2,128,256]{2,1,0:T(8,128)S(1)}, f32[2,128,256]{2,1,0:T(8,128)S(1)}, u32[]{:S(2)}, u32[]{:S(2)}) collective-permute-start(f32[2,128,256]{2,1,0:T(8,128)S(1)} %get-tuple-element.47.refs_9_), channel_id=1, source_target_pairs={{2,4},{3,5},{6,8},{7,9},{10,12},{11,13},{14,16},{15,17},{18,20},{1... | collective-permute-start | bytes 786440 | tf_op jit(solution)/shard_map/ppermute | solution.py:113
  27.6 6.4 %collective-permute-start.11 = (f32[2,128,256]{2,1,0:T(8,128)S(1)}, f32[2,128,256]{2,1,0:T(8,128)S(1)}, u32[]{:S(2)}, u32[]{:S(2)}) collective-permute-start(f32[2,128,256]{2,1,0:T(8,128)S(1)} %get-tuple-element.53), channel_id=1, source_target_pairs={{2,4},{3,5},{6,8},{7,9},{10,12},{11,13},{14,16},{15,17},{18,20},{1... | collective-permute-start | bytes 786440 | tf_op jit(solution)/shard_map/ppermute | solution.py:113
  27.7 2.5 %collective-permute-start.7 = (f32[1,128,256]{2,1,0:T(8,128)S(1)}, f32[1,128,256]{2,1,0:T(8,128)S(1)}, u32[]{:S(2)}, u32[]{:S(2)}) collective-permute-start(f32[1,128,256]{2,1,0:T(8,128)S(1)} %get-tuple-element.49), channel_id=1, source_target_pairs={{0,2},{2,0},{4,6},{6,4},{8,10},{10,8},{12,14},{14,12},{16,18},{18,... | collective-permute-start | bytes 393224 | tf_op jit(solution)/shard_map/ppermute | solution.py:116
  27.7 2.4 %collective-permute-start.8 = (f32[1,128,256]{2,1,0:T(8,128)S(1)}, f32[1,128,256]{2,1,0:T(8,128)S(1)}, u32[]{:S(2)}, u32[]{:S(2)}) collective-permute-start(f32[1,128,256]{2,1,0:T(8,128)S(1)} %get-tuple-element.50), channel_id=1, source_target_pairs={{0,2},{2,0},{4,6},{6,4},{8,10},{10,8},{12,14},{14,12},{16,18},{18,... | collective-permute-start | bytes 393224 | tf_op jit(solution)/shard_map/ppermute | solution.py:116
  28.2 1.9 %collective-permute-start.9 = (f32[1,128,256]{2,1,0:T(8,128)S(1)}, f32[1,128,256]{2,1,0:T(8,128)S(1)}, u32[]{:S(2)}, u32[]{:S(2)}) collective-permute-start(f32[1,128,256]{2,1,0:T(8,128)S(1)} %get-tuple-element.51), channel_id=1, source_target_pairs={{0,2},{2,0},{4,6},{6,4},{8,10},{10,8},{12,14},{14,12},{16,18},{18,... | collective-permute-start | bytes 393224 | tf_op jit(solution)/shard_map/ppermute | solution.py:116
  28.8 1.5 %collective-permute-start.10 = (f32[1,128,256]{2,1,0:T(8,128)S(1)}, f32[1,128,256]{2,1,0:T(8,128)S(1)}, u32[]{:S(2)}, u32[]{:S(2)}) collective-permute-start(f32[1,128,256]{2,1,0:T(8,128)S(1)} %get-tuple-element.52), channel_id=1, source_target_pairs={{0,2},{2,0},{4,6},{6,4},{8,10},{10,8},{12,14},{14,12},{16,18},{18,... | collective-permute-start | bytes 393224 | tf_op jit(solution)/shard_map/ppermute | solution.py:116
  34.9 14.3 %collective-permute-start.13 = (f32[2,128,384]{2,1,0:T(8,128)S(1)}, f32[2,128,384]{2,1,0:T(8,128)S(1)}, u32[]{:S(2)}, u32[]{:S(2)}) collective-permute-start(f32[2,128,384]{2,1,0:T(8,128)S(1)} %get-tuple-element.54.refs_2_.refs_0_.refs_5_), channel_id=1, source_target_pairs={{2,4},{3,5},{6,8},{7,9},{10,12},{11,13},{14,16},{15,17},{18,20},{1... | collective-permute-start | bytes 1179656 | tf_op jit(solution)/shard_map/ppermute | solution.py:113
  35.3 13.0 %collective-permute-start.12 = (f32[2,128,256]{2,1,0:T(8,128)S(1)}, f32[2,128,256]{2,1,0:T(8,128)S(1)}, u32[]{:S(2)}, u32[]{:S(2)}) collective-permute-start(f32[2,128,256]{2,1,0:T(8,128)S(1)} %get-tuple-element.57), channel_id=1, source_target_pairs={{0,1},{1,0},{2,3},{3,2},{4,5},{5,4},{6,7},{7,6},{8,9},{9,8},{10,11... | collective-permute-start | bytes 786440 | tf_op jit(solution)/shard_map/ppermute | solution.py:101
  48.4 6.4 %collective-permute-start.14 = (f32[2,128,256]{2,1,0:T(8,128)S(1)}, f32[2,128,256]{2,1,0:T(8,128)S(1)}, u32[]{:S(2)}, u32[]{:S(2)}) collective-permute-start(f32[2,128,256]{2,1,0:T(8,128)S(1)} %get-tuple-element.59.refs_3_.refs_6_), channel_id=1, source_target_pairs={{2,4},{3,5},{6,8},{7,9},{10,12},{11,13},{14,16},{15,17},{18,20},{1... | collective-permute-start | bytes 786440 | tf_op jit(solution)/shard_map/ppermute | solution.py:113
  48.5 6.4 %collective-permute-start.15 = (f32[2,128,256]{2,1,0:T(8,128)S(1)}, f32[2,128,256]{2,1,0:T(8,128)S(1)}, u32[]{:S(2)}, u32[]{:S(2)}) collective-permute-start(f32[2,128,256]{2,1,0:T(8,128)S(1)} %get-tuple-element.60), channel_id=1, source_target_pairs={{0,2},{2,0},{4,6},{6,4},{8,10},{10,8},{12,14},{14,12},{16,18},{18,... | collective-permute-start | bytes 786440 | tf_op jit(solution)/shard_map/ppermute | solution.py:116
  48.6 6.3 %collective-permute-start.16 = (f32[2,128,256]{2,1,0:T(8,128)S(1)}, f32[2,128,256]{2,1,0:T(8,128)S(1)}, u32[]{:S(2)}, u32[]{:S(2)}) collective-permute-start(f32[2,128,256]{2,1,0:T(8,128)S(1)} %get-tuple-element.61), channel_id=1, source_target_pairs={{0,2},{2,0},{4,6},{6,4},{8,10},{10,8},{12,14},{14,12},{16,18},{18,... | collective-permute-start | bytes 786440 | tf_op jit(solution)/shard_map/ppermute | solution.py:116
  49.0 1.6 %collective-permute-start.17 = (f32[2,128,128]{2,1,0:T(8,128)S(1)}, f32[2,128,128]{2,1,0:T(8,128)S(1)}, u32[]{:S(2)}, u32[]{:S(2)}) collective-permute-start(f32[2,128,128]{2,1,0:T(8,128)S(1)} %get-tuple-element.62), channel_id=1, source_target_pairs={{0,2},{2,0},{4,6},{6,4},{8,10},{10,8},{12,14},{14,12},{16,18},{18,... | collective-permute-start | bytes 393224 | tf_op jit(solution)/shard_map/ppermute | solution.py:116
  57.4 6.4 %collective-permute-start.18 = (f32[2,128,256]{2,1,0:T(8,128)S(1)}, f32[2,128,256]{2,1,0:T(8,128)S(1)}, u32[]{:S(2)}, u32[]{:S(2)}) collective-permute-start(f32[2,128,256]{2,1,0:T(8,128)S(1)} %get-tuple-element.64.refs_9_), channel_id=1, source_target_pairs={{2,4},{3,5},{6,8},{7,9},{10,12},{11,13},{14,16},{15,17},{18,20},{1... | collective-permute-start | bytes 786440 | tf_op jit(solution)/shard_map/ppermute | solution.py:113
  58.2 10.3 %collective-permute-start.23 = (f32[2,128,256]{2,1,0:T(8,128)S(1)}, f32[2,128,256]{2,1,0:T(8,128)S(1)}, u32[]{:S(2)}, u32[]{:S(2)}) collective-permute-start(f32[2,128,256]{2,1,0:T(8,128)S(1)} %get-tuple-element.70), channel_id=1, source_target_pairs={{2,4},{3,5},{6,8},{7,9},{10,12},{11,13},{14,16},{15,17},{18,20},{1... | collective-permute-start | bytes 786440 | tf_op jit(solution)/shard_map/ppermute | solution.py:113
  60.2 7.3 %collective-permute-start.19 = (f32[1,128,256]{2,1,0:T(8,128)S(1)}, f32[1,128,256]{2,1,0:T(8,128)S(1)}, u32[]{:S(2)}, u32[]{:S(2)}) collective-permute-start(f32[1,128,256]{2,1,0:T(8,128)S(1)} %get-tuple-element.66), channel_id=1, source_target_pairs={{0,2},{2,0},{4,6},{6,4},{8,10},{10,8},{12,14},{14,12},{16,18},{18,... | collective-permute-start | bytes 393224 | tf_op jit(solution)/shard_map/ppermute | solution.py:116
  60.2 7.3 %collective-permute-start.20 = (f32[1,128,256]{2,1,0:T(8,128)S(1)}, f32[1,128,256]{2,1,0:T(8,128)S(1)}, u32[]{:S(2)}, u32[]{:S(2)}) collective-permute-start(f32[1,128,256]{2,1,0:T(8,128)S(1)} %get-tuple-element.67), channel_id=1, source_target_pairs={{0,2},{2,0},{4,6},{6,4},{8,10},{10,8},{12,14},{14,12},{16,18},{18,... | collective-permute-start | bytes 393224 | tf_op jit(solution)/shard_map/ppermute | solution.py:116
  60.7 6.8 %collective-permute-start.21 = (f32[1,128,256]{2,1,0:T(8,128)S(1)}, f32[1,128,256]{2,1,0:T(8,128)S(1)}, u32[]{:S(2)}, u32[]{:S(2)}) collective-permute-start(f32[1,128,256]{2,1,0:T(8,128)S(1)} %get-tuple-element.68), channel_id=1, source_target_pairs={{0,2},{2,0},{4,6},{6,4},{8,10},{10,8},{12,14},{14,12},{16,18},{18,... | collective-permute-start | bytes 393224 | tf_op jit(solution)/shard_map/ppermute | solution.py:116
  63.9 3.9 %collective-permute-start.22 = (f32[1,128,256]{2,1,0:T(8,128)S(1)}, f32[1,128,256]{2,1,0:T(8,128)S(1)}, u32[]{:S(2)}, u32[]{:S(2)}) collective-permute-start(f32[1,128,256]{2,1,0:T(8,128)S(1)} %get-tuple-element.69), channel_id=1, source_target_pairs={{0,2},{2,0},{4,6},{6,4},{8,10},{10,8},{12,14},{14,12},{16,18},{18,... | collective-permute-start | bytes 393224 | tf_op jit(solution)/shard_map/ppermute | solution.py:116
  69.2 6.4 %collective-permute-start.24 = (f32[2,128,128]{2,1,0:T(8,128)S(1)}, f32[2,128,128]{2,1,0:T(8,128)S(1)}, u32[]{:S(2)}, u32[]{:S(2)}) collective-permute-start(f32[2,128,128]{2,1,0:T(8,128)S(1)} %shard_map.89.refs_4_), channel_id=1, source_target_pairs={{0,1},{1,0},{2,3},{3,2},{4,5},{5,4},{6,7},{7,6},{8,9},{9,8},{10,11... | collective-permute-start | bytes 393224 | tf_op jit(solution)/shard_map/ppermute | solution.py:101
  (1 other events, 0.7 us)

commit v9 on v8

--- a/solution.py
+++ b/solution.py
@@ -256,16 +256,12 @@
         )
 
 
-def light_kernel(plan, slots, *rest):
+def info_kernel(plan, *rest):
     groups = [rest[k * plan.sides : (k + 1) * plan.sides] for k in range(3)]
-    probe, inverse, info = rest[3 * plan.sides : 3 * plan.sides + 3]
-    pairs = rest[3 * plan.sides + 3 : 4 * plan.sides + 3]
-    padded, canvas, known, sem = rest[4 * plan.sides + 3 :]
-    size = probe.shape[1]
-    half = size // 2
-    s, t = here()
+    info, known, sem = rest[3 * plan.sides :]
+    s, _ = here()
     upper = s % 2 == 0
-    height = half
+    height = groups[0][0].shape[1] - 16
 
     def lines(messages):
         return [messages[0][0, height + 8 : height + 16]] + [message[0, height : height + 8] for message in messages]
@@ -277,11 +273,18 @@
             known[kind * (plan.sides + 1) + turn] = line.astype(jnp.int32)
     copy = pltpu.make_async_copy(known.at[:, 0], info, sem)
     copy.start()
+    copy.wait()
+
+
+def light_kernel(plan, slots, info, probe, _, inverse, *rest):
+    pairs, (padded, canvas) = rest[: plan.sides], rest[plan.sides :]
+    size = probe.shape[1]
+    half = size // 2
+    _, t = here()
     padded[:half] = jnp.zeros((half, size), jnp.float32)
     padded[half + size :] = jnp.zeros((half + 8, size), jnp.float32)
     padded[half : half + size] = probe[0] * probe[0] + probe[1] * probe[1]
     canvas[...] = jnp.zeros(canvas.shape, jnp.float32)
-    copy.wait()
     reach = plan.sides + 1
     spare = jnp.zeros((half, LANES), jnp.float32)
     for down in (-1, 0, 1):
@@ -427,13 +430,13 @@
             for step, values in enumerate(self.tiles(part)):
                 canvas[part, :, lanes(self.tile + step)] += values
 
-    def add_tile_to(self, total, tile):
+    def tiles_at(self, tile, act):
         for step in range(3):
 
             @pl.when(self.tile + step == tile)
             def _(step=step):
                 for part in range(2):
-                    total[part] += self.tiles(part)[step]
+                    act(part, self.tiles(part)[step])
 
 
 def early_sum_kernel(plan, slots, info, *rest):
@@ -446,12 +449,16 @@
         Patch(plan, info, s, far[slot], slot, far_side(s), True).add_to(canvas)
 
 
-def near_sum_kernel(plan, slots, info, early, *rest):
-    near, canvas = rest[: 2 * slots], rest[2 * slots]
-    s, _ = here()
+def base_kernel(plan, slots, layout, pieces, info, early, inverse, *rest):
+    near, refs, (canvas, base) = rest[: 2 * slots], rest[2 * slots : 2 * slots + pieces], rest[2 * slots + pieces :]
+    s, t = here()
     canvas[...] = early[...]
     for slot in range(slots):
         Patch(plan, info, s, near[2 * slot : 2 * slot + 2], slot, -far_side(s)).add_to(canvas)
+    for tile in range(plan.tiles):
+        where = lanes(tile)
+        pick_tile(plan, base.at[:, :, where], layout(refs, t)[0], tile, t)
+        base[:, :, where] -= canvas[:, :, where] * inverse[:, where][None]
 
 
 def last_patch(plan, slots, info, patch):
@@ -459,28 +466,36 @@
     return Patch(plan, info, s, patch, slots - 1, far_side(s), True)
 
 
-def middle_kernel(plan, slots, layout, pieces, info, early, patch, inverse, *rest):
-    refs, (middle, canvas) = rest[:pieces], rest[pieces:]
+def take_off(last, target, base, inverse, tile):
+    target[...] = base[:, :, lanes(tile)]
+
+    def act(part, values):
+        target[part] -= values * inverse[:, lanes(tile)]
+
+    last.tiles_at(tile, act)
+
+
+def middle_kernel(plan, slots, info, base, patch, inverse, middle):
     _, t = here()
-    canvas[...] = early[...]
-    last_patch(plan, slots, info, patch).add_to(canvas)
+    last = last_patch(plan, slots, info, patch)
     for step in range(plan.mid_tiles):
-        tile = plan.mid_start(t) + step
-        where = lanes(step)
-        pick_tile(plan, middle.at[:, :, where], layout(refs, t)[0], tile, t)
-        middle[:, :, where] -= canvas[:, :, lanes(tile)] * inverse[:, lanes(tile)][None]
-
-
-def boundary_kernel(plan, layout, pieces, canvas, inverse, _, *rest):
-    refs, outs = rest[:pieces], rest[pieces:]
+        take_off(last, middle.at[:, :, lanes(step)], base, inverse, plan.mid_start(t) + step)
+
+
+def boundary_kernel(plan, slots, info, early, base, patch, inverse, _, *outs):
     bases, sums = outs[: plan.sides], outs[plan.sides :]
     _, t = here()
-    for base, total, start in zip(bases, sums, plan.pair_starts(t)):
-        total[...] = canvas[:, :, lanes(start, 2)]
+    last = last_patch(plan, slots, info, patch)
+    for pair, total, start in zip(bases, sums, plan.pair_starts(t)):
+        total[...] = early[:, :, lanes(start, 2)]
         for step in range(2):
-            where = lanes(step)
-            pick_tile(plan, base.at[:, :, where], layout(refs, t)[0], start + step, t)
-            base[:, :, where] -= total[:, :, where] * inverse[:, lanes(start + step)][None]
+            part_sum = total.at[:, :, lanes(step)]
+
+            def act(part, values, part_sum=part_sum):
+                part_sum[part] += values
+
+            last.tiles_at(start + step, act)
+            take_off(last, pair.at[:, :, lanes(step)], base, inverse, start + step)
 
 
 def halo_sum_kernel(plan, slots, info, early, patch, *sums):
@@ -488,26 +503,27 @@
     last = last_patch(plan, slots, info, patch)
     for total, tile in zip(sums, plan.halo_tiles(t)):
         total[...] = early[:, :, lanes(tile)]
-        last.add_tile_to(total, tile)
-
-
-def last_kernel(plan, slots, layout, pieces, info, early, patch, inverse, _, *rest):
-    refs, rest = rest[:pieces], rest[pieces:]
-    nearly, bases = rest[0], rest[1 : 1 + plan.sides]
-    current, canvas, sem = rest[1 + plan.sides :]
+
+        def act(part, values, total=total):
+            total[part] += values
+
+        last.tiles_at(tile, act)
+
+
+def last_kernel(plan, slots, info, base, patch, inverse, _, *rest):
+    nearly, bases, (current, sems) = rest[0], rest[1 : 1 + plan.sides], rest[1 + plan.sides :]
     _, t = here()
-    canvas[...] = early[...]
-    last_patch(plan, slots, info, patch).add_to(canvas)
+    last = last_patch(plan, slots, info, patch)
+    copies = []
     for step in range(plan.own):
-        tile = 1 + step
         where = lanes(step)
-        pick_tile(plan, current.at[:, :, where], layout(refs, t)[0], tile, t)
-        current[:, :, where] -= canvas[:, :, lanes(tile)] * inverse[:, lanes(tile)][None]
-    copy = pltpu.make_async_copy(current, nearly, sem)
-    copy.start()
-    for base, tile in zip(bases, plan.edge_tiles(t)):
-        base[...] = current[:, :, lanes(tile - 1)]
-    copy.wait()
+        take_off(last, current.at[:, :, where], base, inverse, 1 + step)
+        copies.append(pltpu.make_async_copy(current.at[:, :, where], nearly.at[:, :, where], sems.at[step]))
+        copies[-1].start()
+    for edge, tile in zip(bases, plan.edge_tiles(t)):
+        edge[...] = current[:, :, lanes(tile - 1)]
+    for copy in copies:
+        copy.wait()
 
 
 def edge_kernel(plan, inverse, *rest):
@@ -581,17 +597,12 @@
     far = [far_block] + [plan.far_rows(message) for message in passed]
     near = [plan.near_rows(piece) for piece in messages]
     own = [object_field] + passed
-    inverse, info, *inverse_pairs = call(
-        lambda *refs: light_kernel(plan, slots, *refs),
-        [shape((half, width), f32), shape((3 * (sides + 1), LANES), jnp.int32)] + [shape((half, 2 * LANES), f32)] * sides,
-        [
-            pltpu.VMEM((2 * size + 8, size), f32),
-            pltpu.VMEM((half, width + 2 * plan.own * LANES), f32),
-            pltpu.VMEM((3 * (sides + 1), 8, LANES), jnp.int32),
-            dma,
-        ],
-        passed + far[1:] + near[:sides] + [probe_field],
-        out_specs=[VMEM, SMEM] + [VMEM] * sides,
+    info = call(
+        lambda *refs: info_kernel(plan, *refs),
+        shape((3 * (sides + 1), LANES), jnp.int32),
+        [pltpu.VMEM((3 * (sides + 1), 8, LANES), jnp.int32), dma],
+        passed + far[1:] + near[:sides],
+        out_specs=SMEM,
     )
 
     def runs_layout(refs, main, count, side_starts):
@@ -634,26 +645,37 @@
             [],
             [info, *inner, *outer_far[:-1]],
         )
-        early = call(
-            lambda *refs: near_sum_kernel(plan, slots, *refs),
-            shape((2, half, width), f32),
+        if sweep == 0:
+            inverse, *inverse_pairs = call(
+                lambda *refs: light_kernel(plan, slots, *refs),
+                [shape((half, width), f32)] + [shape((half, 2 * LANES), f32)] * sides,
+                [
+                    pltpu.VMEM((2 * size + 8, size), f32),
+                    pltpu.VMEM((half, width + 2 * plan.own * LANES), f32),
+                ],
+                [info, probe_field, early],
+                in_specs=[SMEM, VMEM, ANY],
+            )
+        early, base = call(
+            lambda *refs, layout=layout: base_kernel(plan, slots, layout, len(pieces), *refs),
+            [shape((2, half, width), f32)] * 2,
             [],
-            [info, early, *outer_near],
+            [info, early, inverse, *outer_near, *pieces],
         )
         if sweep < ITERS - 1:
-            middle, total = call(
-                lambda *refs, layout=layout: middle_kernel(plan, slots, layout, len(own), *refs),
-                [shape((2, half, plan.mid_tiles * LANES), f32), shape((2, half, width), f32)],
+            middle = call(
+                lambda *refs: middle_kernel(plan, slots, *refs),
+                shape((2, half, plan.mid_tiles * LANES), f32),
                 [],
-                [info, early, outer_far[-1], inverse, *own],
+                [info, base, outer_far[-1], inverse],
             )
             far_middle = plan.far_rows(middle)
             boundary = call(
-                lambda *refs, layout=layout: boundary_kernel(plan, layout, len(own), *refs),
+                lambda *refs: boundary_kernel(plan, slots, *refs),
                 [shape((2, half, 2 * LANES), f32)] * (2 * sides),
                 [],
-                [total, inverse, middle, *own],
-                in_specs=[VMEM, VMEM, ANY] + [VMEM] * len(own),
+                [info, early, base, outer_far[-1], inverse, middle],
+                in_specs=[SMEM] + [VMEM] * 4 + [ANY],
             )
             bases, sums = boundary[:sides], boundary[sides:]
             received = plan.across(sums)
@@ -684,11 +706,11 @@
         [info, early, outer_far[-1]],
     )
     nearly, *bases = call(
-        lambda *refs: last_kernel(plan, slots, layout, len(own), *refs),
+        lambda *refs: last_kernel(plan, slots, *refs),
         [shape((2, half, block_cols), f32)] + [shape((2, half, LANES), f32)] * sides,
-        [pltpu.VMEM((2, half, block_cols), f32), pltpu.VMEM((2, half, width), f32), dma],
-        [info, early, outer_far[-1], inverse, sums[0], *own],
-        in_specs=[SMEM, VMEM, VMEM, VMEM, ANY] + [VMEM] * len(own),
+        [pltpu.VMEM((2, half, block_cols), f32), dma((plan.own,))],
+        [info, base, outer_far[-1], inverse, sums[0]],
+        in_specs=[SMEM, VMEM, VMEM, VMEM, ANY],
         out_specs=[HBM] + [VMEM] * sides,
     )
     received = plan.across(sums)

time: 76.5 us -> 79.5 us (1.039)
  the two profiles are of different devices: /device:TPU:0 before, /device:TPU:10 now
where the time goes in v9:
time: 79.5 us; the launch traced here: 79.2 us
  waiting for transfers between devices  36.1 us (45%)
  Pallas kernels  25.5 us (32%)
  starting transfers between devices  14.6 us (18%)
  local copies, waits for them, and re-layouts  2.69 us (3%)
    pallas_call x20, Pallas kernels, call(): pl.pallas_call(kernel, out_shape=outs, in_specs=in_specs or [SMEM if valu...  25.5 us
    ppermute x8, waiting for transfers between devices, far_rows(): lax.ppermute(values, ('sx', 'sy'), pairs + [(j, i) for i, j in pairs])  20.3 us
    ppermute x3, waiting for transfers between devices, across(): return [lax.ppermute(values[0], axis_name, [(0, 1), (1, 0)])]  13.9 us
    ppermute x8, starting transfers between devices, far_rows(): lax.ppermute(values, ('sx', 'sy'), pairs + [(j, i) for i, j in pairs])  6.83 us
    ppermute x3, starting transfers between devices, across(): return [lax.ppermute(values[0], axis_name, [(0, 1), (1, 0)])]  4.71 us
    ppermute x14, starting transfers between devices, near_rows(): return lax.ppermute(values, 'sx', [(i, i ^ 1) for i in range(self.sx_size)])  3.08 us
    unnamed x16, local copies, waits for them, and re-layouts  2.69 us
    ppermute x14, waiting for transfers between devices, near_rows(): return lax.ppermute(values, 'sx', [(i, i ^ 1) for i in range(self.sx_size)])  1.97 us
  transfers between devices with their start and end apart: 25, of which 12 were waited for; matrix products, arithmetic and copies ran while one was open for 0% of the time, Pallas kernels for 23%

profile of v9, /device:TPU:10, one launch (start us, length us, event | category | flops | bytes accessed | tf_op | source)
XLA Modules:
  0.0 79.2 jit_solution(941691807265074001)
XLA Ops:
  0.7 1.0 %copy-done.1 = f32[2,128,512]{2,1,0:T(8,128)S(1)} copy-done((f32[2,128,512]{2,1,0:T(8,128)S(1)}, f32[2,128,512]{2,1,0:T(8,128)}, u32[]{:S(2)}) %copy-start.1) | copy-done | bytes 524312
  2.4 1.6 %collective-permute-start = (f32[2,136,128]{2,1,0:T(8,128)S(1)}, f32[2,136,128]{2,1,0:T(8,128)S(1)}, u32[]{:S(2)}, u32[]{:S(2)}) collective-permute-start(f32[2,136,128]{2,1,0:T(8,128)S(1)} %shard_map.73), channel_id=1, source_target_pairs={{0,1},{1,0},{2,3},{3,2},{4,5},{5,4},{6,7},{7,6},{8,9},{9,8},{10,11... | collective-permute-start | bytes 417800 | tf_op jit(solution)/shard_map/ppermute | solution.py:101
  3.9 4.4 %collective-permute-done.refs_3_ = f32[2,136,128]{2,1,0:T(8,128)S(1)} collective-permute-done((f32[2,136,128]{2,1,0:T(8,128)S(1)}, f32[2,136,128]{2,1,0:T(8,128)S(1)}, u32[]{:S(2)}, u32[]{:S(2)}) %collective-permute-start) | collective-permute-done | bytes 139296 | tf_op jit(solution)/shard_map/ppermute | solution.py:101
  8.9 0.8 %collective-permute-start.4 = (f32[2,128,256]{2,1,0:T(8,128)S(1)}, f32[2,128,256]{2,1,0:T(8,128)S(1)}, u32[]{:S(2)}, u32[]{:S(2)}) collective-permute-start(f32[2,128,256]{2,1,0:T(8,128)S(1)} %get-tuple-element.41), channel_id=1, source_target_pairs={{0,2},{2,0},{4,6},{6,4},{8,10},{10,8},{12,14},{14,12},{16,18},{18,... | collective-permute-start | bytes 786440 | tf_op jit(solution)/shard_map/ppermute | solution.py:116
  10.3 1.2 %collective-permute-start.1 = (f32[2,144,128]{2,1,0:T(8,128)S(1)}, f32[2,144,128]{2,1,0:T(8,128)S(1)}, u32[]{:S(2)}, u32[]{:S(2)}) collective-permute-start(f32[2,144,128]{2,1,0:T(8,128)S(1)} %get-tuple-element.40.refs_0_.refs_3_.refs_8_), channel_id=1, source_target_pairs={{2,4},{3,5},{6,8},{7,9},{10,12},{11,13},{14,16},{15,17},{18,20},{1... | collective-permute-start | bytes 442376 | tf_op jit(solution)/shard_map/ppermute | solution.py:113
  11.4 0.9 %copy-done.5 = bf16[2,256,256]{2,1,0:T(8,128)(2,1)S(1)} copy-done((bf16[2,256,256]{2,1,0:T(8,128)(2,1)S(1)}, bf16[2,256,256]{2,1,0:T(8,128)(2,1)}, u32[]{:S(2)}) %copy-start.5) | copy-done | bytes 262168
  12.4 1.5 %shard_map.76 = (f32[2,2,256,256]{3,2,1,0:T(8,128)S(1)}, f32[2,256,256]{2,1,0:T(8,128)S(1)}) custom-call(s32[2,2]{1,0:T(2,128)S(1)} %bitcast.6, f32[2,256,256]{2,1,0:T(8,128)S(1)} %copy-done.3, f32[2,256,256]{2,1,0:T(8,128)S(1)} %bitcast.3, bf16[2,256,256]{2,1,0:T(8,128)(2,1)S(1)} %copy-done.5), custom_call_target="tpu_custom_call" | custom-call | flops 100000 | bytes 10000 | tf_op jit(solution)/shard_map/pallas_call | solution.py:543
  13.9 3.7 %collective-permute-done.1.refs_1_.refs_5_.refs_10_ = f32[2,144,128]{2,1,0:T(8,128)S(1)} collective-permute-done((f32[2,144,128]{2,1,0:T(8,128)S(1)}, f32[2,144,128]{2,1,0:T(8,128)S(1)}, u32[]{:S(2)}, u32[]{:S(2)}) %collective-permute-start.1) | collective-permute-done | bytes 147488 | tf_op jit(solution)/shard_map/ppermute | solution.py:113
  17.6 2.6 %shard_map.77 = (f32[2,128,256]{2,1,0:T(8,128)S(1)}, f32[2,128,256]{2,1,0:T(8,128)S(1)}) custom-call(s32[2,2]{1,0:T(2,128)S(1)} %bitcast.7, s32[16]{0:T(128)S(1)} %bitcast.14, f32[2,128,512]{2,1,0:T(8,128)S(1)} %copy-done.2, f32[2,144,128]{2,1,0:T(8,128)S(1)} %get-tuple-element.40.refs_0_.refs_3_.refs_8_, ...), custom_call_target="tpu_custom_call" | custom-call | flops 100000 | bytes 10000 | tf_op jit(solution)/shard_map/pallas_call | solution.py:543
  20.4 1.3 %shard_map.75.refs_13_.refs_0_ = s32[6,128]{1,0:T(8,128)S(1)} custom-call(f32[2,144,128]{2,1,0:T(8,128)S(1)} %get-tuple-element.40.refs_0_.refs_3_.refs_8_, f32[2,144,128]{2,1,0:T(8,128)S(1)} %collective-permute-done.1.refs_1_.refs_5_.refs_10_, f32[2,144,128]{2,1,0:T(8,128)S(1)} %collective-permute-done.2.refs_2_.refs_6_.refs_11_), custom_call_target="tpu_custom_call" | custom-call | flops 100000 | bytes 10000 | tf_op jit(solution)/shard_map/pallas_call | solution.py:543
  21.6 2.7 %shard_map.78 = (f32[2,128,256]{2,1,0:T(8,128)S(1)}, f32[2,128,256]{2,1,0:T(8,128)S(1)}, f32[1,128,256]{2,1,0:T(8,128)S(1)}, f32[1,128,256]{2,1,0:T(8,128)S(1)},...) custom-call(s32[2,2]{1,0:T(2,128)S(1)} %bitcast.9, s32[16]{0:T(128)S(1)} %bitcast.15, ...), custom_call_target="tpu_custom_call" | custom-call | flops 100000 | bytes 10000 | tf_op jit(solution)/shard_map/pallas_call | solution.py:543
  24.4 1.8 %collective-permute-start.11 = (f32[2,128,256]{2,1,0:T(8,128)S(1)}, f32[2,128,256]{2,1,0:T(8,128)S(1)}, u32[]{:S(2)}, u32[]{:S(2)}) collective-permute-start(f32[2,128,256]{2,1,0:T(8,128)S(1)} %get-tuple-element.54), channel_id=1, source_target_pairs={{2,4},{3,5},{6,8},{7,9},{10,12},{11,13},{14,16},{15,17},{18,20},{1... | collective-permute-start | bytes 786440 | tf_op jit(solution)/shard_map/ppermute | solution.py:113
  26.6 2.9 %collective-permute-done.6.refs_3_ = f32[2,128,256]{2,1,0:T(8,128)S(1)} collective-permute-done((f32[2,128,256]{2,1,0:T(8,128)S(1)}, f32[2,128,256]{2,1,0:T(8,128)S(1)}, u32[]{:S(2)}, u32[]{:S(2)}) %collective-permute-start.6) | collective-permute-done | bytes 262176 | tf_op jit(solution)/shard_map/ppermute | solution.py:113
  29.5 0.8 %shard_map.79.refs_2_.refs_1_ = f32[2,128,768]{2,1,0:T(8,128)S(1)} custom-call(s32[6,128]{1,0:T(8,128)S(1)} %shard_map.75.refs_13_.refs_0_, f32[2,128,256]{2,1,0:T(8,128)S(1)} %get-tuple-element.45.refs_1_, f32[2,128,256]{2,1,0:T(8,128)S(1)} %get-tuple-element.47.refs_2_, f32[2,128,256]{2,1,0:T(8,128)S(1)} %collective-permute-done.6.refs_3_), custom_call_target="tpu_custom_call" | custom-call | flops 100000 | bytes 10000 | tf_op jit(solution)/shard_map/pallas_call | solution.py:543
  30.3 3.0 %shard_map.80 = (f32[128,768]{1,0:T(8,128)S(1)}, f32[128,256]{1,0:T(8,128)S(1)}) custom-call(s32[6,128]{1,0:T(8,128)S(1)} %shard_map.75.refs_13_.refs_0_, f32[2,256,256]{2,1,0:T(8,128)S(1)} %copy-done.3, f32[2,128,768]{2,1,0:T(8,128)S(1)} %shard_map.79.refs_2_.refs_1_), custom_call_target="tpu_custom_call" | custom-call | flops 100000 | bytes 10000 | tf_op jit(solution)/shard_map/pallas_call | solution.py:543
  33.4 1.0 %shard_map.81 = (f32[2,128,768]{2,1,0:T(8,128)S(1)}, f32[2,128,768]{2,1,0:T(8,128)S(1)}) custom-call(s32[6,128]{1,0:T(8,128)S(1)} %shard_map.75.refs_13_.refs_0_, f32[2,128,768]{2,1,0:T(8,128)S(1)} %shard_map.79.refs_2_.refs_1_, f32[128,768]{1,0:T(8,128)S(1)} %get-tuple-element.48.refs_2_.refs_3_.refs_4_.refs_0_, ...), custom_call_target="tpu_custom_call" | custom-call | flops 100000 | bytes 10000 | tf_op jit(solution)/shard_map/pallas_call | solution.py:543
  34.4 0.7 shard_map.82.refs_5_.refs_0_.refs_2_.refs_7_
  35.1 2.0 %collective-permute-start.13 = (f32[2,128,384]{2,1,0:T(8,128)S(1)}, f32[2,128,384]{2,1,0:T(8,128)S(1)}, u32[]{:S(2)}, u32[]{:S(2)}) collective-permute-start(f32[2,128,384]{2,1,0:T(8,128)S(1)} %shard_map.82.refs_5_.refs_0_.refs_2_.refs_7_), channel_id=1, source_target_pairs={{2,4},{3,5},{6,8},{7,9},{10,12},{11,13},{14,16},{15,17},{18,20},{1... | collective-permute-start | bytes 1179656 | tf_op jit(solution)/shard_map/ppermute | solution.py:113
  37.1 0.7 shard_map.83
  37.8 1.6 %collective-permute-start.12 = (f32[2,128,256]{2,1,0:T(8,128)S(1)}, f32[2,128,256]{2,1,0:T(8,128)S(1)}, u32[]{:S(2)}, u32[]{:S(2)}) collective-permute-start(f32[2,128,256]{2,1,0:T(8,128)S(1)} %get-tuple-element.57), channel_id=1, source_target_pairs={{0,1},{1,0},{2,3},{3,2},{4,5},{5,4},{6,7},{7,6},{8,9},{9,8},{10,11... | collective-permute-start | bytes 786440 | tf_op jit(solution)/shard_map/ppermute | solution.py:101
  39.4 7.3 %collective-permute-done.12.refs_2_ = f32[2,128,256]{2,1,0:T(8,128)S(1)} collective-permute-done((f32[2,128,256]{2,1,0:T(8,128)S(1)}, f32[2,128,256]{2,1,0:T(8,128)S(1)}, u32[]{:S(2)}, u32[]{:S(2)}) %collective-permute-start.12) | collective-permute-done | bytes 262176 | tf_op jit(solution)/shard_map/ppermute | solution.py:101
  47.6 0.7 collective-permute-done.17.refs_8_.refs_13_
  49.0 7.2 %collective-permute-done.14.refs_5_.refs_10_ = f32[2,128,256]{2,1,0:T(8,128)S(1)} collective-permute-done((f32[2,128,256]{2,1,0:T(8,128)S(1)}, f32[2,128,256]{2,1,0:T(8,128)S(1)}, u32[]{:S(2)}, u32[]{:S(2)}) %collective-permute-start.14) | collective-permute-done | bytes 262176 | tf_op jit(solution)/shard_map/ppermute | solution.py:113
  56.1 2.6 %shard_map.86 = (f32[2,128,256]{2,1,0:T(8,128)S(1)}, f32[2,128,256]{2,1,0:T(8,128)S(1)}) custom-call(s32[2,2]{1,0:T(2,128)S(1)} %bitcast.10, s32[16]{0:T(128)S(1)} %bitcast.16, f32[2,128,384]{2,1,0:T(8,128)S(1)} %shard_map.82.refs_5_.refs_0_.refs_2_.refs_7_, f32[2,128,256]{2,1,0:T(8,128)S(1)} %get-tuple-element.59.refs_3_.refs_8_, ...), custom_call_target="tpu_custom_call" | custom-call | flops 100000 | bytes 10000 | tf_op jit(solution)/shard_map/pallas_call | solution.py:543
  58.8 2.6 %shard_map.87 = (f32[2,128,256]{2,1,0:T(8,128)S(1)}, f32[2,128,256]{2,1,0:T(8,128)S(1)}, f32[1,128,256]{2,1,0:T(8,128)S(1)}, f32[1,128,256]{2,1,0:T(8,128)S(1)},...) custom-call(s32[2,2]{1,0:T(2,128)S(1)} %bitcast.11, s32[16]{0:T(128)S(1)} %bitcast.17, ...), custom_call_target="tpu_custom_call" | custom-call | flops 100000 | bytes 10000 | tf_op jit(solution)/shard_map/pallas_call | solution.py:543
  61.4 1.8 %collective-permute-start.23 = (f32[2,128,256]{2,1,0:T(8,128)S(1)}, f32[2,128,256]{2,1,0:T(8,128)S(1)}, u32[]{:S(2)}, u32[]{:S(2)}) collective-permute-start(f32[2,128,256]{2,1,0:T(8,128)S(1)} %get-tuple-element.71), channel_id=1, source_target_pairs={{2,4},{3,5},{6,8},{7,9},{10,12},{11,13},{14,16},{15,17},{18,20},{1... | collective-permute-start | bytes 786440 | tf_op jit(solution)/shard_map/ppermute | solution.py:113
  63.7 6.1 %collective-permute-done.18.refs_3_ = f32[2,128,256]{2,1,0:T(8,128)S(1)} collective-permute-done((f32[2,128,256]{2,1,0:T(8,128)S(1)}, f32[2,128,256]{2,1,0:T(8,128)S(1)}, u32[]{:S(2)}, u32[]{:S(2)}) %collective-permute-start.18) | collective-permute-done | bytes 262176 | tf_op jit(solution)/shard_map/ppermute | solution.py:113
  69.8 0.8 %shard_map.88.refs_1_ = f32[2,128,768]{2,1,0:T(8,128)S(1)} custom-call(s32[6,128]{1,0:T(8,128)S(1)} %shard_map.75.refs_13_.refs_0_, f32[2,128,256]{2,1,0:T(8,128)S(1)} %get-tuple-element.63.refs_1_, f32[2,128,256]{2,1,0:T(8,128)S(1)} %get-tuple-element.65.refs_2_, f32[2,128,256]{2,1,0:T(8,128)S(1)} %collective-permute-done.18.refs_3_), custom_call_target="tpu_custom_call" | custom-call | flops 100000 | bytes 10000 | tf_op jit(solution)/shard_map/pallas_call | solution.py:543
  71.2 1.0 %shard_map.89 = (f32[2,128,768]{2,1,0:T(8,128)S(1)}, f32[2,128,768]{2,1,0:T(8,128)S(1)}) custom-call(s32[6,128]{1,0:T(8,128)S(1)} %shard_map.75.refs_13_.refs_0_, f32[2,128,768]{2,1,0:T(8,128)S(1)} %shard_map.88.refs_1_, f32[128,768]{1,0:T(8,128)S(1)} %get-tuple-element.48.refs_2_.refs_3_.refs_4_.refs_0_, ...), custom_call_target="tpu_custom_call" | custom-call | flops 100000 | bytes 10000 | tf_op jit(solution)/shard_map/pallas_call | solution.py:543
  73.3 1.5 %collective-permute-start.24 = (f32[2,128,128]{2,1,0:T(8,128)S(1)}, f32[2,128,128]{2,1,0:T(8,128)S(1)}, u32[]{:S(2)}, u32[]{:S(2)}) collective-permute-start(f32[2,128,128]{2,1,0:T(8,128)S(1)} %shard_map.90.refs_4_), channel_id=1, source_target_pairs={{0,1},{1,0},{2,3},{3,2},{4,5},{5,4},{6,7},{7,6},{8,9},{9,8},{10,11... | collective-permute-start | bytes 393224 | tf_op jit(solution)/shard_map/ppermute | solution.py:101
  74.8 1.5 %shard_map.91 = (f32[2,128,512]{2,1,0:T(8,128)}, f32[2,128,128]{2,1,0:T(8,128)S(1)}) custom-call(s32[6,128]{1,0:T(8,128)S(1)} %shard_map.75.refs_13_.refs_0_, f32[2,128,768]{2,1,0:T(8,128)S(1)} %get-tuple-element.70.refs_1_, f32[2,128,256]{2,1,0:T(8,128)S(1)} %collective-permute-done.23.refs_2_, ...), custom_call_target="tpu_custom_call" | custom-call | flops 100000 | bytes 10000 | tf_op jit(solution)/shard_map/pallas_call | solution.py:543
  76.3 2.2 %collective-permute-done.24.refs_2_ = f32[2,128,128]{2,1,0:T(8,128)S(1)} collective-permute-done((f32[2,128,128]{2,1,0:T(8,128)S(1)}, f32[2,128,128]{2,1,0:T(8,128)S(1)}, u32[]{:S(2)}, u32[]{:S(2)}) %collective-permute-start.24) | collective-permute-done | bytes 131104 | tf_op jit(solution)/shard_map/ppermute | solution.py:101
  (54 shorter events, 7.4 us)
Async XLA Ops:
  0.0 17.6 %collective-permute-start.3 = (f32[2,128,512]{2,1,0:T(8,128)}, f32[2,128,512]{2,1,0:T(8,128)S(1)}, u32[]{:S(2)}, u32[]{:S(2)}) collective-permute-start(f32[2,128,512]{2,1,0:T(8,128)} %refs_7_.1), channel_id=1, source_target_pairs={{2,4},{3,5},{6,8},{7,9},{10,12},{11,13},{14,16},{15,17},{18,20},{1... | collective-permute-start | bytes 1572872 | tf_op jit(solution)/shard_map/ppermute | solution.py:113
  0.0 0.7 copy-start.7
  0.7 1.0 %copy-start.1 = (f32[2,128,512]{2,1,0:T(8,128)S(1)}, f32[2,128,512]{2,1,0:T(8,128)}, u32[]{:S(2)}) copy-start(f32[2,128,512]{2,1,0:T(8,128)} %refs_7_.1) | copy-start | bytes 1572868
  1.7 9.7 %copy-start.3 = (f32[2,256,256]{2,1,0:T(8,128)S(1)}, f32[2,256,256]{2,1,0:T(8,128)}, u32[]{:S(2)}) copy-start(f32[2,256,256]{2,1,0:T(8,128)} %refs_1_.1) | copy-start | bytes 1572868
  1.7 9.7 %copy-start.4 = (f32[1,1,2,256,256]{4,3,2,1,0:T(8,128)S(1)}, f32[1,1,2,256,256]{4,3,2,1,0:T(8,128)}, u32[]{:S(2)}) copy-start(f32[1,1,2,256,256]{4,3,2,1,0:T(8,128)} %param.9) | copy-start | bytes 1572868
  2.3 15.3 %copy-start = (bf16[2,2,2,256,256]{4,3,2,1,0:T(8,128)(2,1)S(1)}, bf16[2,2,2,256,256]{4,3,2,1,0:T(8,128)(2,1)}, u32[]{:S(2)}) copy-start(bf16[2,2,2,256,256]{4,3,2,1,0:T(8,128)(2,1)} %constant.4.clone.refs_11_.refs_12_) | copy-start | bytes 3145732
  2.4 6.0 %collective-permute-start = (f32[2,136,128]{2,1,0:T(8,128)S(1)}, f32[2,136,128]{2,1,0:T(8,128)S(1)}, u32[]{:S(2)}, u32[]{:S(2)}) collective-permute-start(f32[2,136,128]{2,1,0:T(8,128)S(1)} %shard_map.73), channel_id=1, source_target_pairs={{0,1},{1,0},{2,3},{3,2},{4,5},{5,4},{6,7},{7,6},{8,9},{9,8},{10,11... | collective-permute-start | bytes 417800 | tf_op jit(solution)/shard_map/ppermute | solution.py:101
  8.9 8.7 %collective-permute-start.4 = (f32[2,128,256]{2,1,0:T(8,128)S(1)}, f32[2,128,256]{2,1,0:T(8,128)S(1)}, u32[]{:S(2)}, u32[]{:S(2)}) collective-permute-start(f32[2,128,256]{2,1,0:T(8,128)S(1)} %get-tuple-element.41), channel_id=1, source_target_pairs={{0,2},{2,0},{4,6},{6,4},{8,10},{10,8},{12,14},{14,12},{16,18},{18,... | collective-permute-start | bytes 786440 | tf_op jit(solution)/shard_map/ppermute | solution.py:116
  9.7 7.9 %collective-permute-start.5 = (f32[2,128,256]{2,1,0:T(8,128)S(1)}, f32[2,128,256]{2,1,0:T(8,128)S(1)}, u32[]{:S(2)}, u32[]{:S(2)}) collective-permute-start(f32[2,128,256]{2,1,0:T(8,128)S(1)} %get-tuple-element.42), channel_id=1, source_target_pairs={{0,2},{2,0},{4,6},{6,4},{8,10},{10,8},{12,14},{14,12},{16,18},{18,... | collective-permute-start | bytes 786440 | tf_op jit(solution)/shard_map/ppermute | solution.py:116
  9.8 4.1 %collective-permute-start.2 = (f32[2,144,128]{2,1,0:T(8,128)S(1)}, f32[2,144,128]{2,1,0:T(8,128)S(1)}, u32[]{:S(2)}, u32[]{:S(2)}) collective-permute-start(f32[2,144,128]{2,1,0:T(8,128)S(1)} %get-tuple-element.40.refs_0_.refs_3_.refs_8_), channel_id=1, source_target_pairs={{0,2},{2,0},{4,6},{6,4},{8,10},{10,8},{12,14},{14,12},{16,18},{18,... | collective-permute-start | bytes 442376 | tf_op jit(solution)/shard_map/ppermute | solution.py:116
  10.3 7.3 %collective-permute-start.1 = (f32[2,144,128]{2,1,0:T(8,128)S(1)}, f32[2,144,128]{2,1,0:T(8,128)S(1)}, u32[]{:S(2)}, u32[]{:S(2)}) collective-permute-start(f32[2,144,128]{2,1,0:T(8,128)S(1)} %get-tuple-element.40.refs_0_.refs_3_.refs_8_), channel_id=1, source_target_pairs={{2,4},{3,5},{6,8},{7,9},{10,12},{11,13},{14,16},{15,17},{18,20},{1... | collective-permute-start | bytes 442376 | tf_op jit(solution)/shard_map/ppermute | solution.py:113
  11.4 1.0 %copy-start.5 = (bf16[2,256,256]{2,1,0:T(8,128)(2,1)S(1)}, bf16[2,256,256]{2,1,0:T(8,128)(2,1)}, u32[]{:S(2)}) copy-start(bf16[2,256,256]{2,1,0:T(8,128)(2,1)} %constant.5.clone.order) | copy-start | bytes 786436
  12.4 5.2 %copy-start.2 = (f32[2,128,512]{2,1,0:T(8,128)S(1)}, f32[2,128,512]{2,1,0:T(8,128)}, u32[]{:S(2)}) copy-start(f32[2,128,512]{2,1,0:T(8,128)} %refs_7_.1) | copy-start | bytes 1572868
  20.3 9.2 %collective-permute-start.6 = (f32[2,128,256]{2,1,0:T(8,128)S(1)}, f32[2,128,256]{2,1,0:T(8,128)S(1)}, u32[]{:S(2)}, u32[]{:S(2)}) collective-permute-start(f32[2,128,256]{2,1,0:T(8,128)S(1)} %get-tuple-element.46.refs_9_), channel_id=1, source_target_pairs={{2,4},{3,5},{6,8},{7,9},{10,12},{11,13},{14,16},{15,17},{18,20},{1... | collective-permute-start | bytes 786440 | tf_op jit(solution)/shard_map/ppermute | solution.py:113
  24.4 10.0 %collective-permute-start.11 = (f32[2,128,256]{2,1,0:T(8,128)S(1)}, f32[2,128,256]{2,1,0:T(8,128)S(1)}, u32[]{:S(2)}, u32[]{:S(2)}) collective-permute-start(f32[2,128,256]{2,1,0:T(8,128)S(1)} %get-tuple-element.54), channel_id=1, source_target_pairs={{2,4},{3,5},{6,8},{7,9},{10,12},{11,13},{14,16},{15,17},{18,20},{1... | collective-permute-start | bytes 786440 | tf_op jit(solution)/shard_map/ppermute | solution.py:113
  26.1 7.2 %collective-permute-start.7 = (f32[1,128,256]{2,1,0:T(8,128)S(1)}, f32[1,128,256]{2,1,0:T(8,128)S(1)}, u32[]{:S(2)}, u32[]{:S(2)}) collective-permute-start(f32[1,128,256]{2,1,0:T(8,128)S(1)} %get-tuple-element.49), channel_id=1, source_target_pairs={{0,2},{2,0},{4,6},{6,4},{8,10},{10,8},{12,14},{14,12},{16,18},{18,... | collective-permute-start | bytes 393224 | tf_op jit(solution)/shard_map/ppermute | solution.py:116
  26.1 7.2 %collective-permute-start.8 = (f32[1,128,256]{2,1,0:T(8,128)S(1)}, f32[1,128,256]{2,1,0:T(8,128)S(1)}, u32[]{:S(2)}, u32[]{:S(2)}) collective-permute-start(f32[1,128,256]{2,1,0:T(8,128)S(1)} %get-tuple-element.50), channel_id=1, source_target_pairs={{0,2},{2,0},{4,6},{6,4},{8,10},{10,8},{12,14},{14,12},{16,18},{18,... | collective-permute-start | bytes 393224 | tf_op jit(solution)/shard_map/ppermute | solution.py:116
  26.6 6.7 %collective-permute-start.9 = (f32[1,128,256]{2,1,0:T(8,128)S(1)}, f32[1,128,256]{2,1,0:T(8,128)S(1)}, u32[]{:S(2)}, u32[]{:S(2)}) collective-permute-start(f32[1,128,256]{2,1,0:T(8,128)S(1)} %get-tuple-element.51), channel_id=1, source_target_pairs={{0,2},{2,0},{4,6},{6,4},{8,10},{10,8},{12,14},{14,12},{16,18},{18,... | collective-permute-start | bytes 393224 | tf_op jit(solution)/shard_map/ppermute | solution.py:116
  29.5 3.8 %collective-permute-start.10 = (f32[1,128,256]{2,1,0:T(8,128)S(1)}, f32[1,128,256]{2,1,0:T(8,128)S(1)}, u32[]{:S(2)}, u32[]{:S(2)}) collective-permute-start(f32[1,128,256]{2,1,0:T(8,128)S(1)} %get-tuple-element.52), channel_id=1, source_target_pairs={{0,2},{2,0},{4,6},{6,4},{8,10},{10,8},{12,14},{14,12},{16,18},{18,... | collective-permute-start | bytes 393224 | tf_op jit(solution)/shard_map/ppermute | solution.py:116
  35.1 12.4 %collective-permute-start.13 = (f32[2,128,384]{2,1,0:T(8,128)S(1)}, f32[2,128,384]{2,1,0:T(8,128)S(1)}, u32[]{:S(2)}, u32[]{:S(2)}) collective-permute-start(f32[2,128,384]{2,1,0:T(8,128)S(1)} %shard_map.82.refs_5_.refs_0_.refs_2_.refs_7_), channel_id=1, source_target_pairs={{2,4},{3,5},{6,8},{7,9},{10,12},{11,13},{14,16},{15,17},{18,20},{1... | collective-permute-start | bytes 1179656 | tf_op jit(solution)/shard_map/ppermute | solution.py:113
  37.8 8.9 %collective-permute-start.12 = (f32[2,128,256]{2,1,0:T(8,128)S(1)}, f32[2,128,256]{2,1,0:T(8,128)S(1)}, u32[]{:S(2)}, u32[]{:S(2)}) collective-permute-start(f32[2,128,256]{2,1,0:T(8,128)S(1)} %get-tuple-element.57), channel_id=1, source_target_pairs={{0,1},{1,0},{2,3},{3,2},{4,5},{5,4},{6,7},{7,6},{8,9},{9,8},{10,11... | collective-permute-start | bytes 786440 | tf_op jit(solution)/shard_map/ppermute | solution.py:101
  46.8 1.4 %collective-permute-start.17 = (f32[2,128,128]{2,1,0:T(8,128)S(1)}, f32[2,128,128]{2,1,0:T(8,128)S(1)}, u32[]{:S(2)}, u32[]{:S(2)}) collective-permute-start(f32[2,128,128]{2,1,0:T(8,128)S(1)} %get-tuple-element.62), channel_id=1, source_target_pairs={{0,2},{2,0},{4,6},{6,4},{8,10},{10,8},{12,14},{14,12},{16,18},{18,... | collective-permute-start | bytes 393224 | tf_op jit(solution)/shard_map/ppermute | solution.py:116
  47.0 1.6 %collective-permute-start.15 = (f32[2,128,256]{2,1,0:T(8,128)S(1)}, f32[2,128,256]{2,1,0:T(8,128)S(1)}, u32[]{:S(2)}, u32[]{:S(2)}) collective-permute-start(f32[2,128,256]{2,1,0:T(8,128)S(1)} %get-tuple-element.60), channel_id=1, source_target_pairs={{0,2},{2,0},{4,6},{6,4},{8,10},{10,8},{12,14},{14,12},{16,18},{18,... | collective-permute-start | bytes 786440 | tf_op jit(solution)/shard_map/ppermute | solution.py:116
  47.4 1.6 %collective-permute-start.16 = (f32[2,128,256]{2,1,0:T(8,128)S(1)}, f32[2,128,256]{2,1,0:T(8,128)S(1)}, u32[]{:S(2)}, u32[]{:S(2)}) collective-permute-start(f32[2,128,256]{2,1,0:T(8,128)S(1)} %get-tuple-element.61), channel_id=1, source_target_pairs={{0,2},{2,0},{4,6},{6,4},{8,10},{10,8},{12,14},{14,12},{16,18},{18,... | collective-permute-start | bytes 786440 | tf_op jit(solution)/shard_map/ppermute | solution.py:116
  47.5 8.6 %collective-permute-start.14 = (f32[2,128,256]{2,1,0:T(8,128)S(1)}, f32[2,128,256]{2,1,0:T(8,128)S(1)}, u32[]{:S(2)}, u32[]{:S(2)}) collective-permute-start(f32[2,128,256]{2,1,0:T(8,128)S(1)} %get-tuple-element.59.refs_3_.refs_8_), channel_id=1, source_target_pairs={{2,4},{3,5},{6,8},{7,9},{10,12},{11,13},{14,16},{15,17},{18,20},{1... | collective-permute-start | bytes 786440 | tf_op jit(solution)/shard_map/ppermute | solution.py:113
  58.7 11.1 %collective-permute-start.18 = (f32[2,128,256]{2,1,0:T(8,128)S(1)}, f32[2,128,256]{2,1,0:T(8,128)S(1)}, u32[]{:S(2)}, u32[]{:S(2)}) collective-permute-start(f32[2,128,256]{2,1,0:T(8,128)S(1)} %get-tuple-element.64.refs_9_), channel_id=1, source_target_pairs={{2,4},{3,5},{6,8},{7,9},{10,12},{11,13},{14,16},{15,17},{18,20},{1... | collective-permute-start | bytes 786440 | tf_op jit(solution)/shard_map/ppermute | solution.py:113
  61.4 11.2 %collective-permute-start.23 = (f32[2,128,256]{2,1,0:T(8,128)S(1)}, f32[2,128,256]{2,1,0:T(8,128)S(1)}, u32[]{:S(2)}, u32[]{:S(2)}) collective-permute-start(f32[2,128,256]{2,1,0:T(8,128)S(1)} %get-tuple-element.71), channel_id=1, source_target_pairs={{2,4},{3,5},{6,8},{7,9},{10,12},{11,13},{14,16},{15,17},{18,20},{1... | collective-permute-start | bytes 786440 | tf_op jit(solution)/shard_map/ppermute | solution.py:113
  63.2 7.5 %collective-permute-start.19 = (f32[1,128,256]{2,1,0:T(8,128)S(1)}, f32[1,128,256]{2,1,0:T(8,128)S(1)}, u32[]{:S(2)}, u32[]{:S(2)}) collective-permute-start(f32[1,128,256]{2,1,0:T(8,128)S(1)} %get-tuple-element.66), channel_id=1, source_target_pairs={{0,2},{2,0},{4,6},{6,4},{8,10},{10,8},{12,14},{14,12},{16,18},{18,... | collective-permute-start | bytes 393224 | tf_op jit(solution)/shard_map/ppermute | solution.py:116
  63.2 7.5 %collective-permute-start.20 = (f32[1,128,256]{2,1,0:T(8,128)S(1)}, f32[1,128,256]{2,1,0:T(8,128)S(1)}, u32[]{:S(2)}, u32[]{:S(2)}) collective-permute-start(f32[1,128,256]{2,1,0:T(8,128)S(1)} %get-tuple-element.67), channel_id=1, source_target_pairs={{0,2},{2,0},{4,6},{6,4},{8,10},{10,8},{12,14},{14,12},{16,18},{18,... | collective-permute-start | bytes 393224 | tf_op jit(solution)/shard_map/ppermute | solution.py:116
  63.7 7.0 %collective-permute-start.21 = (f32[1,128,256]{2,1,0:T(8,128)S(1)}, f32[1,128,256]{2,1,0:T(8,128)S(1)}, u32[]{:S(2)}, u32[]{:S(2)}) collective-permute-start(f32[1,128,256]{2,1,0:T(8,128)S(1)} %get-tuple-element.68), channel_id=1, source_target_pairs={{0,2},{2,0},{4,6},{6,4},{8,10},{10,8},{12,14},{14,12},{16,18},{18,... | collective-permute-start | bytes 393224 | tf_op jit(solution)/shard_map/ppermute | solution.py:116
  69.8 1.3 %collective-permute-start.22 = (f32[1,128,256]{2,1,0:T(8,128)S(1)}, f32[1,128,256]{2,1,0:T(8,128)S(1)}, u32[]{:S(2)}, u32[]{:S(2)}) collective-permute-start(f32[1,128,256]{2,1,0:T(8,128)S(1)} %get-tuple-element.69), channel_id=1, source_target_pairs={{0,2},{2,0},{4,6},{6,4},{8,10},{10,8},{12,14},{14,12},{16,18},{18,... | collective-permute-start | bytes 393224 | tf_op jit(solution)/shard_map/ppermute | solution.py:116
  73.3 5.2 %collective-permute-start.24 = (f32[2,128,128]{2,1,0:T(8,128)S(1)}, f32[2,128,128]{2,1,0:T(8,128)S(1)}, u32[]{:S(2)}, u32[]{:S(2)}) collective-permute-start(f32[2,128,128]{2,1,0:T(8,128)S(1)} %shard_map.90.refs_4_), channel_id=1, source_target_pairs={{0,1},{1,0},{2,3},{3,2},{4,5},{5,4},{6,7},{7,6},{8,9},{9,8},{10,11... | collective-permute-start | bytes 393224 | tf_op jit(solution)/shard_map/ppermute | solution.py:101
  (1 other events, 0.7 us)

commit v10 on v9

--- a/solution.py
+++ b/solution.py
@@ -214,18 +214,18 @@
     spread(block, near)
 
 
-def pair_kernel(sides, middle, *rest):
-    bases, received, inverses, results = (rest[k * sides : (k + 1) * sides] for k in range(4))
-    near = rest[4 * sides :]
-    for base, other, inverse, result, copy in zip(bases, received, inverses, results, near):
-        values = base[...] - other[...] * inverse[...][None]
+def pair_kernel(plan, base, early, inverse, middle, *rest):
+    sides = plan.sides
+    sums, received, results = (rest[k * sides : (k + 1) * sides] for k in range(3))
+    near = rest[3 * sides :]
+    _, t = here()
+    for total, other, result, copy, start in zip(sums, received, results, near, plan.pair_starts(t)):
+        where = lanes(start, 2)
+        missing = total[...] + other[...] - early[:, :, where]
+        values = base[:, :, where] - missing * inverse[:, where][None]
         result[...] = values
         copy[...] = values
     spread(middle, near[sides:])
-
-
-def token_kernel(_, token):
-    token[...] = jnp.zeros(token.shape, jnp.float32)
 
 
 def prepare_kernel(centres, probe, amps, order, rolled, ordered, padded):
@@ -276,8 +276,7 @@
     copy.wait()
 
 
-def light_kernel(plan, slots, info, probe, _, inverse, *rest):
-    pairs, (padded, canvas) = rest[: plan.sides], rest[plan.sides :]
+def light_kernel(plan, slots, info, probe, _, inverse, padded, canvas):
     size = probe.shape[1]
     half = size // 2
     _, t = here()
@@ -307,10 +306,7 @@
             return carry
 
         lax.fori_loop(0, reach * slots, add, 0)
-    result = 1.0 / (canvas[:, lanes(plan.own, plan.tiles)] + DAMPING)
-    inverse[...] = result
-    for pair, start in zip(pairs, plan.pair_starts(t)):
-        pair[...] = inverse[:, lanes(start, 2)]
+    inverse[...] = 1.0 / (canvas[:, lanes(plan.own, plan.tiles)] + DAMPING)
 
 
 def term_kernel(plan, slot, layout, pieces, copied, centres, counts, *rest):
@@ -394,17 +390,21 @@
         inner[1] = term_imag[half:]
 
     for index, source in enumerate((*earlier, outer)):
-        for part in range(2 if near_outers else 0):
-            near_outers[2 * index + part][0] = source[part]
+        line = 0
+        for target in near_outers:
+            rows = target.shape[1]
+            target[2 * index : 2 * index + 2] = source[:, line : line + rows]
+            line += rows
 
 
 class Patch:
     def __init__(self, plan, info, s, patch, slot, down, far=False):
-        half = (patch[0] if isinstance(patch, (list, tuple)) else patch).shape[1]
+        runs = patch if isinstance(patch, (list, tuple)) else [patch]
+        half = sum(run.shape[1] for run in runs)
         index = (1 if down is None else 1 + down) * (plan.sides + 1)
         row = info[index, 2 * slot]
         col = info[index, 2 * slot + 1]
-        self.parts = patch if isinstance(patch, (list, tuple)) else [patch.at[0:1], patch.at[1:2]]
+        self.runs = runs
         self.tile = col // LANES
         self.first = self.tile % 2
         self.from_tile = lax.broadcasted_iota(jnp.int32, (half, LANES), 1) >= col % LANES
@@ -417,7 +417,7 @@
             self.rows = (line >= jnp.where(down > 0, row, 0)) & (line < after)
 
     def lines(self, part, place):
-        values = self.parts[part][0, :, lanes(place)]
+        values = jnp.concatenate([run[part, :, lanes(place)] for run in self.runs], axis=0)
         return values if self.rows is None else jnp.where(self.rows, values, 0.0)
 
     def tiles(self, part):
@@ -440,21 +440,21 @@
 
 
 def early_sum_kernel(plan, slots, info, *rest):
-    inner, far, canvas = rest[:slots], rest[slots : 2 * slots - 1], rest[2 * slots - 1]
+    inner, near, canvas = rest[:slots], rest[slots:-1], rest[-1]
     s, _ = here()
     canvas[...] = jnp.zeros(canvas.shape, jnp.float32)
     for slot in range(slots):
         Patch(plan, info, s, inner[slot], slot, None).add_to(canvas)
+        runs = [run.at[2 * slot : 2 * slot + 2] for run in near]
+        Patch(plan, info, s, runs, slot, -far_side(s)).add_to(canvas)
+
+
+def base_kernel(plan, slots, layout, pieces, info, early, inverse, *rest):
+    far, refs, (canvas, base) = rest[: slots - 1], rest[slots - 1 : slots - 1 + pieces], rest[slots - 1 + pieces :]
+    s, t = here()
+    canvas[...] = early[...]
     for slot in range(slots - 1):
         Patch(plan, info, s, far[slot], slot, far_side(s), True).add_to(canvas)
-
-
-def base_kernel(plan, slots, layout, pieces, info, early, inverse, *rest):
-    near, refs, (canvas, base) = rest[: 2 * slots], rest[2 * slots : 2 * slots + pieces], rest[2 * slots + pieces :]
-    s, t = here()
-    canvas[...] = early[...]
-    for slot in range(slots):
-        Patch(plan, info, s, near[2 * slot : 2 * slot + 2], slot, -far_side(s)).add_to(canvas)
     for tile in range(plan.tiles):
         where = lanes(tile)
         pick_tile(plan, base.at[:, :, where], layout(refs, t)[0], tile, t)
@@ -475,27 +475,24 @@
     last.tiles_at(tile, act)
 
 
-def middle_kernel(plan, slots, info, base, patch, inverse, middle):
+def middle_kernel(plan, slots, info, base, patch, inverse, _, middle):
     _, t = here()
     last = last_patch(plan, slots, info, patch)
     for step in range(plan.mid_tiles):
         take_off(last, middle.at[:, :, lanes(step)], base, inverse, plan.mid_start(t) + step)
 
 
-def boundary_kernel(plan, slots, info, early, base, patch, inverse, _, *outs):
-    bases, sums = outs[: plan.sides], outs[plan.sides :]
+def boundary_kernel(plan, slots, info, early, patch, *sums):
     _, t = here()
     last = last_patch(plan, slots, info, patch)
-    for pair, total, start in zip(bases, sums, plan.pair_starts(t)):
+    for total, start in zip(sums, plan.pair_starts(t)):
         total[...] = early[:, :, lanes(start, 2)]
         for step in range(2):
-            part_sum = total.at[:, :, lanes(step)]
-
-            def act(part, values, part_sum=part_sum):
-                part_sum[part] += values
+
+            def act(part, values, total=total, step=step):
+                total[part, :, lanes(step)] += values
 
             last.tiles_at(start + step, act)
-            take_off(last, pair.at[:, :, lanes(step)], base, inverse, start + step)
 
 
 def halo_sum_kernel(plan, slots, info, early, patch, *sums):
@@ -619,6 +616,8 @@
     layout = first_layout
     token = spots
 
+    third = half // 24 * 8
+    near_heights = [half - 2 * third, third, third]
     for sweep in range(ITERS):
         pieces = own + far + near
         inner, outer, outer_far = [], [], []
@@ -630,7 +629,7 @@
                 lambda *refs, slot=slot, layout=layout, copied=len(earlier): term_kernel(
                     plan, slot, layout, len(pieces), copied, *refs
                 ),
-                [patch] * 2 + [shape((1, half, size), f32)] * (2 * slots * last),
+                [patch] * 2 + [shape((2 * slots, rows, size), f32) for rows in near_heights if last],
                 [pltpu.VMEM((2, size, size), f32), pltpu.VMEM((3, 3, 2, half, LANES), f32)],
                 [spots, counts, *pieces, *earlier, rolled, ordered, tables, token],
             )
@@ -639,66 +638,58 @@
             outer_far.append(plan.far_rows(outer_part))
             token = info if sweep == 0 else token
         outer_near = [plan.near_rows(copy) for copy in copies]
+        if sweep == 0:
+            inverse = call(
+                lambda *refs: light_kernel(plan, slots, *refs),
+                shape((half, width), f32),
+                [
+                    pltpu.VMEM((2 * size + 8, size), f32),
+                    pltpu.VMEM((half, width + 2 * plan.own * LANES), f32),
+                ],
+                [info, probe_field, copies[0]],
+                in_specs=[SMEM, VMEM, ANY],
+            )
         early = call(
             lambda *refs: early_sum_kernel(plan, slots, *refs),
             shape((2, half, width), f32),
             [],
-            [info, *inner, *outer_far[:-1]],
+            [info, *inner, *outer_near],
         )
-        if sweep == 0:
-            inverse, *inverse_pairs = call(
-                lambda *refs: light_kernel(plan, slots, *refs),
-                [shape((half, width), f32)] + [shape((half, 2 * LANES), f32)] * sides,
-                [
-                    pltpu.VMEM((2 * size + 8, size), f32),
-                    pltpu.VMEM((half, width + 2 * plan.own * LANES), f32),
-                ],
-                [info, probe_field, early],
-                in_specs=[SMEM, VMEM, ANY],
-            )
         early, base = call(
             lambda *refs, layout=layout: base_kernel(plan, slots, layout, len(pieces), *refs),
             [shape((2, half, width), f32)] * 2,
             [],
-            [info, early, inverse, *outer_near, *pieces],
+            [info, early, inverse, *outer_far[:-1], *pieces],
         )
         if sweep < ITERS - 1:
+            sums = call(
+                lambda *refs: boundary_kernel(plan, slots, *refs),
+                [shape((2, half, 2 * LANES), f32)] * sides,
+                [],
+                [info, early, outer_far[-1]],
+            )
+            received = plan.across(sums)
             middle = call(
                 lambda *refs: middle_kernel(plan, slots, *refs),
                 shape((2, half, plan.mid_tiles * LANES), f32),
                 [],
-                [info, base, outer_far[-1], inverse],
+                [info, base, outer_far[-1], inverse, sums[0]],
+                in_specs=[SMEM, VMEM, VMEM, VMEM, ANY],
             )
             far_middle = plan.far_rows(middle)
-            boundary = call(
-                lambda *refs: boundary_kernel(plan, slots, *refs),
-                [shape((2, half, 2 * LANES), f32)] * (2 * sides),
-                [],
-                [info, early, base, outer_far[-1], inverse, middle],
-                in_specs=[SMEM] + [VMEM] * 4 + [ANY],
-            )
-            bases, sums = boundary[:sides], boundary[sides:]
-            received = plan.across(sums)
             near_runs = [shape((2, half, count * LANES), f32) for count in chunks(plan.mid_tiles)]
             updated = call(
-                lambda *refs: pair_kernel(sides, *refs),
+                lambda *refs: pair_kernel(plan, *refs),
                 [shape((2, half, 2 * LANES), f32)] * (2 * sides) + near_runs,
                 [],
-                [middle, *bases, *received, *inverse_pairs],
+                [base, early, inverse, middle, *sums, *received],
             )
             pairs = updated[:sides]
             own = [middle] + pairs
             far = [far_middle] + [plan.far_rows(piece) for piece in pairs]
             near = [plan.near_rows(piece) for piece in updated[sides:]]
             layout = later_layout
-            token = call(
-                token_kernel,
-                shape((8, LANES), f32),
-                [],
-                [far_middle],
-                in_specs=[ANY],
-                flops=10**11,
-            )
+            token = spots
     sums = call(
         lambda *refs: halo_sum_kernel(plan, slots, *refs),
         [shape((2, half, LANES), f32)] * sides,

time: 79.5 us -> 74.5 us (0.937)
  waiting for transfers between devices: 36.1 us -> 33.8 us
  local copies, waits for them, and re-layouts: 2.69 us -> 1.74 us
  Pallas kernels: 25.5 us -> 24.7 us
  starting transfers between devices: 14.6 us -> 13.8 us
    ppermute x3, waiting for transfers between devices: 13.9 us -> 10.1 us  [across(): return [lax.ppermute(values[0], axis_name, [(0, 1), (1, 0)])]]
    ppermute x8, starting transfers between devices: 6.83 us -> 5.3 us  [far_rows(): lax.ppermute(values, ('sx', 'sy'), pairs + [(j, i) for i, j in pairs])]
    ppermute x8, waiting for transfers between devices: 20.3 us -> 21.3 us  [far_rows(): lax.ppermute(values, ('sx', 'sy'), pairs + [(j, i) for i, j in pairs])]
    unnamed x16, local copies, waits for them, and re-layouts: 2.69 us -> 1.74 us
    pallas_call x20 -> x19, Pallas kernels: 25.5 us -> 24.7 us  [call(): pl.pallas_call(kernel, out_shape=outs, in_specs=in_specs or [SMEM if valu...]
    ppermute x14 -> x12, starting transfers between devices: 3.08 us -> 3.7 us  [near_rows(): return lax.ppermute(values, 'sx', [(i, i ^ 1) for i in range(self.sx_size)])]
    ppermute x14 -> x12, waiting for transfers between devices: 1.97 us -> 2.41 us  [near_rows(): return lax.ppermute(values, 'sx', [(i, i ^ 1) for i in range(self.sx_size)])]
  transfers between devices with their start and end apart: 25 -> 23, of which waited for: 12 -> 13; matrix products, arithmetic and copies ran while one was open for 0% -> 0% of each run, Pallas kernels for 23% -> 24%
where the time goes in v10:
time: 74.5 us; the launch traced here: 74.3 us
  waiting for transfers between devices  33.8 us (45%)
  Pallas kernels  24.7 us (33%)
  starting transfers between devices  13.8 us (19%)
  local copies, waits for them, and re-layouts  1.74 us (2%)
    pallas_call x19, Pallas kernels, call(): pl.pallas_call(kernel, out_shape=outs, in_specs=in_specs or [SMEM if valu...  24.7 us
    ppermute x8, waiting for transfers between devices, far_rows(): lax.ppermute(values, ('sx', 'sy'), pairs + [(j, i) for i, j in pairs])  21.3 us
    ppermute x3, waiting for transfers between devices, across(): return [lax.ppermute(values[0], axis_name, [(0, 1), (1, 0)])]  10.1 us
    ppermute x8, starting transfers between devices, far_rows(): lax.ppermute(values, ('sx', 'sy'), pairs + [(j, i) for i, j in pairs])  5.3 us
    ppermute x3, starting transfers between devices, across(): return [lax.ppermute(values[0], axis_name, [(0, 1), (1, 0)])]  4.78 us
    ppermute x12, starting transfers between devices, near_rows(): return lax.ppermute(values, 'sx', [(i, i ^ 1) for i in range(self.sx_size)])  3.7 us
    ppermute x12, waiting for transfers between devices, near_rows(): return lax.ppermute(values, 'sx', [(i, i ^ 1) for i in range(self.sx_size)])  2.41 us
    unnamed x16, local copies, waits for them, and re-layouts  1.74 us
  transfers between devices with their start and end apart: 23, of which 13 were waited for; matrix products, arithmetic and copies ran while one was open for 0% of the time, Pallas kernels for 24%

profile of v10, /device:TPU:10, one launch (start us, length us, event | category | flops | bytes accessed | tf_op | source)
XLA Modules:
  0.0 74.3 jit_solution(12755498506494361936)
XLA Ops:
  0.7 1.0 %copy-done.1 = f32[2,128,512]{2,1,0:T(8,128)S(1)} copy-done((f32[2,128,512]{2,1,0:T(8,128)S(1)}, f32[2,128,512]{2,1,0:T(8,128)}, u32[]{:S(2)}) %copy-start.1) | copy-done | bytes 524312
  2.4 1.6 %collective-permute-start = (f32[2,136,128]{2,1,0:T(8,128)S(1)}, f32[2,136,128]{2,1,0:T(8,128)S(1)}, u32[]{:S(2)}, u32[]{:S(2)}) collective-permute-start(f32[2,136,128]{2,1,0:T(8,128)S(1)} %shard_map.73), channel_id=1, source_target_pairs={{0,1},{1,0},{2,3},{3,2},{4,5},{5,4},{6,7},{7,6},{8,9},{9,8},{10,11... | collective-permute-start | bytes 417800 | tf_op jit(solution)/shard_map/ppermute | solution.py:101
  3.9 4.4 %collective-permute-done.refs_3_ = f32[2,136,128]{2,1,0:T(8,128)S(1)} collective-permute-done((f32[2,136,128]{2,1,0:T(8,128)S(1)}, f32[2,136,128]{2,1,0:T(8,128)S(1)}, u32[]{:S(2)}, u32[]{:S(2)}) %collective-permute-start) | collective-permute-done | bytes 139296 | tf_op jit(solution)/shard_map/ppermute | solution.py:101
  8.9 0.8 %collective-permute-start.4 = (f32[2,128,256]{2,1,0:T(8,128)S(1)}, f32[2,128,256]{2,1,0:T(8,128)S(1)}, u32[]{:S(2)}, u32[]{:S(2)}) collective-permute-start(f32[2,128,256]{2,1,0:T(8,128)S(1)} %get-tuple-element.35), channel_id=1, source_target_pairs={{0,2},{2,0},{4,6},{6,4},{8,10},{10,8},{12,14},{14,12},{16,18},{18,... | collective-permute-start | bytes 786440 | tf_op jit(solution)/shard_map/ppermute | solution.py:116
  10.3 1.2 %collective-permute-start.1 = (f32[2,144,128]{2,1,0:T(8,128)S(1)}, f32[2,144,128]{2,1,0:T(8,128)S(1)}, u32[]{:S(2)}, u32[]{:S(2)}) collective-permute-start(f32[2,144,128]{2,1,0:T(8,128)S(1)} %get-tuple-element.34.refs_0_.refs_3_.refs_5_), channel_id=1, source_target_pairs={{2,4},{3,5},{6,8},{7,9},{10,12},{11,13},{14,16},{15,17},{18,20},{1... | collective-permute-start | bytes 442376 | tf_op jit(solution)/shard_map/ppermute | solution.py:113
  11.5 1.5 %shard_map.76 = (f32[2,2,256,256]{3,2,1,0:T(8,128)S(1)}, f32[2,256,256]{2,1,0:T(8,128)S(1)}) custom-call(s32[2,2]{1,0:T(2,128)S(1)} %bitcast.6, f32[2,256,256]{2,1,0:T(8,128)S(1)} %copy-done.3, f32[2,256,256]{2,1,0:T(8,128)S(1)} %bitcast.3, bf16[2,256,256]{2,1,0:T(8,128)(2,1)S(1)} %copy-done.5), custom_call_target="tpu_custom_call" | custom-call | flops 100000 | bytes 10000 | tf_op jit(solution)/shard_map/pallas_call | solution.py:540
  13.0 4.6 %collective-permute-done.1.refs_1_.refs_5_.refs_7_ = f32[2,144,128]{2,1,0:T(8,128)S(1)} collective-permute-done((f32[2,144,128]{2,1,0:T(8,128)S(1)}, f32[2,144,128]{2,1,0:T(8,128)S(1)}, u32[]{:S(2)}, u32[]{:S(2)}) %collective-permute-start.1) | collective-permute-done | bytes 147488 | tf_op jit(solution)/shard_map/ppermute | solution.py:113
  17.6 1.2 %shard_map.75.refs_13_.refs_0_ = s32[6,128]{1,0:T(8,128)S(1)} custom-call(f32[2,144,128]{2,1,0:T(8,128)S(1)} %get-tuple-element.34.refs_0_.refs_3_.refs_5_, f32[2,144,128]{2,1,0:T(8,128)S(1)} %collective-permute-done.1.refs_1_.refs_5_.refs_7_, f32[2,144,128]{2,1,0:T(8,128)S(1)} %collective-permute-done.2.refs_2_.refs_6_.refs_8_), custom_call_target="tpu_custom_call" | custom-call | flops 100000 | bytes 10000 | tf_op jit(solution)/shard_map/pallas_call | solution.py:540
  18.9 2.6 %shard_map.77 = (f32[2,128,256]{2,1,0:T(8,128)S(1)}, f32[2,128,256]{2,1,0:T(8,128)S(1)}) custom-call(s32[2,2]{1,0:T(2,128)S(1)} %bitcast.7, s32[16]{0:T(128)S(1)} %bitcast.16, f32[2,128,512]{2,1,0:T(8,128)S(1)} %copy-done.2, f32[2,144,128]{2,1,0:T(8,128)S(1)} %get-tuple-element.34.refs_0_.refs_3_.refs_5_, ...), custom_call_target="tpu_custom_call" | custom-call | flops 100000 | bytes 10000 | tf_op jit(solution)/shard_map/pallas_call | solution.py:540
  21.6 2.7 %shard_map.78 = (f32[2,128,256]{2,1,0:T(8,128)S(1)}, f32[2,128,256]{2,1,0:T(8,128)S(1)}, f32[4,48,256]{2,1,0:T(8,128)S(1)}, f32[4,40,256]{2,1,0:T(8,128)S(1)}, f32[4,40,256]{2,1,0:T(8,128)S(1)}) custom-call(s32[2,2]{1,0:T(2,128)S(1)} %bitcast.9, s32[16]{0:T(128)S(1)} %bitcast.17, f32[2,128,512]{2,1,0:T(8,128)S(1)} %copy-done.2, ...), custom_call_target="tpu_custom_call" | custom-call | flops 100000 | bytes 10000 | tf_op jit(solution)/shard_map/pallas_call | solution.py:540
  24.3 1.8 %collective-permute-start.10 = (f32[2,128,256]{2,1,0:T(8,128)S(1)}, f32[2,128,256]{2,1,0:T(8,128)S(1)}, u32[]{:S(2)}, u32[]{:S(2)}) collective-permute-start(f32[2,128,256]{2,1,0:T(8,128)S(1)} %get-tuple-element.46), channel_id=1, source_target_pairs={{2,4},{3,5},{6,8},{7,9},{10,12},{11,13},{14,16},{15,17},{18,20},{1... | collective-permute-start | bytes 786440 | tf_op jit(solution)/shard_map/ppermute | solution.py:113
  26.6 2.3 %shard_map.79.refs_2_.refs_3_.refs_0_ = f32[128,768]{1,0:T(8,128)S(1)} custom-call(s32[6,128]{1,0:T(8,128)S(1)} %shard_map.75.refs_13_.refs_0_, f32[2,256,256]{2,1,0:T(8,128)S(1)} %copy-done.3, f32[4,48,256]{2,1,0:T(8,128)S(1)} %get-tuple-element.40.refs_2_), custom_call_target="tpu_custom_call" | custom-call | flops 100000 | bytes 10000 | tf_op jit(solution)/shard_map/pallas_call | solution.py:540
  29.0 0.9 %shard_map.80.refs_1_ = f32[2,128,768]{2,1,0:T(8,128)S(1)} custom-call(s32[6,128]{1,0:T(8,128)S(1)} %shard_map.75.refs_13_.refs_0_, f32[2,128,256]{2,1,0:T(8,128)S(1)} %get-tuple-element.41.refs_1_, f32[2,128,256]{2,1,0:T(8,128)S(1)} %get-tuple-element.42.refs_2_, f32[4,48,256]{2,1,0:T(8,128)S(1)} %collective-permute-done.6.refs_3_, ...), custom_call_target="tpu_custom_call" | custom-call | flops 100000 | bytes 10000 | tf_op jit(solution)/shard_map/pallas_call | solution.py:540
  29.8 2.6 %collective-permute-done.9.refs_3_ = f32[2,128,256]{2,1,0:T(8,128)S(1)} collective-permute-done((f32[2,128,256]{2,1,0:T(8,128)S(1)}, f32[2,128,256]{2,1,0:T(8,128)S(1)}, u32[]{:S(2)}, u32[]{:S(2)}) %collective-permute-start.9) | collective-permute-done | bytes 262176 | tf_op jit(solution)/shard_map/ppermute | solution.py:113
  32.4 0.9 %shard_map.81 = (f32[2,128,768]{2,1,0:T(8,128)S(1)}, f32[2,128,768]{2,1,0:T(8,128)S(1)}) custom-call(s32[6,128]{1,0:T(8,128)S(1)} %shard_map.75.refs_13_.refs_0_, f32[2,128,768]{2,1,0:T(8,128)S(1)} %shard_map.80.refs_1_, f32[128,768]{1,0:T(8,128)S(1)} %shard_map.79.refs_2_.refs_3_.refs_0_, f32[2,128,256]{2,1,0:T(8,128)S(1)} %collective-permute-done.9.refs_3_, ...), custom_call_target="tpu_custom_call" | custom-call | flops 100000 | bytes 10000 | tf_op jit(solution)/shard_map/pallas_call | solution.py:540
  33.4 1.9 %collective-permute-done.10.refs_2_ = f32[2,128,256]{2,1,0:T(8,128)S(1)} collective-permute-done((f32[2,128,256]{2,1,0:T(8,128)S(1)}, f32[2,128,256]{2,1,0:T(8,128)S(1)}, u32[]{:S(2)}, u32[]{:S(2)}) %collective-permute-start.10) | collective-permute-done | bytes 262176 | tf_op jit(solution)/shard_map/ppermute | solution.py:113
  35.9 1.6 %collective-permute-start.11 = (f32[2,128,256]{2,1,0:T(8,128)S(1)}, f32[2,128,256]{2,1,0:T(8,128)S(1)}, u32[]{:S(2)}, u32[]{:S(2)}) collective-permute-start(f32[2,128,256]{2,1,0:T(8,128)S(1)} %shard_map.82.refs_4_), channel_id=1, source_target_pairs={{0,1},{1,0},{2,3},{3,2},{4,5},{5,4},{6,7},{7,6},{8,9},{9,8},{10,11... | collective-permute-start | bytes 786440 | tf_op jit(solution)/shard_map/ppermute | solution.py:101
  38.6 3.7 %collective-permute-done.11.refs_5_ = f32[2,128,256]{2,1,0:T(8,128)S(1)} collective-permute-done((f32[2,128,256]{2,1,0:T(8,128)S(1)}, f32[2,128,256]{2,1,0:T(8,128)S(1)}, u32[]{:S(2)}, u32[]{:S(2)}) %collective-permute-start.11) | collective-permute-done | bytes 262176 | tf_op jit(solution)/shard_map/ppermute | solution.py:101
  43.1 0.8 %collective-permute-start.16 = (f32[2,128,128]{2,1,0:T(8,128)S(1)}, f32[2,128,128]{2,1,0:T(8,128)S(1)}, u32[]{:S(2)}, u32[]{:S(2)}) collective-permute-start(f32[2,128,128]{2,1,0:T(8,128)S(1)} %get-tuple-element.51), channel_id=1, source_target_pairs={{0,2},{2,0},{4,6},{6,4},{8,10},{10,8},{12,14},{14,12},{16,18},{18,... | collective-permute-start | bytes 393224 | tf_op jit(solution)/shard_map/ppermute | solution.py:116
  43.8 1.0 %collective-permute-done.16.refs_8_.refs_10_ = f32[2,128,128]{2,1,0:T(8,128)S(1)} collective-permute-done((f32[2,128,128]{2,1,0:T(8,128)S(1)}, f32[2,128,128]{2,1,0:T(8,128)S(1)}, u32[]{:S(2)}, u32[]{:S(2)}) %collective-permute-start.16) | collective-permute-done | bytes 131104 | tf_op jit(solution)/shard_map/ppermute | solution.py:116
  45.5 6.1 %collective-permute-done.13.refs_5_.refs_7_ = f32[2,128,256]{2,1,0:T(8,128)S(1)} collective-permute-done((f32[2,128,256]{2,1,0:T(8,128)S(1)}, f32[2,128,256]{2,1,0:T(8,128)S(1)}, u32[]{:S(2)}, u32[]{:S(2)}) %collective-permute-start.13) | collective-permute-done | bytes 262176 | tf_op jit(solution)/shard_map/ppermute | solution.py:113
  51.7 2.6 %shard_map.85 = (f32[2,128,256]{2,1,0:T(8,128)S(1)}, f32[2,128,256]{2,1,0:T(8,128)S(1)}) custom-call(s32[2,2]{1,0:T(2,128)S(1)} %bitcast.10, s32[16]{0:T(128)S(1)} %bitcast.18, f32[2,128,384]{2,1,0:T(8,128)S(1)} %shard_map.83.refs_3_.refs_2_.refs_4_, f32[2,128,256]{2,1,0:T(8,128)S(1)} %get-tuple-element.48.refs_3_.refs_5_, ...), custom_call_target="tpu_custom_call" | custom-call | flops 100000 | bytes 10000 | tf_op jit(solution)/shard_map/pallas_call | solution.py:540
  54.5 2.6 %shard_map.86 = (f32[2,128,256]{2,1,0:T(8,128)S(1)}, f32[2,128,256]{2,1,0:T(8,128)S(1)}, f32[4,48,256]{2,1,0:T(8,128)S(1)}, f32[4,40,256]{2,1,0:T(8,128)S(1)}, f32[4,40,256]{2,1,0:T(8,128)S(1)}) custom-call(s32[2,2]{1,0:T(2,128)S(1)} %bitcast.12, s32[16]{0:T(128)S(1)} %bitcast.19, f32[2,128,384]{2,1,0:T(8,128)S(1)} %shard_map.83.refs_3_.refs_2_.refs_4_, ...), custom_call_target="tpu_custom_call" | custom-call | flops 100000 | bytes 10000 | tf_op jit(solution)/shard_map/pallas_call | solution.py:540
  57.2 1.6 %collective-permute-start.21 = (f32[2,128,256]{2,1,0:T(8,128)S(1)}, f32[2,128,256]{2,1,0:T(8,128)S(1)}, u32[]{:S(2)}, u32[]{:S(2)}) collective-permute-start(f32[2,128,256]{2,1,0:T(8,128)S(1)} %get-tuple-element.59), channel_id=1, source_target_pairs={{2,4},{3,5},{6,8},{7,9},{10,12},{11,13},{14,16},{15,17},{18,20},{1... | collective-permute-start | bytes 786440 | tf_op jit(solution)/shard_map/ppermute | solution.py:113
  59.3 1.2 %collective-permute-done.18.refs_4_ = f32[4,40,256]{2,1,0:T(8,128)S(1)} collective-permute-done((f32[4,40,256]{2,1,0:T(8,128)S(1)}, f32[4,40,256]{2,1,0:T(8,128)S(1)}, u32[]{:S(2)}, u32[]{:S(2)}) %collective-permute-start.18) | collective-permute-done | bytes 163872 | tf_op jit(solution)/shard_map/ppermute | solution.py:116
  60.7 0.9 %shard_map.87.refs_1_ = f32[2,128,768]{2,1,0:T(8,128)S(1)} custom-call(s32[6,128]{1,0:T(8,128)S(1)} %shard_map.75.refs_13_.refs_0_, f32[2,128,256]{2,1,0:T(8,128)S(1)} %get-tuple-element.52.refs_1_, f32[2,128,256]{2,1,0:T(8,128)S(1)} %get-tuple-element.54.refs_2_, f32[4,48,256]{2,1,0:T(8,128)S(1)} %collective-permute-done.17.refs_3_, ...), custom_call_target="tpu_custom_call" | custom-call | flops 100000 | bytes 10000 | tf_op jit(solution)/shard_map/pallas_call | solution.py:540
  61.5 3.5 %collective-permute-done.20.refs_3_ = f32[2,128,256]{2,1,0:T(8,128)S(1)} collective-permute-done((f32[2,128,256]{2,1,0:T(8,128)S(1)}, f32[2,128,256]{2,1,0:T(8,128)S(1)}, u32[]{:S(2)}, u32[]{:S(2)}) %collective-permute-start.20) | collective-permute-done | bytes 262176 | tf_op jit(solution)/shard_map/ppermute | solution.py:113
  65.1 0.9 %shard_map.88 = (f32[2,128,768]{2,1,0:T(8,128)S(1)}, f32[2,128,768]{2,1,0:T(8,128)S(1)}) custom-call(s32[6,128]{1,0:T(8,128)S(1)} %shard_map.75.refs_13_.refs_0_, f32[2,128,768]{2,1,0:T(8,128)S(1)} %shard_map.87.refs_1_, f32[128,768]{1,0:T(8,128)S(1)} %shard_map.79.refs_2_.refs_3_.refs_0_, f32[2,128,256]{2,1,0:T(8,128)S(1)} %collective-permute-done.20.refs_3_, ...), custom_call_target="tpu_custom_call" | custom-call | flops 100000 | bytes 10000 | tf_op jit(solution)/shard_map/pallas_call | solution.py:540
  66.0 1.9 %collective-permute-done.21.refs_2_ = f32[2,128,256]{2,1,0:T(8,128)S(1)} collective-permute-done((f32[2,128,256]{2,1,0:T(8,128)S(1)}, f32[2,128,256]{2,1,0:T(8,128)S(1)}, u32[]{:S(2)}, u32[]{:S(2)}) %collective-permute-start.21) | collective-permute-done | bytes 262176 | tf_op jit(solution)/shard_map/ppermute | solution.py:113
  68.6 1.6 %collective-permute-start.22 = (f32[2,128,128]{2,1,0:T(8,128)S(1)}, f32[2,128,128]{2,1,0:T(8,128)S(1)}, u32[]{:S(2)}, u32[]{:S(2)}) collective-permute-start(f32[2,128,128]{2,1,0:T(8,128)S(1)} %shard_map.89.refs_4_), channel_id=1, source_target_pairs={{0,1},{1,0},{2,3},{3,2},{4,5},{5,4},{6,7},{7,6},{8,9},{9,8},{10,11... | collective-permute-start | bytes 393224 | tf_op jit(solution)/shard_map/ppermute | solution.py:101
  70.2 1.5 %shard_map.90 = (f32[2,128,512]{2,1,0:T(8,128)}, f32[2,128,128]{2,1,0:T(8,128)S(1)}) custom-call(s32[6,128]{1,0:T(8,128)S(1)} %shard_map.75.refs_13_.refs_0_, f32[2,128,768]{2,1,0:T(8,128)S(1)} %get-tuple-element.58.refs_1_, f32[2,128,256]{2,1,0:T(8,128)S(1)} %collective-permute-done.21.refs_2_, f32[128,768]{1,0:T(8,128)S(1)} %shard_map.79.refs_2_.refs_3_.refs_0_, ...), custom_call_target="tpu_custom_call" | custom-call | flops 100000 | bytes 10000 | tf_op jit(solution)/shard_map/pallas_call | solution.py:540
  71.6 2.0 %collective-permute-done.22.refs_2_ = f32[2,128,128]{2,1,0:T(8,128)S(1)} collective-permute-done((f32[2,128,128]{2,1,0:T(8,128)S(1)}, f32[2,128,128]{2,1,0:T(8,128)S(1)}, u32[]{:S(2)}, u32[]{:S(2)}) %collective-permute-start.22) | collective-permute-done | bytes 131104 | tf_op jit(solution)/shard_map/ppermute | solution.py:101
  (49 shorter events, 8.6 us)
Async XLA Ops:
  0.0 18.9 %collective-permute-start.3 = (f32[2,128,512]{2,1,0:T(8,128)}, f32[2,128,512]{2,1,0:T(8,128)S(1)}, u32[]{:S(2)}, u32[]{:S(2)}) collective-permute-start(f32[2,128,512]{2,1,0:T(8,128)} %refs_4_.1), channel_id=1, source_target_pairs={{2,4},{3,5},{6,8},{7,9},{10,12},{11,13},{14,16},{15,17},{18,20},{1... | collective-permute-start | bytes 1572872 | tf_op jit(solution)/shard_map/ppermute | solution.py:113
  0.0 0.7 copy-start.6
  0.0 0.7 copy-start.7
  0.7 1.0 %copy-start.1 = (f32[2,128,512]{2,1,0:T(8,128)S(1)}, f32[2,128,512]{2,1,0:T(8,128)}, u32[]{:S(2)}) copy-start(f32[2,128,512]{2,1,0:T(8,128)} %refs_4_.1) | copy-start | bytes 1572868
  1.7 9.7 %copy-start.3 = (f32[2,256,256]{2,1,0:T(8,128)S(1)}, f32[2,256,256]{2,1,0:T(8,128)}, u32[]{:S(2)}) copy-start(f32[2,256,256]{2,1,0:T(8,128)} %refs_1_.1) | copy-start | bytes 1572868
  1.7 9.7 %copy-start.4 = (f32[1,1,2,256,256]{4,3,2,1,0:T(8,128)S(1)}, f32[1,1,2,256,256]{4,3,2,1,0:T(8,128)}, u32[]{:S(2)}) copy-start(f32[1,1,2,256,256]{4,3,2,1,0:T(8,128)} %param.9) | copy-start | bytes 1572868
  2.3 9.1 %copy-start.5 = (bf16[2,256,256]{2,1,0:T(8,128)(2,1)S(1)}, bf16[2,256,256]{2,1,0:T(8,128)(2,1)}, u32[]{:S(2)}) copy-start(bf16[2,256,256]{2,1,0:T(8,128)(2,1)} %constant.5.clone.order) | copy-start | bytes 786436
  2.4 6.0 %collective-permute-start = (f32[2,136,128]{2,1,0:T(8,128)S(1)}, f32[2,136,128]{2,1,0:T(8,128)S(1)}, u32[]{:S(2)}, u32[]{:S(2)}) collective-permute-start(f32[2,136,128]{2,1,0:T(8,128)S(1)} %shard_map.73), channel_id=1, source_target_pairs={{0,1},{1,0},{2,3},{3,2},{4,5},{5,4},{6,7},{7,6},{8,9},{9,8},{10,11... | collective-permute-start | bytes 417800 | tf_op jit(solution)/shard_map/ppermute | solution.py:101
  8.9 10.0 %copy-start = (bf16[2,2,2,256,256]{4,3,2,1,0:T(8,128)(2,1)S(1)}, bf16[2,2,2,256,256]{4,3,2,1,0:T(8,128)(2,1)}, u32[]{:S(2)}) copy-start(bf16[2,2,2,256,256]{4,3,2,1,0:T(8,128)(2,1)} %constant.4.clone.refs_11_.refs_12_) | copy-start | bytes 3145732
  8.9 9.9 %collective-permute-start.4 = (f32[2,128,256]{2,1,0:T(8,128)S(1)}, f32[2,128,256]{2,1,0:T(8,128)S(1)}, u32[]{:S(2)}, u32[]{:S(2)}) collective-permute-start(f32[2,128,256]{2,1,0:T(8,128)S(1)} %get-tuple-element.35), channel_id=1, source_target_pairs={{0,2},{2,0},{4,6},{6,4},{8,10},{10,8},{12,14},{14,12},{16,18},{18,... | collective-permute-start | bytes 786440 | tf_op jit(solution)/shard_map/ppermute | solution.py:116
  9.8 9.1 %collective-permute-start.5 = (f32[2,128,256]{2,1,0:T(8,128)S(1)}, f32[2,128,256]{2,1,0:T(8,128)S(1)}, u32[]{:S(2)}, u32[]{:S(2)}) collective-permute-start(f32[2,128,256]{2,1,0:T(8,128)S(1)} %get-tuple-element.36), channel_id=1, source_target_pairs={{0,2},{2,0},{4,6},{6,4},{8,10},{10,8},{12,14},{14,12},{16,18},{18,... | collective-permute-start | bytes 786440 | tf_op jit(solution)/shard_map/ppermute | solution.py:116
  9.8 3.2 %collective-permute-start.2 = (f32[2,144,128]{2,1,0:T(8,128)S(1)}, f32[2,144,128]{2,1,0:T(8,128)S(1)}, u32[]{:S(2)}, u32[]{:S(2)}) collective-permute-start(f32[2,144,128]{2,1,0:T(8,128)S(1)} %get-tuple-element.34.refs_0_.refs_3_.refs_5_), channel_id=1, source_target_pairs={{0,2},{2,0},{4,6},{6,4},{8,10},{10,8},{12,14},{14,12},{16,18},{18,... | collective-permute-start | bytes 442376 | tf_op jit(solution)/shard_map/ppermute | solution.py:116
  10.3 7.3 %collective-permute-start.1 = (f32[2,144,128]{2,1,0:T(8,128)S(1)}, f32[2,144,128]{2,1,0:T(8,128)S(1)}, u32[]{:S(2)}, u32[]{:S(2)}) collective-permute-start(f32[2,144,128]{2,1,0:T(8,128)S(1)} %get-tuple-element.34.refs_0_.refs_3_.refs_5_), channel_id=1, source_target_pairs={{2,4},{3,5},{6,8},{7,9},{10,12},{11,13},{14,16},{15,17},{18,20},{1... | collective-permute-start | bytes 442376 | tf_op jit(solution)/shard_map/ppermute | solution.py:113
  11.4 7.4 %copy-start.2 = (f32[2,128,512]{2,1,0:T(8,128)S(1)}, f32[2,128,512]{2,1,0:T(8,128)}, u32[]{:S(2)}) copy-start(f32[2,128,512]{2,1,0:T(8,128)} %refs_4_.1) | copy-start | bytes 1572868
  21.5 10.9 %collective-permute-start.9 = (f32[2,128,256]{2,1,0:T(8,128)S(1)}, f32[2,128,256]{2,1,0:T(8,128)S(1)}, u32[]{:S(2)}, u32[]{:S(2)}) collective-permute-start(f32[2,128,256]{2,1,0:T(8,128)S(1)} %get-tuple-element.39.refs_9_), channel_id=1, source_target_pairs={{2,4},{3,5},{6,8},{7,9},{10,12},{11,13},{14,16},{15,17},{18,20},{1... | collective-permute-start | bytes 786440 | tf_op jit(solution)/shard_map/ppermute | solution.py:113
  24.3 10.9 %collective-permute-start.10 = (f32[2,128,256]{2,1,0:T(8,128)S(1)}, f32[2,128,256]{2,1,0:T(8,128)S(1)}, u32[]{:S(2)}, u32[]{:S(2)}) collective-permute-start(f32[2,128,256]{2,1,0:T(8,128)S(1)} %get-tuple-element.46), channel_id=1, source_target_pairs={{2,4},{3,5},{6,8},{7,9},{10,12},{11,13},{14,16},{15,17},{18,20},{1... | collective-permute-start | bytes 786440 | tf_op jit(solution)/shard_map/ppermute | solution.py:113
  26.1 2.9 %collective-permute-start.6 = (f32[4,48,256]{2,1,0:T(8,128)S(1)}, f32[4,48,256]{2,1,0:T(8,128)S(1)}, u32[]{:S(2)}, u32[]{:S(2)}) collective-permute-start(f32[4,48,256]{2,1,0:T(8,128)S(1)} %get-tuple-element.40.refs_2_), channel_id=1, source_target_pairs={{0,2},{2,0},{4,6},{6,4},{8,10},{10,8},{12,14},{14,12},{16,18},{18,... | collective-permute-start | bytes 589832 | tf_op jit(solution)/shard_map/ppermute | solution.py:116
  26.1 2.8 %collective-permute-start.7 = (f32[4,40,256]{2,1,0:T(8,128)S(1)}, f32[4,40,256]{2,1,0:T(8,128)S(1)}, u32[]{:S(2)}, u32[]{:S(2)}) collective-permute-start(f32[4,40,256]{2,1,0:T(8,128)S(1)} %get-tuple-element.43), channel_id=1, source_target_pairs={{0,2},{2,0},{4,6},{6,4},{8,10},{10,8},{12,14},{14,12},{16,18},{18,... | collective-permute-start | bytes 491528 | tf_op jit(solution)/shard_map/ppermute | solution.py:116
  26.6 2.3 %collective-permute-start.8 = (f32[4,40,256]{2,1,0:T(8,128)S(1)}, f32[4,40,256]{2,1,0:T(8,128)S(1)}, u32[]{:S(2)}, u32[]{:S(2)}) collective-permute-start(f32[4,40,256]{2,1,0:T(8,128)S(1)} %get-tuple-element.44), channel_id=1, source_target_pairs={{0,2},{2,0},{4,6},{6,4},{8,10},{10,8},{12,14},{14,12},{16,18},{18,... | collective-permute-start | bytes 491528 | tf_op jit(solution)/shard_map/ppermute | solution.py:116
  35.9 6.4 %collective-permute-start.11 = (f32[2,128,256]{2,1,0:T(8,128)S(1)}, f32[2,128,256]{2,1,0:T(8,128)S(1)}, u32[]{:S(2)}, u32[]{:S(2)}) collective-permute-start(f32[2,128,256]{2,1,0:T(8,128)S(1)} %shard_map.82.refs_4_), channel_id=1, source_target_pairs={{0,1},{1,0},{2,3},{3,2},{4,5},{5,4},{6,7},{7,6},{8,9},{9,8},{10,11... | collective-permute-start | bytes 786440 | tf_op jit(solution)/shard_map/ppermute | solution.py:101
  38.2 7.3 %collective-permute-start.12 = (f32[2,128,384]{2,1,0:T(8,128)S(1)}, f32[2,128,384]{2,1,0:T(8,128)S(1)}, u32[]{:S(2)}, u32[]{:S(2)}) collective-permute-start(f32[2,128,384]{2,1,0:T(8,128)S(1)} %shard_map.83.refs_3_.refs_2_.refs_4_), channel_id=1, source_target_pairs={{2,4},{3,5},{6,8},{7,9},{10,12},{11,13},{14,16},{15,17},{18,20},{1... | collective-permute-start | bytes 1179656 | tf_op jit(solution)/shard_map/ppermute | solution.py:113
  42.5 3.0 %collective-permute-start.14 = (f32[2,128,256]{2,1,0:T(8,128)S(1)}, f32[2,128,256]{2,1,0:T(8,128)S(1)}, u32[]{:S(2)}, u32[]{:S(2)}) collective-permute-start(f32[2,128,256]{2,1,0:T(8,128)S(1)} %get-tuple-element.49), channel_id=1, source_target_pairs={{0,2},{2,0},{4,6},{6,4},{8,10},{10,8},{12,14},{14,12},{16,18},{18,... | collective-permute-start | bytes 786440 | tf_op jit(solution)/shard_map/ppermute | solution.py:116
  42.6 3.0 %collective-permute-start.15 = (f32[2,128,256]{2,1,0:T(8,128)S(1)}, f32[2,128,256]{2,1,0:T(8,128)S(1)}, u32[]{:S(2)}, u32[]{:S(2)}) collective-permute-start(f32[2,128,256]{2,1,0:T(8,128)S(1)} %get-tuple-element.50), channel_id=1, source_target_pairs={{0,2},{2,0},{4,6},{6,4},{8,10},{10,8},{12,14},{14,12},{16,18},{18,... | collective-permute-start | bytes 786440 | tf_op jit(solution)/shard_map/ppermute | solution.py:116
  43.1 8.6 %collective-permute-start.13 = (f32[2,128,256]{2,1,0:T(8,128)S(1)}, f32[2,128,256]{2,1,0:T(8,128)S(1)}, u32[]{:S(2)}, u32[]{:S(2)}) collective-permute-start(f32[2,128,256]{2,1,0:T(8,128)S(1)} %get-tuple-element.48.refs_3_.refs_5_), channel_id=1, source_target_pairs={{2,4},{3,5},{6,8},{7,9},{10,12},{11,13},{14,16},{15,17},{18,20},{1... | collective-permute-start | bytes 786440 | tf_op jit(solution)/shard_map/ppermute | solution.py:113
  43.1 1.8 %collective-permute-start.16 = (f32[2,128,128]{2,1,0:T(8,128)S(1)}, f32[2,128,128]{2,1,0:T(8,128)S(1)}, u32[]{:S(2)}, u32[]{:S(2)}) collective-permute-start(f32[2,128,128]{2,1,0:T(8,128)S(1)} %get-tuple-element.51), channel_id=1, source_target_pairs={{0,2},{2,0},{4,6},{6,4},{8,10},{10,8},{12,14},{14,12},{16,18},{18,... | collective-permute-start | bytes 393224 | tf_op jit(solution)/shard_map/ppermute | solution.py:116
  54.3 10.8 %collective-permute-start.20 = (f32[2,128,256]{2,1,0:T(8,128)S(1)}, f32[2,128,256]{2,1,0:T(8,128)S(1)}, u32[]{:S(2)}, u32[]{:S(2)}) collective-permute-start(f32[2,128,256]{2,1,0:T(8,128)S(1)} %get-tuple-element.53.refs_9_), channel_id=1, source_target_pairs={{2,4},{3,5},{6,8},{7,9},{10,12},{11,13},{14,16},{15,17},{18,20},{1... | collective-permute-start | bytes 786440 | tf_op jit(solution)/shard_map/ppermute | solution.py:113
  57.2 10.7 %collective-permute-start.21 = (f32[2,128,256]{2,1,0:T(8,128)S(1)}, f32[2,128,256]{2,1,0:T(8,128)S(1)}, u32[]{:S(2)}, u32[]{:S(2)}) collective-permute-start(f32[2,128,256]{2,1,0:T(8,128)S(1)} %get-tuple-element.59), channel_id=1, source_target_pairs={{2,4},{3,5},{6,8},{7,9},{10,12},{11,13},{14,16},{15,17},{18,20},{1... | collective-permute-start | bytes 786440 | tf_op jit(solution)/shard_map/ppermute | solution.py:113
  58.8 1.9 %collective-permute-start.17 = (f32[4,48,256]{2,1,0:T(8,128)S(1)}, f32[4,48,256]{2,1,0:T(8,128)S(1)}, u32[]{:S(2)}, u32[]{:S(2)}) collective-permute-start(f32[4,48,256]{2,1,0:T(8,128)S(1)} %get-tuple-element.55), channel_id=1, source_target_pairs={{0,2},{2,0},{4,6},{6,4},{8,10},{10,8},{12,14},{14,12},{16,18},{18,... | collective-permute-start | bytes 589832 | tf_op jit(solution)/shard_map/ppermute | solution.py:116
  58.8 1.7 %collective-permute-start.18 = (f32[4,40,256]{2,1,0:T(8,128)S(1)}, f32[4,40,256]{2,1,0:T(8,128)S(1)}, u32[]{:S(2)}, u32[]{:S(2)}) collective-permute-start(f32[4,40,256]{2,1,0:T(8,128)S(1)} %get-tuple-element.56), channel_id=1, source_target_pairs={{0,2},{2,0},{4,6},{6,4},{8,10},{10,8},{12,14},{14,12},{16,18},{18,... | collective-permute-start | bytes 491528 | tf_op jit(solution)/shard_map/ppermute | solution.py:116
  59.3 1.4 %collective-permute-start.19 = (f32[4,40,256]{2,1,0:T(8,128)S(1)}, f32[4,40,256]{2,1,0:T(8,128)S(1)}, u32[]{:S(2)}, u32[]{:S(2)}) collective-permute-start(f32[4,40,256]{2,1,0:T(8,128)S(1)} %get-tuple-element.57), channel_id=1, source_target_pairs={{0,2},{2,0},{4,6},{6,4},{8,10},{10,8},{12,14},{14,12},{16,18},{18,... | collective-permute-start | bytes 491528 | tf_op jit(solution)/shard_map/ppermute | solution.py:116
  68.6 5.0 %collective-permute-start.22 = (f32[2,128,128]{2,1,0:T(8,128)S(1)}, f32[2,128,128]{2,1,0:T(8,128)S(1)}, u32[]{:S(2)}, u32[]{:S(2)}) collective-permute-start(f32[2,128,128]{2,1,0:T(8,128)S(1)} %shard_map.89.refs_4_), channel_id=1, source_target_pairs={{0,1},{1,0},{2,3},{3,2},{4,5},{5,4},{6,7},{7,6},{8,9},{9,8},{10,11... | collective-permute-start | bytes 393224 | tf_op jit(solution)/shard_map/ppermute | solution.py:101

commit v11 on v10

--- a/solution.py
+++ b/solution.py
@@ -69,7 +69,8 @@
 
 
 class Plan:
-    def __init__(self, sx_size, sy_size, block_cols):
+    def __init__(self, sx_size, sy_size, block_rows, block_cols):
+        self.rows = block_rows
         self.sx_size = sx_size
         self.sy_size = sy_size
         self.own = block_cols // LANES
@@ -202,16 +203,16 @@
         copy.wait()
 
 
-def halo_message_kernel(plan, block, centres, counts, *rest):
-    s, _ = here()
-    received, messages, near = rest[: plan.sides], rest[plan.sides : 2 * plan.sides], rest[2 * plan.sides :]
-    own = info_rows(centres, counts[s])
-    for source, message in zip(received, messages):
-        rows = source.shape[1]
-        message[:, :rows] = source[...]
-        message[0, rows:] = own
-        message[1, rows:] = own
-    spread(block, near)
+def halo_message_kernel(plan, centres, counts, *rest):
+    received, far, near = (rest[k * plan.sides : (k + 1) * plan.sides] for k in range(3))
+    own = info_rows(centres, counts[lax.axis_index("sx")])
+    for source, *messages in zip(received, far, near):
+        for message in messages:
+            rows = source.shape[1]
+            message[:, :rows] = source[...]
+            for line in range(rows, message.shape[1], 8):
+                message[0, line : line + 8] = own
+                message[1, line : line + 8] = own
 
 
 def pair_kernel(plan, base, early, inverse, middle, *rest):
@@ -258,10 +259,10 @@
 
 def info_kernel(plan, *rest):
     groups = [rest[k * plan.sides : (k + 1) * plan.sides] for k in range(3)]
-    info, known, sem = rest[3 * plan.sides :]
+    _, info, known, sem = rest[3 * plan.sides :]
     s, _ = here()
     upper = s % 2 == 0
-    height = groups[0][0].shape[1] - 16
+    height = plan.rows
 
     def lines(messages):
         return [messages[0][0, height + 8 : height + 16]] + [message[0, height : height + 8] for message in messages]
@@ -311,7 +312,7 @@
 
 def term_kernel(plan, slot, layout, pieces, copied, centres, counts, *rest):
     refs, rest = rest[:pieces], rest[pieces:]
-    earlier, (probe, amps, tables, _, outer, inner), rest = rest[:copied], rest[copied : copied + 6], rest[copied + 6 :]
+    earlier, (probe, amps, tables, outer, inner), rest = rest[:copied], rest[copied : copied + 5], rest[copied + 5 :]
     near_outers, (window, picked) = rest[:-2], rest[-2:]
     size = probe.shape[2]
     half = size // 2
@@ -407,7 +408,9 @@
         self.runs = runs
         self.tile = col // LANES
         self.first = self.tile % 2
-        self.from_tile = lax.broadcasted_iota(jnp.int32, (half, LANES), 1) >= col % LANES
+        self.rest = col % LANES
+        self.lane = lax.broadcasted_iota(jnp.int32, (half, LANES), 1)
+        self.from_tile = self.lane >= self.rest
         self.rows = None
         if down is not None:
             line = lax.broadcasted_iota(jnp.int32, (half, LANES), 0)
@@ -430,13 +433,12 @@
             for step, values in enumerate(self.tiles(part)):
                 canvas[part, :, lanes(self.tile + step)] += values
 
-    def tiles_at(self, tile, act):
-        for step in range(3):
-
-            @pl.when(self.tile + step == tile)
-            def _(step=step):
-                for part in range(2):
-                    act(part, self.tiles(part)[step])
+    def at(self, part, tile):
+        step = tile - self.tile
+        first = jnp.where(step == 0, self.rest, 0)
+        after = jnp.where(step == 2, self.rest, jnp.where((step < 0) | (step > 2), 0, LANES))
+        inside = (self.lane >= first) & (self.lane < after)
+        return jnp.where(inside, self.lines(part, tile % 2), 0.0)
 
 
 def early_sum_kernel(plan, slots, info, *rest):
@@ -467,12 +469,8 @@
 
 
 def take_off(last, target, base, inverse, tile):
-    target[...] = base[:, :, lanes(tile)]
-
-    def act(part, values):
-        target[part] -= values * inverse[:, lanes(tile)]
-
-    last.tiles_at(tile, act)
+    for part in range(2):
+        target[part] = base[part, :, lanes(tile)] - last.at(part, tile) * inverse[:, lanes(tile)]
 
 
 def middle_kernel(plan, slots, info, base, patch, inverse, _, middle):
@@ -486,25 +484,17 @@
     _, t = here()
     last = last_patch(plan, slots, info, patch)
     for total, start in zip(sums, plan.pair_starts(t)):
-        total[...] = early[:, :, lanes(start, 2)]
         for step in range(2):
-
-            def act(part, values, total=total, step=step):
-                total[part, :, lanes(step)] += values
-
-            last.tiles_at(start + step, act)
+            for part in range(2):
+                total[part, :, lanes(step)] = early[part, :, lanes(start + step)] + last.at(part, start + step)
 
 
 def halo_sum_kernel(plan, slots, info, early, patch, *sums):
     _, t = here()
     last = last_patch(plan, slots, info, patch)
     for total, tile in zip(sums, plan.halo_tiles(t)):
-        total[...] = early[:, :, lanes(tile)]
-
-        def act(part, values, total=total):
-            total[part] += values
-
-        last.tiles_at(tile, act)
+        for part in range(2):
+            total[part] = early[part, :, lanes(tile)] + last.at(part, tile)
 
 
 def last_kernel(plan, slots, info, base, patch, inverse, _, *rest):
@@ -577,35 +567,27 @@
     )
     halos = plan.across(messages)
     far_block = plan.far_rows(object_field)
+    near_block = plan.near_rows(object_field)
     rolled, ordered = call(
         prepare_kernel,
         [shape((slots, 2, size, size), f32), shape((slots, size, size), f32)],
         [pltpu.VMEM((2, 2 * size + 8, size), f32)],
         [spots, probe_field, own_amps, order],
     )
-    near_runs = [shape((2, half, count * LANES), f32) for count in chunks(plan.own)]
     messages = call(
         lambda *refs: halo_message_kernel(plan, *refs),
-        [shape((2, half + 16, LANES), f32)] * sides + near_runs,
+        [shape((2, half + 24, LANES), f32)] * sides + [shape((2, half + 16, LANES), f32)] * sides,
         [],
-        [object_field, spots, counts, *halos],
+        [spots, counts, *halos],
     )
-    passed = messages[:sides]
-    far = [far_block] + [plan.far_rows(message) for message in passed]
-    near = [plan.near_rows(piece) for piece in messages]
+    passed = messages[sides:]
+    far = [far_block] + [plan.far_rows(message) for message in messages[:sides]]
+    near = [plan.near_rows(message) for message in passed] + [near_block]
     own = [object_field] + passed
-    info = call(
-        lambda *refs: info_kernel(plan, *refs),
-        shape((3 * (sides + 1), LANES), jnp.int32),
-        [pltpu.VMEM((3 * (sides + 1), 8, LANES), jnp.int32), dma],
-        passed + far[1:] + near[:sides],
-        out_specs=SMEM,
-    )
-
     def runs_layout(refs, main, count, side_starts):
         starts = [main] + side_starts
         own, far, near = refs[: 1 + sides], refs[1 + sides : 2 + 2 * sides], refs[2 + 2 * sides :]
-        return lay_out(own, starts), lay_out(far, starts), lay_out(near, side_starts + chunk_starts(main, count))
+        return lay_out(own, starts), lay_out(far, starts), lay_out(near, side_starts + (chunk_starts(main, count) if len(near) > 1 + sides else [main]))
 
     def first_layout(refs, t):
         return runs_layout(refs, 1, plan.own, plan.halo_tiles(t))
@@ -614,7 +596,6 @@
         return runs_layout(refs, plan.mid_start(t), plan.mid_tiles, plan.pair_starts(t))
 
     layout = first_layout
-    token = spots
 
     third = half // 24 * 8
     near_heights = [half - 2 * third, third, third]
@@ -631,12 +612,20 @@
                 ),
                 [patch] * 2 + [shape((2 * slots, rows, size), f32) for rows in near_heights if last],
                 [pltpu.VMEM((2, size, size), f32), pltpu.VMEM((3, 3, 2, half, LANES), f32)],
-                [spots, counts, *pieces, *earlier, rolled, ordered, tables, token],
+                [spots, counts, *pieces, *earlier, rolled, ordered, tables],
             )
             inner.append(inner_part)
             outer.append(outer_part)
             outer_far.append(plan.far_rows(outer_part))
-            token = info if sweep == 0 else token
+            if sweep == 0 and last:
+                info = call(
+                    lambda *refs: info_kernel(plan, *refs),
+                    shape((3 * (sides + 1), LANES), jnp.int32),
+                    [pltpu.VMEM((3 * (sides + 1), 8, LANES), jnp.int32), dma],
+                    passed + far[1:] + near[:sides] + [outer_part],
+                    in_specs=[VMEM] * (3 * sides) + [ANY],
+                    out_specs=SMEM,
+                )
         outer_near = [plan.near_rows(copy) for copy in copies]
         if sweep == 0:
             inverse = call(
@@ -689,7 +678,6 @@
             far = [far_middle] + [plan.far_rows(piece) for piece in pairs]
             near = [plan.near_rows(piece) for piece in updated[sides:]]
             layout = later_layout
-            token = spots
     sums = call(
         lambda *refs: halo_sum_kernel(plan, slots, *refs),
         [shape((2, half, LANES), f32)] * sides,
@@ -720,7 +708,7 @@
     sizes = dict(mesh.shape)
 
     def per_device(object_field, *rest):
-        plan = Plan(sizes["sx"], sizes["sy"], object_field.shape[2])
+        plan = Plan(sizes["sx"], sizes["sy"], *object_field.shape[1:])
         return on_device(plan, object_field, *rest)
 
     return jax.shard_map(

time: 74.5 us -> 73.8 us (level)
  Pallas kernels: 24.7 us -> 21 us
  waiting for transfers between devices: 33.8 us -> 30.2 us
  starting transfers between devices: 13.8 us -> 17.3 us
  local copies, waits for them, and re-layouts: 1.74 us -> 4.77 us
    ppermute x8, waiting for transfers between devices: 21.3 us -> 16.7 us  [far_rows(): lax.ppermute(values, ('sx', 'sy'), pairs + [(j, i) for i, j in pairs])]
    pallas_call x19, Pallas kernels: 24.7 us -> 21 us  [call(): pl.pallas_call(kernel, out_shape=outs, in_specs=in_specs or [SMEM if valu...]
    ppermute x8, starting transfers between devices: 5.3 us -> 8.5 us  [far_rows(): lax.ppermute(values, ('sx', 'sy'), pairs + [(j, i) for i, j in pairs])]
    unnamed x16 -> x18, local copies, waits for them, and re-layouts: 1.74 us -> 4.77 us
    ppermute x3, waiting for transfers between devices: 10.1 us -> 11.1 us  [across(): return [lax.ppermute(values[0], axis_name, [(0, 1), (1, 0)])]]
    ppermute x12 -> x11, starting transfers between devices: 3.7 us -> 4.15 us  [near_rows(): return lax.ppermute(values, 'sx', [(i, i ^ 1) for i in range(self.sx_size)])]
    ppermute x12 -> x11, waiting for transfers between devices: 2.41 us -> 2.4 us  [near_rows(): return lax.ppermute(values, 'sx', [(i, i ^ 1) for i in range(self.sx_size)])]
  transfers between devices with their start and end apart: 23 -> 22, of which waited for: 13 -> 13; matrix products, arithmetic and copies ran while one was open for 0% -> 0% of each run, Pallas kernels for 24% -> 19%
where the time goes in v11:
time: 73.8 us; the launch traced here: 73.5 us
  waiting for transfers between devices  30.2 us (41%)
  Pallas kernels  21 us (28%)
  starting transfers between devices  17.3 us (23%)
  local copies, waits for them, and re-layouts  4.77 us (6%)
    pallas_call x19, Pallas kernels, call(): pl.pallas_call(kernel, out_shape=outs, in_specs=in_specs or [SMEM if valu...  21 us
    ppermute x8, waiting for transfers between devices, far_rows(): lax.ppermute(values, ('sx', 'sy'), pairs + [(j, i) for i, j in pairs])  16.7 us
    ppermute x3, waiting for transfers between devices, across(): return [lax.ppermute(values[0], axis_name, [(0, 1), (1, 0)])]  11.1 us
    ppermute x8, starting transfers between devices, far_rows(): lax.ppermute(values, ('sx', 'sy'), pairs + [(j, i) for i, j in pairs])  8.5 us
    unnamed x18, local copies, waits for them, and re-layouts  4.77 us
    ppermute x3, starting transfers between devices, across(): return [lax.ppermute(values[0], axis_name, [(0, 1), (1, 0)])]  4.69 us
    ppermute x11, starting transfers between devices, near_rows(): return lax.ppermute(values, 'sx', [(i, i ^ 1) for i in range(self.sx_size)])  4.15 us
    ppermute x11, waiting for transfers between devices, near_rows(): return lax.ppermute(values, 'sx', [(i, i ^ 1) for i in range(self.sx_size)])  2.4 us
  transfers between devices with their start and end apart: 22, of which 13 were waited for; matrix products, arithmetic and copies ran while one was open for 0% of the time, Pallas kernels for 19%

profile of v11, /device:TPU:10, one launch (start us, length us, event | category | flops | bytes accessed | tf_op | source)
XLA Modules:
  0.0 73.5 jit_solution(4209277136348040205)
XLA Ops:
  1.3 1.0 %copy-done.1 = f32[2,128,512]{2,1,0:T(8,128)S(1)} copy-done((f32[2,128,512]{2,1,0:T(8,128)S(1)}, f32[2,128,512]{2,1,0:T(8,128)}, u32[]{:S(2)}) %copy-start.1) | copy-done | bytes 524312
  3.0 1.6 %collective-permute-start = (f32[2,136,128]{2,1,0:T(8,128)S(1)}, f32[2,136,128]{2,1,0:T(8,128)S(1)}, u32[]{:S(2)}, u32[]{:S(2)}) collective-permute-start(f32[2,136,128]{2,1,0:T(8,128)S(1)} %shard_map.73), channel_id=1, source_target_pairs={{0,1},{1,0},{2,3},{3,2},{4,5},{5,4},{6,7},{7,6},{8,9},{9,8},{10,11... | collective-permute-start | bytes 417800 | tf_op jit(solution)/shard_map/ppermute | solution.py:102
  4.6 5.0 %collective-permute-done.refs_2_ = f32[2,136,128]{2,1,0:T(8,128)S(1)} collective-permute-done((f32[2,136,128]{2,1,0:T(8,128)S(1)}, f32[2,136,128]{2,1,0:T(8,128)S(1)}, u32[]{:S(2)}, u32[]{:S(2)}) %collective-permute-start) | collective-permute-done | bytes 139296 | tf_op jit(solution)/shard_map/ppermute | solution.py:102
  10.2 1.7 %collective-permute-start.2 = (f32[2,144,128]{2,1,0:T(8,128)S(1)}, f32[2,144,128]{2,1,0:T(8,128)S(1)}, u32[]{:S(2)}, u32[]{:S(2)}) collective-permute-start(f32[2,144,128]{2,1,0:T(8,128)S(1)} %get-tuple-element.33.refs_3_.refs_0_.refs_5_), channel_id=1, source_target_pairs={{0,2},{2,0},{4,6},{6,4},{8,10},{10,8},{12,14},{14,12},{16,18},{18,... | collective-permute-start | bytes 442376 | tf_op jit(solution)/shard_map/ppermute | solution.py:117
  11.9 1.0 %copy-done.3 = f32[2,256,256]{2,1,0:T(8,128)S(1)} copy-done((f32[2,256,256]{2,1,0:T(8,128)S(1)}, f32[2,256,256]{2,1,0:T(8,128)}, u32[]{:S(2)}) %copy-start.3) | copy-done | bytes 524312
  12.9 1.0 %copy-done.5 = f32[1,1,2,256,256]{4,3,2,1,0:T(8,128)S(1)} copy-done((f32[1,1,2,256,256]{4,3,2,1,0:T(8,128)S(1)}, f32[1,1,2,256,256]{4,3,2,1,0:T(8,128)}, u32[]{:S(2)}) %copy-start.5) | copy-done | bytes 524312
  14.0 0.9 %copy-done.6 = bf16[2,256,256]{2,1,0:T(8,128)(2,1)S(1)} copy-done((bf16[2,256,256]{2,1,0:T(8,128)(2,1)S(1)}, bf16[2,256,256]{2,1,0:T(8,128)(2,1)}, u32[]{:S(2)}) %copy-start.6) | copy-done | bytes 262168
  14.9 1.5 %shard_map.75 = (f32[2,2,256,256]{3,2,1,0:T(8,128)S(1)}, f32[2,256,256]{2,1,0:T(8,128)S(1)}) custom-call(s32[2,2]{1,0:T(2,128)S(1)} %bitcast.6, f32[2,256,256]{2,1,0:T(8,128)S(1)} %copy-done.3, f32[2,256,256]{2,1,0:T(8,128)S(1)} %bitcast.3, bf16[2,256,256]{2,1,0:T(8,128)(2,1)S(1)} %copy-done.6), custom_call_target="tpu_custom_call" | custom-call | flops 100000 | bytes 10000 | tf_op jit(solution)/shard_map/pallas_call | solution.py:530
  16.5 1.3 %collective-permute-done.1.refs_5_.refs_1_.refs_7_ = f32[2,152,128]{2,1,0:T(8,128)S(1)} collective-permute-done((f32[2,152,128]{2,1,0:T(8,128)S(1)}, f32[2,152,128]{2,1,0:T(8,128)S(1)}, u32[]{:S(2)}, u32[]{:S(2)}) %collective-permute-start.1) | collective-permute-done | bytes 155680 | tf_op jit(solution)/shard_map/ppermute | solution.py:114
  17.8 2.6 %shard_map.76 = (f32[2,128,256]{2,1,0:T(8,128)S(1)}, f32[2,128,256]{2,1,0:T(8,128)S(1)}) custom-call(s32[2,2]{1,0:T(2,128)S(1)} %bitcast.7, s32[16]{0:T(128)S(1)} %bitcast.13, f32[2,128,512]{2,1,0:T(8,128)S(1)} %copy-done.2, f32[2,144,128]{2,1,0:T(8,128)S(1)} %get-tuple-element.33.refs_3_.refs_0_.refs_5_, ...), custom_call_target="tpu_custom_call" | custom-call | flops 100000 | bytes 10000 | tf_op jit(solution)/shard_map/pallas_call | solution.py:530
  21.8 3.2 %collective-permute-start.9 = (f32[2,128,256]{2,1,0:T(8,128)S(1)}, f32[2,128,256]{2,1,0:T(8,128)S(1)}, u32[]{:S(2)}, u32[]{:S(2)}) collective-permute-start(f32[2,128,256]{2,1,0:T(8,128)S(1)} %get-tuple-element.38.refs_3_), channel_id=1, source_target_pairs={{2,4},{3,5},{6,8},{7,9},{10,12},{11,13},{14,16},{15,17},{18,20},{1... | collective-permute-start | bytes 786440 | tf_op jit(solution)/shard_map/ppermute | solution.py:114
  25.5 1.2 %shard_map.78.refs_0_ = s32[6,128]{1,0:T(8,128)S(1)} custom-call(f32[2,144,128]{2,1,0:T(8,128)S(1)} %get-tuple-element.33.refs_3_.refs_0_.refs_5_, f32[2,152,128]{2,1,0:T(8,128)S(1)} %collective-permute-done.1.refs_5_.refs_1_.refs_7_, f32[2,144,128]{2,1,0:T(8,128)S(1)} %collective-permute-done.2.refs_6_.refs_2_.refs_8_, ...), custom_call_target="tpu_custom_call" | custom-call | flops 100000 | bytes 10000 | tf_op jit(solution)/shard_map/pallas_call | solution.py:530
  26.7 2.6 %shard_map.79.refs_2_.refs_3_.refs_0_ = f32[128,768]{1,0:T(8,128)S(1)} custom-call(s32[6,128]{1,0:T(8,128)S(1)} %shard_map.78.refs_0_, f32[2,256,256]{2,1,0:T(8,128)S(1)} %copy-done.4, f32[4,48,256]{2,1,0:T(8,128)S(1)} %get-tuple-element.39.refs_2_), custom_call_target="tpu_custom_call" | custom-call | flops 100000 | bytes 10000 | tf_op jit(solution)/shard_map/pallas_call | solution.py:530
  29.4 0.9 %shard_map.80.refs_1_ = f32[2,128,768]{2,1,0:T(8,128)S(1)} custom-call(s32[6,128]{1,0:T(8,128)S(1)} %shard_map.78.refs_0_, f32[2,128,256]{2,1,0:T(8,128)S(1)} %get-tuple-element.40.refs_1_, f32[2,128,256]{2,1,0:T(8,128)S(1)} %get-tuple-element.41.refs_2_, f32[4,48,256]{2,1,0:T(8,128)S(1)} %collective-permute-done.5.refs_3_, ...), custom_call_target="tpu_custom_call" | custom-call | flops 100000 | bytes 10000 | tf_op jit(solution)/shard_map/pallas_call | solution.py:530
  30.3 1.5 %collective-permute-done.8.refs_3_ = f32[2,128,256]{2,1,0:T(8,128)S(1)} collective-permute-done((f32[2,128,256]{2,1,0:T(8,128)S(1)}, f32[2,128,256]{2,1,0:T(8,128)S(1)}, u32[]{:S(2)}, u32[]{:S(2)}) %collective-permute-start.8) | collective-permute-done | bytes 262176 | tf_op jit(solution)/shard_map/ppermute | solution.py:114
  31.7 0.9 %shard_map.81 = (f32[2,128,768]{2,1,0:T(8,128)S(1)}, f32[2,128,768]{2,1,0:T(8,128)S(1)}) custom-call(s32[6,128]{1,0:T(8,128)S(1)} %shard_map.78.refs_0_, f32[2,128,768]{2,1,0:T(8,128)S(1)} %shard_map.80.refs_1_, f32[128,768]{1,0:T(8,128)S(1)} %shard_map.79.refs_2_.refs_3_.refs_0_, f32[2,128,256]{2,1,0:T(8,128)S(1)} %collective-permute-done.8.refs_3_, ...), custom_call_target="tpu_custom_call" | custom-call | flops 100000 | bytes 10000 | tf_op jit(solution)/shard_map/pallas_call | solution.py:530
  32.7 1.9 %collective-permute-done.9.refs_2_ = f32[2,128,256]{2,1,0:T(8,128)S(1)} collective-permute-done((f32[2,128,256]{2,1,0:T(8,128)S(1)}, f32[2,128,256]{2,1,0:T(8,128)S(1)}, u32[]{:S(2)}, u32[]{:S(2)}) %collective-permute-start.9) | collective-permute-done | bytes 262176 | tf_op jit(solution)/shard_map/ppermute | solution.py:114
  35.2 1.6 %collective-permute-start.10 = (f32[2,128,256]{2,1,0:T(8,128)S(1)}, f32[2,128,256]{2,1,0:T(8,128)S(1)}, u32[]{:S(2)}, u32[]{:S(2)}) collective-permute-start(f32[2,128,256]{2,1,0:T(8,128)S(1)} %shard_map.82.refs_4_), channel_id=1, source_target_pairs={{0,1},{1,0},{2,3},{3,2},{4,5},{5,4},{6,7},{7,6},{8,9},{9,8},{10,11... | collective-permute-start | bytes 786440 | tf_op jit(solution)/shard_map/ppermute | solution.py:102
  37.5 4.1 %collective-permute-done.10.refs_5_ = f32[2,128,256]{2,1,0:T(8,128)S(1)} collective-permute-done((f32[2,128,256]{2,1,0:T(8,128)S(1)}, f32[2,128,256]{2,1,0:T(8,128)S(1)}, u32[]{:S(2)}, u32[]{:S(2)}) %collective-permute-start.10) | collective-permute-done | bytes 262176 | tf_op jit(solution)/shard_map/ppermute | solution.py:102
  42.4 0.9 %collective-permute-start.15 = (f32[2,128,128]{2,1,0:T(8,128)S(1)}, f32[2,128,128]{2,1,0:T(8,128)S(1)}, u32[]{:S(2)}, u32[]{:S(2)}) collective-permute-start(f32[2,128,128]{2,1,0:T(8,128)S(1)} %get-tuple-element.49), channel_id=1, source_target_pairs={{0,2},{2,0},{4,6},{6,4},{8,10},{10,8},{12,14},{14,12},{16,18},{18,... | collective-permute-start | bytes 393224 | tf_op jit(solution)/shard_map/ppermute | solution.py:117
  43.2 1.0 %collective-permute-done.15.refs_8_.refs_10_ = f32[2,128,128]{2,1,0:T(8,128)S(1)} collective-permute-done((f32[2,128,128]{2,1,0:T(8,128)S(1)}, f32[2,128,128]{2,1,0:T(8,128)S(1)}, u32[]{:S(2)}, u32[]{:S(2)}) %collective-permute-start.15) | collective-permute-done | bytes 131104 | tf_op jit(solution)/shard_map/ppermute | solution.py:117
  44.2 5.6 %collective-permute-done.11.refs_4_.refs_6_ = f32[2,128,384]{2,1,0:T(8,128)S(1)} collective-permute-done((f32[2,128,384]{2,1,0:T(8,128)S(1)}, f32[2,128,384]{2,1,0:T(8,128)S(1)}, u32[]{:S(2)}, u32[]{:S(2)}) %collective-permute-start.11) | collective-permute-done | bytes 393248 | tf_op jit(solution)/shard_map/ppermute | solution.py:114
  49.8 2.8 %collective-permute-done.12.refs_5_.refs_7_ = f32[2,128,256]{2,1,0:T(8,128)S(1)} collective-permute-done((f32[2,128,256]{2,1,0:T(8,128)S(1)}, f32[2,128,256]{2,1,0:T(8,128)S(1)}, u32[]{:S(2)}, u32[]{:S(2)}) %collective-permute-start.12) | collective-permute-done | bytes 262176 | tf_op jit(solution)/shard_map/ppermute | solution.py:114
  52.6 2.6 %shard_map.85 = (f32[2,128,256]{2,1,0:T(8,128)S(1)}, f32[2,128,256]{2,1,0:T(8,128)S(1)}) custom-call(s32[2,2]{1,0:T(2,128)S(1)} %bitcast.9, s32[16]{0:T(128)S(1)} %bitcast.15, f32[2,128,384]{2,1,0:T(8,128)S(1)} %shard_map.83.refs_3_.refs_2_.refs_4_, f32[2,128,256]{2,1,0:T(8,128)S(1)} %get-tuple-element.46.refs_3_.refs_5_, ...), custom_call_target="tpu_custom_call" | custom-call | flops 100000 | bytes 10000 | tf_op jit(solution)/shard_map/pallas_call | solution.py:530
  56.0 3.7 %collective-permute-start.20 = (f32[2,128,256]{2,1,0:T(8,128)S(1)}, f32[2,128,256]{2,1,0:T(8,128)S(1)}, u32[]{:S(2)}, u32[]{:S(2)}) collective-permute-start(f32[2,128,256]{2,1,0:T(8,128)S(1)} %get-tuple-element.57), channel_id=1, source_target_pairs={{2,4},{3,5},{6,8},{7,9},{10,12},{11,13},{14,16},{15,17},{18,20},{1... | collective-permute-start | bytes 786440 | tf_op jit(solution)/shard_map/ppermute | solution.py:114
  60.2 1.2 %collective-permute-done.17.refs_4_ = f32[4,40,256]{2,1,0:T(8,128)S(1)} collective-permute-done((f32[4,40,256]{2,1,0:T(8,128)S(1)}, f32[4,40,256]{2,1,0:T(8,128)S(1)}, u32[]{:S(2)}, u32[]{:S(2)}) %collective-permute-start.17) | collective-permute-done | bytes 163872 | tf_op jit(solution)/shard_map/ppermute | solution.py:117
  62.5 1.9 %collective-permute-done.19.refs_3_ = f32[2,128,256]{2,1,0:T(8,128)S(1)} collective-permute-done((f32[2,128,256]{2,1,0:T(8,128)S(1)}, f32[2,128,256]{2,1,0:T(8,128)S(1)}, u32[]{:S(2)}, u32[]{:S(2)}) %collective-permute-start.19) | collective-permute-done | bytes 262176 | tf_op jit(solution)/shard_map/ppermute | solution.py:114
  64.3 0.9 %shard_map.88 = (f32[2,128,768]{2,1,0:T(8,128)S(1)}, f32[2,128,768]{2,1,0:T(8,128)S(1)}) custom-call(s32[6,128]{1,0:T(8,128)S(1)} %shard_map.78.refs_0_, f32[2,128,768]{2,1,0:T(8,128)S(1)} %shard_map.87.refs_1_, f32[128,768]{1,0:T(8,128)S(1)} %shard_map.79.refs_2_.refs_3_.refs_0_, f32[2,128,256]{2,1,0:T(8,128)S(1)} %collective-permute-done.19.refs_3_, ...), custom_call_target="tpu_custom_call" | custom-call | flops 100000 | bytes 10000 | tf_op jit(solution)/shard_map/pallas_call | solution.py:530
  65.3 1.9 %collective-permute-done.20.refs_2_ = f32[2,128,256]{2,1,0:T(8,128)S(1)} collective-permute-done((f32[2,128,256]{2,1,0:T(8,128)S(1)}, f32[2,128,256]{2,1,0:T(8,128)S(1)}, u32[]{:S(2)}, u32[]{:S(2)}) %collective-permute-start.20) | collective-permute-done | bytes 262176 | tf_op jit(solution)/shard_map/ppermute | solution.py:114
  67.8 1.6 %collective-permute-start.21 = (f32[2,128,128]{2,1,0:T(8,128)S(1)}, f32[2,128,128]{2,1,0:T(8,128)S(1)}, u32[]{:S(2)}, u32[]{:S(2)}) collective-permute-start(f32[2,128,128]{2,1,0:T(8,128)S(1)} %shard_map.89.refs_4_), channel_id=1, source_target_pairs={{0,1},{1,0},{2,3},{3,2},{4,5},{5,4},{6,7},{7,6},{8,9},{9,8},{10,11... | collective-permute-start | bytes 393224 | tf_op jit(solution)/shard_map/ppermute | solution.py:102
  69.4 1.5 %shard_map.90 = (f32[2,128,512]{2,1,0:T(8,128)}, f32[2,128,128]{2,1,0:T(8,128)S(1)}) custom-call(s32[6,128]{1,0:T(8,128)S(1)} %shard_map.78.refs_0_, f32[2,128,768]{2,1,0:T(8,128)S(1)} %get-tuple-element.56.refs_1_, f32[2,128,256]{2,1,0:T(8,128)S(1)} %collective-permute-done.20.refs_2_, f32[128,768]{1,0:T(8,128)S(1)} %shard_map.79.refs_2_.refs_3_.refs_0_, ...), custom_call_target="tpu_custom_call" | custom-call | flops 100000 | bytes 10000 | tf_op jit(solution)/shard_map/pallas_call | solution.py:530
  70.8 2.0 %collective-permute-done.21.refs_2_ = f32[2,128,128]{2,1,0:T(8,128)S(1)} collective-permute-done((f32[2,128,128]{2,1,0:T(8,128)S(1)}, f32[2,128,128]{2,1,0:T(8,128)S(1)}, u32[]{:S(2)}, u32[]{:S(2)}) %collective-permute-start.21) | collective-permute-done | bytes 131104 | tf_op jit(solution)/shard_map/ppermute | solution.py:102
  (49 shorter events, 10.3 us)
Async XLA Ops:
  0.0 17.8 %collective-permute-start.4 = (f32[2,128,512]{2,1,0:T(8,128)}, f32[2,128,512]{2,1,0:T(8,128)S(1)}, u32[]{:S(2)}, u32[]{:S(2)}) collective-permute-start(f32[2,128,512]{2,1,0:T(8,128)} %refs_4_.1), channel_id=1, source_target_pairs={{0,2},{2,0},{4,6},{6,4},{8,10},{10,8},{12,14},{14,12},{16,18},{18,... | collective-permute-start | bytes 1572872 | tf_op jit(solution)/shard_map/ppermute | solution.py:117
  0.0 17.8 %collective-permute-start.3 = (f32[2,128,512]{2,1,0:T(8,128)}, f32[2,128,512]{2,1,0:T(8,128)S(1)}, u32[]{:S(2)}, u32[]{:S(2)}) collective-permute-start(f32[2,128,512]{2,1,0:T(8,128)} %refs_4_.1), channel_id=1, source_target_pairs={{2,4},{3,5},{6,8},{7,9},{10,12},{11,13},{14,16},{15,17},{18,20},{1... | collective-permute-start | bytes 1572872 | tf_op jit(solution)/shard_map/ppermute | solution.py:114
  0.7 0.7 copy-start.7
  0.7 0.7 copy-start.8
  1.3 1.0 %copy-start.1 = (f32[2,128,512]{2,1,0:T(8,128)S(1)}, f32[2,128,512]{2,1,0:T(8,128)}, u32[]{:S(2)}) copy-start(f32[2,128,512]{2,1,0:T(8,128)} %refs_4_.1) | copy-start | bytes 1572868
  2.4 15.4 %copy-start = (bf16[2,2,2,256,256]{4,3,2,1,0:T(8,128)(2,1)S(1)}, bf16[2,2,2,256,256]{4,3,2,1,0:T(8,128)(2,1)}, u32[]{:S(2)}) copy-start(bf16[2,2,2,256,256]{4,3,2,1,0:T(8,128)(2,1)} %constant.4.clone.refs_10_.refs_11_.refs_12_) | copy-start | bytes 3145732
  3.0 6.6 %collective-permute-start = (f32[2,136,128]{2,1,0:T(8,128)S(1)}, f32[2,136,128]{2,1,0:T(8,128)S(1)}, u32[]{:S(2)}, u32[]{:S(2)}) collective-permute-start(f32[2,136,128]{2,1,0:T(8,128)S(1)} %shard_map.73), channel_id=1, source_target_pairs={{0,1},{1,0},{2,3},{3,2},{4,5},{5,4},{6,7},{7,6},{8,9},{9,8},{10,11... | collective-permute-start | bytes 417800 | tf_op jit(solution)/shard_map/ppermute | solution.py:102
  10.1 7.6 %collective-permute-start.1 = (f32[2,152,128]{2,1,0:T(8,128)S(1)}, f32[2,152,128]{2,1,0:T(8,128)S(1)}, u32[]{:S(2)}, u32[]{:S(2)}) collective-permute-start(f32[2,152,128]{2,1,0:T(8,128)S(1)} %get-tuple-element.34), channel_id=1, source_target_pairs={{2,4},{3,5},{6,8},{7,9},{10,12},{11,13},{14,16},{15,17},{18,20},{1... | collective-permute-start | bytes 466952 | tf_op jit(solution)/shard_map/ppermute | solution.py:114
  10.2 6.3 %collective-permute-start.2 = (f32[2,144,128]{2,1,0:T(8,128)S(1)}, f32[2,144,128]{2,1,0:T(8,128)S(1)}, u32[]{:S(2)}, u32[]{:S(2)}) collective-permute-start(f32[2,144,128]{2,1,0:T(8,128)S(1)} %get-tuple-element.33.refs_3_.refs_0_.refs_5_), channel_id=1, source_target_pairs={{0,2},{2,0},{4,6},{6,4},{8,10},{10,8},{12,14},{14,12},{16,18},{18,... | collective-permute-start | bytes 442376 | tf_op jit(solution)/shard_map/ppermute | solution.py:117
  11.9 1.0 %copy-start.3 = (f32[2,256,256]{2,1,0:T(8,128)S(1)}, f32[2,256,256]{2,1,0:T(8,128)}, u32[]{:S(2)}) copy-start(f32[2,256,256]{2,1,0:T(8,128)} %refs_1_.1) | copy-start | bytes 1572868
  12.9 1.0 %copy-start.5 = (f32[1,1,2,256,256]{4,3,2,1,0:T(8,128)S(1)}, f32[1,1,2,256,256]{4,3,2,1,0:T(8,128)}, u32[]{:S(2)}) copy-start(f32[1,1,2,256,256]{4,3,2,1,0:T(8,128)} %param.9) | copy-start | bytes 1572868
  14.0 0.9 %copy-start.6 = (bf16[2,256,256]{2,1,0:T(8,128)(2,1)S(1)}, bf16[2,256,256]{2,1,0:T(8,128)(2,1)}, u32[]{:S(2)}) copy-start(bf16[2,256,256]{2,1,0:T(8,128)(2,1)} %constant.5.clone.order) | copy-start | bytes 786436
  14.9 2.9 %copy-start.2 = (f32[2,128,512]{2,1,0:T(8,128)S(1)}, f32[2,128,512]{2,1,0:T(8,128)}, u32[]{:S(2)}) copy-start(f32[2,128,512]{2,1,0:T(8,128)} %refs_4_.1) | copy-start | bytes 1572868
  20.4 11.3 %collective-permute-start.8 = (f32[2,128,256]{2,1,0:T(8,128)S(1)}, f32[2,128,256]{2,1,0:T(8,128)S(1)}, u32[]{:S(2)}, u32[]{:S(2)}) collective-permute-start(f32[2,128,256]{2,1,0:T(8,128)S(1)} %get-tuple-element.37.refs_8_), channel_id=1, source_target_pairs={{2,4},{3,5},{6,8},{7,9},{10,12},{11,13},{14,16},{15,17},{18,20},{1... | collective-permute-start | bytes 786440 | tf_op jit(solution)/shard_map/ppermute | solution.py:114
  21.8 5.0 %copy-start.4 = (f32[2,256,256]{2,1,0:T(8,128)S(1)}, f32[2,256,256]{2,1,0:T(8,128)}, u32[]{:S(2)}) copy-start(f32[2,256,256]{2,1,0:T(8,128)} %refs_1_.1) | copy-start | bytes 1572868
  21.8 12.7 %collective-permute-start.9 = (f32[2,128,256]{2,1,0:T(8,128)S(1)}, f32[2,128,256]{2,1,0:T(8,128)S(1)}, u32[]{:S(2)}, u32[]{:S(2)}) collective-permute-start(f32[2,128,256]{2,1,0:T(8,128)S(1)} %get-tuple-element.38.refs_3_), channel_id=1, source_target_pairs={{2,4},{3,5},{6,8},{7,9},{10,12},{11,13},{14,16},{15,17},{18,20},{1... | collective-permute-start | bytes 786440 | tf_op jit(solution)/shard_map/ppermute | solution.py:114
  24.9 4.4 %collective-permute-start.5 = (f32[4,48,256]{2,1,0:T(8,128)S(1)}, f32[4,48,256]{2,1,0:T(8,128)S(1)}, u32[]{:S(2)}, u32[]{:S(2)}) collective-permute-start(f32[4,48,256]{2,1,0:T(8,128)S(1)} %get-tuple-element.39.refs_2_), channel_id=1, source_target_pairs={{0,2},{2,0},{4,6},{6,4},{8,10},{10,8},{12,14},{14,12},{16,18},{18,... | collective-permute-start | bytes 589832 | tf_op jit(solution)/shard_map/ppermute | solution.py:117
  24.9 4.4 %collective-permute-start.6 = (f32[4,40,256]{2,1,0:T(8,128)S(1)}, f32[4,40,256]{2,1,0:T(8,128)S(1)}, u32[]{:S(2)}, u32[]{:S(2)}) collective-permute-start(f32[4,40,256]{2,1,0:T(8,128)S(1)} %get-tuple-element.42), channel_id=1, source_target_pairs={{0,2},{2,0},{4,6},{6,4},{8,10},{10,8},{12,14},{14,12},{16,18},{18,... | collective-permute-start | bytes 491528 | tf_op jit(solution)/shard_map/ppermute | solution.py:117
  25.5 3.9 %collective-permute-start.7 = (f32[4,40,256]{2,1,0:T(8,128)S(1)}, f32[4,40,256]{2,1,0:T(8,128)S(1)}, u32[]{:S(2)}, u32[]{:S(2)}) collective-permute-start(f32[4,40,256]{2,1,0:T(8,128)S(1)} %get-tuple-element.43), channel_id=1, source_target_pairs={{0,2},{2,0},{4,6},{6,4},{8,10},{10,8},{12,14},{14,12},{16,18},{18,... | collective-permute-start | bytes 491528 | tf_op jit(solution)/shard_map/ppermute | solution.py:117
  35.2 6.4 %collective-permute-start.10 = (f32[2,128,256]{2,1,0:T(8,128)S(1)}, f32[2,128,256]{2,1,0:T(8,128)S(1)}, u32[]{:S(2)}, u32[]{:S(2)}) collective-permute-start(f32[2,128,256]{2,1,0:T(8,128)S(1)} %shard_map.82.refs_4_), channel_id=1, source_target_pairs={{0,1},{1,0},{2,3},{3,2},{4,5},{5,4},{6,7},{7,6},{8,9},{9,8},{10,11... | collective-permute-start | bytes 786440 | tf_op jit(solution)/shard_map/ppermute | solution.py:102
  37.5 12.4 %collective-permute-start.11 = (f32[2,128,384]{2,1,0:T(8,128)S(1)}, f32[2,128,384]{2,1,0:T(8,128)S(1)}, u32[]{:S(2)}, u32[]{:S(2)}) collective-permute-start(f32[2,128,384]{2,1,0:T(8,128)S(1)} %shard_map.83.refs_3_.refs_2_.refs_4_), channel_id=1, source_target_pairs={{2,4},{3,5},{6,8},{7,9},{10,12},{11,13},{14,16},{15,17},{18,20},{1... | collective-permute-start | bytes 1179656 | tf_op jit(solution)/shard_map/ppermute | solution.py:114
  41.7 8.1 %collective-permute-start.13 = (f32[2,128,256]{2,1,0:T(8,128)S(1)}, f32[2,128,256]{2,1,0:T(8,128)S(1)}, u32[]{:S(2)}, u32[]{:S(2)}) collective-permute-start(f32[2,128,256]{2,1,0:T(8,128)S(1)} %get-tuple-element.47), channel_id=1, source_target_pairs={{0,2},{2,0},{4,6},{6,4},{8,10},{10,8},{12,14},{14,12},{16,18},{18,... | collective-permute-start | bytes 786440 | tf_op jit(solution)/shard_map/ppermute | solution.py:117
  41.8 8.0 %collective-permute-start.14 = (f32[2,128,256]{2,1,0:T(8,128)S(1)}, f32[2,128,256]{2,1,0:T(8,128)S(1)}, u32[]{:S(2)}, u32[]{:S(2)}) collective-permute-start(f32[2,128,256]{2,1,0:T(8,128)S(1)} %get-tuple-element.48), channel_id=1, source_target_pairs={{0,2},{2,0},{4,6},{6,4},{8,10},{10,8},{12,14},{14,12},{16,18},{18,... | collective-permute-start | bytes 786440 | tf_op jit(solution)/shard_map/ppermute | solution.py:117
  42.3 10.3 %collective-permute-start.12 = (f32[2,128,256]{2,1,0:T(8,128)S(1)}, f32[2,128,256]{2,1,0:T(8,128)S(1)}, u32[]{:S(2)}, u32[]{:S(2)}) collective-permute-start(f32[2,128,256]{2,1,0:T(8,128)S(1)} %get-tuple-element.46.refs_3_.refs_5_), channel_id=1, source_target_pairs={{2,4},{3,5},{6,8},{7,9},{10,12},{11,13},{14,16},{15,17},{18,20},{1... | collective-permute-start | bytes 786440 | tf_op jit(solution)/shard_map/ppermute | solution.py:114
  42.4 1.9 %collective-permute-start.15 = (f32[2,128,128]{2,1,0:T(8,128)S(1)}, f32[2,128,128]{2,1,0:T(8,128)S(1)}, u32[]{:S(2)}, u32[]{:S(2)}) collective-permute-start(f32[2,128,128]{2,1,0:T(8,128)S(1)} %get-tuple-element.49), channel_id=1, source_target_pairs={{0,2},{2,0},{4,6},{6,4},{8,10},{10,8},{12,14},{14,12},{16,18},{18,... | collective-permute-start | bytes 393224 | tf_op jit(solution)/shard_map/ppermute | solution.py:117
  55.2 9.1 %collective-permute-start.19 = (f32[2,128,256]{2,1,0:T(8,128)S(1)}, f32[2,128,256]{2,1,0:T(8,128)S(1)}, u32[]{:S(2)}, u32[]{:S(2)}) collective-permute-start(f32[2,128,256]{2,1,0:T(8,128)S(1)} %get-tuple-element.51.refs_9_), channel_id=1, source_target_pairs={{2,4},{3,5},{6,8},{7,9},{10,12},{11,13},{14,16},{15,17},{18,20},{1... | collective-permute-start | bytes 786440 | tf_op jit(solution)/shard_map/ppermute | solution.py:114
  56.0 11.2 %collective-permute-start.20 = (f32[2,128,256]{2,1,0:T(8,128)S(1)}, f32[2,128,256]{2,1,0:T(8,128)S(1)}, u32[]{:S(2)}, u32[]{:S(2)}) collective-permute-start(f32[2,128,256]{2,1,0:T(8,128)S(1)} %get-tuple-element.57), channel_id=1, source_target_pairs={{2,4},{3,5},{6,8},{7,9},{10,12},{11,13},{14,16},{15,17},{18,20},{1... | collective-permute-start | bytes 786440 | tf_op jit(solution)/shard_map/ppermute | solution.py:114
  59.7 1.9 %collective-permute-start.16 = (f32[4,48,256]{2,1,0:T(8,128)S(1)}, f32[4,48,256]{2,1,0:T(8,128)S(1)}, u32[]{:S(2)}, u32[]{:S(2)}) collective-permute-start(f32[4,48,256]{2,1,0:T(8,128)S(1)} %get-tuple-element.53), channel_id=1, source_target_pairs={{0,2},{2,0},{4,6},{6,4},{8,10},{10,8},{12,14},{14,12},{16,18},{18,... | collective-permute-start | bytes 589832 | tf_op jit(solution)/shard_map/ppermute | solution.py:117
  59.7 1.7 %collective-permute-start.17 = (f32[4,40,256]{2,1,0:T(8,128)S(1)}, f32[4,40,256]{2,1,0:T(8,128)S(1)}, u32[]{:S(2)}, u32[]{:S(2)}) collective-permute-start(f32[4,40,256]{2,1,0:T(8,128)S(1)} %get-tuple-element.54), channel_id=1, source_target_pairs={{0,2},{2,0},{4,6},{6,4},{8,10},{10,8},{12,14},{14,12},{16,18},{18,... | collective-permute-start | bytes 491528 | tf_op jit(solution)/shard_map/ppermute | solution.py:117
  60.2 1.4 %collective-permute-start.18 = (f32[4,40,256]{2,1,0:T(8,128)S(1)}, f32[4,40,256]{2,1,0:T(8,128)S(1)}, u32[]{:S(2)}, u32[]{:S(2)}) collective-permute-start(f32[4,40,256]{2,1,0:T(8,128)S(1)} %get-tuple-element.55), channel_id=1, source_target_pairs={{0,2},{2,0},{4,6},{6,4},{8,10},{10,8},{12,14},{14,12},{16,18},{18,... | collective-permute-start | bytes 491528 | tf_op jit(solution)/shard_map/ppermute | solution.py:117
  67.8 5.0 %collective-permute-start.21 = (f32[2,128,128]{2,1,0:T(8,128)S(1)}, f32[2,128,128]{2,1,0:T(8,128)S(1)}, u32[]{:S(2)}, u32[]{:S(2)}) collective-permute-start(f32[2,128,128]{2,1,0:T(8,128)S(1)} %shard_map.89.refs_4_), channel_id=1, source_target_pairs={{0,1},{1,0},{2,3},{3,2},{4,5},{5,4},{6,7},{7,6},{8,9},{9,8},{10,11... | collective-permute-start | bytes 393224 | tf_op jit(solution)/shard_map/ppermute | solution.py:102

commit v12 on v11

--- a/solution.py
+++ b/solution.py
@@ -203,9 +203,10 @@
         copy.wait()
 
 
-def halo_message_kernel(plan, centres, counts, *rest):
+def halo_message_kernel(plan, centres, counts, _, *rest):
     received, far, near = (rest[k * plan.sides : (k + 1) * plan.sides] for k in range(3))
     own = info_rows(centres, counts[lax.axis_index("sx")])
+    rest[-1][...] = own
     for source, *messages in zip(received, far, near):
         for message in messages:
             rows = source.shape[1]
@@ -310,16 +311,17 @@
     inverse[...] = 1.0 / (canvas[:, lanes(plan.own, plan.tiles)] + DAMPING)
 
 
-def term_kernel(plan, slot, layout, pieces, copied, centres, counts, *rest):
+def term_kernel(plan, slot, layout, pieces, copied, slots, spot, *rest):
     refs, rest = rest[:pieces], rest[pieces:]
     earlier, (probe, amps, tables, outer, inner), rest = rest[:copied], rest[copied : copied + 5], rest[copied + 5 :]
     near_outers, (window, picked) = rest[:-2], rest[-2:]
     size = probe.shape[2]
     half = size // 2
     s, t = here()
-    row = centres[slot, 0]
-    col = centres[slot, 1]
-    alive = slot < counts[s]
+    line = spot[0:1]
+    lane = lax.broadcasted_iota(jnp.int32, line.shape, 1)
+    row, col, count = (jnp.sum(jnp.where(lane == k, line, 0.0)).astype(jnp.int32) for k in (2 * slot, 2 * slot + 1, 2 * slots))
+    alive = slot < count
 
     @pl.when(jnp.logical_not(alive))
     def _():
@@ -433,12 +435,18 @@
             for step, values in enumerate(self.tiles(part)):
                 canvas[part, :, lanes(self.tile + step)] += values
 
-    def at(self, part, tile):
+    def mask(self, tile):
         step = tile - self.tile
         first = jnp.where(step == 0, self.rest, 0)
         after = jnp.where(step == 2, self.rest, jnp.where((step < 0) | (step > 2), 0, LANES))
         inside = (self.lane >= first) & (self.lane < after)
-        return jnp.where(inside, self.lines(part, tile % 2), 0.0)
+        if self.rows is not None:
+            inside = inside & self.rows
+        return jnp.where(inside, 1.0, 0.0)
+
+
+def part_of(patch, mask, part, tile):
+    return patch[part, :, lanes(tile % 2)] * mask[:, lanes(tile)]
 
 
 def early_sum_kernel(plan, slots, info, *rest):
@@ -452,59 +460,53 @@
 
 
 def base_kernel(plan, slots, layout, pieces, info, early, inverse, *rest):
-    far, refs, (canvas, base) = rest[: slots - 1], rest[slots - 1 : slots - 1 + pieces], rest[slots - 1 + pieces :]
+    far, refs, (canvas, base, mask) = rest[: slots - 1], rest[slots - 1 : slots - 1 + pieces], rest[slots - 1 + pieces :]
     s, t = here()
     canvas[...] = early[...]
     for slot in range(slots - 1):
         Patch(plan, info, s, far[slot], slot, far_side(s), True).add_to(canvas)
+    last = Patch(plan, info, s, canvas, slots - 1, far_side(s), True)
     for tile in range(plan.tiles):
         where = lanes(tile)
         pick_tile(plan, base.at[:, :, where], layout(refs, t)[0], tile, t)
         base[:, :, where] -= canvas[:, :, where] * inverse[:, where][None]
-
-
-def last_patch(plan, slots, info, patch):
-    s, _ = here()
-    return Patch(plan, info, s, patch, slots - 1, far_side(s), True)
-
-
-def take_off(last, target, base, inverse, tile):
+        mask[:, where] = last.mask(tile)
+
+
+def take_off(patch, mask, target, base, inverse, tile):
     for part in range(2):
-        target[part] = base[part, :, lanes(tile)] - last.at(part, tile) * inverse[:, lanes(tile)]
-
-
-def middle_kernel(plan, slots, info, base, patch, inverse, _, middle):
+        target[part] = base[part, :, lanes(tile)] - part_of(patch, mask, part, tile) * inverse[:, lanes(tile)]
+
+
+def middle_kernel(plan, base, patch, mask, inverse, _, middle):
     _, t = here()
-    last = last_patch(plan, slots, info, patch)
     for step in range(plan.mid_tiles):
-        take_off(last, middle.at[:, :, lanes(step)], base, inverse, plan.mid_start(t) + step)
-
-
-def boundary_kernel(plan, slots, info, early, patch, *sums):
+        take_off(patch, mask, middle.at[:, :, lanes(step)], base, inverse, plan.mid_start(t) + step)
+
+
+def boundary_kernel(plan, early, patch, mask, *sums):
     _, t = here()
-    last = last_patch(plan, slots, info, patch)
     for total, start in zip(sums, plan.pair_starts(t)):
         for step in range(2):
+            tile = start + step
             for part in range(2):
-                total[part, :, lanes(step)] = early[part, :, lanes(start + step)] + last.at(part, start + step)
-
-
-def halo_sum_kernel(plan, slots, info, early, patch, *sums):
+                total[part, :, lanes(step)] = early[part, :, lanes(tile)] + part_of(patch, mask, part, tile)
+
+
+def halo_sum_kernel(plan, early, patch, mask, *sums):
     _, t = here()
-    last = last_patch(plan, slots, info, patch)
     for total, tile in zip(sums, plan.halo_tiles(t)):
         for part in range(2):
-            total[part] = early[part, :, lanes(tile)] + last.at(part, tile)
-
-
-def last_kernel(plan, slots, info, base, patch, inverse, _, *rest):
+            total[part] = early[part, :, lanes(tile)] + part_of(patch, mask, part, tile)
+
+
+def last_kernel(plan, base, patch, mask, inverse, _, *rest):
     nearly, bases, (current, sems) = rest[0], rest[1 : 1 + plan.sides], rest[1 + plan.sides :]
     _, t = here()
-    last = last_patch(plan, slots, info, patch)
     copies = []
     for step in range(plan.own):
         where = lanes(step)
-        take_off(last, current.at[:, :, where], base, inverse, 1 + step)
+        take_off(patch, mask, current.at[:, :, where], base, inverse, 1 + step)
         copies.append(pltpu.make_async_copy(current.at[:, :, where], nearly.at[:, :, where], sems.at[step]))
         copies[-1].start()
     for edge, tile in zip(bases, plan.edge_tiles(t)):
@@ -576,11 +578,12 @@
     )
     messages = call(
         lambda *refs: halo_message_kernel(plan, *refs),
-        [shape((2, half + 24, LANES), f32)] * sides + [shape((2, half + 16, LANES), f32)] * sides,
+        [shape((2, half + 24, LANES), f32)] * sides + [shape((2, half + 16, LANES), f32)] * sides + [shape((8, LANES), f32)],
         [],
-        [spots, counts, *halos],
+        [spots, counts, ordered, *halos],
+        in_specs=[SMEM, SMEM, ANY] + [VMEM] * sides,
     )
-    passed = messages[sides:]
+    passed, own_spot = messages[sides:-1], messages[-1]
     far = [far_block] + [plan.far_rows(message) for message in messages[:sides]]
     near = [plan.near_rows(message) for message in passed] + [near_block]
     own = [object_field] + passed
@@ -608,11 +611,11 @@
             patch = shape((2, half, size), f32)
             outer_part, inner_part, *copies = call(
                 lambda *refs, slot=slot, layout=layout, copied=len(earlier): term_kernel(
-                    plan, slot, layout, len(pieces), copied, *refs
+                    plan, slot, layout, len(pieces), copied, slots, *refs
                 ),
                 [patch] * 2 + [shape((2 * slots, rows, size), f32) for rows in near_heights if last],
                 [pltpu.VMEM((2, size, size), f32), pltpu.VMEM((3, 3, 2, half, LANES), f32)],
-                [spots, counts, *pieces, *earlier, rolled, ordered, tables],
+                [own_spot, *pieces, *earlier, rolled, ordered, tables],
             )
             inner.append(inner_part)
             outer.append(outer_part)
@@ -644,26 +647,26 @@
             [],
             [info, *inner, *outer_near],
         )
-        early, base = call(
+        early, base, mask = call(
             lambda *refs, layout=layout: base_kernel(plan, slots, layout, len(pieces), *refs),
-            [shape((2, half, width), f32)] * 2,
+            [shape((2, half, width), f32)] * 2 + [shape((half, width), f32)],
             [],
             [info, early, inverse, *outer_far[:-1], *pieces],
         )
         if sweep < ITERS - 1:
             sums = call(
-                lambda *refs: boundary_kernel(plan, slots, *refs),
+                lambda *refs: boundary_kernel(plan, *refs),
                 [shape((2, half, 2 * LANES), f32)] * sides,
                 [],
-                [info, early, outer_far[-1]],
+                [early, outer_far[-1], mask],
             )
             received = plan.across(sums)
             middle = call(
-                lambda *refs: middle_kernel(plan, slots, *refs),
+                lambda *refs: middle_kernel(plan, *refs),
                 shape((2, half, plan.mid_tiles * LANES), f32),
                 [],
-                [info, base, outer_far[-1], inverse, sums[0]],
-                in_specs=[SMEM, VMEM, VMEM, VMEM, ANY],
+                [base, outer_far[-1], mask, inverse, sums[0]],
+                in_specs=[VMEM] * 4 + [ANY],
             )
             far_middle = plan.far_rows(middle)
             near_runs = [shape((2, half, count * LANES), f32) for count in chunks(plan.mid_tiles)]
@@ -679,17 +682,17 @@
             near = [plan.near_rows(piece) for piece in updated[sides:]]
             layout = later_layout
     sums = call(
-        lambda *refs: halo_sum_kernel(plan, slots, *refs),
+        lambda *refs: halo_sum_kernel(plan, *refs),
         [shape((2, half, LANES), f32)] * sides,
         [],
-        [info, early, outer_far[-1]],
+        [early, outer_far[-1], mask],
     )
     nearly, *bases = call(
-        lambda *refs: last_kernel(plan, slots, *refs),
+        lambda *refs: last_kernel(plan, *refs),
         [shape((2, half, block_cols), f32)] + [shape((2, half, LANES), f32)] * sides,
         [pltpu.VMEM((2, half, block_cols), f32), dma((plan.own,))],
-        [info, base, outer_far[-1], inverse, sums[0]],
-        in_specs=[SMEM, VMEM, VMEM, VMEM, ANY],
+        [base, outer_far[-1], mask, inverse, sums[0]],
+        in_specs=[VMEM] * 4 + [ANY],
         out_specs=[HBM] + [VMEM] * sides,
     )
     received = plan.across(sums)

time: 73.8 us -> 71.2 us (0.965)
  starting transfers between devices: 17.3 us -> 13.7 us
  waiting for transfers between devices: 30.2 us -> 32.5 us
  local copies, waits for them, and re-layouts: 4.77 us -> 3.73 us
    ppermute x8, waiting for transfers between devices: 16.7 us -> 20.3 us  [far_rows(): lax.ppermute(values, ('sx', 'sy'), pairs + [(j, i) for i, j in pairs])]
    ppermute x8, starting transfers between devices: 8.5 us -> 5.23 us  [far_rows(): lax.ppermute(values, ('sx', 'sy'), pairs + [(j, i) for i, j in pairs])]
    ppermute x3, waiting for transfers between devices: 11.1 us -> 8.77 us  [across(): return [lax.ppermute(values[0], axis_name, [(0, 1), (1, 0)])]]
    unnamed x18 -> x16, local copies, waits for them, and re-layouts: 4.77 us -> 3.73 us
    ppermute x11, waiting for transfers between devices: 2.4 us -> 3.41 us  [near_rows(): return lax.ppermute(values, 'sx', [(i, i ^ 1) for i in range(self.sx_size)])]
  transfers between devices with their start and end apart: 22 -> 22, of which waited for: 13 -> 14; matrix products, arithmetic and copies ran while one was open for 0% -> 0% of each run, Pallas kernels for 19% -> 22%
where the time goes in v12:
time: 71.2 us; the launch traced here: 70.9 us
  waiting for transfers between devices  32.5 us (46%)
  Pallas kernels  20.8 us (29%)
  starting transfers between devices  13.7 us (19%)
  local copies, waits for them, and re-layouts  3.73 us (5%)
    pallas_call x19, Pallas kernels, call(): pl.pallas_call(kernel, out_shape=outs, in_specs=in_specs or [SMEM if valu...  20.8 us
    ppermute x8, waiting for transfers between devices, far_rows(): lax.ppermute(values, ('sx', 'sy'), pairs + [(j, i) for i, j in pairs])  20.3 us
    ppermute x3, waiting for transfers between devices, across(): return [lax.ppermute(values[0], axis_name, [(0, 1), (1, 0)])]  8.77 us
    ppermute x8, starting transfers between devices, far_rows(): lax.ppermute(values, ('sx', 'sy'), pairs + [(j, i) for i, j in pairs])  5.23 us
    ppermute x3, starting transfers between devices, across(): return [lax.ppermute(values[0], axis_name, [(0, 1), (1, 0)])]  4.7 us
    ppermute x11, starting transfers between devices, near_rows(): return lax.ppermute(values, 'sx', [(i, i ^ 1) for i in range(self.sx_size)])  3.75 us
    unnamed x16, local copies, waits for them, and re-layouts  3.73 us
    ppermute x11, waiting for transfers between devices, near_rows(): return lax.ppermute(values, 'sx', [(i, i ^ 1) for i in range(self.sx_size)])  3.41 us
  transfers between devices with their start and end apart: 22, of which 14 were waited for; matrix products, arithmetic and copies ran while one was open for 0% of the time, Pallas kernels for 22%

profile of v12, /device:TPU:10, one launch (start us, length us, event | category | flops | bytes accessed | tf_op | source)
XLA Modules:
  0.0 70.9 jit_solution(13743307515039694925)
XLA Ops:
  1.3 1.0 %copy-done.1 = f32[2,128,512]{2,1,0:T(8,128)S(1)} copy-done((f32[2,128,512]{2,1,0:T(8,128)S(1)}, f32[2,128,512]{2,1,0:T(8,128)}, u32[]{:S(2)}) %copy-start.1) | copy-done | bytes 524312
  3.0 1.6 %collective-permute-start = (f32[2,136,128]{2,1,0:T(8,128)S(1)}, f32[2,136,128]{2,1,0:T(8,128)S(1)}, u32[]{:S(2)}, u32[]{:S(2)}) collective-permute-start(f32[2,136,128]{2,1,0:T(8,128)S(1)} %shard_map.74), channel_id=1, source_target_pairs={{0,1},{1,0},{2,3},{3,2},{4,5},{5,4},{6,7},{7,6},{8,9},{9,8},{10,11... | collective-permute-start | bytes 417800 | tf_op jit(solution)/shard_map/ppermute | solution.py:102
  4.6 1.0 %copy-done.4 = f32[1,1,2,256,256]{4,3,2,1,0:T(8,128)S(1)} copy-done((f32[1,1,2,256,256]{4,3,2,1,0:T(8,128)S(1)}, f32[1,1,2,256,256]{4,3,2,1,0:T(8,128)}, u32[]{:S(2)}) %copy-start.4) | copy-done | bytes 524312
  5.6 0.9 %copy-done.5 = bf16[2,256,256]{2,1,0:T(8,128)(2,1)S(1)} copy-done((bf16[2,256,256]{2,1,0:T(8,128)(2,1)S(1)}, bf16[2,256,256]{2,1,0:T(8,128)(2,1)}, u32[]{:S(2)}) %copy-start.5) | copy-done | bytes 262168
  6.6 1.5 %shard_map.73 = (f32[2,2,256,256]{3,2,1,0:T(8,128)S(1)}, f32[2,256,256]{2,1,0:T(8,128)S(1)}) custom-call(s32[2,2]{1,0:T(2,128)S(1)} %bitcast.5, f32[2,256,256]{2,1,0:T(8,128)S(1)} %copy-done.3, f32[2,256,256]{2,1,0:T(8,128)S(1)} %bitcast.3, bf16[2,256,256]{2,1,0:T(8,128)(2,1)S(1)} %copy-done.5), custom_call_target="tpu_custom_call" | custom-call | flops 100000 | bytes 10000 | tf_op jit(solution)/shard_map/pallas_call | solution.py:532
  8.1 1.4 %collective-permute-done.refs_3_ = f32[2,136,128]{2,1,0:T(8,128)S(1)} collective-permute-done((f32[2,136,128]{2,1,0:T(8,128)S(1)}, f32[2,136,128]{2,1,0:T(8,128)S(1)}, u32[]{:S(2)}, u32[]{:S(2)}) %collective-permute-start) | collective-permute-done | bytes 139296 | tf_op jit(solution)/shard_map/ppermute | solution.py:102
  10.2 1.7 %collective-permute-start.2 = (f32[2,144,128]{2,1,0:T(8,128)S(1)}, f32[2,144,128]{2,1,0:T(8,128)S(1)}, u32[]{:S(2)}, u32[]{:S(2)}) collective-permute-start(f32[2,144,128]{2,1,0:T(8,128)S(1)} %get-tuple-element.37.refs_2_.refs_0_.refs_5_), channel_id=1, source_target_pairs={{0,2},{2,0},{4,6},{6,4},{8,10},{10,8},{12,14},{14,12},{16,18},{18,... | collective-permute-start | bytes 442376 | tf_op jit(solution)/shard_map/ppermute | solution.py:117
  11.9 1.0 %collective-permute-done.2.refs_5_.refs_2_.refs_8_ = f32[2,144,128]{2,1,0:T(8,128)S(1)} collective-permute-done((f32[2,144,128]{2,1,0:T(8,128)S(1)}, f32[2,144,128]{2,1,0:T(8,128)S(1)}, u32[]{:S(2)}, u32[]{:S(2)}) %collective-permute-start.2) | collective-permute-done | bytes 147488 | tf_op jit(solution)/shard_map/ppermute | solution.py:117
  12.9 4.9 %collective-permute-done.1.refs_4_.refs_1_.refs_7_ = f32[2,152,128]{2,1,0:T(8,128)S(1)} collective-permute-done((f32[2,152,128]{2,1,0:T(8,128)S(1)}, f32[2,152,128]{2,1,0:T(8,128)S(1)}, u32[]{:S(2)}, u32[]{:S(2)}) %collective-permute-start.1) | collective-permute-done | bytes 155680 | tf_op jit(solution)/shard_map/ppermute | solution.py:114
  17.8 2.1 %shard_map.76 = (f32[2,128,256]{2,1,0:T(8,128)S(1)}, f32[2,128,256]{2,1,0:T(8,128)S(1)}) custom-call(f32[8,128]{1,0:T(8,128)S(1)} %get-tuple-element.39.refs_0_, f32[2,128,512]{2,1,0:T(8,128)S(1)} %copy-done.2, f32[2,144,128]{2,1,0:T(8,128)S(1)} %get-tuple-element.37.refs_2_.refs_0_.refs_5_, f32[2,128,512]{2,1,0:T(8,128)S(1)} %collective-permute-done.3.refs_3_.refs_6_, ...), custom_call_target="tpu_custom_call" | custom-call | flops 100000 | bytes 10000 | tf_op jit(solution)/shard_map/pallas_call | solution.py:532
  20.7 2.2 %shard_map.77 = (f32[2,128,256]{2,1,0:T(8,128)S(1)}, f32[2,128,256]{2,1,0:T(8,128)S(1)}, f32[4,48,256]{2,1,0:T(8,128)S(1)}, f32[4,40,256]{2,1,0:T(8,128)S(1)}, f32[4,40,256]{2,1,0:T(8,128)S(1)}) custom-call(f32[8,128]{1,0:T(8,128)S(1)} %get-tuple-element.39.refs_0_, f32[2,128,512]{2,1,0:T(8,128)S(1)} %copy-done.2, ...), custom_call_target="tpu_custom_call" | custom-call | flops 100000 | bytes 10000 | tf_op jit(solution)/shard_map/pallas_call | solution.py:532
  22.9 1.2 %collective-permute-start.9 = (f32[2,128,256]{2,1,0:T(8,128)S(1)}, f32[2,128,256]{2,1,0:T(8,128)S(1)}, u32[]{:S(2)}, u32[]{:S(2)}) collective-permute-start(f32[2,128,256]{2,1,0:T(8,128)S(1)} %get-tuple-element.42.refs_3_), channel_id=1, source_target_pairs={{2,4},{3,5},{6,8},{7,9},{10,12},{11,13},{14,16},{15,17},{18,20},{1... | collective-permute-start | bytes 786440 | tf_op jit(solution)/shard_map/ppermute | solution.py:114
  24.5 1.2 %shard_map.78.refs_0_ = s32[6,128]{1,0:T(8,128)S(1)} custom-call(f32[2,144,128]{2,1,0:T(8,128)S(1)} %get-tuple-element.37.refs_2_.refs_0_.refs_5_, f32[2,152,128]{2,1,0:T(8,128)S(1)} %collective-permute-done.1.refs_4_.refs_1_.refs_7_, f32[2,144,128]{2,1,0:T(8,128)S(1)} %collective-permute-done.2.refs_5_.refs_2_.refs_8_, ...), custom_call_target="tpu_custom_call" | custom-call | flops 100000 | bytes 10000 | tf_op jit(solution)/shard_map/pallas_call | solution.py:532
  25.8 2.8 %shard_map.79.refs_2_.refs_3_.refs_0_ = f32[128,768]{1,0:T(8,128)S(1)} custom-call(s32[6,128]{1,0:T(8,128)S(1)} %shard_map.78.refs_0_, f32[2,256,256]{2,1,0:T(8,128)S(1)} %copy-done.3, f32[4,48,256]{2,1,0:T(8,128)S(1)} %get-tuple-element.43.refs_2_), custom_call_target="tpu_custom_call" | custom-call | flops 100000 | bytes 10000 | tf_op jit(solution)/shard_map/pallas_call | solution.py:532
  28.6 0.9 %shard_map.80.refs_1_ = f32[2,128,768]{2,1,0:T(8,128)S(1)} custom-call(s32[6,128]{1,0:T(8,128)S(1)} %shard_map.78.refs_0_, f32[2,128,256]{2,1,0:T(8,128)S(1)} %get-tuple-element.44.refs_1_, f32[2,128,256]{2,1,0:T(8,128)S(1)} %get-tuple-element.45.refs_2_, f32[4,48,256]{2,1,0:T(8,128)S(1)} %collective-permute-done.5.refs_3_, ...), custom_call_target="tpu_custom_call" | custom-call | flops 100000 | bytes 10000 | tf_op jit(solution)/shard_map/pallas_call | solution.py:532
  29.5 1.3 %collective-permute-done.8.refs_3_ = f32[2,128,256]{2,1,0:T(8,128)S(1)} collective-permute-done((f32[2,128,256]{2,1,0:T(8,128)S(1)}, f32[2,128,256]{2,1,0:T(8,128)S(1)}, u32[]{:S(2)}, u32[]{:S(2)}) %collective-permute-start.8) | collective-permute-done | bytes 262176 | tf_op jit(solution)/shard_map/ppermute | solution.py:114
  30.8 1.0 %shard_map.81 = (f32[2,128,768]{2,1,0:T(8,128)S(1)}, f32[2,128,768]{2,1,0:T(8,128)S(1)}, f32[128,768]{1,0:T(8,128)S(1)}) custom-call(s32[6,128]{1,0:T(8,128)S(1)} %shard_map.78.refs_0_, f32[2,128,768]{2,1,0:T(8,128)S(1)} %shard_map.80.refs_1_, f32[128,768]{1,0:T(8,128)S(1)} %shard_map.79.refs_2_.refs_3_.refs_0_, ...), custom_call_target="tpu_custom_call" | custom-call | flops 100000 | bytes 10000 | tf_op jit(solution)/shard_map/pallas_call | solution.py:532
  31.8 1.8 %collective-permute-done.9.refs_1_ = f32[2,128,256]{2,1,0:T(8,128)S(1)} collective-permute-done((f32[2,128,256]{2,1,0:T(8,128)S(1)}, f32[2,128,256]{2,1,0:T(8,128)S(1)}, u32[]{:S(2)}, u32[]{:S(2)}) %collective-permute-start.9) | collective-permute-done | bytes 262176 | tf_op jit(solution)/shard_map/ppermute | solution.py:114
  33.7 1.6 %collective-permute-start.10 = (f32[2,128,256]{2,1,0:T(8,128)S(1)}, f32[2,128,256]{2,1,0:T(8,128)S(1)}, u32[]{:S(2)}, u32[]{:S(2)}) collective-permute-start(f32[2,128,256]{2,1,0:T(8,128)S(1)} %shard_map.82.refs_4_), channel_id=1, source_target_pairs={{0,1},{1,0},{2,3},{3,2},{4,5},{5,4},{6,7},{7,6},{8,9},{9,8},{10,11... | collective-permute-start | bytes 786440 | tf_op jit(solution)/shard_map/ppermute | solution.py:102
  35.4 4.7 %collective-permute-done.10.refs_5_ = f32[2,128,256]{2,1,0:T(8,128)S(1)} collective-permute-done((f32[2,128,256]{2,1,0:T(8,128)S(1)}, f32[2,128,256]{2,1,0:T(8,128)S(1)}, u32[]{:S(2)}, u32[]{:S(2)}) %collective-permute-start.10) | collective-permute-done | bytes 262176 | tf_op jit(solution)/shard_map/ppermute | solution.py:102
  41.9 1.0 %collective-permute-done.15.refs_7_.refs_10_ = f32[2,128,128]{2,1,0:T(8,128)S(1)} collective-permute-done((f32[2,128,128]{2,1,0:T(8,128)S(1)}, f32[2,128,128]{2,1,0:T(8,128)S(1)}, u32[]{:S(2)}, u32[]{:S(2)}) %collective-permute-start.15) | collective-permute-done | bytes 131104 | tf_op jit(solution)/shard_map/ppermute | solution.py:117
  42.9 3.3 %collective-permute-done.11.refs_3_.refs_6_ = f32[2,128,384]{2,1,0:T(8,128)S(1)} collective-permute-done((f32[2,128,384]{2,1,0:T(8,128)S(1)}, f32[2,128,384]{2,1,0:T(8,128)S(1)}, u32[]{:S(2)}, u32[]{:S(2)}) %collective-permute-start.11) | collective-permute-done | bytes 393248 | tf_op jit(solution)/shard_map/ppermute | solution.py:114
  46.2 4.1 %collective-permute-done.12.refs_4_.refs_7_ = f32[2,128,256]{2,1,0:T(8,128)S(1)} collective-permute-done((f32[2,128,256]{2,1,0:T(8,128)S(1)}, f32[2,128,256]{2,1,0:T(8,128)S(1)}, u32[]{:S(2)}, u32[]{:S(2)}) %collective-permute-start.12) | collective-permute-done | bytes 262176 | tf_op jit(solution)/shard_map/ppermute | solution.py:114
  50.3 2.1 %shard_map.85 = (f32[2,128,256]{2,1,0:T(8,128)S(1)}, f32[2,128,256]{2,1,0:T(8,128)S(1)}) custom-call(f32[8,128]{1,0:T(8,128)S(1)} %get-tuple-element.39.refs_0_, f32[2,128,384]{2,1,0:T(8,128)S(1)} %shard_map.83.refs_3_.refs_1_.refs_4_, f32[2,128,256]{2,1,0:T(8,128)S(1)} %get-tuple-element.51.refs_2_.refs_5_, ...), custom_call_target="tpu_custom_call" | custom-call | flops 100000 | bytes 10000 | tf_op jit(solution)/shard_map/pallas_call | solution.py:532
  53.1 2.2 %shard_map.86 = (f32[2,128,256]{2,1,0:T(8,128)S(1)}, f32[2,128,256]{2,1,0:T(8,128)S(1)}, f32[4,48,256]{2,1,0:T(8,128)S(1)}, f32[4,40,256]{2,1,0:T(8,128)S(1)}, f32[4,40,256]{2,1,0:T(8,128)S(1)}) custom-call(f32[8,128]{1,0:T(8,128)S(1)} %get-tuple-element.39.refs_0_, f32[2,128,384]{2,1,0:T(8,128)S(1)} %shard_map.83.refs_3_.refs_1_.refs_4_, ...), custom_call_target="tpu_custom_call" | custom-call | flops 100000 | bytes 10000 | tf_op jit(solution)/shard_map/pallas_call | solution.py:532
  55.3 1.2 %collective-permute-start.20 = (f32[2,128,256]{2,1,0:T(8,128)S(1)}, f32[2,128,256]{2,1,0:T(8,128)S(1)}, u32[]{:S(2)}, u32[]{:S(2)}) collective-permute-start(f32[2,128,256]{2,1,0:T(8,128)S(1)} %get-tuple-element.62), channel_id=1, source_target_pairs={{2,4},{3,5},{6,8},{7,9},{10,12},{11,13},{14,16},{15,17},{18,20},{1... | collective-permute-start | bytes 786440 | tf_op jit(solution)/shard_map/ppermute | solution.py:114
  57.0 1.2 %collective-permute-done.17.refs_4_ = f32[4,40,256]{2,1,0:T(8,128)S(1)} collective-permute-done((f32[4,40,256]{2,1,0:T(8,128)S(1)}, f32[4,40,256]{2,1,0:T(8,128)S(1)}, u32[]{:S(2)}, u32[]{:S(2)}) %collective-permute-start.17) | collective-permute-done | bytes 163872 | tf_op jit(solution)/shard_map/ppermute | solution.py:117
  59.3 3.1 %collective-permute-done.19.refs_3_ = f32[2,128,256]{2,1,0:T(8,128)S(1)} collective-permute-done((f32[2,128,256]{2,1,0:T(8,128)S(1)}, f32[2,128,256]{2,1,0:T(8,128)S(1)}, u32[]{:S(2)}, u32[]{:S(2)}) %collective-permute-start.19) | collective-permute-done | bytes 262176 | tf_op jit(solution)/shard_map/ppermute | solution.py:114
  62.3 1.0 %shard_map.88 = (f32[2,128,768]{2,1,0:T(8,128)S(1)}, f32[2,128,768]{2,1,0:T(8,128)S(1)}, f32[128,768]{1,0:T(8,128)S(1)}) custom-call(s32[6,128]{1,0:T(8,128)S(1)} %shard_map.78.refs_0_, f32[2,128,768]{2,1,0:T(8,128)S(1)} %shard_map.87.refs_1_, f32[128,768]{1,0:T(8,128)S(1)} %shard_map.79.refs_2_.refs_3_.refs_0_, ...), custom_call_target="tpu_custom_call" | custom-call | flops 100000 | bytes 10000 | tf_op jit(solution)/shard_map/pallas_call | solution.py:532
  63.3 1.8 %collective-permute-done.20.refs_1_ = f32[2,128,256]{2,1,0:T(8,128)S(1)} collective-permute-done((f32[2,128,256]{2,1,0:T(8,128)S(1)}, f32[2,128,256]{2,1,0:T(8,128)S(1)}, u32[]{:S(2)}, u32[]{:S(2)}) %collective-permute-start.20) | collective-permute-done | bytes 262176 | tf_op jit(solution)/shard_map/ppermute | solution.py:114
  65.2 1.6 %collective-permute-start.21 = (f32[2,128,128]{2,1,0:T(8,128)S(1)}, f32[2,128,128]{2,1,0:T(8,128)S(1)}, u32[]{:S(2)}, u32[]{:S(2)}) collective-permute-start(f32[2,128,128]{2,1,0:T(8,128)S(1)} %shard_map.89.refs_4_), channel_id=1, source_target_pairs={{0,1},{1,0},{2,3},{3,2},{4,5},{5,4},{6,7},{7,6},{8,9},{9,8},{10,11... | collective-permute-start | bytes 393224 | tf_op jit(solution)/shard_map/ppermute | solution.py:102
  67.6 2.6 %collective-permute-done.21.refs_2_ = f32[2,128,128]{2,1,0:T(8,128)S(1)} collective-permute-done((f32[2,128,128]{2,1,0:T(8,128)S(1)}, f32[2,128,128]{2,1,0:T(8,128)S(1)}, u32[]{:S(2)}, u32[]{:S(2)}) %collective-permute-start.21) | collective-permute-done | bytes 131104 | tf_op jit(solution)/shard_map/ppermute | solution.py:102
  (47 shorter events, 9.7 us)
Async XLA Ops:
  0.0 17.8 %collective-permute-start.4 = (f32[2,128,512]{2,1,0:T(8,128)}, f32[2,128,512]{2,1,0:T(8,128)S(1)}, u32[]{:S(2)}, u32[]{:S(2)}) collective-permute-start(f32[2,128,512]{2,1,0:T(8,128)} %refs_4_.1), channel_id=1, source_target_pairs={{0,2},{2,0},{4,6},{6,4},{8,10},{10,8},{12,14},{14,12},{16,18},{18,... | collective-permute-start | bytes 1572872 | tf_op jit(solution)/shard_map/ppermute | solution.py:117
  0.0 17.8 %collective-permute-start.3 = (f32[2,128,512]{2,1,0:T(8,128)}, f32[2,128,512]{2,1,0:T(8,128)S(1)}, u32[]{:S(2)}, u32[]{:S(2)}) collective-permute-start(f32[2,128,512]{2,1,0:T(8,128)} %refs_4_.1), channel_id=1, source_target_pairs={{2,4},{3,5},{6,8},{7,9},{10,12},{11,13},{14,16},{15,17},{18,20},{1... | collective-permute-start | bytes 1572872 | tf_op jit(solution)/shard_map/ppermute | solution.py:114
  0.7 0.7 copy-start.6
  0.7 0.7 copy-start.7
  1.3 1.0 %copy-start.1 = (f32[2,128,512]{2,1,0:T(8,128)S(1)}, f32[2,128,512]{2,1,0:T(8,128)}, u32[]{:S(2)}) copy-start(f32[2,128,512]{2,1,0:T(8,128)} %refs_4_.1) | copy-start | bytes 1572868
  2.4 2.2 %copy-start.3 = (f32[2,256,256]{2,1,0:T(8,128)S(1)}, f32[2,256,256]{2,1,0:T(8,128)}, u32[]{:S(2)}) copy-start(f32[2,256,256]{2,1,0:T(8,128)} %refs_1_.5) | copy-start | bytes 1572868
  3.0 14.8 %copy-start = (bf16[2,2,2,256,256]{4,3,2,1,0:T(8,128)(2,1)S(1)}, bf16[2,2,2,256,256]{4,3,2,1,0:T(8,128)(2,1)}, u32[]{:S(2)}) copy-start(bf16[2,2,2,256,256]{4,3,2,1,0:T(8,128)(2,1)} %constant.4.clone.refs_9_.refs_10_.refs_11_) | copy-start | bytes 3145732
  3.0 6.6 %collective-permute-start = (f32[2,136,128]{2,1,0:T(8,128)S(1)}, f32[2,136,128]{2,1,0:T(8,128)S(1)}, u32[]{:S(2)}, u32[]{:S(2)}) collective-permute-start(f32[2,136,128]{2,1,0:T(8,128)S(1)} %shard_map.74), channel_id=1, source_target_pairs={{0,1},{1,0},{2,3},{3,2},{4,5},{5,4},{6,7},{7,6},{8,9},{9,8},{10,11... | collective-permute-start | bytes 417800 | tf_op jit(solution)/shard_map/ppermute | solution.py:102
  4.6 1.0 %copy-start.4 = (f32[1,1,2,256,256]{4,3,2,1,0:T(8,128)S(1)}, f32[1,1,2,256,256]{4,3,2,1,0:T(8,128)}, u32[]{:S(2)}) copy-start(f32[1,1,2,256,256]{4,3,2,1,0:T(8,128)} %param.9) | copy-start | bytes 1572868
  5.6 0.9 %copy-start.5 = (bf16[2,256,256]{2,1,0:T(8,128)(2,1)S(1)}, bf16[2,256,256]{2,1,0:T(8,128)(2,1)}, u32[]{:S(2)}) copy-start(bf16[2,256,256]{2,1,0:T(8,128)(2,1)} %constant.5.clone.order) | copy-start | bytes 786436
  8.1 9.7 %copy-start.2 = (f32[2,128,512]{2,1,0:T(8,128)S(1)}, f32[2,128,512]{2,1,0:T(8,128)}, u32[]{:S(2)}) copy-start(f32[2,128,512]{2,1,0:T(8,128)} %refs_4_.1) | copy-start | bytes 1572868
  10.1 7.6 %collective-permute-start.1 = (f32[2,152,128]{2,1,0:T(8,128)S(1)}, f32[2,152,128]{2,1,0:T(8,128)S(1)}, u32[]{:S(2)}, u32[]{:S(2)}) collective-permute-start(f32[2,152,128]{2,1,0:T(8,128)S(1)} %get-tuple-element.38), channel_id=1, source_target_pairs={{2,4},{3,5},{6,8},{7,9},{10,12},{11,13},{14,16},{15,17},{18,20},{1... | collective-permute-start | bytes 466952 | tf_op jit(solution)/shard_map/ppermute | solution.py:114
  10.2 2.7 %collective-permute-start.2 = (f32[2,144,128]{2,1,0:T(8,128)S(1)}, f32[2,144,128]{2,1,0:T(8,128)S(1)}, u32[]{:S(2)}, u32[]{:S(2)}) collective-permute-start(f32[2,144,128]{2,1,0:T(8,128)S(1)} %get-tuple-element.37.refs_2_.refs_0_.refs_5_), channel_id=1, source_target_pairs={{0,2},{2,0},{4,6},{6,4},{8,10},{10,8},{12,14},{14,12},{16,18},{18,... | collective-permute-start | bytes 442376 | tf_op jit(solution)/shard_map/ppermute | solution.py:117
  19.9 10.8 %collective-permute-start.8 = (f32[2,128,256]{2,1,0:T(8,128)S(1)}, f32[2,128,256]{2,1,0:T(8,128)S(1)}, u32[]{:S(2)}, u32[]{:S(2)}) collective-permute-start(f32[2,128,256]{2,1,0:T(8,128)S(1)} %get-tuple-element.41.refs_7_), channel_id=1, source_target_pairs={{2,4},{3,5},{6,8},{7,9},{10,12},{11,13},{14,16},{15,17},{18,20},{1... | collective-permute-start | bytes 786440 | tf_op jit(solution)/shard_map/ppermute | solution.py:114
  22.9 10.7 %collective-permute-start.9 = (f32[2,128,256]{2,1,0:T(8,128)S(1)}, f32[2,128,256]{2,1,0:T(8,128)S(1)}, u32[]{:S(2)}, u32[]{:S(2)}) collective-permute-start(f32[2,128,256]{2,1,0:T(8,128)S(1)} %get-tuple-element.42.refs_3_), channel_id=1, source_target_pairs={{2,4},{3,5},{6,8},{7,9},{10,12},{11,13},{14,16},{15,17},{18,20},{1... | collective-permute-start | bytes 786440 | tf_op jit(solution)/shard_map/ppermute | solution.py:114
  24.0 4.6 %collective-permute-start.5 = (f32[4,48,256]{2,1,0:T(8,128)S(1)}, f32[4,48,256]{2,1,0:T(8,128)S(1)}, u32[]{:S(2)}, u32[]{:S(2)}) collective-permute-start(f32[4,48,256]{2,1,0:T(8,128)S(1)} %get-tuple-element.43.refs_2_), channel_id=1, source_target_pairs={{0,2},{2,0},{4,6},{6,4},{8,10},{10,8},{12,14},{14,12},{16,18},{18,... | collective-permute-start | bytes 589832 | tf_op jit(solution)/shard_map/ppermute | solution.py:117
  24.0 4.6 %collective-permute-start.6 = (f32[4,40,256]{2,1,0:T(8,128)S(1)}, f32[4,40,256]{2,1,0:T(8,128)S(1)}, u32[]{:S(2)}, u32[]{:S(2)}) collective-permute-start(f32[4,40,256]{2,1,0:T(8,128)S(1)} %get-tuple-element.46), channel_id=1, source_target_pairs={{0,2},{2,0},{4,6},{6,4},{8,10},{10,8},{12,14},{14,12},{16,18},{18,... | collective-permute-start | bytes 491528 | tf_op jit(solution)/shard_map/ppermute | solution.py:117
  24.5 4.1 %collective-permute-start.7 = (f32[4,40,256]{2,1,0:T(8,128)S(1)}, f32[4,40,256]{2,1,0:T(8,128)S(1)}, u32[]{:S(2)}, u32[]{:S(2)}) collective-permute-start(f32[4,40,256]{2,1,0:T(8,128)S(1)} %get-tuple-element.47), channel_id=1, source_target_pairs={{0,2},{2,0},{4,6},{6,4},{8,10},{10,8},{12,14},{14,12},{16,18},{18,... | collective-permute-start | bytes 491528 | tf_op jit(solution)/shard_map/ppermute | solution.py:117
  33.7 6.4 %collective-permute-start.10 = (f32[2,128,256]{2,1,0:T(8,128)S(1)}, f32[2,128,256]{2,1,0:T(8,128)S(1)}, u32[]{:S(2)}, u32[]{:S(2)}) collective-permute-start(f32[2,128,256]{2,1,0:T(8,128)S(1)} %shard_map.82.refs_4_), channel_id=1, source_target_pairs={{0,1},{1,0},{2,3},{3,2},{4,5},{5,4},{6,7},{7,6},{8,9},{9,8},{10,11... | collective-permute-start | bytes 786440 | tf_op jit(solution)/shard_map/ppermute | solution.py:102
  35.3 10.9 %collective-permute-start.11 = (f32[2,128,384]{2,1,0:T(8,128)S(1)}, f32[2,128,384]{2,1,0:T(8,128)S(1)}, u32[]{:S(2)}, u32[]{:S(2)}) collective-permute-start(f32[2,128,384]{2,1,0:T(8,128)S(1)} %shard_map.83.refs_3_.refs_1_.refs_4_), channel_id=1, source_target_pairs={{2,4},{3,5},{6,8},{7,9},{10,12},{11,13},{14,16},{15,17},{18,20},{1... | collective-permute-start | bytes 1179656 | tf_op jit(solution)/shard_map/ppermute | solution.py:114
  40.2 6.0 %collective-permute-start.13 = (f32[2,128,256]{2,1,0:T(8,128)S(1)}, f32[2,128,256]{2,1,0:T(8,128)S(1)}, u32[]{:S(2)}, u32[]{:S(2)}) collective-permute-start(f32[2,128,256]{2,1,0:T(8,128)S(1)} %get-tuple-element.52), channel_id=1, source_target_pairs={{0,2},{2,0},{4,6},{6,4},{8,10},{10,8},{12,14},{14,12},{16,18},{18,... | collective-permute-start | bytes 786440 | tf_op jit(solution)/shard_map/ppermute | solution.py:117
  40.3 6.0 %collective-permute-start.14 = (f32[2,128,256]{2,1,0:T(8,128)S(1)}, f32[2,128,256]{2,1,0:T(8,128)S(1)}, u32[]{:S(2)}, u32[]{:S(2)}) collective-permute-start(f32[2,128,256]{2,1,0:T(8,128)S(1)} %get-tuple-element.53), channel_id=1, source_target_pairs={{0,2},{2,0},{4,6},{6,4},{8,10},{10,8},{12,14},{14,12},{16,18},{18,... | collective-permute-start | bytes 786440 | tf_op jit(solution)/shard_map/ppermute | solution.py:117
  40.8 9.6 %collective-permute-start.12 = (f32[2,128,256]{2,1,0:T(8,128)S(1)}, f32[2,128,256]{2,1,0:T(8,128)S(1)}, u32[]{:S(2)}, u32[]{:S(2)}) collective-permute-start(f32[2,128,256]{2,1,0:T(8,128)S(1)} %get-tuple-element.51.refs_2_.refs_5_), channel_id=1, source_target_pairs={{2,4},{3,5},{6,8},{7,9},{10,12},{11,13},{14,16},{15,17},{18,20},{1... | collective-permute-start | bytes 786440 | tf_op jit(solution)/shard_map/ppermute | solution.py:114
  41.5 1.5 %collective-permute-start.15 = (f32[2,128,128]{2,1,0:T(8,128)S(1)}, f32[2,128,128]{2,1,0:T(8,128)S(1)}, u32[]{:S(2)}, u32[]{:S(2)}) collective-permute-start(f32[2,128,128]{2,1,0:T(8,128)S(1)} %get-tuple-element.54), channel_id=1, source_target_pairs={{0,2},{2,0},{4,6},{6,4},{8,10},{10,8},{12,14},{14,12},{16,18},{18,... | collective-permute-start | bytes 393224 | tf_op jit(solution)/shard_map/ppermute | solution.py:117
  52.5 9.9 %collective-permute-start.19 = (f32[2,128,256]{2,1,0:T(8,128)S(1)}, f32[2,128,256]{2,1,0:T(8,128)S(1)}, u32[]{:S(2)}, u32[]{:S(2)}) collective-permute-start(f32[2,128,256]{2,1,0:T(8,128)S(1)} %get-tuple-element.56.refs_8_), channel_id=1, source_target_pairs={{2,4},{3,5},{6,8},{7,9},{10,12},{11,13},{14,16},{15,17},{18,20},{1... | collective-permute-start | bytes 786440 | tf_op jit(solution)/shard_map/ppermute | solution.py:114
  55.3 9.9 %collective-permute-start.20 = (f32[2,128,256]{2,1,0:T(8,128)S(1)}, f32[2,128,256]{2,1,0:T(8,128)S(1)}, u32[]{:S(2)}, u32[]{:S(2)}) collective-permute-start(f32[2,128,256]{2,1,0:T(8,128)S(1)} %get-tuple-element.62), channel_id=1, source_target_pairs={{2,4},{3,5},{6,8},{7,9},{10,12},{11,13},{14,16},{15,17},{18,20},{1... | collective-permute-start | bytes 786440 | tf_op jit(solution)/shard_map/ppermute | solution.py:114
  56.5 1.9 %collective-permute-start.16 = (f32[4,48,256]{2,1,0:T(8,128)S(1)}, f32[4,48,256]{2,1,0:T(8,128)S(1)}, u32[]{:S(2)}, u32[]{:S(2)}) collective-permute-start(f32[4,48,256]{2,1,0:T(8,128)S(1)} %get-tuple-element.58), channel_id=1, source_target_pairs={{0,2},{2,0},{4,6},{6,4},{8,10},{10,8},{12,14},{14,12},{16,18},{18,... | collective-permute-start | bytes 589832 | tf_op jit(solution)/shard_map/ppermute | solution.py:117
  56.5 1.7 %collective-permute-start.17 = (f32[4,40,256]{2,1,0:T(8,128)S(1)}, f32[4,40,256]{2,1,0:T(8,128)S(1)}, u32[]{:S(2)}, u32[]{:S(2)}) collective-permute-start(f32[4,40,256]{2,1,0:T(8,128)S(1)} %get-tuple-element.59), channel_id=1, source_target_pairs={{0,2},{2,0},{4,6},{6,4},{8,10},{10,8},{12,14},{14,12},{16,18},{18,... | collective-permute-start | bytes 491528 | tf_op jit(solution)/shard_map/ppermute | solution.py:117
  57.0 1.4 %collective-permute-start.18 = (f32[4,40,256]{2,1,0:T(8,128)S(1)}, f32[4,40,256]{2,1,0:T(8,128)S(1)}, u32[]{:S(2)}, u32[]{:S(2)}) collective-permute-start(f32[4,40,256]{2,1,0:T(8,128)S(1)} %get-tuple-element.60), channel_id=1, source_target_pairs={{0,2},{2,0},{4,6},{6,4},{8,10},{10,8},{12,14},{14,12},{16,18},{18,... | collective-permute-start | bytes 491528 | tf_op jit(solution)/shard_map/ppermute | solution.py:117
  65.2 5.0 %collective-permute-start.21 = (f32[2,128,128]{2,1,0:T(8,128)S(1)}, f32[2,128,128]{2,1,0:T(8,128)S(1)}, u32[]{:S(2)}, u32[]{:S(2)}) collective-permute-start(f32[2,128,128]{2,1,0:T(8,128)S(1)} %shard_map.89.refs_4_), channel_id=1, source_target_pairs={{0,1},{1,0},{2,3},{3,2},{4,5},{5,4},{6,7},{7,6},{8,9},{9,8},{10,11... | collective-permute-start | bytes 393224 | tf_op jit(solution)/shard_map/ppermute | solution.py:102

commit v13 on v12

--- a/solution.py
+++ b/solution.py
@@ -89,6 +89,9 @@
 
     def edge_tiles(self, t):
         return [1 + right * (self.tiles - 3) for right in self.rights(t)]
+
+    def first_parity(self, t):
+        return 1 - t if self.paired else 0
 
     def mid_start(self, t):
         return 1 + t if self.paired else 2
@@ -311,10 +314,10 @@
     inverse[...] = 1.0 / (canvas[:, lanes(plan.own, plan.tiles)] + DAMPING)
 
 
-def term_kernel(plan, slot, layout, pieces, copied, slots, spot, *rest):
+def term_kernel(plan, slot, layout, pieces, copied, halves, slots, spot, *rest):
     refs, rest = rest[:pieces], rest[pieces:]
     earlier, (probe, amps, tables, outer, inner), rest = rest[:copied], rest[copied : copied + 5], rest[copied + 5 :]
-    near_outers, (window, picked) = rest[:-2], rest[-2:]
+    outer_halves, near_outers, (window, picked) = rest[:halves], rest[halves:-2], rest[-2:]
     size = probe.shape[2]
     half = size // 2
     s, t = here()
@@ -392,6 +395,9 @@
         inner[0] = term_real[half:]
         inner[1] = term_imag[half:]
 
+    for index, target in enumerate(outer_halves):
+        first = plan.first_parity(t)
+        target[...] = outer[:, :, lanes(first if index == 0 else 1 - first)]
     for index, source in enumerate((*earlier, outer)):
         line = 0
         for target in near_outers:
@@ -445,8 +451,13 @@
         return jnp.where(inside, 1.0, 0.0)
 
 
-def part_of(patch, mask, part, tile):
-    return patch[part, :, lanes(tile % 2)] * mask[:, lanes(tile)]
+def part_of(plan, patch, mask, part, tile):
+    if isinstance(patch, (list, tuple)):
+        first = plan.first_parity(lax.axis_index("sy"))
+        values = jnp.where(tile % 2 == first, patch[0][part], patch[1][part])
+    else:
+        values = patch[part, :, lanes(tile % 2)]
+    return values * mask[:, lanes(tile)]
 
 
 def early_sum_kernel(plan, slots, info, *rest):
@@ -473,15 +484,15 @@
         mask[:, where] = last.mask(tile)
 
 
-def take_off(patch, mask, target, base, inverse, tile):
+def take_off(plan, patch, mask, target, base, inverse, tile):
     for part in range(2):
-        target[part] = base[part, :, lanes(tile)] - part_of(patch, mask, part, tile) * inverse[:, lanes(tile)]
+        target[part] = base[part, :, lanes(tile)] - part_of(plan, patch, mask, part, tile) * inverse[:, lanes(tile)]
 
 
 def middle_kernel(plan, base, patch, mask, inverse, _, middle):
     _, t = here()
     for step in range(plan.mid_tiles):
-        take_off(patch, mask, middle.at[:, :, lanes(step)], base, inverse, plan.mid_start(t) + step)
+        take_off(plan, patch, mask, middle.at[:, :, lanes(step)], base, inverse, plan.mid_start(t) + step)
 
 
 def boundary_kernel(plan, early, patch, mask, *sums):
@@ -490,23 +501,25 @@
         for step in range(2):
             tile = start + step
             for part in range(2):
-                total[part, :, lanes(step)] = early[part, :, lanes(tile)] + part_of(patch, mask, part, tile)
-
-
-def halo_sum_kernel(plan, early, patch, mask, *sums):
+                total[part, :, lanes(step)] = early[part, :, lanes(tile)] + part_of(plan, patch, mask, part, tile)
+
+
+def halo_sum_kernel(plan, early, mask, *rest):
+    halves, sums = rest[: plan.sides], rest[plan.sides :]
     _, t = here()
-    for total, tile in zip(sums, plan.halo_tiles(t)):
+    for half, total, tile in zip(halves, sums, plan.halo_tiles(t)):
         for part in range(2):
-            total[part] = early[part, :, lanes(tile)] + part_of(patch, mask, part, tile)
-
-
-def last_kernel(plan, base, patch, mask, inverse, _, *rest):
+            total[part] = early[part, :, lanes(tile)] + half[part] * mask[:, lanes(tile)]
+
+
+def last_kernel(plan, base, mask, inverse, _, first, second, *rest):
     nearly, bases, (current, sems) = rest[0], rest[1 : 1 + plan.sides], rest[1 + plan.sides :]
+    patch = [first, second]
     _, t = here()
     copies = []
     for step in range(plan.own):
         where = lanes(step)
-        take_off(patch, mask, current.at[:, :, where], base, inverse, 1 + step)
+        take_off(plan, patch, mask, current.at[:, :, where], base, inverse, 1 + step)
         copies.append(pltpu.make_async_copy(current.at[:, :, where], nearly.at[:, :, where], sems.at[step]))
         copies[-1].start()
     for edge, tile in zip(bases, plan.edge_tiles(t)):
@@ -550,7 +563,7 @@
     slots = amplitudes.shape[2]
     block_rows = object_field.shape[1]
     block_cols = object_field.shape[2]
-    assert block_rows == half and block_cols % LANES == 0 and half == LANES
+    assert block_rows == half and block_cols % (2 * LANES) == 0 and half == LANES
     width = plan.tiles * LANES
     sides = plan.sides
     spots = centres[0, 0]
@@ -609,17 +622,21 @@
             last = slot == slots - 1
             earlier = outer if last else []
             patch = shape((2, half, size), f32)
+            halves = 2 if last and sweep == ITERS - 1 else 0
             outer_part, inner_part, *copies = call(
-                lambda *refs, slot=slot, layout=layout, copied=len(earlier): term_kernel(
-                    plan, slot, layout, len(pieces), copied, slots, *refs
+                lambda *refs, slot=slot, layout=layout, copied=len(earlier), halves=halves: term_kernel(
+                    plan, slot, layout, len(pieces), copied, halves, slots, *refs
                 ),
-                [patch] * 2 + [shape((2 * slots, rows, size), f32) for rows in near_heights if last],
+                [patch] * 2
+                + [shape((2, half, LANES), f32)] * halves
+                + [shape((2 * slots, rows, size), f32) for rows in near_heights if last],
                 [pltpu.VMEM((2, size, size), f32), pltpu.VMEM((3, 3, 2, half, LANES), f32)],
                 [own_spot, *pieces, *earlier, rolled, ordered, tables],
             )
+            outer_halves, copies = copies[:halves], copies[halves:]
             inner.append(inner_part)
             outer.append(outer_part)
-            outer_far.append(plan.far_rows(outer_part))
+            outer_far.append([plan.far_rows(part) for part in outer_halves] if halves else plan.far_rows(outer_part))
             if sweep == 0 and last:
                 info = call(
                     lambda *refs: info_kernel(plan, *refs),
@@ -685,14 +702,14 @@
         lambda *refs: halo_sum_kernel(plan, *refs),
         [shape((2, half, LANES), f32)] * sides,
         [],
-        [early, outer_far[-1], mask],
+        [early, mask, *outer_far[-1][:sides]],
     )
     nearly, *bases = call(
         lambda *refs: last_kernel(plan, *refs),
         [shape((2, half, block_cols), f32)] + [shape((2, half, LANES), f32)] * sides,
         [pltpu.VMEM((2, half, block_cols), f32), dma((plan.own,))],
-        [base, outer_far[-1], mask, inverse, sums[0]],
-        in_specs=[VMEM] * 4 + [ANY],
+        [base, mask, inverse, sums[0], *outer_far[-1]],
+        in_specs=[VMEM] * 3 + [ANY] + [VMEM] * 2,
         out_specs=[HBM] + [VMEM] * sides,
     )
     received = plan.across(sums)

time: 71.2 us -> 70.5 us (level)
  the two profiles are of different devices: /device:TPU:10 before, /device:TPU:17 now
where the time goes in v13:
time: 70.5 us; the launch traced here: 69.9 us
  waiting for transfers between devices  28.4 us (40%)
  Pallas kernels  21.5 us (30%)
  starting transfers between devices  16 us (23%)
  local copies, waits for them, and re-layouts  3.73 us (5%)
    pallas_call x19, Pallas kernels, call(): pl.pallas_call(kernel, out_shape=outs, in_specs=in_specs or [SMEM if valu...  21.5 us
    ppermute x9, waiting for transfers between devices, far_rows(): lax.ppermute(values, ('sx', 'sy'), pairs + [(j, i) for i, j in pairs])  19.2 us
    ppermute x9, starting transfers between devices, far_rows(): lax.ppermute(values, ('sx', 'sy'), pairs + [(j, i) for i, j in pairs])  10.5 us
    ppermute x3, waiting for transfers between devices, across(): return [lax.ppermute(values[0], axis_name, [(0, 1), (1, 0)])]  5.39 us
    ppermute x11, waiting for transfers between devices, near_rows(): return lax.ppermute(values, 'sx', [(i, i ^ 1) for i in range(self.sx_size)])  3.85 us
    unnamed x16, local copies, waits for them, and re-layouts  3.73 us
    ppermute x3, starting transfers between devices, across(): return [lax.ppermute(values[0], axis_name, [(0, 1), (1, 0)])]  3.06 us
    ppermute x11, starting transfers between devices, near_rows(): return lax.ppermute(values, 'sx', [(i, i ^ 1) for i in range(self.sx_size)])  2.45 us
  transfers between devices with their start and end apart: 23, of which 14 were waited for; matrix products, arithmetic and copies ran while one was open for 0% of the time, Pallas kernels for 24%

profile of v13, /device:TPU:17, one launch (start us, length us, event | category | flops | bytes accessed | tf_op | source)
XLA Modules:
  0.0 69.9 jit_solution(16531917124533604921)
XLA Ops:
  0.7 1.1 %collective-permute-start.3 = (f32[2,128,512]{2,1,0:T(8,128)}, f32[2,128,512]{2,1,0:T(8,128)S(1)}, u32[]{:S(2)}, u32[]{:S(2)}) collective-permute-start(f32[2,128,512]{2,1,0:T(8,128)} %refs_4_.1), channel_id=1, source_target_pairs={{2,4},{3,5},{6,8},{7,9},{10,12},{11,13},{14,16},{15,17},{18,20},{1... | collective-permute-start | bytes 1572872 | tf_op jit(solution)/shard_map/ppermute | solution.py:117
  2.5 1.0 %copy-done.1 = f32[2,128,512]{2,1,0:T(8,128)S(1)} copy-done((f32[2,128,512]{2,1,0:T(8,128)S(1)}, f32[2,128,512]{2,1,0:T(8,128)}, u32[]{:S(2)}) %copy-start.1) | copy-done | bytes 524312
  4.1 1.3 %collective-permute-start = (f32[2,136,128]{2,1,0:T(8,128)S(1)}, f32[2,136,128]{2,1,0:T(8,128)S(1)}, u32[]{:S(2)}, u32[]{:S(2)}) collective-permute-start(f32[2,136,128]{2,1,0:T(8,128)S(1)} %shard_map.74), channel_id=1, source_target_pairs={{0,1},{1,0},{2,3},{3,2},{4,5},{5,4},{6,7},{7,6},{8,9},{9,8},{10,11... | collective-permute-start | bytes 417800 | tf_op jit(solution)/shard_map/ppermute | solution.py:105
  5.4 1.0 %copy-done.4 = f32[1,1,2,256,256]{4,3,2,1,0:T(8,128)S(1)} copy-done((f32[1,1,2,256,256]{4,3,2,1,0:T(8,128)S(1)}, f32[1,1,2,256,256]{4,3,2,1,0:T(8,128)}, u32[]{:S(2)}) %copy-start.4) | copy-done | bytes 524312
  6.5 0.9 %copy-done.5 = bf16[2,256,256]{2,1,0:T(8,128)(2,1)S(1)} copy-done((bf16[2,256,256]{2,1,0:T(8,128)(2,1)S(1)}, bf16[2,256,256]{2,1,0:T(8,128)(2,1)}, u32[]{:S(2)}) %copy-start.5) | copy-done | bytes 262168
  7.4 1.5 %shard_map.73 = (f32[2,2,256,256]{3,2,1,0:T(8,128)S(1)}, f32[2,256,256]{2,1,0:T(8,128)S(1)}) custom-call(s32[2,2]{1,0:T(2,128)S(1)} %bitcast.5, f32[2,256,256]{2,1,0:T(8,128)S(1)} %copy-done.3, f32[2,256,256]{2,1,0:T(8,128)S(1)} %bitcast.3, bf16[2,256,256]{2,1,0:T(8,128)(2,1)S(1)} %copy-done.5), custom_call_target="tpu_custom_call" | custom-call | flops 100000 | bytes 10000 | tf_op jit(solution)/shard_map/pallas_call | solution.py:545
  9.6 2.4 %collective-permute-start.1 = (f32[2,152,128]{2,1,0:T(8,128)S(1)}, f32[2,152,128]{2,1,0:T(8,128)S(1)}, u32[]{:S(2)}, u32[]{:S(2)}) collective-permute-start(f32[2,152,128]{2,1,0:T(8,128)S(1)} %get-tuple-element.39), channel_id=1, source_target_pairs={{2,4},{3,5},{6,8},{7,9},{10,12},{11,13},{14,16},{15,17},{18,20},{1... | collective-permute-start | bytes 466952 | tf_op jit(solution)/shard_map/ppermute | solution.py:117
  12.0 1.3 %collective-permute-done.2.refs_5_.refs_2_.refs_8_ = f32[2,144,128]{2,1,0:T(8,128)S(1)} collective-permute-done((f32[2,144,128]{2,1,0:T(8,128)S(1)}, f32[2,144,128]{2,1,0:T(8,128)S(1)}, u32[]{:S(2)}, u32[]{:S(2)}) %collective-permute-start.2) | collective-permute-done | bytes 147488 | tf_op jit(solution)/shard_map/ppermute | solution.py:120
  13.3 5.1 %collective-permute-done.1.refs_4_.refs_1_.refs_7_ = f32[2,152,128]{2,1,0:T(8,128)S(1)} collective-permute-done((f32[2,152,128]{2,1,0:T(8,128)S(1)}, f32[2,152,128]{2,1,0:T(8,128)S(1)}, u32[]{:S(2)}, u32[]{:S(2)}) %collective-permute-start.1) | collective-permute-done | bytes 155680 | tf_op jit(solution)/shard_map/ppermute | solution.py:117
  18.5 2.1 %shard_map.76 = (f32[2,128,256]{2,1,0:T(8,128)S(1)}, f32[2,128,256]{2,1,0:T(8,128)S(1)}) custom-call(f32[8,128]{1,0:T(8,128)S(1)} %get-tuple-element.40.refs_0_, f32[2,128,512]{2,1,0:T(8,128)S(1)} %copy-done.2, f32[2,144,128]{2,1,0:T(8,128)S(1)} %get-tuple-element.38.refs_2_.refs_0_.refs_5_, f32[2,128,512]{2,1,0:T(8,128)S(1)} %collective-permute-done.3.refs_3_.refs_6_, ...), custom_call_target="tpu_custom_call" | custom-call | flops 100000 | bytes 10000 | tf_op jit(solution)/shard_map/pallas_call | solution.py:545
  20.6 1.2 %collective-permute-start.8 = (f32[2,128,256]{2,1,0:T(8,128)S(1)}, f32[2,128,256]{2,1,0:T(8,128)S(1)}, u32[]{:S(2)}, u32[]{:S(2)}) collective-permute-start(f32[2,128,256]{2,1,0:T(8,128)S(1)} %get-tuple-element.42.refs_7_), channel_id=1, source_target_pairs={{2,4},{3,5},{6,8},{7,9},{10,12},{11,13},{14,16},{15,17},{18,20},{1... | collective-permute-start | bytes 786440 | tf_op jit(solution)/shard_map/ppermute | solution.py:117
  21.8 2.2 %shard_map.77 = (f32[2,128,256]{2,1,0:T(8,128)S(1)}, f32[2,128,256]{2,1,0:T(8,128)S(1)}, f32[4,48,256]{2,1,0:T(8,128)S(1)}, f32[4,40,256]{2,1,0:T(8,128)S(1)}, f32[4,40,256]{2,1,0:T(8,128)S(1)}) custom-call(f32[8,128]{1,0:T(8,128)S(1)} %get-tuple-element.40.refs_0_, f32[2,128,512]{2,1,0:T(8,128)S(1)} %copy-done.2, ...), custom_call_target="tpu_custom_call" | custom-call | flops 100000 | bytes 10000 | tf_op jit(solution)/shard_map/pallas_call | solution.py:545
  24.7 1.2 %shard_map.78.refs_0_ = s32[6,128]{1,0:T(8,128)S(1)} custom-call(f32[2,144,128]{2,1,0:T(8,128)S(1)} %get-tuple-element.38.refs_2_.refs_0_.refs_5_, f32[2,152,128]{2,1,0:T(8,128)S(1)} %collective-permute-done.1.refs_4_.refs_1_.refs_7_, f32[2,144,128]{2,1,0:T(8,128)S(1)} %collective-permute-done.2.refs_5_.refs_2_.refs_8_, ...), custom_call_target="tpu_custom_call" | custom-call | flops 100000 | bytes 10000 | tf_op jit(solution)/shard_map/pallas_call | solution.py:545
  26.0 2.8 %shard_map.79.refs_2_.refs_3_.refs_0_ = f32[128,768]{1,0:T(8,128)S(1)} custom-call(s32[6,128]{1,0:T(8,128)S(1)} %shard_map.78.refs_0_, f32[2,256,256]{2,1,0:T(8,128)S(1)} %copy-done.3, f32[4,48,256]{2,1,0:T(8,128)S(1)} %get-tuple-element.44.refs_2_), custom_call_target="tpu_custom_call" | custom-call | flops 100000 | bytes 10000 | tf_op jit(solution)/shard_map/pallas_call | solution.py:545
  30.5 1.0 %shard_map.81 = (f32[2,128,768]{2,1,0:T(8,128)S(1)}, f32[2,128,768]{2,1,0:T(8,128)S(1)}, f32[128,768]{1,0:T(8,128)S(1)}) custom-call(s32[6,128]{1,0:T(8,128)S(1)} %shard_map.78.refs_0_, f32[2,128,768]{2,1,0:T(8,128)S(1)} %shard_map.80.refs_1_, f32[128,768]{1,0:T(8,128)S(1)} %shard_map.79.refs_2_.refs_3_.refs_0_, ...), custom_call_target="tpu_custom_call" | custom-call | flops 100000 | bytes 10000 | tf_op jit(solution)/shard_map/pallas_call | solution.py:545
  31.5 1.8 %collective-permute-done.9.refs_1_ = f32[2,128,256]{2,1,0:T(8,128)S(1)} collective-permute-done((f32[2,128,256]{2,1,0:T(8,128)S(1)}, f32[2,128,256]{2,1,0:T(8,128)S(1)}, u32[]{:S(2)}, u32[]{:S(2)}) %collective-permute-start.9) | collective-permute-done | bytes 262176 | tf_op jit(solution)/shard_map/ppermute | solution.py:117
  33.3 1.3 %collective-permute-start.10 = (f32[2,128,256]{2,1,0:T(8,128)S(1)}, f32[2,128,256]{2,1,0:T(8,128)S(1)}, u32[]{:S(2)}, u32[]{:S(2)}) collective-permute-start(f32[2,128,256]{2,1,0:T(8,128)S(1)} %shard_map.82.refs_4_), channel_id=1, source_target_pairs={{0,1},{1,0},{2,3},{3,2},{4,5},{5,4},{6,7},{7,6},{8,9},{9,8},{10,11... | collective-permute-start | bytes 786440 | tf_op jit(solution)/shard_map/ppermute | solution.py:105
  34.7 2.5 %collective-permute-start.11 = (f32[2,128,384]{2,1,0:T(8,128)S(1)}, f32[2,128,384]{2,1,0:T(8,128)S(1)}, u32[]{:S(2)}, u32[]{:S(2)}) collective-permute-start(f32[2,128,384]{2,1,0:T(8,128)S(1)} %shard_map.83.refs_3_.refs_1_.refs_4_), channel_id=1, source_target_pairs={{2,4},{3,5},{6,8},{7,9},{10,12},{11,13},{14,16},{15,17},{18,20},{1... | collective-permute-start | bytes 1179656 | tf_op jit(solution)/shard_map/ppermute | solution.py:117
  37.2 3.1 %collective-permute-done.10.refs_5_ = f32[2,128,256]{2,1,0:T(8,128)S(1)} collective-permute-done((f32[2,128,256]{2,1,0:T(8,128)S(1)}, f32[2,128,256]{2,1,0:T(8,128)S(1)}, u32[]{:S(2)}, u32[]{:S(2)}) %collective-permute-start.10) | collective-permute-done | bytes 262176 | tf_op jit(solution)/shard_map/ppermute | solution.py:105
  41.0 1.5 %collective-permute-start.12 = (f32[2,128,256]{2,1,0:T(8,128)S(1)}, f32[2,128,256]{2,1,0:T(8,128)S(1)}, u32[]{:S(2)}, u32[]{:S(2)}) collective-permute-start(f32[2,128,256]{2,1,0:T(8,128)S(1)} %get-tuple-element.52.refs_2_.refs_5_), channel_id=1, source_target_pairs={{2,4},{3,5},{6,8},{7,9},{10,12},{11,13},{14,16},{15,17},{18,20},{1... | collective-permute-start | bytes 786440 | tf_op jit(solution)/shard_map/ppermute | solution.py:117
  42.5 1.3 %collective-permute-done.15.refs_7_.refs_10_ = f32[2,128,128]{2,1,0:T(8,128)S(1)} collective-permute-done((f32[2,128,128]{2,1,0:T(8,128)S(1)}, f32[2,128,128]{2,1,0:T(8,128)S(1)}, u32[]{:S(2)}, u32[]{:S(2)}) %collective-permute-start.15) | collective-permute-done | bytes 131104 | tf_op jit(solution)/shard_map/ppermute | solution.py:120
  43.9 4.2 %collective-permute-done.11.refs_3_.refs_6_ = f32[2,128,384]{2,1,0:T(8,128)S(1)} collective-permute-done((f32[2,128,384]{2,1,0:T(8,128)S(1)}, f32[2,128,384]{2,1,0:T(8,128)S(1)}, u32[]{:S(2)}, u32[]{:S(2)}) %collective-permute-start.11) | collective-permute-done | bytes 393248 | tf_op jit(solution)/shard_map/ppermute | solution.py:117
  48.1 2.8 %collective-permute-done.12.refs_4_.refs_7_ = f32[2,128,256]{2,1,0:T(8,128)S(1)} collective-permute-done((f32[2,128,256]{2,1,0:T(8,128)S(1)}, f32[2,128,256]{2,1,0:T(8,128)S(1)}, u32[]{:S(2)}, u32[]{:S(2)}) %collective-permute-start.12) | collective-permute-done | bytes 262176 | tf_op jit(solution)/shard_map/ppermute | solution.py:117
  50.9 2.1 %shard_map.85 = (f32[2,128,256]{2,1,0:T(8,128)S(1)}, f32[2,128,256]{2,1,0:T(8,128)S(1)}) custom-call(f32[8,128]{1,0:T(8,128)S(1)} %get-tuple-element.40.refs_0_, f32[2,128,384]{2,1,0:T(8,128)S(1)} %shard_map.83.refs_3_.refs_1_.refs_4_, f32[2,128,256]{2,1,0:T(8,128)S(1)} %get-tuple-element.52.refs_2_.refs_5_, ...), custom_call_target="tpu_custom_call" | custom-call | flops 100000 | bytes 10000 | tf_op jit(solution)/shard_map/pallas_call | solution.py:545
  53.0 1.1 %collective-permute-start.19 = (f32[2,128,256]{2,1,0:T(8,128)S(1)}, f32[2,128,256]{2,1,0:T(8,128)S(1)}, u32[]{:S(2)}, u32[]{:S(2)}) collective-permute-start(f32[2,128,256]{2,1,0:T(8,128)S(1)} %get-tuple-element.57.refs_8_), channel_id=1, source_target_pairs={{2,4},{3,5},{6,8},{7,9},{10,12},{11,13},{14,16},{15,17},{18,20},{1... | collective-permute-start | bytes 786440 | tf_op jit(solution)/shard_map/ppermute | solution.py:117
  54.2 2.9 %shard_map.86 = (f32[2,128,256]{2,1,0:T(8,128)}, f32[2,128,256]{2,1,0:T(8,128)S(1)}, f32[2,128,128]{2,1,0:T(8,128)S(1)}, f32[2,128,128]{2,1,0:T(8,128)S(1)}, f32...) custom-call(f32[8,128]{1,0:T(8,128)S(1)} %get-tuple-element.40.refs_0_, ...), custom_call_target="tpu_custom_call" | custom-call | flops 100000 | bytes 10000 | tf_op jit(solution)/shard_map/pallas_call | solution.py:545
  57.6 1.2 %collective-permute-done.17.refs_4_ = f32[4,40,256]{2,1,0:T(8,128)S(1)} collective-permute-done((f32[4,40,256]{2,1,0:T(8,128)S(1)}, f32[4,40,256]{2,1,0:T(8,128)S(1)}, u32[]{:S(2)}, u32[]{:S(2)}) %collective-permute-start.17) | collective-permute-done | bytes 163872 | tf_op jit(solution)/shard_map/ppermute | solution.py:120
  60.2 1.4 %collective-permute-done.19.refs_3_ = f32[2,128,256]{2,1,0:T(8,128)S(1)} collective-permute-done((f32[2,128,256]{2,1,0:T(8,128)S(1)}, f32[2,128,256]{2,1,0:T(8,128)S(1)}, u32[]{:S(2)}, u32[]{:S(2)}) %collective-permute-start.19) | collective-permute-done | bytes 262176 | tf_op jit(solution)/shard_map/ppermute | solution.py:117
  61.6 1.0 %shard_map.88 = (f32[2,128,768]{2,1,0:T(8,128)S(1)}, f32[2,128,768]{2,1,0:T(8,128)S(1)}, f32[128,768]{1,0:T(8,128)S(1)}) custom-call(s32[6,128]{1,0:T(8,128)S(1)} %shard_map.78.refs_0_, f32[2,128,768]{2,1,0:T(8,128)S(1)} %shard_map.87.refs_1_, f32[128,768]{1,0:T(8,128)S(1)} %shard_map.79.refs_2_.refs_3_.refs_0_, ...), custom_call_target="tpu_custom_call" | custom-call | flops 100000 | bytes 10000 | tf_op jit(solution)/shard_map/pallas_call | solution.py:545
  62.6 2.2 %collective-permute-done.20.refs_2_.refs_4_ = f32[2,128,128]{2,1,0:T(8,128)S(1)} collective-permute-done((f32[2,128,128]{2,1,0:T(8,128)S(1)}, f32[2,128,128]{2,1,0:T(8,128)S(1)}, u32[]{:S(2)}, u32[]{:S(2)}) %collective-permute-start.20) | collective-permute-done | bytes 131104 | tf_op jit(solution)/shard_map/ppermute | solution.py:117
  65.3 0.9 %collective-permute-done.21.refs_5_ = f32[2,128,128]{2,1,0:T(8,128)S(1)} collective-permute-done((f32[2,128,128]{2,1,0:T(8,128)S(1)}, f32[2,128,128]{2,1,0:T(8,128)S(1)}, u32[]{:S(2)}, u32[]{:S(2)}) %collective-permute-start.21) | collective-permute-done | bytes 131104 | tf_op jit(solution)/shard_map/ppermute | solution.py:117
  67.0 2.2 %collective-permute-done.22.refs_2_ = f32[2,128,128]{2,1,0:T(8,128)S(1)} collective-permute-done((f32[2,128,128]{2,1,0:T(8,128)S(1)}, f32[2,128,128]{2,1,0:T(8,128)S(1)}, u32[]{:S(2)}, u32[]{:S(2)}) %collective-permute-start.22) | collective-permute-done | bytes 131104 | tf_op jit(solution)/shard_map/ppermute | solution.py:105
  (49 shorter events, 9.9 us)
Async XLA Ops:
  0.0 18.4 %collective-permute-start.4 = (f32[2,128,512]{2,1,0:T(8,128)}, f32[2,128,512]{2,1,0:T(8,128)S(1)}, u32[]{:S(2)}, u32[]{:S(2)}) collective-permute-start(f32[2,128,512]{2,1,0:T(8,128)} %refs_4_.1), channel_id=1, source_target_pairs={{0,2},{2,0},{4,6},{6,4},{8,10},{10,8},{12,14},{14,12},{16,18},{18,... | collective-permute-start | bytes 1572872 | tf_op jit(solution)/shard_map/ppermute | solution.py:120
  0.7 17.8 %collective-permute-start.3 = (f32[2,128,512]{2,1,0:T(8,128)}, f32[2,128,512]{2,1,0:T(8,128)S(1)}, u32[]{:S(2)}, u32[]{:S(2)}) collective-permute-start(f32[2,128,512]{2,1,0:T(8,128)} %refs_4_.1), channel_id=1, source_target_pairs={{2,4},{3,5},{6,8},{7,9},{10,12},{11,13},{14,16},{15,17},{18,20},{1... | collective-permute-start | bytes 1572872 | tf_op jit(solution)/shard_map/ppermute | solution.py:117
  1.8 0.7 copy-start.6
  1.8 0.7 copy-start.7
  2.5 1.0 %copy-start.1 = (f32[2,128,512]{2,1,0:T(8,128)S(1)}, f32[2,128,512]{2,1,0:T(8,128)}, u32[]{:S(2)}) copy-start(f32[2,128,512]{2,1,0:T(8,128)} %refs_4_.1) | copy-start | bytes 1572868
  3.5 1.9 %copy-start.3 = (f32[2,256,256]{2,1,0:T(8,128)S(1)}, f32[2,256,256]{2,1,0:T(8,128)}, u32[]{:S(2)}) copy-start(f32[2,256,256]{2,1,0:T(8,128)} %refs_1_.5) | copy-start | bytes 1572868
  4.1 14.3 %copy-start = (bf16[2,2,2,256,256]{4,3,2,1,0:T(8,128)(2,1)S(1)}, bf16[2,2,2,256,256]{4,3,2,1,0:T(8,128)(2,1)}, u32[]{:S(2)}) copy-start(bf16[2,2,2,256,256]{4,3,2,1,0:T(8,128)(2,1)} %constant.4.clone.refs_9_.refs_10_.refs_11_) | copy-start | bytes 3145732
  4.1 4.9 %collective-permute-start = (f32[2,136,128]{2,1,0:T(8,128)S(1)}, f32[2,136,128]{2,1,0:T(8,128)S(1)}, u32[]{:S(2)}, u32[]{:S(2)}) collective-permute-start(f32[2,136,128]{2,1,0:T(8,128)S(1)} %shard_map.74), channel_id=1, source_target_pairs={{0,1},{1,0},{2,3},{3,2},{4,5},{5,4},{6,7},{7,6},{8,9},{9,8},{10,11... | collective-permute-start | bytes 417800 | tf_op jit(solution)/shard_map/ppermute | solution.py:105
  5.4 1.0 %copy-start.4 = (f32[1,1,2,256,256]{4,3,2,1,0:T(8,128)S(1)}, f32[1,1,2,256,256]{4,3,2,1,0:T(8,128)}, u32[]{:S(2)}) copy-start(f32[1,1,2,256,256]{4,3,2,1,0:T(8,128)} %param.9) | copy-start | bytes 1572868
  6.5 0.9 %copy-start.5 = (bf16[2,256,256]{2,1,0:T(8,128)(2,1)S(1)}, bf16[2,256,256]{2,1,0:T(8,128)(2,1)}, u32[]{:S(2)}) copy-start(bf16[2,256,256]{2,1,0:T(8,128)(2,1)} %constant.5.clone.order) | copy-start | bytes 786436
  8.9 9.5 %copy-start.2 = (f32[2,128,512]{2,1,0:T(8,128)S(1)}, f32[2,128,512]{2,1,0:T(8,128)}, u32[]{:S(2)}) copy-start(f32[2,128,512]{2,1,0:T(8,128)} %refs_4_.1) | copy-start | bytes 1572868
  9.6 8.8 %collective-permute-start.1 = (f32[2,152,128]{2,1,0:T(8,128)S(1)}, f32[2,152,128]{2,1,0:T(8,128)S(1)}, u32[]{:S(2)}, u32[]{:S(2)}) collective-permute-start(f32[2,152,128]{2,1,0:T(8,128)S(1)} %get-tuple-element.39), channel_id=1, source_target_pairs={{2,4},{3,5},{6,8},{7,9},{10,12},{11,13},{14,16},{15,17},{18,20},{1... | collective-permute-start | bytes 466952 | tf_op jit(solution)/shard_map/ppermute | solution.py:117
  12.0 1.4 %collective-permute-start.2 = (f32[2,144,128]{2,1,0:T(8,128)S(1)}, f32[2,144,128]{2,1,0:T(8,128)S(1)}, u32[]{:S(2)}, u32[]{:S(2)}) collective-permute-start(f32[2,144,128]{2,1,0:T(8,128)S(1)} %get-tuple-element.38.refs_2_.refs_0_.refs_5_), channel_id=1, source_target_pairs={{0,2},{2,0},{4,6},{6,4},{8,10},{10,8},{12,14},{14,12},{16,18},{18,... | collective-permute-start | bytes 442376 | tf_op jit(solution)/shard_map/ppermute | solution.py:120
  20.6 9.9 %collective-permute-start.8 = (f32[2,128,256]{2,1,0:T(8,128)S(1)}, f32[2,128,256]{2,1,0:T(8,128)S(1)}, u32[]{:S(2)}, u32[]{:S(2)}) collective-permute-start(f32[2,128,256]{2,1,0:T(8,128)S(1)} %get-tuple-element.42.refs_7_), channel_id=1, source_target_pairs={{2,4},{3,5},{6,8},{7,9},{10,12},{11,13},{14,16},{15,17},{18,20},{1... | collective-permute-start | bytes 786440 | tf_op jit(solution)/shard_map/ppermute | solution.py:117
  24.0 9.3 %collective-permute-start.9 = (f32[2,128,256]{2,1,0:T(8,128)S(1)}, f32[2,128,256]{2,1,0:T(8,128)S(1)}, u32[]{:S(2)}, u32[]{:S(2)}) collective-permute-start(f32[2,128,256]{2,1,0:T(8,128)S(1)} %get-tuple-element.43.refs_3_), channel_id=1, source_target_pairs={{2,4},{3,5},{6,8},{7,9},{10,12},{11,13},{14,16},{15,17},{18,20},{1... | collective-permute-start | bytes 786440 | tf_op jit(solution)/shard_map/ppermute | solution.py:117
  24.1 4.7 %collective-permute-start.5 = (f32[4,48,256]{2,1,0:T(8,128)S(1)}, f32[4,48,256]{2,1,0:T(8,128)S(1)}, u32[]{:S(2)}, u32[]{:S(2)}) collective-permute-start(f32[4,48,256]{2,1,0:T(8,128)S(1)} %get-tuple-element.44.refs_2_), channel_id=1, source_target_pairs={{0,2},{2,0},{4,6},{6,4},{8,10},{10,8},{12,14},{14,12},{16,18},{18,... | collective-permute-start | bytes 589832 | tf_op jit(solution)/shard_map/ppermute | solution.py:120
  24.2 4.6 %collective-permute-start.6 = (f32[4,40,256]{2,1,0:T(8,128)S(1)}, f32[4,40,256]{2,1,0:T(8,128)S(1)}, u32[]{:S(2)}, u32[]{:S(2)}) collective-permute-start(f32[4,40,256]{2,1,0:T(8,128)S(1)} %get-tuple-element.47), channel_id=1, source_target_pairs={{0,2},{2,0},{4,6},{6,4},{8,10},{10,8},{12,14},{14,12},{16,18},{18,... | collective-permute-start | bytes 491528 | tf_op jit(solution)/shard_map/ppermute | solution.py:120
  24.7 4.2 %collective-permute-start.7 = (f32[4,40,256]{2,1,0:T(8,128)S(1)}, f32[4,40,256]{2,1,0:T(8,128)S(1)}, u32[]{:S(2)}, u32[]{:S(2)}) collective-permute-start(f32[4,40,256]{2,1,0:T(8,128)S(1)} %get-tuple-element.48), channel_id=1, source_target_pairs={{0,2},{2,0},{4,6},{6,4},{8,10},{10,8},{12,14},{14,12},{16,18},{18,... | collective-permute-start | bytes 491528 | tf_op jit(solution)/shard_map/ppermute | solution.py:120
  33.3 7.0 %collective-permute-start.10 = (f32[2,128,256]{2,1,0:T(8,128)S(1)}, f32[2,128,256]{2,1,0:T(8,128)S(1)}, u32[]{:S(2)}, u32[]{:S(2)}) collective-permute-start(f32[2,128,256]{2,1,0:T(8,128)S(1)} %shard_map.82.refs_4_), channel_id=1, source_target_pairs={{0,1},{1,0},{2,3},{3,2},{4,5},{5,4},{6,7},{7,6},{8,9},{9,8},{10,11... | collective-permute-start | bytes 786440 | tf_op jit(solution)/shard_map/ppermute | solution.py:105
  34.7 13.4 %collective-permute-start.11 = (f32[2,128,384]{2,1,0:T(8,128)S(1)}, f32[2,128,384]{2,1,0:T(8,128)S(1)}, u32[]{:S(2)}, u32[]{:S(2)}) collective-permute-start(f32[2,128,384]{2,1,0:T(8,128)S(1)} %shard_map.83.refs_3_.refs_1_.refs_4_), channel_id=1, source_target_pairs={{2,4},{3,5},{6,8},{7,9},{10,12},{11,13},{14,16},{15,17},{18,20},{1... | collective-permute-start | bytes 1179656 | tf_op jit(solution)/shard_map/ppermute | solution.py:117
  40.4 7.7 %collective-permute-start.13 = (f32[2,128,256]{2,1,0:T(8,128)S(1)}, f32[2,128,256]{2,1,0:T(8,128)S(1)}, u32[]{:S(2)}, u32[]{:S(2)}) collective-permute-start(f32[2,128,256]{2,1,0:T(8,128)S(1)} %get-tuple-element.53), channel_id=1, source_target_pairs={{0,2},{2,0},{4,6},{6,4},{8,10},{10,8},{12,14},{14,12},{16,18},{18,... | collective-permute-start | bytes 786440 | tf_op jit(solution)/shard_map/ppermute | solution.py:120
  40.5 7.6 %collective-permute-start.14 = (f32[2,128,256]{2,1,0:T(8,128)S(1)}, f32[2,128,256]{2,1,0:T(8,128)S(1)}, u32[]{:S(2)}, u32[]{:S(2)}) collective-permute-start(f32[2,128,256]{2,1,0:T(8,128)S(1)} %get-tuple-element.54), channel_id=1, source_target_pairs={{0,2},{2,0},{4,6},{6,4},{8,10},{10,8},{12,14},{14,12},{16,18},{18,... | collective-permute-start | bytes 786440 | tf_op jit(solution)/shard_map/ppermute | solution.py:120
  41.0 9.9 %collective-permute-start.12 = (f32[2,128,256]{2,1,0:T(8,128)S(1)}, f32[2,128,256]{2,1,0:T(8,128)S(1)}, u32[]{:S(2)}, u32[]{:S(2)}) collective-permute-start(f32[2,128,256]{2,1,0:T(8,128)S(1)} %get-tuple-element.52.refs_2_.refs_5_), channel_id=1, source_target_pairs={{2,4},{3,5},{6,8},{7,9},{10,12},{11,13},{14,16},{15,17},{18,20},{1... | collective-permute-start | bytes 786440 | tf_op jit(solution)/shard_map/ppermute | solution.py:117
  42.5 1.3 %collective-permute-start.15 = (f32[2,128,128]{2,1,0:T(8,128)S(1)}, f32[2,128,128]{2,1,0:T(8,128)S(1)}, u32[]{:S(2)}, u32[]{:S(2)}) collective-permute-start(f32[2,128,128]{2,1,0:T(8,128)S(1)} %get-tuple-element.55), channel_id=1, source_target_pairs={{0,2},{2,0},{4,6},{6,4},{8,10},{10,8},{12,14},{14,12},{16,18},{18,... | collective-permute-start | bytes 393224 | tf_op jit(solution)/shard_map/ppermute | solution.py:120
  53.0 8.6 %collective-permute-start.19 = (f32[2,128,256]{2,1,0:T(8,128)S(1)}, f32[2,128,256]{2,1,0:T(8,128)S(1)}, u32[]{:S(2)}, u32[]{:S(2)}) collective-permute-start(f32[2,128,256]{2,1,0:T(8,128)S(1)} %get-tuple-element.57.refs_8_), channel_id=1, source_target_pairs={{2,4},{3,5},{6,8},{7,9},{10,12},{11,13},{14,16},{15,17},{18,20},{1... | collective-permute-start | bytes 786440 | tf_op jit(solution)/shard_map/ppermute | solution.py:117
  57.0 2.3 %collective-permute-start.16 = (f32[4,48,256]{2,1,0:T(8,128)S(1)}, f32[4,48,256]{2,1,0:T(8,128)S(1)}, u32[]{:S(2)}, u32[]{:S(2)}) collective-permute-start(f32[4,48,256]{2,1,0:T(8,128)S(1)} %get-tuple-element.59), channel_id=1, source_target_pairs={{0,2},{2,0},{4,6},{6,4},{8,10},{10,8},{12,14},{14,12},{16,18},{18,... | collective-permute-start | bytes 589832 | tf_op jit(solution)/shard_map/ppermute | solution.py:120
  57.0 1.7 %collective-permute-start.17 = (f32[4,40,256]{2,1,0:T(8,128)S(1)}, f32[4,40,256]{2,1,0:T(8,128)S(1)}, u32[]{:S(2)}, u32[]{:S(2)}) collective-permute-start(f32[4,40,256]{2,1,0:T(8,128)S(1)} %get-tuple-element.60), channel_id=1, source_target_pairs={{0,2},{2,0},{4,6},{6,4},{8,10},{10,8},{12,14},{14,12},{16,18},{18,... | collective-permute-start | bytes 491528 | tf_op jit(solution)/shard_map/ppermute | solution.py:120
  57.6 1.8 %collective-permute-start.18 = (f32[4,40,256]{2,1,0:T(8,128)S(1)}, f32[4,40,256]{2,1,0:T(8,128)S(1)}, u32[]{:S(2)}, u32[]{:S(2)}) collective-permute-start(f32[4,40,256]{2,1,0:T(8,128)S(1)} %get-tuple-element.61), channel_id=1, source_target_pairs={{0,2},{2,0},{4,6},{6,4},{8,10},{10,8},{12,14},{14,12},{16,18},{18,... | collective-permute-start | bytes 491528 | tf_op jit(solution)/shard_map/ppermute | solution.py:120
  57.6 7.2 %collective-permute-start.20 = (f32[2,128,128]{2,1,0:T(8,128)S(1)}, f32[2,128,128]{2,1,0:T(8,128)S(1)}, u32[]{:S(2)}, u32[]{:S(2)}) collective-permute-start(f32[2,128,128]{2,1,0:T(8,128)S(1)} %get-tuple-element.65), channel_id=1, source_target_pairs={{2,4},{3,5},{6,8},{7,9},{10,12},{11,13},{14,16},{15,17},{18,20},{1... | collective-permute-start | bytes 393224 | tf_op jit(solution)/shard_map/ppermute | solution.py:117
  58.7 7.4 %collective-permute-start.21 = (f32[2,128,128]{2,1,0:T(8,128)S(1)}, f32[2,128,128]{2,1,0:T(8,128)S(1)}, u32[]{:S(2)}, u32[]{:S(2)}) collective-permute-start(f32[2,128,128]{2,1,0:T(8,128)S(1)} %get-tuple-element.66), channel_id=1, source_target_pairs={{2,4},{3,5},{6,8},{7,9},{10,12},{11,13},{14,16},{15,17},{18,20},{1... | collective-permute-start | bytes 393224 | tf_op jit(solution)/shard_map/ppermute | solution.py:117
  64.8 4.4 %collective-permute-start.22 = (f32[2,128,128]{2,1,0:T(8,128)S(1)}, f32[2,128,128]{2,1,0:T(8,128)S(1)}, u32[]{:S(2)}, u32[]{:S(2)}) collective-permute-start(f32[2,128,128]{2,1,0:T(8,128)S(1)} %shard_map.89.refs_3_), channel_id=1, source_target_pairs={{0,1},{1,0},{2,3},{3,2},{4,5},{5,4},{6,7},{7,6},{8,9},{9,8},{10,11... | collective-permute-start | bytes 393224 | tf_op jit(solution)/shard_map/ppermute | solution.py:105

commit v14 on v13

--- a/solution.py
+++ b/solution.py
@@ -231,6 +231,10 @@
         result[...] = values
         copy[...] = values
     spread(middle, near[sides:])
+
+
+def spot_kernel(spot, _, copy):
+    copy[...] = spot[...]
 
 
 def prepare_kernel(centres, probe, amps, order, rolled, ordered, padded):
@@ -316,7 +320,11 @@
 
 def term_kernel(plan, slot, layout, pieces, copied, halves, slots, spot, *rest):
     refs, rest = rest[:pieces], rest[pieces:]
-    earlier, (probe, amps, tables, outer, inner), rest = rest[:copied], rest[copied : copied + 5], rest[copied + 5 :]
+    earlier, (probe, amps, tables, inner), rest = rest[:copied], rest[copied : copied + 4], rest[copied + 4 :]
+    if halves:
+        outer, rest = rest[-1], rest[:-1]
+    else:
+        outer, rest = rest[0], rest[1:]
     outer_halves, near_outers, (window, picked) = rest[:halves], rest[halves:-2], rest[-2:]
     size = probe.shape[2]
     half = size // 2
@@ -489,13 +497,13 @@
         target[part] = base[part, :, lanes(tile)] - part_of(plan, patch, mask, part, tile) * inverse[:, lanes(tile)]
 
 
-def middle_kernel(plan, base, patch, mask, inverse, _, middle):
+def middle_kernel(plan, base, patch, mask, inverse, middle):
     _, t = here()
     for step in range(plan.mid_tiles):
         take_off(plan, patch, mask, middle.at[:, :, lanes(step)], base, inverse, plan.mid_start(t) + step)
 
 
-def boundary_kernel(plan, early, patch, mask, *sums):
+def boundary_kernel(plan, early, patch, mask, _, *sums):
     _, t = here()
     for total, start in zip(sums, plan.pair_starts(t)):
         for step in range(2):
@@ -623,16 +631,18 @@
             earlier = outer if last else []
             patch = shape((2, half, size), f32)
             halves = 2 if last and sweep == ITERS - 1 else 0
-            outer_part, inner_part, *copies = call(
+            inner_part, *copies = call(
                 lambda *refs, slot=slot, layout=layout, copied=len(earlier), halves=halves: term_kernel(
                     plan, slot, layout, len(pieces), copied, halves, slots, *refs
                 ),
-                [patch] * 2
-                + [shape((2, half, LANES), f32)] * halves
+                [patch]
+                + ([shape((2, half, LANES), f32)] * halves or [patch])
                 + [shape((2 * slots, rows, size), f32) for rows in near_heights if last],
-                [pltpu.VMEM((2, size, size), f32), pltpu.VMEM((3, 3, 2, half, LANES), f32)],
+                [pltpu.VMEM((2, size, size), f32), pltpu.VMEM((3, 3, 2, half, LANES), f32)]
+                + [pltpu.VMEM((2, half, size), f32)] * (halves > 0),
                 [own_spot, *pieces, *earlier, rolled, ordered, tables],
             )
+            outer_part = None if halves else copies.pop(0)
             outer_halves, copies = copies[:halves], copies[halves:]
             inner.append(inner_part)
             outer.append(outer_part)
@@ -671,21 +681,21 @@
             [info, early, inverse, *outer_far[:-1], *pieces],
         )
         if sweep < ITERS - 1:
+            middle = call(
+                lambda *refs: middle_kernel(plan, *refs),
+                shape((2, half, plan.mid_tiles * LANES), f32),
+                [],
+                [base, outer_far[-1], mask, inverse],
+            )
+            far_middle = plan.far_rows(middle)
             sums = call(
                 lambda *refs: boundary_kernel(plan, *refs),
                 [shape((2, half, 2 * LANES), f32)] * sides,
                 [],
-                [early, outer_far[-1], mask],
+                [early, outer_far[-1], mask, middle],
+                in_specs=[VMEM] * 3 + [ANY],
             )
             received = plan.across(sums)
-            middle = call(
-                lambda *refs: middle_kernel(plan, *refs),
-                shape((2, half, plan.mid_tiles * LANES), f32),
-                [],
-                [base, outer_far[-1], mask, inverse, sums[0]],
-                in_specs=[VMEM] * 4 + [ANY],
-            )
-            far_middle = plan.far_rows(middle)
             near_runs = [shape((2, half, count * LANES), f32) for count in chunks(plan.mid_tiles)]
             updated = call(
                 lambda *refs: pair_kernel(plan, *refs),
@@ -698,6 +708,14 @@
             far = [far_middle] + [plan.far_rows(piece) for piece in pairs]
             near = [plan.near_rows(piece) for piece in updated[sides:]]
             layout = later_layout
+            own_spot = call(
+                spot_kernel,
+                shape(own_spot.shape, f32),
+                [],
+                [own_spot, far_middle],
+                in_specs=[VMEM, ANY],
+                flops=10**11,
+            )
     sums = call(
         lambda *refs: halo_sum_kernel(plan, *refs),
         [shape((2, half, LANES), f32)] * sides,

time: 70.5 us -> 71.7 us (1.017)
  the two profiles are of different devices: /device:TPU:17 before, /device:TPU:10 now
where the time goes in v14:
time: 71.7 us; the launch traced here: 70.9 us
  waiting for transfers between devices  32.5 us (45%)
  starting transfers between devices  17.7 us (25%)
  Pallas kernels  16.6 us (23%)
  local copies, waits for them, and re-layouts  3.73 us (5%)
    ppermute x9, waiting for transfers between devices, far_rows(): lax.ppermute(values, ('sx', 'sy'), pairs + [(j, i) for i, j in pairs])  21.8 us
    pallas_call x20, Pallas kernels, call(): pl.pallas_call(kernel, out_shape=outs, in_specs=in_specs or [SMEM if valu...  16.6 us
    ppermute x3, waiting for transfers between devices, across(): return [lax.ppermute(values[0], axis_name, [(0, 1), (1, 0)])]  9.63 us
    ppermute x9, starting transfers between devices, far_rows(): lax.ppermute(values, ('sx', 'sy'), pairs + [(j, i) for i, j in pairs])  9.47 us
    ppermute x3, starting transfers between devices, across(): return [lax.ppermute(values[0], axis_name, [(0, 1), (1, 0)])]  4.77 us
    unnamed x16, local copies, waits for them, and re-layouts  3.73 us
    ppermute x11, starting transfers between devices, near_rows(): return lax.ppermute(values, 'sx', [(i, i ^ 1) for i in range(self.sx_size)])  3.5 us
  transfers between devices with their start and end apart: 23, of which 11 were waited for; matrix products, arithmetic and copies ran while one was open for 0% of the time, Pallas kernels for 16%

profile of v14, /device:TPU:10, one launch (start us, length us, event | category | flops | bytes accessed | tf_op | source)
XLA Modules:
  0.0 70.9 jit_solution(2384988025113500132)
XLA Ops:
  1.3 1.0 %copy-done.1 = f32[2,128,512]{2,1,0:T(8,128)S(1)} copy-done((f32[2,128,512]{2,1,0:T(8,128)S(1)}, f32[2,128,512]{2,1,0:T(8,128)}, u32[]{:S(2)}) %copy-start.1) | copy-done | bytes 524312
  3.0 1.6 %collective-permute-start = (f32[2,136,128]{2,1,0:T(8,128)S(1)}, f32[2,136,128]{2,1,0:T(8,128)S(1)}, u32[]{:S(2)}, u32[]{:S(2)}) collective-permute-start(f32[2,136,128]{2,1,0:T(8,128)S(1)} %shard_map.74), channel_id=1, source_target_pairs={{0,1},{1,0},{2,3},{3,2},{4,5},{5,4},{6,7},{7,6},{8,9},{9,8},{10,11... | collective-permute-start | bytes 417800 | tf_op jit(solution)/shard_map/ppermute | solution.py:105
  4.6 1.0 %copy-done.4 = f32[1,1,2,256,256]{4,3,2,1,0:T(8,128)S(1)} copy-done((f32[1,1,2,256,256]{4,3,2,1,0:T(8,128)S(1)}, f32[1,1,2,256,256]{4,3,2,1,0:T(8,128)}, u32[]{:S(2)}) %copy-start.4) | copy-done | bytes 524312
  5.6 0.9 %copy-done.5 = bf16[2,256,256]{2,1,0:T(8,128)(2,1)S(1)} copy-done((bf16[2,256,256]{2,1,0:T(8,128)(2,1)S(1)}, bf16[2,256,256]{2,1,0:T(8,128)(2,1)}, u32[]{:S(2)}) %copy-start.5) | copy-done | bytes 262168
  6.6 1.5 %shard_map.73 = (f32[2,2,256,256]{3,2,1,0:T(8,128)S(1)}, f32[2,256,256]{2,1,0:T(8,128)S(1)}) custom-call(s32[2,2]{1,0:T(2,128)S(1)} %bitcast.5, f32[2,256,256]{2,1,0:T(8,128)S(1)} %copy-done.3, f32[2,256,256]{2,1,0:T(8,128)S(1)} %bitcast.3, bf16[2,256,256]{2,1,0:T(8,128)(2,1)S(1)} %copy-done.5), custom_call_target="tpu_custom_call" | custom-call | flops 100000 | bytes 10000 | tf_op jit(solution)/shard_map/pallas_call | solution.py:553
  8.1 1.4 %collective-permute-done.refs_3_ = f32[2,136,128]{2,1,0:T(8,128)S(1)} collective-permute-done((f32[2,136,128]{2,1,0:T(8,128)S(1)}, f32[2,136,128]{2,1,0:T(8,128)S(1)}, u32[]{:S(2)}, u32[]{:S(2)}) %collective-permute-start) | collective-permute-done | bytes 139296 | tf_op jit(solution)/shard_map/ppermute | solution.py:105
  10.2 1.7 %collective-permute-start.2 = (f32[2,144,128]{2,1,0:T(8,128)S(1)}, f32[2,144,128]{2,1,0:T(8,128)S(1)}, u32[]{:S(2)}, u32[]{:S(2)}) collective-permute-start(f32[2,144,128]{2,1,0:T(8,128)S(1)} %get-tuple-element.38.refs_2_.refs_0_.refs_5_), channel_id=1, source_target_pairs={{0,2},{2,0},{4,6},{6,4},{8,10},{10,8},{12,14},{14,12},{16,18},{18,... | collective-permute-start | bytes 442376 | tf_op jit(solution)/shard_map/ppermute | solution.py:120
  11.9 1.0 %collective-permute-done.2.refs_5_.refs_2_.refs_8_ = f32[2,144,128]{2,1,0:T(8,128)S(1)} collective-permute-done((f32[2,144,128]{2,1,0:T(8,128)S(1)}, f32[2,144,128]{2,1,0:T(8,128)S(1)}, u32[]{:S(2)}, u32[]{:S(2)}) %collective-permute-start.2) | collective-permute-done | bytes 147488 | tf_op jit(solution)/shard_map/ppermute | solution.py:120
  12.9 4.9 %collective-permute-done.1.refs_4_.refs_1_.refs_7_ = f32[2,152,128]{2,1,0:T(8,128)S(1)} collective-permute-done((f32[2,152,128]{2,1,0:T(8,128)S(1)}, f32[2,152,128]{2,1,0:T(8,128)S(1)}, u32[]{:S(2)}, u32[]{:S(2)}) %collective-permute-start.1) | collective-permute-done | bytes 155680 | tf_op jit(solution)/shard_map/ppermute | solution.py:117
  17.8 2.2 %shard_map.76 = (f32[2,128,256]{2,1,0:T(8,128)S(1)}, f32[2,128,256]{2,1,0:T(8,128)S(1)}) custom-call(f32[8,128]{1,0:T(8,128)S(1)} %get-tuple-element.40.refs_0_.spot, f32[2,128,512]{2,1,0:T(8,128)S(1)} %copy-done.2, f32[2,144,128]{2,1,0:T(8,128)S(1)} %get-tuple-element.38.refs_2_.refs_0_.refs_5_, f32[2,128,512]{2,1,0:T(8,128)S(1)} %collective-permute-done.3.refs_3_.refs_6_, ...), custom_call_target="tpu_custom_call" | custom-call | flops 100000 | bytes 10000 | tf_op jit(solution)/shard_map/pallas_call | solution.py:553
  20.0 0.7 collective-permute-start.8
  20.9 3.2 %collective-permute-start.9 = (f32[2,128,256]{2,1,0:T(8,128)S(1)}, f32[2,128,256]{2,1,0:T(8,128)S(1)}, u32[]{:S(2)}, u32[]{:S(2)}) collective-permute-start(f32[2,128,256]{2,1,0:T(8,128)S(1)} %get-tuple-element.43.refs_3_), channel_id=1, source_target_pairs={{2,4},{3,5},{6,8},{7,9},{10,12},{11,13},{14,16},{15,17},{18,20},{1... | collective-permute-start | bytes 786440 | tf_op jit(solution)/shard_map/ppermute | solution.py:117
  24.5 1.2 %shard_map.78.refs_0_ = s32[6,128]{1,0:T(8,128)S(1)} custom-call(f32[2,144,128]{2,1,0:T(8,128)S(1)} %get-tuple-element.38.refs_2_.refs_0_.refs_5_, f32[2,152,128]{2,1,0:T(8,128)S(1)} %collective-permute-done.1.refs_4_.refs_1_.refs_7_, f32[2,144,128]{2,1,0:T(8,128)S(1)} %collective-permute-done.2.refs_5_.refs_2_.refs_8_, ...), custom_call_target="tpu_custom_call" | custom-call | flops 100000 | bytes 10000 | tf_op jit(solution)/shard_map/pallas_call | solution.py:553
  25.8 2.5 %shard_map.79.refs_2_.refs_3_.refs_0_ = f32[128,768]{1,0:T(8,128)S(1)} custom-call(s32[6,128]{1,0:T(8,128)S(1)} %shard_map.78.refs_0_, f32[2,256,256]{2,1,0:T(8,128)S(1)} %copy-done.3, f32[4,48,256]{2,1,0:T(8,128)S(1)} %get-tuple-element.44.refs_2_), custom_call_target="tpu_custom_call" | custom-call | flops 100000 | bytes 10000 | tf_op jit(solution)/shard_map/pallas_call | solution.py:553
  28.3 0.9 %shard_map.80.refs_1_ = f32[2,128,768]{2,1,0:T(8,128)S(1)} custom-call(s32[6,128]{1,0:T(8,128)S(1)} %shard_map.78.refs_0_, f32[2,128,256]{2,1,0:T(8,128)S(1)} %get-tuple-element.45.refs_1_, f32[2,128,256]{2,1,0:T(8,128)S(1)} %get-tuple-element.46.refs_2_, f32[4,48,256]{2,1,0:T(8,128)S(1)} %collective-permute-done.5.refs_3_, ...), custom_call_target="tpu_custom_call" | custom-call | flops 100000 | bytes 10000 | tf_op jit(solution)/shard_map/pallas_call | solution.py:553
  29.2 1.6 %collective-permute-done.8.refs_3_ = f32[2,128,256]{2,1,0:T(8,128)S(1)} collective-permute-done((f32[2,128,256]{2,1,0:T(8,128)S(1)}, f32[2,128,256]{2,1,0:T(8,128)S(1)}, u32[]{:S(2)}, u32[]{:S(2)}) %collective-permute-start.8) | collective-permute-done | bytes 262176 | tf_op jit(solution)/shard_map/ppermute | solution.py:117
  30.8 1.0 %shard_map.81 = (f32[2,128,768]{2,1,0:T(8,128)S(1)}, f32[2,128,768]{2,1,0:T(8,128)S(1)}, f32[128,768]{1,0:T(8,128)S(1)}) custom-call(s32[6,128]{1,0:T(8,128)S(1)} %shard_map.78.refs_0_, f32[2,128,768]{2,1,0:T(8,128)S(1)} %shard_map.80.refs_1_, f32[128,768]{1,0:T(8,128)S(1)} %shard_map.79.refs_2_.refs_3_.refs_0_, ...), custom_call_target="tpu_custom_call" | custom-call | flops 100000 | bytes 10000 | tf_op jit(solution)/shard_map/pallas_call | solution.py:553
  31.8 1.8 %collective-permute-done.9.refs_1_ = f32[2,128,256]{2,1,0:T(8,128)S(1)} collective-permute-done((f32[2,128,256]{2,1,0:T(8,128)S(1)}, f32[2,128,256]{2,1,0:T(8,128)S(1)}, u32[]{:S(2)}, u32[]{:S(2)}) %collective-permute-start.9) | collective-permute-done | bytes 262176 | tf_op jit(solution)/shard_map/ppermute | solution.py:117
  33.8 1.6 %collective-permute-start.11 = (f32[2,128,256]{2,1,0:T(8,128)S(1)}, f32[2,128,256]{2,1,0:T(8,128)S(1)}, u32[]{:S(2)}, u32[]{:S(2)}) collective-permute-start(f32[2,128,256]{2,1,0:T(8,128)S(1)} %shard_map.84.refs_4_), channel_id=1, source_target_pairs={{0,1},{1,0},{2,3},{3,2},{4,5},{5,4},{6,7},{7,6},{8,9},{9,8},{10,11... | collective-permute-start | bytes 786440 | tf_op jit(solution)/shard_map/ppermute | solution.py:105
  35.4 5.6 %collective-permute-done.11.refs_5_ = f32[2,128,256]{2,1,0:T(8,128)S(1)} collective-permute-done((f32[2,128,256]{2,1,0:T(8,128)S(1)}, f32[2,128,256]{2,1,0:T(8,128)S(1)}, u32[]{:S(2)}, u32[]{:S(2)}) %collective-permute-start.11) | collective-permute-done | bytes 262176 | tf_op jit(solution)/shard_map/ppermute | solution.py:105
  41.8 1.6 %collective-permute-done.10._.refs_3_.refs_6_ = f32[2,128,384]{2,1,0:T(8,128)S(1)} collective-permute-done((f32[2,128,384]{2,1,0:T(8,128)S(1)}, f32[2,128,384]{2,1,0:T(8,128)S(1)}, u32[]{:S(2)}, u32[]{:S(2)}) %collective-permute-start.10) | collective-permute-done | bytes 393248 | tf_op jit(solution)/shard_map/ppermute | solution.py:117
  43.4 7.0 %collective-permute-done.12.refs_4_.refs_7_ = f32[2,128,256]{2,1,0:T(8,128)S(1)} collective-permute-done((f32[2,128,256]{2,1,0:T(8,128)S(1)}, f32[2,128,256]{2,1,0:T(8,128)S(1)}, u32[]{:S(2)}, u32[]{:S(2)}) %collective-permute-start.12) | collective-permute-done | bytes 262176 | tf_op jit(solution)/shard_map/ppermute | solution.py:117
  50.4 2.1 %shard_map.86 = (f32[2,128,256]{2,1,0:T(8,128)S(1)}, f32[2,128,256]{2,1,0:T(8,128)S(1)}) custom-call(f32[8,128]{1,0:T(8,128)S(1)} %shard_map.83.refs_0_, f32[2,128,384]{2,1,0:T(8,128)S(1)} %shard_map.82.refs_3_.refs_1_.refs_4_, f32[2,128,256]{2,1,0:T(8,128)S(1)} %get-tuple-element.52.refs_2_.refs_5_, ...), custom_call_target="tpu_custom_call" | custom-call | flops 100000 | bytes 10000 | tf_op jit(solution)/shard_map/pallas_call | solution.py:553
  53.5 3.7 %collective-permute-start.20 = (f32[2,128,128]{2,1,0:T(8,128)S(1)}, f32[2,128,128]{2,1,0:T(8,128)S(1)}, u32[]{:S(2)}, u32[]{:S(2)}) collective-permute-start(f32[2,128,128]{2,1,0:T(8,128)S(1)} %get-tuple-element.65), channel_id=1, source_target_pairs={{2,4},{3,5},{6,8},{7,9},{10,12},{11,13},{14,16},{15,17},{18,20},{1... | collective-permute-start | bytes 393224 | tf_op jit(solution)/shard_map/ppermute | solution.py:117
  57.2 1.1 %collective-permute-start.21 = (f32[2,128,128]{2,1,0:T(8,128)S(1)}, f32[2,128,128]{2,1,0:T(8,128)S(1)}, u32[]{:S(2)}, u32[]{:S(2)}) collective-permute-start(f32[2,128,128]{2,1,0:T(8,128)S(1)} %get-tuple-element.66), channel_id=1, source_target_pairs={{2,4},{3,5},{6,8},{7,9},{10,12},{11,13},{14,16},{15,17},{18,20},{1... | collective-permute-start | bytes 393224 | tf_op jit(solution)/shard_map/ppermute | solution.py:117
  58.3 0.9 %shard_map.88.refs_1_ = f32[2,128,768]{2,1,0:T(8,128)S(1)} custom-call(s32[6,128]{1,0:T(8,128)S(1)} %shard_map.78.refs_0_, f32[2,128,256]{2,1,0:T(8,128)S(1)} %get-tuple-element.56.refs_1_, f32[2,128,256]{2,1,0:T(8,128)S(1)} %get-tuple-element.58.refs_2_, f32[4,48,256]{2,1,0:T(8,128)S(1)} %collective-permute-done.16.refs_3_, ...), custom_call_target="tpu_custom_call" | custom-call | flops 100000 | bytes 10000 | tf_op jit(solution)/shard_map/pallas_call | solution.py:553
  59.1 3.2 %collective-permute-done.19.refs_3_ = f32[2,128,256]{2,1,0:T(8,128)S(1)} collective-permute-done((f32[2,128,256]{2,1,0:T(8,128)S(1)}, f32[2,128,256]{2,1,0:T(8,128)S(1)}, u32[]{:S(2)}, u32[]{:S(2)}) %collective-permute-start.19) | collective-permute-done | bytes 262176 | tf_op jit(solution)/shard_map/ppermute | solution.py:117
  62.3 1.0 %shard_map.89 = (f32[2,128,768]{2,1,0:T(8,128)S(1)}, f32[2,128,768]{2,1,0:T(8,128)S(1)}, f32[128,768]{1,0:T(8,128)S(1)}) custom-call(s32[6,128]{1,0:T(8,128)S(1)} %shard_map.78.refs_0_, f32[2,128,768]{2,1,0:T(8,128)S(1)} %shard_map.88.refs_1_, f32[128,768]{1,0:T(8,128)S(1)} %shard_map.79.refs_2_.refs_3_.refs_0_, ...), custom_call_target="tpu_custom_call" | custom-call | flops 100000 | bytes 10000 | tf_op jit(solution)/shard_map/pallas_call | solution.py:553
  63.3 1.8 %collective-permute-done.20.refs_2_.refs_4_ = f32[2,128,128]{2,1,0:T(8,128)S(1)} collective-permute-done((f32[2,128,128]{2,1,0:T(8,128)S(1)}, f32[2,128,128]{2,1,0:T(8,128)S(1)}, u32[]{:S(2)}, u32[]{:S(2)}) %collective-permute-start.20) | collective-permute-done | bytes 131104 | tf_op jit(solution)/shard_map/ppermute | solution.py:117
  65.1 1.6 %collective-permute-start.22 = (f32[2,128,128]{2,1,0:T(8,128)S(1)}, f32[2,128,128]{2,1,0:T(8,128)S(1)}, u32[]{:S(2)}, u32[]{:S(2)}) collective-permute-start(f32[2,128,128]{2,1,0:T(8,128)S(1)} %shard_map.90.refs_3_), channel_id=1, source_target_pairs={{0,1},{1,0},{2,3},{3,2},{4,5},{5,4},{6,7},{7,6},{8,9},{9,8},{10,11... | collective-permute-start | bytes 393224 | tf_op jit(solution)/shard_map/ppermute | solution.py:105
  66.7 0.9 %shard_map.91 = (f32[2,128,512]{2,1,0:T(8,128)}, f32[2,128,128]{2,1,0:T(8,128)S(1)}) custom-call(f32[2,128,768]{2,1,0:T(8,128)S(1)} %get-tuple-element.62.refs_0_, f32[128,768]{1,0:T(8,128)S(1)} %get-tuple-element.63.refs_1_, f32[128,768]{1,0:T(8,128)S(1)} %shard_map.79.refs_2_.refs_3_.refs_0_, f32[2,128,128]{2,1,0:T(8,128)S(1)} %shard_map.90.refs_3_, ...), custom_call_target="tpu_custom_call" | custom-call | flops 100000 | bytes 10000 | tf_op jit(solution)/shard_map/pallas_call | solution.py:553
  67.6 2.6 %collective-permute-done.22.refs_2_ = f32[2,128,128]{2,1,0:T(8,128)S(1)} collective-permute-done((f32[2,128,128]{2,1,0:T(8,128)S(1)}, f32[2,128,128]{2,1,0:T(8,128)S(1)}, u32[]{:S(2)}, u32[]{:S(2)}) %collective-permute-start.22) | collective-permute-done | bytes 131104 | tf_op jit(solution)/shard_map/ppermute | solution.py:105
  (50 shorter events, 6.0 us)
Async XLA Ops:
  0.0 17.8 %collective-permute-start.4 = (f32[2,128,512]{2,1,0:T(8,128)}, f32[2,128,512]{2,1,0:T(8,128)S(1)}, u32[]{:S(2)}, u32[]{:S(2)}) collective-permute-start(f32[2,128,512]{2,1,0:T(8,128)} %refs_4_.1), channel_id=1, source_target_pairs={{0,2},{2,0},{4,6},{6,4},{8,10},{10,8},{12,14},{14,12},{16,18},{18,... | collective-permute-start | bytes 1572872 | tf_op jit(solution)/shard_map/ppermute | solution.py:120
  0.0 17.8 %collective-permute-start.3 = (f32[2,128,512]{2,1,0:T(8,128)}, f32[2,128,512]{2,1,0:T(8,128)S(1)}, u32[]{:S(2)}, u32[]{:S(2)}) collective-permute-start(f32[2,128,512]{2,1,0:T(8,128)} %refs_4_.1), channel_id=1, source_target_pairs={{2,4},{3,5},{6,8},{7,9},{10,12},{11,13},{14,16},{15,17},{18,20},{1... | collective-permute-start | bytes 1572872 | tf_op jit(solution)/shard_map/ppermute | solution.py:117
  0.7 0.7 copy-start.6
  0.7 0.7 copy-start.7
  1.3 1.0 %copy-start.1 = (f32[2,128,512]{2,1,0:T(8,128)S(1)}, f32[2,128,512]{2,1,0:T(8,128)}, u32[]{:S(2)}) copy-start(f32[2,128,512]{2,1,0:T(8,128)} %refs_4_.1) | copy-start | bytes 1572868
  2.4 2.2 %copy-start.3 = (f32[2,256,256]{2,1,0:T(8,128)S(1)}, f32[2,256,256]{2,1,0:T(8,128)}, u32[]{:S(2)}) copy-start(f32[2,256,256]{2,1,0:T(8,128)} %refs_1_.5) | copy-start | bytes 1572868
  3.0 14.8 %copy-start = (bf16[2,2,2,256,256]{4,3,2,1,0:T(8,128)(2,1)S(1)}, bf16[2,2,2,256,256]{4,3,2,1,0:T(8,128)(2,1)}, u32[]{:S(2)}) copy-start(bf16[2,2,2,256,256]{4,3,2,1,0:T(8,128)(2,1)} %constant.4.clone.refs_9_.refs_10_.refs_11_) | copy-start | bytes 3145732
  3.0 6.6 %collective-permute-start = (f32[2,136,128]{2,1,0:T(8,128)S(1)}, f32[2,136,128]{2,1,0:T(8,128)S(1)}, u32[]{:S(2)}, u32[]{:S(2)}) collective-permute-start(f32[2,136,128]{2,1,0:T(8,128)S(1)} %shard_map.74), channel_id=1, source_target_pairs={{0,1},{1,0},{2,3},{3,2},{4,5},{5,4},{6,7},{7,6},{8,9},{9,8},{10,11... | collective-permute-start | bytes 417800 | tf_op jit(solution)/shard_map/ppermute | solution.py:105
  4.6 1.0 %copy-start.4 = (f32[1,1,2,256,256]{4,3,2,1,0:T(8,128)S(1)}, f32[1,1,2,256,256]{4,3,2,1,0:T(8,128)}, u32[]{:S(2)}) copy-start(f32[1,1,2,256,256]{4,3,2,1,0:T(8,128)} %param.9) | copy-start | bytes 1572868
  5.6 0.9 %copy-start.5 = (bf16[2,256,256]{2,1,0:T(8,128)(2,1)S(1)}, bf16[2,256,256]{2,1,0:T(8,128)(2,1)}, u32[]{:S(2)}) copy-start(bf16[2,256,256]{2,1,0:T(8,128)(2,1)} %constant.5.clone.order) | copy-start | bytes 786436
  8.1 9.7 %copy-start.2 = (f32[2,128,512]{2,1,0:T(8,128)S(1)}, f32[2,128,512]{2,1,0:T(8,128)}, u32[]{:S(2)}) copy-start(f32[2,128,512]{2,1,0:T(8,128)} %refs_4_.1) | copy-start | bytes 1572868
  10.1 7.6 %collective-permute-start.1 = (f32[2,152,128]{2,1,0:T(8,128)S(1)}, f32[2,152,128]{2,1,0:T(8,128)S(1)}, u32[]{:S(2)}, u32[]{:S(2)}) collective-permute-start(f32[2,152,128]{2,1,0:T(8,128)S(1)} %get-tuple-element.39), channel_id=1, source_target_pairs={{2,4},{3,5},{6,8},{7,9},{10,12},{11,13},{14,16},{15,17},{18,20},{1... | collective-permute-start | bytes 466952 | tf_op jit(solution)/shard_map/ppermute | solution.py:117
  10.2 2.7 %collective-permute-start.2 = (f32[2,144,128]{2,1,0:T(8,128)S(1)}, f32[2,144,128]{2,1,0:T(8,128)S(1)}, u32[]{:S(2)}, u32[]{:S(2)}) collective-permute-start(f32[2,144,128]{2,1,0:T(8,128)S(1)} %get-tuple-element.38.refs_2_.refs_0_.refs_5_), channel_id=1, source_target_pairs={{0,2},{2,0},{4,6},{6,4},{8,10},{10,8},{12,14},{14,12},{16,18},{18,... | collective-permute-start | bytes 442376 | tf_op jit(solution)/shard_map/ppermute | solution.py:120
  20.0 10.8 %collective-permute-start.8 = (f32[2,128,256]{2,1,0:T(8,128)S(1)}, f32[2,128,256]{2,1,0:T(8,128)S(1)}, u32[]{:S(2)}, u32[]{:S(2)}) collective-permute-start(f32[2,128,256]{2,1,0:T(8,128)S(1)} %get-tuple-element.42.refs_7_), channel_id=1, source_target_pairs={{2,4},{3,5},{6,8},{7,9},{10,12},{11,13},{14,16},{15,17},{18,20},{1... | collective-permute-start | bytes 786440 | tf_op jit(solution)/shard_map/ppermute | solution.py:117
  20.9 12.7 %collective-permute-start.9 = (f32[2,128,256]{2,1,0:T(8,128)S(1)}, f32[2,128,256]{2,1,0:T(8,128)S(1)}, u32[]{:S(2)}, u32[]{:S(2)}) collective-permute-start(f32[2,128,256]{2,1,0:T(8,128)S(1)} %get-tuple-element.43.refs_3_), channel_id=1, source_target_pairs={{2,4},{3,5},{6,8},{7,9},{10,12},{11,13},{14,16},{15,17},{18,20},{1... | collective-permute-start | bytes 786440 | tf_op jit(solution)/shard_map/ppermute | solution.py:117
  24.0 4.3 %collective-permute-start.5 = (f32[4,48,256]{2,1,0:T(8,128)S(1)}, f32[4,48,256]{2,1,0:T(8,128)S(1)}, u32[]{:S(2)}, u32[]{:S(2)}) collective-permute-start(f32[4,48,256]{2,1,0:T(8,128)S(1)} %get-tuple-element.44.refs_2_), channel_id=1, source_target_pairs={{0,2},{2,0},{4,6},{6,4},{8,10},{10,8},{12,14},{14,12},{16,18},{18,... | collective-permute-start | bytes 589832 | tf_op jit(solution)/shard_map/ppermute | solution.py:120
  24.0 4.2 %collective-permute-start.6 = (f32[4,40,256]{2,1,0:T(8,128)S(1)}, f32[4,40,256]{2,1,0:T(8,128)S(1)}, u32[]{:S(2)}, u32[]{:S(2)}) collective-permute-start(f32[4,40,256]{2,1,0:T(8,128)S(1)} %get-tuple-element.47), channel_id=1, source_target_pairs={{0,2},{2,0},{4,6},{6,4},{8,10},{10,8},{12,14},{14,12},{16,18},{18,... | collective-permute-start | bytes 491528 | tf_op jit(solution)/shard_map/ppermute | solution.py:120
  24.5 3.8 %collective-permute-start.7 = (f32[4,40,256]{2,1,0:T(8,128)S(1)}, f32[4,40,256]{2,1,0:T(8,128)S(1)}, u32[]{:S(2)}, u32[]{:S(2)}) collective-permute-start(f32[4,40,256]{2,1,0:T(8,128)S(1)} %get-tuple-element.48), channel_id=1, source_target_pairs={{0,2},{2,0},{4,6},{6,4},{8,10},{10,8},{12,14},{14,12},{16,18},{18,... | collective-permute-start | bytes 491528 | tf_op jit(solution)/shard_map/ppermute | solution.py:120
  33.7 9.7 %collective-permute-start.10 = (f32[2,128,384]{2,1,0:T(8,128)S(1)}, f32[2,128,384]{2,1,0:T(8,128)S(1)}, u32[]{:S(2)}, u32[]{:S(2)}) collective-permute-start(f32[2,128,384]{2,1,0:T(8,128)S(1)} %shard_map.82.refs_3_.refs_1_.refs_4_), channel_id=1, source_target_pairs={{2,4},{3,5},{6,8},{7,9},{10,12},{11,13},{14,16},{15,17},{18,20},{1... | collective-permute-start | bytes 1179656 | tf_op jit(solution)/shard_map/ppermute | solution.py:117
  33.8 7.2 %collective-permute-start.11 = (f32[2,128,256]{2,1,0:T(8,128)S(1)}, f32[2,128,256]{2,1,0:T(8,128)S(1)}, u32[]{:S(2)}, u32[]{:S(2)}) collective-permute-start(f32[2,128,256]{2,1,0:T(8,128)S(1)} %shard_map.84.refs_4_), channel_id=1, source_target_pairs={{0,1},{1,0},{2,3},{3,2},{4,5},{5,4},{6,7},{7,6},{8,9},{9,8},{10,11... | collective-permute-start | bytes 786440 | tf_op jit(solution)/shard_map/ppermute | solution.py:105
  41.1 2.2 %collective-permute-start.15 = (f32[2,128,128]{2,1,0:T(8,128)S(1)}, f32[2,128,128]{2,1,0:T(8,128)S(1)}, u32[]{:S(2)}, u32[]{:S(2)}) collective-permute-start(f32[2,128,128]{2,1,0:T(8,128)S(1)} %get-tuple-element.55), channel_id=1, source_target_pairs={{0,2},{2,0},{4,6},{6,4},{8,10},{10,8},{12,14},{14,12},{16,18},{18,... | collective-permute-start | bytes 393224 | tf_op jit(solution)/shard_map/ppermute | solution.py:120
  41.2 2.2 %collective-permute-start.13 = (f32[2,128,256]{2,1,0:T(8,128)S(1)}, f32[2,128,256]{2,1,0:T(8,128)S(1)}, u32[]{:S(2)}, u32[]{:S(2)}) collective-permute-start(f32[2,128,256]{2,1,0:T(8,128)S(1)} %get-tuple-element.53), channel_id=1, source_target_pairs={{0,2},{2,0},{4,6},{6,4},{8,10},{10,8},{12,14},{14,12},{16,18},{18,... | collective-permute-start | bytes 786440 | tf_op jit(solution)/shard_map/ppermute | solution.py:120
  41.7 1.7 %collective-permute-start.14 = (f32[2,128,256]{2,1,0:T(8,128)S(1)}, f32[2,128,256]{2,1,0:T(8,128)S(1)}, u32[]{:S(2)}, u32[]{:S(2)}) collective-permute-start(f32[2,128,256]{2,1,0:T(8,128)S(1)} %get-tuple-element.54), channel_id=1, source_target_pairs={{0,2},{2,0},{4,6},{6,4},{8,10},{10,8},{12,14},{14,12},{16,18},{18,... | collective-permute-start | bytes 786440 | tf_op jit(solution)/shard_map/ppermute | solution.py:120
  41.8 8.6 %collective-permute-start.12 = (f32[2,128,256]{2,1,0:T(8,128)S(1)}, f32[2,128,256]{2,1,0:T(8,128)S(1)}, u32[]{:S(2)}, u32[]{:S(2)}) collective-permute-start(f32[2,128,256]{2,1,0:T(8,128)S(1)} %get-tuple-element.52.refs_2_.refs_5_), channel_id=1, source_target_pairs={{2,4},{3,5},{6,8},{7,9},{10,12},{11,13},{14,16},{15,17},{18,20},{1... | collective-permute-start | bytes 786440 | tf_op jit(solution)/shard_map/ppermute | solution.py:117
  52.5 9.8 %collective-permute-start.19 = (f32[2,128,256]{2,1,0:T(8,128)S(1)}, f32[2,128,256]{2,1,0:T(8,128)S(1)}, u32[]{:S(2)}, u32[]{:S(2)}) collective-permute-start(f32[2,128,256]{2,1,0:T(8,128)S(1)} %get-tuple-element.57.refs_8_), channel_id=1, source_target_pairs={{2,4},{3,5},{6,8},{7,9},{10,12},{11,13},{14,16},{15,17},{18,20},{1... | collective-permute-start | bytes 786440 | tf_op jit(solution)/shard_map/ppermute | solution.py:117
  52.8 5.4 %collective-permute-start.16 = (f32[4,48,256]{2,1,0:T(8,128)S(1)}, f32[4,48,256]{2,1,0:T(8,128)S(1)}, u32[]{:S(2)}, u32[]{:S(2)}) collective-permute-start(f32[4,48,256]{2,1,0:T(8,128)S(1)} %get-tuple-element.59), channel_id=1, source_target_pairs={{0,2},{2,0},{4,6},{6,4},{8,10},{10,8},{12,14},{14,12},{16,18},{18,... | collective-permute-start | bytes 589832 | tf_op jit(solution)/shard_map/ppermute | solution.py:120
  52.9 4.3 %collective-permute-start.17 = (f32[4,40,256]{2,1,0:T(8,128)S(1)}, f32[4,40,256]{2,1,0:T(8,128)S(1)}, u32[]{:S(2)}, u32[]{:S(2)}) collective-permute-start(f32[4,40,256]{2,1,0:T(8,128)S(1)} %get-tuple-element.60), channel_id=1, source_target_pairs={{0,2},{2,0},{4,6},{6,4},{8,10},{10,8},{12,14},{14,12},{16,18},{18,... | collective-permute-start | bytes 491528 | tf_op jit(solution)/shard_map/ppermute | solution.py:120
  53.4 4.8 %collective-permute-start.18 = (f32[4,40,256]{2,1,0:T(8,128)S(1)}, f32[4,40,256]{2,1,0:T(8,128)S(1)}, u32[]{:S(2)}, u32[]{:S(2)}) collective-permute-start(f32[4,40,256]{2,1,0:T(8,128)S(1)} %get-tuple-element.61), channel_id=1, source_target_pairs={{0,2},{2,0},{4,6},{6,4},{8,10},{10,8},{12,14},{14,12},{16,18},{18,... | collective-permute-start | bytes 491528 | tf_op jit(solution)/shard_map/ppermute | solution.py:120
  53.5 11.6 %collective-permute-start.20 = (f32[2,128,128]{2,1,0:T(8,128)S(1)}, f32[2,128,128]{2,1,0:T(8,128)S(1)}, u32[]{:S(2)}, u32[]{:S(2)}) collective-permute-start(f32[2,128,128]{2,1,0:T(8,128)S(1)} %get-tuple-element.65), channel_id=1, source_target_pairs={{2,4},{3,5},{6,8},{7,9},{10,12},{11,13},{14,16},{15,17},{18,20},{1... | collective-permute-start | bytes 393224 | tf_op jit(solution)/shard_map/ppermute | solution.py:117
  57.2 9.5 %collective-permute-start.21 = (f32[2,128,128]{2,1,0:T(8,128)S(1)}, f32[2,128,128]{2,1,0:T(8,128)S(1)}, u32[]{:S(2)}, u32[]{:S(2)}) collective-permute-start(f32[2,128,128]{2,1,0:T(8,128)S(1)} %get-tuple-element.66), channel_id=1, source_target_pairs={{2,4},{3,5},{6,8},{7,9},{10,12},{11,13},{14,16},{15,17},{18,20},{1... | collective-permute-start | bytes 393224 | tf_op jit(solution)/shard_map/ppermute | solution.py:117
  65.1 5.0 %collective-permute-start.22 = (f32[2,128,128]{2,1,0:T(8,128)S(1)}, f32[2,128,128]{2,1,0:T(8,128)S(1)}, u32[]{:S(2)}, u32[]{:S(2)}) collective-permute-start(f32[2,128,128]{2,1,0:T(8,128)S(1)} %shard_map.90.refs_3_), channel_id=1, source_target_pairs={{0,1},{1,0},{2,3},{3,2},{4,5},{5,4},{6,7},{7,6},{8,9},{9,8},{10,11... | collective-permute-start | bytes 393224 | tf_op jit(solution)/shard_map/ppermute | solution.py:105

commit v15 on v13

--- a/solution.py
+++ b/solution.py
@@ -207,16 +207,19 @@
 
 
 def halo_message_kernel(plan, centres, counts, _, *rest):
-    received, far, near = (rest[k * plan.sides : (k + 1) * plan.sides] for k in range(3))
+    sides = plan.sides
+    received, far, halos, infos = (rest[k * sides : (k + 1) * sides] for k in range(4))
     own = info_rows(centres, counts[lax.axis_index("sx")])
     rest[-1][...] = own
-    for source, *messages in zip(received, far, near):
-        for message in messages:
-            rows = source.shape[1]
-            message[:, :rows] = source[...]
-            for line in range(rows, message.shape[1], 8):
-                message[0, line : line + 8] = own
-                message[1, line : line + 8] = own
+    upper_line = lax.broadcasted_iota(jnp.int32, own.shape, 0) == 0
+    for source, message, halo, info in zip(received, far, halos, infos):
+        rows = halo.shape[1]
+        both = jnp.where(upper_line, own, pltpu.roll(source[0, rows : rows + 8], 1, 0))
+        halo[...] = source[:, :rows]
+        info[...] = both
+        message[:, :rows] = source[:, :rows]
+        message[0, rows:] = both
+        message[1, rows:] = both
 
 
 def pair_kernel(plan, base, early, inverse, middle, *rest):
@@ -262,20 +265,21 @@
 
 
 def info_kernel(plan, *rest):
-    groups = [rest[k * plan.sides : (k + 1) * plan.sides] for k in range(3)]
+    home, far, other = (rest[k * plan.sides : (k + 1) * plan.sides] for k in range(3))
     _, info, known, sem = rest[3 * plan.sides :]
     s, _ = here()
     upper = s % 2 == 0
-    height = plan.rows
+    width = plan.sides + 1
 
     def lines(messages):
-        return [messages[0][0, height + 8 : height + 16]] + [message[0, height : height + 8] for message in messages]
-
-    own, far, near = (lines(messages) for messages in groups)
-    far = [jnp.where(plan.outermost(s), 0.0, line) for line in far]
-    for turn in range(plan.sides + 1):
+        return [messages[0]] + [pltpu.roll(message, 7, 0) for message in messages]
+
+    own = lines([line[...] for line in home])
+    near = lines([line[...] for line in other])
+    far = lines([jnp.where(plan.outermost(s), 0.0, message[0, plan.rows :]) for message in far])
+    for turn in range(width):
         for kind, line in ((0, jnp.where(upper, far[turn], near[turn])), (1, own[turn]), (2, jnp.where(upper, near[turn], far[turn]))):
-            known[kind * (plan.sides + 1) + turn] = line.astype(jnp.int32)
+            known[kind * width + turn] = line.astype(jnp.int32)
     copy = pltpu.make_async_copy(known.at[:, 0], info, sem)
     copy.start()
     copy.wait()
@@ -316,7 +320,11 @@
 
 def term_kernel(plan, slot, layout, pieces, copied, halves, slots, spot, *rest):
     refs, rest = rest[:pieces], rest[pieces:]
-    earlier, (probe, amps, tables, outer, inner), rest = rest[:copied], rest[copied : copied + 5], rest[copied + 5 :]
+    earlier, (probe, amps, tables, inner), rest = rest[:copied], rest[copied : copied + 4], rest[copied + 4 :]
+    if halves:
+        outer, rest = rest[-1], rest[:-1]
+    else:
+        outer, rest = rest[0], rest[1:]
     outer_halves, near_outers, (window, picked) = rest[:halves], rest[halves:-2], rest[-2:]
     size = probe.shape[2]
     half = size // 2
@@ -591,12 +599,15 @@
     )
     messages = call(
         lambda *refs: halo_message_kernel(plan, *refs),
-        [shape((2, half + 24, LANES), f32)] * sides + [shape((2, half + 16, LANES), f32)] * sides + [shape((8, LANES), f32)],
+        [shape((2, half + 8, LANES), f32)] * sides
+        + [shape((2, half, LANES), f32)] * sides
+        + [shape((8, LANES), f32)] * (sides + 1),
         [],
         [spots, counts, ordered, *halos],
         in_specs=[SMEM, SMEM, ANY] + [VMEM] * sides,
     )
-    passed, own_spot = messages[sides:-1], messages[-1]
+    passed, lines, own_spot = messages[sides : 2 * sides], messages[2 * sides : -1], messages[-1]
+    near_lines = [plan.near_rows(line) for line in lines]
     far = [far_block] + [plan.far_rows(message) for message in messages[:sides]]
     near = [plan.near_rows(message) for message in passed] + [near_block]
     own = [object_field] + passed
@@ -623,16 +634,18 @@
             earlier = outer if last else []
             patch = shape((2, half, size), f32)
             halves = 2 if last and sweep == ITERS - 1 else 0
-            outer_part, inner_part, *copies = call(
+            inner_part, *copies = call(
                 lambda *refs, slot=slot, layout=layout, copied=len(earlier), halves=halves: term_kernel(
                     plan, slot, layout, len(pieces), copied, halves, slots, *refs
                 ),
-                [patch] * 2
-                + [shape((2, half, LANES), f32)] * halves
+                [patch]
+                + ([shape((2, half, LANES), f32)] * halves or [patch])
                 + [shape((2 * slots, rows, size), f32) for rows in near_heights if last],
-                [pltpu.VMEM((2, size, size), f32), pltpu.VMEM((3, 3, 2, half, LANES), f32)],
+                [pltpu.VMEM((2, size, size), f32), pltpu.VMEM((3, 3, 2, half, LANES), f32)]
+                + [pltpu.VMEM((2, half, size), f32)] * (halves > 0),
                 [own_spot, *pieces, *earlier, rolled, ordered, tables],
             )
+            outer_part = None if halves else copies.pop(0)
             outer_halves, copies = copies[:halves], copies[halves:]
             inner.append(inner_part)
             outer.append(outer_part)
@@ -642,7 +655,7 @@
                     lambda *refs: info_kernel(plan, *refs),
                     shape((3 * (sides + 1), LANES), jnp.int32),
                     [pltpu.VMEM((3 * (sides + 1), 8, LANES), jnp.int32), dma],
-                    passed + far[1:] + near[:sides] + [outer_part],
+                    lines + far[1:] + near_lines + [outer_part],
                     in_specs=[VMEM] * (3 * sides) + [ANY],
                     out_specs=SMEM,
                 )

time: 70.5 us -> 70.5 us (level)
  the two profiles are of different devices: /device:TPU:17 before, /device:TPU:9 now
where the time goes in v15:
time: 70.5 us; the launch traced here: 70.2 us
  waiting for transfers between devices  28.8 us (41%)
  Pallas kernels  20.6 us (29%)
  starting transfers between devices  16.9 us (24%)
  local copies, waits for them, and re-layouts  3.73 us (5%)
    pallas_call x19, Pallas kernels, call(): pl.pallas_call(kernel, out_shape=outs, in_specs=in_specs or [SMEM if valu...  20.6 us
    ppermute x9, waiting for transfers between devices, far_rows(): lax.ppermute(values, ('sx', 'sy'), pairs + [(j, i) for i, j in pairs])  18.7 us
    ppermute x9, starting transfers between devices, far_rows(): lax.ppermute(values, ('sx', 'sy'), pairs + [(j, i) for i, j in pairs])  11.3 us
    ppermute x3, waiting for transfers between devices, across(): return [lax.ppermute(values[0], axis_name, [(0, 1), (1, 0)])]  5.45 us
    ppermute x12, waiting for transfers between devices, near_rows(): return lax.ppermute(values, 'sx', [(i, i ^ 1) for i in range(self.sx_size)])  4.65 us
    unnamed x16, local copies, waits for them, and re-layouts  3.73 us
    ppermute x3, starting transfers between devices, across(): return [lax.ppermute(values[0], axis_name, [(0, 1), (1, 0)])]  2.82 us
    ppermute x12, starting transfers between devices, near_rows(): return lax.ppermute(values, 'sx', [(i, i ^ 1) for i in range(self.sx_size)])  2.77 us
  transfers between devices with their start and end apart: 24, of which 14 were waited for; matrix products, arithmetic and copies ran while one was open for 0% of the time, Pallas kernels for 22%

profile of v15, /device:TPU:9, one launch (start us, length us, event | category | flops | bytes accessed | tf_op | source)
XLA Modules:
  0.0 70.2 jit_solution(10782382862985785494)
XLA Ops:
  0.7 1.1 %collective-permute-start.3 = (f32[2,128,512]{2,1,0:T(8,128)}, f32[2,128,512]{2,1,0:T(8,128)S(1)}, u32[]{:S(2)}, u32[]{:S(2)}) collective-permute-start(f32[2,128,512]{2,1,0:T(8,128)} %refs_4_.1), channel_id=1, source_target_pairs={{2,4},{3,5},{6,8},{7,9},{10,12},{11,13},{14,16},{15,17},{18,20},{1... | collective-permute-start | bytes 1572872 | tf_op jit(solution)/shard_map/ppermute | solution.py:117
  2.5 1.0 %copy-done.1 = f32[2,128,512]{2,1,0:T(8,128)S(1)} copy-done((f32[2,128,512]{2,1,0:T(8,128)S(1)}, f32[2,128,512]{2,1,0:T(8,128)}, u32[]{:S(2)}) %copy-start.1) | copy-done | bytes 524312
  4.1 1.3 %collective-permute-start = (f32[2,136,128]{2,1,0:T(8,128)S(1)}, f32[2,136,128]{2,1,0:T(8,128)S(1)}, u32[]{:S(2)}, u32[]{:S(2)}) collective-permute-start(f32[2,136,128]{2,1,0:T(8,128)S(1)} %shard_map.74), channel_id=1, source_target_pairs={{0,1},{1,0},{2,3},{3,2},{4,5},{5,4},{6,7},{7,6},{8,9},{9,8},{10,11... | collective-permute-start | bytes 417800 | tf_op jit(solution)/shard_map/ppermute | solution.py:105
  5.4 1.0 %copy-done.4 = f32[1,1,2,256,256]{4,3,2,1,0:T(8,128)S(1)} copy-done((f32[1,1,2,256,256]{4,3,2,1,0:T(8,128)S(1)}, f32[1,1,2,256,256]{4,3,2,1,0:T(8,128)}, u32[]{:S(2)}) %copy-start.4) | copy-done | bytes 524312
  6.5 0.9 %copy-done.5 = bf16[2,256,256]{2,1,0:T(8,128)(2,1)S(1)} copy-done((bf16[2,256,256]{2,1,0:T(8,128)(2,1)S(1)}, bf16[2,256,256]{2,1,0:T(8,128)(2,1)}, u32[]{:S(2)}) %copy-start.5) | copy-done | bytes 262168
  7.4 1.5 %shard_map.73 = (f32[2,2,256,256]{3,2,1,0:T(8,128)S(1)}, f32[2,256,256]{2,1,0:T(8,128)S(1)}) custom-call(s32[2,2]{1,0:T(2,128)S(1)} %bitcast.5, f32[2,256,256]{2,1,0:T(8,128)S(1)} %copy-done.3, f32[2,256,256]{2,1,0:T(8,128)S(1)} %bitcast.3, bf16[2,256,256]{2,1,0:T(8,128)(2,1)S(1)} %copy-done.5), custom_call_target="tpu_custom_call" | custom-call | flops 100000 | bytes 10000 | tf_op jit(solution)/shard_map/pallas_call | solution.py:553
  9.6 2.4 %collective-permute-start.1 = (f32[2,136,128]{2,1,0:T(8,128)S(1)}, f32[2,136,128]{2,1,0:T(8,128)S(1)}, u32[]{:S(2)}, u32[]{:S(2)}) collective-permute-start(f32[2,136,128]{2,1,0:T(8,128)S(1)} %get-tuple-element.40), channel_id=1, source_target_pairs={{2,4},{3,5},{6,8},{7,9},{10,12},{11,13},{14,16},{15,17},{18,20},{1... | collective-permute-start | bytes 417800 | tf_op jit(solution)/shard_map/ppermute | solution.py:117
  12.0 1.3 %collective-permute-done.4.refs_5_.refs_8_ = f32[2,128,128]{2,1,0:T(8,128)S(1)} collective-permute-done((f32[2,128,128]{2,1,0:T(8,128)S(1)}, f32[2,128,128]{2,1,0:T(8,128)S(1)}, u32[]{:S(2)}, u32[]{:S(2)}) %collective-permute-start.4) | collective-permute-done | bytes 131104 | tf_op jit(solution)/shard_map/ppermute | solution.py:120
  13.3 4.8 %collective-permute-done.1.refs_4_.refs_1_.refs_7_ = f32[2,136,128]{2,1,0:T(8,128)S(1)} collective-permute-done((f32[2,136,128]{2,1,0:T(8,128)S(1)}, f32[2,136,128]{2,1,0:T(8,128)S(1)}, u32[]{:S(2)}, u32[]{:S(2)}) %collective-permute-start.1) | collective-permute-done | bytes 139296 | tf_op jit(solution)/shard_map/ppermute | solution.py:117
  18.1 2.2 %shard_map.76 = (f32[2,128,256]{2,1,0:T(8,128)S(1)}, f32[2,128,256]{2,1,0:T(8,128)S(1)}) custom-call(f32[8,128]{1,0:T(8,128)S(1)} %get-tuple-element.41.refs_0_, f32[2,128,512]{2,1,0:T(8,128)S(1)} %copy-done.2, f32[2,128,128]{2,1,0:T(8,128)S(1)} %get-tuple-element.42.refs_2_.refs_5_, f32[2,128,512]{2,1,0:T(8,128)S(1)} %collective-permute-done.3.refs_3_.refs_6_, ...), custom_call_target="tpu_custom_call" | custom-call | flops 100000 | bytes 10000 | tf_op jit(solution)/shard_map/pallas_call | solution.py:553
  20.3 1.1 %collective-permute-start.9 = (f32[2,128,256]{2,1,0:T(8,128)S(1)}, f32[2,128,256]{2,1,0:T(8,128)S(1)}, u32[]{:S(2)}, u32[]{:S(2)}) collective-permute-start(f32[2,128,256]{2,1,0:T(8,128)S(1)} %get-tuple-element.44.refs_7_), channel_id=1, source_target_pairs={{2,4},{3,5},{6,8},{7,9},{10,12},{11,13},{14,16},{15,17},{18,20},{1... | collective-permute-start | bytes 786440 | tf_op jit(solution)/shard_map/ppermute | solution.py:117
  21.4 2.2 %shard_map.77 = (f32[2,128,256]{2,1,0:T(8,128)S(1)}, f32[2,128,256]{2,1,0:T(8,128)S(1)}, f32[4,48,256]{2,1,0:T(8,128)S(1)}, f32[4,40,256]{2,1,0:T(8,128)S(1)}, f32[4,40,256]{2,1,0:T(8,128)S(1)}) custom-call(f32[8,128]{1,0:T(8,128)S(1)} %get-tuple-element.41.refs_0_, f32[2,128,512]{2,1,0:T(8,128)S(1)} %copy-done.2, ...), custom_call_target="tpu_custom_call" | custom-call | flops 100000 | bytes 10000 | tf_op jit(solution)/shard_map/pallas_call | solution.py:553
  25.4 1.3 %shard_map.78.refs_0_ = s32[6,128]{1,0:T(8,128)S(1)} custom-call(f32[8,128]{1,0:T(8,128)S(1)} %get-tuple-element.39.refs_0_, f32[2,136,128]{2,1,0:T(8,128)S(1)} %collective-permute-done.1.refs_4_.refs_1_.refs_7_, f32[8,128]{1,0:T(8,128)S(1)} %collective-permute-done.2.refs_2_, f32[2,128,256]{2,1,0:T(8,128)S(1)} %get-tuple-element.45.refs_3_), custom_call_target="tpu_custom_call" | custom-call | flops 100000 | bytes 10000 | tf_op jit(solution)/shard_map/pallas_call | solution.py:553
  26.7 2.5 %shard_map.79.refs_2_.refs_3_.refs_0_ = f32[128,768]{1,0:T(8,128)S(1)} custom-call(s32[6,128]{1,0:T(8,128)S(1)} %shard_map.78.refs_0_, f32[2,256,256]{2,1,0:T(8,128)S(1)} %copy-done.3, f32[4,48,256]{2,1,0:T(8,128)S(1)} %get-tuple-element.46.refs_2_), custom_call_target="tpu_custom_call" | custom-call | flops 100000 | bytes 10000 | tf_op jit(solution)/shard_map/pallas_call | solution.py:553
  30.3 1.0 %shard_map.81 = (f32[2,128,768]{2,1,0:T(8,128)S(1)}, f32[2,128,768]{2,1,0:T(8,128)S(1)}, f32[128,768]{1,0:T(8,128)S(1)}) custom-call(s32[6,128]{1,0:T(8,128)S(1)} %shard_map.78.refs_0_, f32[2,128,768]{2,1,0:T(8,128)S(1)} %shard_map.80.refs_1_, f32[128,768]{1,0:T(8,128)S(1)} %shard_map.79.refs_2_.refs_3_.refs_0_, ...), custom_call_target="tpu_custom_call" | custom-call | flops 100000 | bytes 10000 | tf_op jit(solution)/shard_map/pallas_call | solution.py:553
  31.3 1.8 %collective-permute-done.10.refs_1_ = f32[2,128,256]{2,1,0:T(8,128)S(1)} collective-permute-done((f32[2,128,256]{2,1,0:T(8,128)S(1)}, f32[2,128,256]{2,1,0:T(8,128)S(1)}, u32[]{:S(2)}, u32[]{:S(2)}) %collective-permute-start.10) | collective-permute-done | bytes 262176 | tf_op jit(solution)/shard_map/ppermute | solution.py:117
  33.2 1.3 %collective-permute-start.11 = (f32[2,128,256]{2,1,0:T(8,128)S(1)}, f32[2,128,256]{2,1,0:T(8,128)S(1)}, u32[]{:S(2)}, u32[]{:S(2)}) collective-permute-start(f32[2,128,256]{2,1,0:T(8,128)S(1)} %shard_map.82.refs_4_), channel_id=1, source_target_pairs={{0,1},{1,0},{2,3},{3,2},{4,5},{5,4},{6,7},{7,6},{8,9},{9,8},{10,11... | collective-permute-start | bytes 786440 | tf_op jit(solution)/shard_map/ppermute | solution.py:105
  34.5 2.4 %collective-permute-start.12 = (f32[2,128,384]{2,1,0:T(8,128)S(1)}, f32[2,128,384]{2,1,0:T(8,128)S(1)}, u32[]{:S(2)}, u32[]{:S(2)}) collective-permute-start(f32[2,128,384]{2,1,0:T(8,128)S(1)} %shard_map.83.refs_3_.refs_1_.refs_4_), channel_id=1, source_target_pairs={{2,4},{3,5},{6,8},{7,9},{10,12},{11,13},{14,16},{15,17},{18,20},{1... | collective-permute-start | bytes 1179656 | tf_op jit(solution)/shard_map/ppermute | solution.py:117
  37.0 3.3 %collective-permute-done.11.refs_5_ = f32[2,128,256]{2,1,0:T(8,128)S(1)} collective-permute-done((f32[2,128,256]{2,1,0:T(8,128)S(1)}, f32[2,128,256]{2,1,0:T(8,128)S(1)}, u32[]{:S(2)}, u32[]{:S(2)}) %collective-permute-start.11) | collective-permute-done | bytes 262176 | tf_op jit(solution)/shard_map/ppermute | solution.py:105
  40.9 1.5 %collective-permute-start.13 = (f32[2,128,256]{2,1,0:T(8,128)S(1)}, f32[2,128,256]{2,1,0:T(8,128)S(1)}, u32[]{:S(2)}, u32[]{:S(2)}) collective-permute-start(f32[2,128,256]{2,1,0:T(8,128)S(1)} %get-tuple-element.54.refs_2_.refs_5_), channel_id=1, source_target_pairs={{2,4},{3,5},{6,8},{7,9},{10,12},{11,13},{14,16},{15,17},{18,20},{1... | collective-permute-start | bytes 786440 | tf_op jit(solution)/shard_map/ppermute | solution.py:117
  42.4 1.3 %collective-permute-done.16.refs_7_.refs_10_ = f32[2,128,128]{2,1,0:T(8,128)S(1)} collective-permute-done((f32[2,128,128]{2,1,0:T(8,128)S(1)}, f32[2,128,128]{2,1,0:T(8,128)S(1)}, u32[]{:S(2)}, u32[]{:S(2)}) %collective-permute-start.16) | collective-permute-done | bytes 131104 | tf_op jit(solution)/shard_map/ppermute | solution.py:120
  43.7 4.3 %collective-permute-done.12.refs_3_.refs_6_ = f32[2,128,384]{2,1,0:T(8,128)S(1)} collective-permute-done((f32[2,128,384]{2,1,0:T(8,128)S(1)}, f32[2,128,384]{2,1,0:T(8,128)S(1)}, u32[]{:S(2)}, u32[]{:S(2)}) %collective-permute-start.12) | collective-permute-done | bytes 393248 | tf_op jit(solution)/shard_map/ppermute | solution.py:117
  48.0 2.8 %collective-permute-done.13.refs_4_.refs_7_ = f32[2,128,256]{2,1,0:T(8,128)S(1)} collective-permute-done((f32[2,128,256]{2,1,0:T(8,128)S(1)}, f32[2,128,256]{2,1,0:T(8,128)S(1)}, u32[]{:S(2)}, u32[]{:S(2)}) %collective-permute-start.13) | collective-permute-done | bytes 262176 | tf_op jit(solution)/shard_map/ppermute | solution.py:117
  50.8 2.1 %shard_map.85 = (f32[2,128,256]{2,1,0:T(8,128)S(1)}, f32[2,128,256]{2,1,0:T(8,128)S(1)}) custom-call(f32[8,128]{1,0:T(8,128)S(1)} %get-tuple-element.41.refs_0_, f32[2,128,384]{2,1,0:T(8,128)S(1)} %shard_map.83.refs_3_.refs_1_.refs_4_, f32[2,128,256]{2,1,0:T(8,128)S(1)} %get-tuple-element.54.refs_2_.refs_5_, ...), custom_call_target="tpu_custom_call" | custom-call | flops 100000 | bytes 10000 | tf_op jit(solution)/shard_map/pallas_call | solution.py:553
  53.0 2.1 %collective-permute-start.20 = (f32[2,128,256]{2,1,0:T(8,128)S(1)}, f32[2,128,256]{2,1,0:T(8,128)S(1)}, u32[]{:S(2)}, u32[]{:S(2)}) collective-permute-start(f32[2,128,256]{2,1,0:T(8,128)S(1)} %get-tuple-element.59.refs_8_), channel_id=1, source_target_pairs={{2,4},{3,5},{6,8},{7,9},{10,12},{11,13},{14,16},{15,17},{18,20},{1... | collective-permute-start | bytes 786440 | tf_op jit(solution)/shard_map/ppermute | solution.py:117
  55.1 2.2 %shard_map.86 = (f32[2,128,256]{2,1,0:T(8,128)S(1)}, f32[2,128,128]{2,1,0:T(8,128)S(1)}, f32[2,128,128]{2,1,0:T(8,128)S(1)}, f32[4,48,256]{2,1,0:T(8,128)S(1)}, ...) custom-call(f32[8,128]{1,0:T(8,128)S(1)} %get-tuple-element.41.refs_0_, ...), custom_call_target="tpu_custom_call" | custom-call | flops 100000 | bytes 10000 | tf_op jit(solution)/shard_map/pallas_call | solution.py:553
  57.9 1.1 %collective-permute-done.18.refs_4_ = f32[4,40,256]{2,1,0:T(8,128)S(1)} collective-permute-done((f32[4,40,256]{2,1,0:T(8,128)S(1)}, f32[4,40,256]{2,1,0:T(8,128)S(1)}, u32[]{:S(2)}, u32[]{:S(2)}) %collective-permute-start.18) | collective-permute-done | bytes 163872 | tf_op jit(solution)/shard_map/ppermute | solution.py:120
  60.6 1.0 %shard_map.88 = (f32[2,128,768]{2,1,0:T(8,128)S(1)}, f32[2,128,768]{2,1,0:T(8,128)S(1)}, f32[128,768]{1,0:T(8,128)S(1)}) custom-call(s32[6,128]{1,0:T(8,128)S(1)} %shard_map.78.refs_0_, f32[2,128,768]{2,1,0:T(8,128)S(1)} %shard_map.87.refs_1_, f32[128,768]{1,0:T(8,128)S(1)} %shard_map.79.refs_2_.refs_3_.refs_0_, ...), custom_call_target="tpu_custom_call" | custom-call | flops 100000 | bytes 10000 | tf_op jit(solution)/shard_map/pallas_call | solution.py:553
  61.5 3.6 %collective-permute-done.21.refs_2_.refs_4_ = f32[2,128,128]{2,1,0:T(8,128)S(1)} collective-permute-done((f32[2,128,128]{2,1,0:T(8,128)S(1)}, f32[2,128,128]{2,1,0:T(8,128)S(1)}, u32[]{:S(2)}, u32[]{:S(2)}) %collective-permute-start.21) | collective-permute-done | bytes 131104 | tf_op jit(solution)/shard_map/ppermute | solution.py:117
  65.4 1.1 %collective-permute-done.22.refs_5_ = f32[2,128,128]{2,1,0:T(8,128)S(1)} collective-permute-done((f32[2,128,128]{2,1,0:T(8,128)S(1)}, f32[2,128,128]{2,1,0:T(8,128)S(1)}, u32[]{:S(2)}, u32[]{:S(2)}) %collective-permute-start.22) | collective-permute-done | bytes 131104 | tf_op jit(solution)/shard_map/ppermute | solution.py:117
  66.5 0.9 %shard_map.90 = (f32[2,128,512]{2,1,0:T(8,128)}, f32[2,128,128]{2,1,0:T(8,128)S(1)}) custom-call(f32[2,128,768]{2,1,0:T(8,128)S(1)} %get-tuple-element.64.refs_0_, f32[128,768]{1,0:T(8,128)S(1)} %get-tuple-element.65.refs_1_, f32[128,768]{1,0:T(8,128)S(1)} %shard_map.79.refs_2_.refs_3_.refs_0_, f32[2,128,128]{2,1,0:T(8,128)S(1)} %shard_map.89.refs_3_, ...), custom_call_target="tpu_custom_call" | custom-call | flops 100000 | bytes 10000 | tf_op jit(solution)/shard_map/pallas_call | solution.py:553
  67.4 2.1 %collective-permute-done.23.refs_2_ = f32[2,128,128]{2,1,0:T(8,128)S(1)} collective-permute-done((f32[2,128,128]{2,1,0:T(8,128)S(1)}, f32[2,128,128]{2,1,0:T(8,128)S(1)}, u32[]{:S(2)}, u32[]{:S(2)}) %collective-permute-start.23) | collective-permute-done | bytes 131104 | tf_op jit(solution)/shard_map/ppermute | solution.py:105
  (51 shorter events, 9.5 us)
Async XLA Ops:
  0.0 18.1 %collective-permute-start.5 = (f32[2,128,512]{2,1,0:T(8,128)}, f32[2,128,512]{2,1,0:T(8,128)S(1)}, u32[]{:S(2)}, u32[]{:S(2)}) collective-permute-start(f32[2,128,512]{2,1,0:T(8,128)} %refs_4_.1), channel_id=1, source_target_pairs={{0,2},{2,0},{4,6},{6,4},{8,10},{10,8},{12,14},{14,12},{16,18},{18,... | collective-permute-start | bytes 1572872 | tf_op jit(solution)/shard_map/ppermute | solution.py:120
  0.7 17.4 %collective-permute-start.3 = (f32[2,128,512]{2,1,0:T(8,128)}, f32[2,128,512]{2,1,0:T(8,128)S(1)}, u32[]{:S(2)}, u32[]{:S(2)}) collective-permute-start(f32[2,128,512]{2,1,0:T(8,128)} %refs_4_.1), channel_id=1, source_target_pairs={{2,4},{3,5},{6,8},{7,9},{10,12},{11,13},{14,16},{15,17},{18,20},{1... | collective-permute-start | bytes 1572872 | tf_op jit(solution)/shard_map/ppermute | solution.py:117
  1.8 0.7 copy-start.6
  1.8 0.7 copy-start.7
  2.5 1.0 %copy-start.1 = (f32[2,128,512]{2,1,0:T(8,128)S(1)}, f32[2,128,512]{2,1,0:T(8,128)}, u32[]{:S(2)}) copy-start(f32[2,128,512]{2,1,0:T(8,128)} %refs_4_.1) | copy-start | bytes 1572868
  3.5 1.9 %copy-start.3 = (f32[2,256,256]{2,1,0:T(8,128)S(1)}, f32[2,256,256]{2,1,0:T(8,128)}, u32[]{:S(2)}) copy-start(f32[2,256,256]{2,1,0:T(8,128)} %refs_1_.5) | copy-start | bytes 1572868
  4.1 14.0 %copy-start = (bf16[2,2,2,256,256]{4,3,2,1,0:T(8,128)(2,1)S(1)}, bf16[2,2,2,256,256]{4,3,2,1,0:T(8,128)(2,1)}, u32[]{:S(2)}) copy-start(bf16[2,2,2,256,256]{4,3,2,1,0:T(8,128)(2,1)} %constant.4.clone.refs_9_.refs_10_.refs_11_) | copy-start | bytes 3145732
  4.1 4.9 %collective-permute-start = (f32[2,136,128]{2,1,0:T(8,128)S(1)}, f32[2,136,128]{2,1,0:T(8,128)S(1)}, u32[]{:S(2)}, u32[]{:S(2)}) collective-permute-start(f32[2,136,128]{2,1,0:T(8,128)S(1)} %shard_map.74), channel_id=1, source_target_pairs={{0,1},{1,0},{2,3},{3,2},{4,5},{5,4},{6,7},{7,6},{8,9},{9,8},{10,11... | collective-permute-start | bytes 417800 | tf_op jit(solution)/shard_map/ppermute | solution.py:105
  5.4 1.0 %copy-start.4 = (f32[1,1,2,256,256]{4,3,2,1,0:T(8,128)S(1)}, f32[1,1,2,256,256]{4,3,2,1,0:T(8,128)}, u32[]{:S(2)}) copy-start(f32[1,1,2,256,256]{4,3,2,1,0:T(8,128)} %param.9) | copy-start | bytes 1572868
  6.5 0.9 %copy-start.5 = (bf16[2,256,256]{2,1,0:T(8,128)(2,1)S(1)}, bf16[2,256,256]{2,1,0:T(8,128)(2,1)}, u32[]{:S(2)}) copy-start(bf16[2,256,256]{2,1,0:T(8,128)(2,1)} %constant.5.clone.order) | copy-start | bytes 786436
  9.0 9.2 %copy-start.2 = (f32[2,128,512]{2,1,0:T(8,128)S(1)}, f32[2,128,512]{2,1,0:T(8,128)}, u32[]{:S(2)}) copy-start(f32[2,128,512]{2,1,0:T(8,128)} %refs_4_.1) | copy-start | bytes 1572868
  9.6 8.5 %collective-permute-start.1 = (f32[2,136,128]{2,1,0:T(8,128)S(1)}, f32[2,136,128]{2,1,0:T(8,128)S(1)}, u32[]{:S(2)}, u32[]{:S(2)}) collective-permute-start(f32[2,136,128]{2,1,0:T(8,128)S(1)} %get-tuple-element.40), channel_id=1, source_target_pairs={{2,4},{3,5},{6,8},{7,9},{10,12},{11,13},{14,16},{15,17},{18,20},{1... | collective-permute-start | bytes 417800 | tf_op jit(solution)/shard_map/ppermute | solution.py:117
  12.0 1.3 %collective-permute-start.4 = (f32[2,128,128]{2,1,0:T(8,128)S(1)}, f32[2,128,128]{2,1,0:T(8,128)S(1)}, u32[]{:S(2)}, u32[]{:S(2)}) collective-permute-start(f32[2,128,128]{2,1,0:T(8,128)S(1)} %get-tuple-element.42.refs_2_.refs_5_), channel_id=1, source_target_pairs={{0,2},{2,0},{4,6},{6,4},{8,10},{10,8},{12,14},{14,12},{16,18},{18,... | collective-permute-start | bytes 393224 | tf_op jit(solution)/shard_map/ppermute | solution.py:120
  20.3 10.0 %collective-permute-start.9 = (f32[2,128,256]{2,1,0:T(8,128)S(1)}, f32[2,128,256]{2,1,0:T(8,128)S(1)}, u32[]{:S(2)}, u32[]{:S(2)}) collective-permute-start(f32[2,128,256]{2,1,0:T(8,128)S(1)} %get-tuple-element.44.refs_7_), channel_id=1, source_target_pairs={{2,4},{3,5},{6,8},{7,9},{10,12},{11,13},{14,16},{15,17},{18,20},{1... | collective-permute-start | bytes 786440 | tf_op jit(solution)/shard_map/ppermute | solution.py:117
  23.6 9.5 %collective-permute-start.10 = (f32[2,128,256]{2,1,0:T(8,128)S(1)}, f32[2,128,256]{2,1,0:T(8,128)S(1)}, u32[]{:S(2)}, u32[]{:S(2)}) collective-permute-start(f32[2,128,256]{2,1,0:T(8,128)S(1)} %get-tuple-element.45.refs_3_), channel_id=1, source_target_pairs={{2,4},{3,5},{6,8},{7,9},{10,12},{11,13},{14,16},{15,17},{18,20},{1... | collective-permute-start | bytes 786440 | tf_op jit(solution)/shard_map/ppermute | solution.py:117
  23.7 5.5 %collective-permute-start.6 = (f32[4,48,256]{2,1,0:T(8,128)S(1)}, f32[4,48,256]{2,1,0:T(8,128)S(1)}, u32[]{:S(2)}, u32[]{:S(2)}) collective-permute-start(f32[4,48,256]{2,1,0:T(8,128)S(1)} %get-tuple-element.46.refs_2_), channel_id=1, source_target_pairs={{0,2},{2,0},{4,6},{6,4},{8,10},{10,8},{12,14},{14,12},{16,18},{18,... | collective-permute-start | bytes 589832 | tf_op jit(solution)/shard_map/ppermute | solution.py:120
  23.8 1.4 %collective-permute-start.2 = (f32[8,128]{1,0:T(8,128)S(1)}, f32[8,128]{1,0:T(8,128)S(1)}, u32[]{:S(2)}, u32[]{:S(2)}) collective-permute-start(f32[8,128]{1,0:T(8,128)S(1)} %get-tuple-element.39.refs_0_), channel_id=1, source_target_pairs={{0,2},{2,0},{4,6},{6,4},{8,10},{10,8},{12,14},{14,12},{16,18},{18,... | collective-permute-start | bytes 12296 | tf_op jit(solution)/shard_map/ppermute | solution.py:120
  24.3 4.9 %collective-permute-start.7 = (f32[4,40,256]{2,1,0:T(8,128)S(1)}, f32[4,40,256]{2,1,0:T(8,128)S(1)}, u32[]{:S(2)}, u32[]{:S(2)}) collective-permute-start(f32[4,40,256]{2,1,0:T(8,128)S(1)} %get-tuple-element.49), channel_id=1, source_target_pairs={{0,2},{2,0},{4,6},{6,4},{8,10},{10,8},{12,14},{14,12},{16,18},{18,... | collective-permute-start | bytes 491528 | tf_op jit(solution)/shard_map/ppermute | solution.py:120
  25.2 4.0 %collective-permute-start.8 = (f32[4,40,256]{2,1,0:T(8,128)S(1)}, f32[4,40,256]{2,1,0:T(8,128)S(1)}, u32[]{:S(2)}, u32[]{:S(2)}) collective-permute-start(f32[4,40,256]{2,1,0:T(8,128)S(1)} %get-tuple-element.50), channel_id=1, source_target_pairs={{0,2},{2,0},{4,6},{6,4},{8,10},{10,8},{12,14},{14,12},{16,18},{18,... | collective-permute-start | bytes 491528 | tf_op jit(solution)/shard_map/ppermute | solution.py:120
  33.2 7.1 %collective-permute-start.11 = (f32[2,128,256]{2,1,0:T(8,128)S(1)}, f32[2,128,256]{2,1,0:T(8,128)S(1)}, u32[]{:S(2)}, u32[]{:S(2)}) collective-permute-start(f32[2,128,256]{2,1,0:T(8,128)S(1)} %shard_map.82.refs_4_), channel_id=1, source_target_pairs={{0,1},{1,0},{2,3},{3,2},{4,5},{5,4},{6,7},{7,6},{8,9},{9,8},{10,11... | collective-permute-start | bytes 786440 | tf_op jit(solution)/shard_map/ppermute | solution.py:105
  34.5 13.5 %collective-permute-start.12 = (f32[2,128,384]{2,1,0:T(8,128)S(1)}, f32[2,128,384]{2,1,0:T(8,128)S(1)}, u32[]{:S(2)}, u32[]{:S(2)}) collective-permute-start(f32[2,128,384]{2,1,0:T(8,128)S(1)} %shard_map.83.refs_3_.refs_1_.refs_4_), channel_id=1, source_target_pairs={{2,4},{3,5},{6,8},{7,9},{10,12},{11,13},{14,16},{15,17},{18,20},{1... | collective-permute-start | bytes 1179656 | tf_op jit(solution)/shard_map/ppermute | solution.py:117
  40.3 7.7 %collective-permute-start.14 = (f32[2,128,256]{2,1,0:T(8,128)S(1)}, f32[2,128,256]{2,1,0:T(8,128)S(1)}, u32[]{:S(2)}, u32[]{:S(2)}) collective-permute-start(f32[2,128,256]{2,1,0:T(8,128)S(1)} %get-tuple-element.55), channel_id=1, source_target_pairs={{0,2},{2,0},{4,6},{6,4},{8,10},{10,8},{12,14},{14,12},{16,18},{18,... | collective-permute-start | bytes 786440 | tf_op jit(solution)/shard_map/ppermute | solution.py:120
  40.4 7.6 %collective-permute-start.15 = (f32[2,128,256]{2,1,0:T(8,128)S(1)}, f32[2,128,256]{2,1,0:T(8,128)S(1)}, u32[]{:S(2)}, u32[]{:S(2)}) collective-permute-start(f32[2,128,256]{2,1,0:T(8,128)S(1)} %get-tuple-element.56), channel_id=1, source_target_pairs={{0,2},{2,0},{4,6},{6,4},{8,10},{10,8},{12,14},{14,12},{16,18},{18,... | collective-permute-start | bytes 786440 | tf_op jit(solution)/shard_map/ppermute | solution.py:120
  40.9 9.9 %collective-permute-start.13 = (f32[2,128,256]{2,1,0:T(8,128)S(1)}, f32[2,128,256]{2,1,0:T(8,128)S(1)}, u32[]{:S(2)}, u32[]{:S(2)}) collective-permute-start(f32[2,128,256]{2,1,0:T(8,128)S(1)} %get-tuple-element.54.refs_2_.refs_5_), channel_id=1, source_target_pairs={{2,4},{3,5},{6,8},{7,9},{10,12},{11,13},{14,16},{15,17},{18,20},{1... | collective-permute-start | bytes 786440 | tf_op jit(solution)/shard_map/ppermute | solution.py:117
  42.4 1.3 %collective-permute-start.16 = (f32[2,128,128]{2,1,0:T(8,128)S(1)}, f32[2,128,128]{2,1,0:T(8,128)S(1)}, u32[]{:S(2)}, u32[]{:S(2)}) collective-permute-start(f32[2,128,128]{2,1,0:T(8,128)S(1)} %get-tuple-element.57), channel_id=1, source_target_pairs={{0,2},{2,0},{4,6},{6,4},{8,10},{10,8},{12,14},{14,12},{16,18},{18,... | collective-permute-start | bytes 393224 | tf_op jit(solution)/shard_map/ppermute | solution.py:120
  53.0 7.6 %collective-permute-start.20 = (f32[2,128,256]{2,1,0:T(8,128)S(1)}, f32[2,128,256]{2,1,0:T(8,128)S(1)}, u32[]{:S(2)}, u32[]{:S(2)}) collective-permute-start(f32[2,128,256]{2,1,0:T(8,128)S(1)} %get-tuple-element.59.refs_8_), channel_id=1, source_target_pairs={{2,4},{3,5},{6,8},{7,9},{10,12},{11,13},{14,16},{15,17},{18,20},{1... | collective-permute-start | bytes 786440 | tf_op jit(solution)/shard_map/ppermute | solution.py:117
  57.3 2.4 %collective-permute-start.17 = (f32[4,48,256]{2,1,0:T(8,128)S(1)}, f32[4,48,256]{2,1,0:T(8,128)S(1)}, u32[]{:S(2)}, u32[]{:S(2)}) collective-permute-start(f32[4,48,256]{2,1,0:T(8,128)S(1)} %get-tuple-element.61), channel_id=1, source_target_pairs={{0,2},{2,0},{4,6},{6,4},{8,10},{10,8},{12,14},{14,12},{16,18},{18,... | collective-permute-start | bytes 589832 | tf_op jit(solution)/shard_map/ppermute | solution.py:120
  57.3 1.7 %collective-permute-start.18 = (f32[4,40,256]{2,1,0:T(8,128)S(1)}, f32[4,40,256]{2,1,0:T(8,128)S(1)}, u32[]{:S(2)}, u32[]{:S(2)}) collective-permute-start(f32[4,40,256]{2,1,0:T(8,128)S(1)} %get-tuple-element.62), channel_id=1, source_target_pairs={{0,2},{2,0},{4,6},{6,4},{8,10},{10,8},{12,14},{14,12},{16,18},{18,... | collective-permute-start | bytes 491528 | tf_op jit(solution)/shard_map/ppermute | solution.py:120
  57.8 1.8 %collective-permute-start.19 = (f32[4,40,256]{2,1,0:T(8,128)S(1)}, f32[4,40,256]{2,1,0:T(8,128)S(1)}, u32[]{:S(2)}, u32[]{:S(2)}) collective-permute-start(f32[4,40,256]{2,1,0:T(8,128)S(1)} %get-tuple-element.63), channel_id=1, source_target_pairs={{0,2},{2,0},{4,6},{6,4},{8,10},{10,8},{12,14},{14,12},{16,18},{18,... | collective-permute-start | bytes 491528 | tf_op jit(solution)/shard_map/ppermute | solution.py:120
  57.9 7.2 %collective-permute-start.21 = (f32[2,128,128]{2,1,0:T(8,128)S(1)}, f32[2,128,128]{2,1,0:T(8,128)S(1)}, u32[]{:S(2)}, u32[]{:S(2)}) collective-permute-start(f32[2,128,128]{2,1,0:T(8,128)S(1)} %get-tuple-element.67), channel_id=1, source_target_pairs={{2,4},{3,5},{6,8},{7,9},{10,12},{11,13},{14,16},{15,17},{18,20},{1... | collective-permute-start | bytes 393224 | tf_op jit(solution)/shard_map/ppermute | solution.py:117
  59.0 7.5 %collective-permute-start.22 = (f32[2,128,128]{2,1,0:T(8,128)S(1)}, f32[2,128,128]{2,1,0:T(8,128)S(1)}, u32[]{:S(2)}, u32[]{:S(2)}) collective-permute-start(f32[2,128,128]{2,1,0:T(8,128)S(1)} %get-tuple-element.68), channel_id=1, source_target_pairs={{2,4},{3,5},{6,8},{7,9},{10,12},{11,13},{14,16},{15,17},{18,20},{1... | collective-permute-start | bytes 393224 | tf_op jit(solution)/shard_map/ppermute | solution.py:117
  65.2 4.4 %collective-permute-start.23 = (f32[2,128,128]{2,1,0:T(8,128)S(1)}, f32[2,128,128]{2,1,0:T(8,128)S(1)}, u32[]{:S(2)}, u32[]{:S(2)}) collective-permute-start(f32[2,128,128]{2,1,0:T(8,128)S(1)} %shard_map.89.refs_3_), channel_id=1, source_target_pairs={{0,1},{1,0},{2,3},{3,2},{4,5},{5,4},{6,7},{7,6},{8,9},{9,8},{10,11... | collective-permute-start | bytes 393224 | tf_op jit(solution)/shard_map/ppermute | solution.py:105
